TPU v7x, 32 devices: a whole 2x2x4 slice. The times are simulated.
32 devices in a mesh: dp: 8 (over z, x), tensor: 4 (over y, core).
Axes of the slice: x: 2, y: 2, z: 4, core: 2. Of those that a mesh axis runs over, the one named last changes fastest.
Arguments:
- hidden_in: bfloat16 [16384, 768], P(('dp', 'tensor')), may hold values from -6 to 6
- w_qkv: bfloat16 [3, 768, 768], P(None, 'dp', 'tensor'), may hold values from -0.21875 to 0.21875
- b_qkv: bfloat16 [3, 768], P(None, 'tensor'), may hold values from -1.5 to 1.5
- w_out: bfloat16 [768, 768], P('tensor', 'dp'), may hold values from -3.5 to 3.5
- b_out: bfloat16 [768], P('dp'), may hold values from -1.5 to 1.5
- w_fc: bfloat16 [768, 3072], P('dp', 'tensor'), may hold values from -0.21875 to 0.21875
- b_fc: bfloat16 [3072], P('tensor'), may hold values from -2.5 to 2.5
- w_fc2: bfloat16 [3072, 768], P('tensor', 'dp'), may hold values from -0.109375 to 0.109375
- b_fc2: bfloat16 [768], P('dp'), may hold values from -1.5 to 1.5
- ln1_gain: bfloat16 [768], P('dp'), may hold values from 0.25 to 1.75
- ln1_bias: bfloat16 [768], P('dp'), may hold values from -1.5 to 1.5
- ln2_gain: bfloat16 [768], P('dp'), may hold values from 0.25 to 1.75
- ln2_bias: bfloat16 [768], P('dp'), may hold values from -1.5 to 1.5
- segment_ids: int32 [16384], P('dp'), may hold values from 0 to 24, as said below
- positions: int32 [16384], P('dp'), may hold values from 0 to 1533, as said below
- cotangent: bfloat16 [16384, 768], P(('dp', 'tensor')), may hold values from -6 to 6
Outputs:
- layer_out: bfloat16 [16384, 768], P(('dp', 'tensor'))
- d_hidden_in: bfloat16 [16384, 768], P(('dp', 'tensor'))
- d_w_qkv: float32 [3, 768, 768], P(None, 'dp', 'tensor')
- d_b_qkv: float32 [3, 768], P(None, 'tensor')
- d_w_out: float32 [768, 768], P('tensor', 'dp')
- d_b_out: float32 [768], P('dp')
- d_w_fc: float32 [768, 3072], P('dp', 'tensor')
- d_b_fc: float32 [3072], P('tensor')
- d_w_fc2: float32 [3072, 768], P('tensor', 'dp')
- d_b_fc2: float32 [768], P('dp')
- d_ln1_gain: float32 [768], P('dp')
- d_ln1_bias: float32 [768], P('dp')
- d_ln2_gain: float32 [768], P('dp')
- d_ln2_bias: float32 [768], P('dp')
Inputs may be any that keep to these rules, and one draw needn't show every extreme that they name: `segment_ids`: document numbers along the whole stream start at 0 and never fall; every document lies within the token ranges of two neighbouring blocks of 2048 tokens (blocks aligned from the stream's start), and every border between two such blocks lies inside a document. Of a document that crosses such a border, at most 767 tokens lie in the block before the border and at most as many in the block after it; some document has exactly that many on both sides. `positions`: A token's position counts from 0 at the first token of its document and rises by one per token.
All inputs are finite; a program needn't handle non-finite values.
Results may differ from a plain program's by a relative error of at most 0.0099.
Values may be sent and summed in bfloat16 or wider, within the bound.
No kernel may reach another device: no remote copies, remote signals or barrier semaphores. Data moves between devices by JAX's collectives and lax.ppermute only.
A program may use at most 192 MiB of HBM per device.

v0:
```python
import functools

import jax
import jax.numpy as jnp
from jax import lax
from jax.experimental import pallas as pl
from jax.experimental.pallas import tpu as pltpu
from jax.sharding import PartitionSpec as P

HEAD_DIM = 64
ROT = 16
BLK = 256
SLOTS = (0, 2, 1, 3)

norm_eps = 1e-05
big_negative = -1e30
rope_base = 10000.0
inv_sqrt_two = 0.7071067811865476
inv_sqrt_two_pi = 0.3989422804014327

f32 = jnp.float32
bf16 = jnp.bfloat16


def mm(a, b, ca, cb):
    return lax.dot_general(a, b, (((ca,), (cb,)), ((), ())), preferred_element_type=f32)


def params(**kw):
    return pltpu.CompilerParams(vmem_limit_bytes=56 * 1024 * 1024, **kw)


def cost(flops, moved, exps=0):
    return pl.CostEstimate(flops=int(flops), bytes_accessed=int(moved), transcendentals=int(exps))


def shaped(shape, dtype):
    return jax.ShapeDtypeStruct(shape, dtype)


def passed_along(block, axis, distance):
    devices = range(lax.axis_size(axis))
    route = [(i - distance, i) for i in devices if i - distance in devices]
    return lax.ppermute(block, axis, route)


def swapped(block, axis, bit):
    route = [(i, i ^ bit) for i in range(lax.axis_size(axis))]
    return lax.ppermute(block, axis, route)


def ring_order(n):
    return list(range(0, n, 2)) + list(range(n - 1, 0, -2))


def ring_gather(block, axis):
    n = lax.axis_size(axis)
    if n > 8:
        return [lax.all_gather(block, axis, axis=0, tiled=True)], jnp.zeros((1,), jnp.int32)
    ring = ring_order(n)
    ahead = [(ring[r], ring[(r + 1) % n]) for r in range(n)]
    behind = [(b, a) for a, b in ahead]
    table = []
    for device in range(n):
        at = ring.index(device)
        row = [device]
        for step in range(1, n // 2 + 1):
            row.append(ring[(at - step) % n])
            if step < n - step:
                row.append(ring[(at + step) % n])
        table.append(row)
    pieces = [block]
    from_left = from_right = block
    for step in range(1, n // 2 + 1):
        from_left = lax.ppermute(from_left, axis, ahead)
        pieces.append(from_left)
        if step < n - step:
            from_right = lax.ppermute(from_right, axis, behind)
            pieces.append(from_right)
    return pieces, jnp.asarray(table, jnp.int32)[lax.axis_index(axis)]


def gather_rows(block):
    far = swapped(block, "tensor", 2)
    near = swapped(block, "tensor", 1)
    both = swapped(far, "tensor", 1)
    return jnp.concatenate([block, far, near, both], axis=0)


def scatter_rows(keep, send):
    count = keep.shape[0] // 2
    came = swapped(send, "tensor", 1)
    other = (keep[count:].astype(f32) + came[count:].astype(f32)).astype(bf16)
    far = swapped(other, "tensor", 2)
    return keep[:count].astype(f32) + came[:count].astype(f32) + far.astype(f32)


def summed_over(vec, axis):
    n = lax.axis_size(axis)
    bit = 1
    while bit < n:
        vec = vec + swapped(vec, axis, bit)
        bit *= 2
    return vec


def assemble(piece_refs, owner_ref, out_ref):
    for n, ref in enumerate(piece_refs):
        rows = ref.shape[0]
        out_ref[pl.ds(pl.multiple_of(owner_ref[n] * rows, rows), rows), :] = ref[...]


def norm_rows(x):
    center = x - jnp.mean(x, axis=-1, keepdims=True)
    inv_std = lax.rsqrt(jnp.mean(center * center, axis=-1, keepdims=True) + norm_eps)
    return center * inv_std


def ff_kernel(pieces, owner_ref, x_ref, g_ref, b_ref, *refs):
    fc_refs, fc2_refs = refs[:pieces], refs[pieces : 2 * pieces]
    out_ref, u_ref, grads_ref, vec_ref, small_ref = refs[2 * pieces : 2 * pieces + 5]
    packed, fc2_w, fc_acc, fc2_acc = refs[2 * pieces + 5 :]
    step = pl.program_id(0)
    ff = fc2_w.shape[1]

    @pl.when(step == 0)
    def _():
        assemble(fc_refs, owner_ref, packed)
        assemble(fc2_refs, owner_ref, fc2_w)
        vec_ref[...] = packed[:, ff:].astype(f32).T[:8]
        fc_acc[...] = jnp.zeros_like(fc_acc)
        fc2_acc[...] = jnp.zeros_like(fc2_acc)
        small_ref[...] = jnp.zeros_like(small_ref)

    fc_w = packed[:, :ff]
    gain, shift = vec_ref[4:5, :], vec_ref[5:6, :]
    normed = norm_rows(x_ref[...].astype(f32))
    normed_two = (normed * gain + shift).astype(bf16)
    pre = mm(normed_two, fc_w, 1, 0) + b_ref[...]
    cdf = 0.5 + 0.5 * lax.erf(pre * inv_sqrt_two)
    act = (pre * cdf).astype(bf16)
    slope = cdf + pre * (jnp.exp(-0.5 * pre * pre) * inv_sqrt_two_pi)
    out_ref[...] = mm(act, fc2_w[...], 1, 1).astype(bf16)
    g = g_ref[...]
    pre_grad = (mm(g, fc2_w[...], 1, 0) * slope).astype(bf16)
    two_grad = mm(pre_grad, fc_w, 1, 1)
    u_ref[...] = (two_grad * gain).astype(bf16)
    fc_acc[...] += mm(normed_two, pre_grad, 0, 0)
    fc2_acc[...] += mm(g, act, 0, 0)
    small_ref[0:1, :] += jnp.sum(two_grad * normed, axis=0, keepdims=True)
    small_ref[1:2, :] += jnp.sum(two_grad, axis=0, keepdims=True)
    small_ref[2:3, :] += jnp.sum(g.astype(f32), axis=0, keepdims=True)
    small_ref[3:4, :] += jnp.sum(pre_grad.astype(f32), axis=0, keepdims=True)

    @pl.when(step == pl.num_programs(0) - 1)
    def _():
        grads_ref[:, :ff] = fc_acc[...].astype(bf16)
        grads_ref[:, ff:] = fc2_acc[...].astype(bf16)


def feed_forward(owner, x, g, b_fc, fc_pieces, fc2_pieces, ff):
    tokens, dim = x.shape
    rows = tokens // 4
    spec = pl.BlockSpec((rows, dim), lambda s, *_: (s, 0))
    whole = lambda shape: pl.BlockSpec(shape, lambda s, *_: (0, 0))
    return pl.pallas_call(
        functools.partial(ff_kernel, len(fc_pieces)),
        grid_spec=pltpu.PrefetchScalarGridSpec(
            num_scalar_prefetch=1,
            grid=(4,),
            in_specs=[spec, spec, whole((1, ff))] + [whole(p.shape) for p in fc_pieces + fc2_pieces],
            out_specs=[spec, spec, whole((dim, 2 * ff)), whole((8, dim)), whole((8, dim))],
            scratch_shapes=[
                pltpu.VMEM((dim, fc_pieces[0].shape[1]), bf16),
                pltpu.VMEM((dim, ff), bf16),
                pltpu.VMEM((dim, ff), f32),
                pltpu.VMEM((dim, ff), f32),
            ],
        ),
        out_shape=[
            shaped((tokens, dim), bf16),
            shaped((tokens, dim), bf16),
            shaped((dim, 2 * ff), bf16),
            shaped((8, dim), f32),
            shaped((8, dim), f32),
        ],
        compiler_params=params(),
        cost_estimate=cost(12 * tokens * dim * ff, 8 * tokens * dim + 8 * dim * ff, 2 * tokens * ff),
        name="feed_forward",
    )(owner, x, g, b_fc, *fc_pieces, *fc2_pieces)


def turned(x, cos_t, sin_t):
    half = ROT // 2
    out = []
    for h in range(x.shape[0] // HEAD_DIM):
        a = x[h * HEAD_DIM : h * HEAD_DIM + half]
        b = x[h * HEAD_DIM + half : h * HEAD_DIM + ROT]
        out += [a * cos_t - b * sin_t, b * cos_t + a * sin_t, x[h * HEAD_DIM + ROT : (h + 1) * HEAD_DIM]]
    return jnp.concatenate(out, axis=0)


def project_kernel(pieces, owner_ref, place_ref, x_ref, g_ref, vec_ref, b_ref, cos_ref, sin_ref, *refs):
    w_refs = refs[:pieces]
    normed_ref, q_ref, k_ref, v_ref, do_ref, wt_ref, packed = refs[pieces:]
    feat = q_ref.shape[0]

    @pl.when(pl.program_id(0) == 0)
    def _():
        assemble(w_refs, owner_ref, packed)
        wt_ref[...] = packed[...].astype(f32).T.astype(bf16)

    normed = norm_rows(x_ref[...].astype(f32))
    normed_one = (normed * vec_ref[2:3, :] + vec_ref[3:4, :]).astype(bf16)
    normed_ref[...] = normed_one
    proj = mm(wt_ref[: 3 * feat, :], normed_one, 1, 1) + b_ref[...]
    cos_t, sin_t = cos_ref[...], sin_ref[...]
    q_ref[...] = (turned(proj[:feat], cos_t, sin_t) * HEAD_DIM ** (-0.5)).astype(bf16)
    k_ref[...] = turned(proj[feat : 2 * feat], cos_t, sin_t).astype(bf16)
    v_ref[...] = proj[2 * feat :].astype(bf16)
    do_ref[...] = mm(wt_ref[3 * feat :, :], g_ref[...], 1, 1).astype(bf16)


def project(owner, places, x, g, vec, b_col, cos_t, sin_t, pieces, feat):
    tokens, dim = x.shape
    rows = tokens // 4
    spec = pl.BlockSpec((rows, dim), lambda s, *_: (s, 0))
    placed = lambda r: pl.BlockSpec((r, rows), lambda s, owner, place: (0, place[s]))
    whole = lambda shape: pl.BlockSpec(shape, lambda s, *_: (0, 0))
    width = pieces[0].shape[1]
    return pl.pallas_call(
        functools.partial(project_kernel, len(pieces)),
        grid_spec=pltpu.PrefetchScalarGridSpec(
            num_scalar_prefetch=2,
            grid=(4,),
            in_specs=[spec, spec, whole(vec.shape), whole(b_col.shape), placed(ROT // 2), placed(ROT // 2)]
            + [whole(p.shape) for p in pieces],
            out_specs=[spec, placed(feat), placed(feat), placed(feat), placed(feat), whole((width, dim))],
            scratch_shapes=[pltpu.VMEM((dim, width), bf16)],
        ),
        out_shape=[shaped((tokens, dim), bf16)]
        + [shaped((feat, tokens), bf16)] * 4
        + [shaped((width, dim), bf16)],
        compiler_params=params(),
        cost_estimate=cost(8 * tokens * dim * feat, 6 * tokens * dim + 4 * dim * width),
        name="project",
    )(owner, places, x, g, vec, b_col, cos_t, sin_t, *pieces)


def key_mask(chunk, lo_row, hi_row, shape):
    idx = chunk * BLK + lax.broadcasted_iota(jnp.int32, shape, 0)
    return (idx >= lo_row) & (idx <= hi_row)


def attn_fwd_kernel(heads, halo, first_ref, q_ref, k_ref, v_ref, left_ref, lo_ref, o_ref, lse_ref, keys, values):
    i = pl.program_id(0)
    first = first_ref[i]
    last = i + halo // BLK
    feat = k_ref.shape[0]

    @pl.when(i == 0)
    def _():
        keys[:, :halo] = left_ref[:feat, :]
        keys[:, halo:] = k_ref[...]
        values[:, :halo] = left_ref[feat:, :]
        values[:, halo:] = v_ref[...]

    lo_row = lo_ref[...]
    hi_row = halo + i * BLK + lax.broadcasted_iota(jnp.int32, (1, BLK), 1)

    def step(c, carry):
        cols = pl.ds(pl.multiple_of(c * BLK, BLK), BLK)
        ok = key_mask(c, lo_row, hi_row, (BLK, BLK))
        out = []
        for h in range(heads):
            top, total, acc = carry[h]
            feats = pl.ds(h * HEAD_DIM, HEAD_DIM)
            s = mm(keys[feats, cols], q_ref[feats, :], 0, 0)
            s = jnp.where(ok, s, big_negative)
            new_top = jnp.maximum(top, jnp.max(s, axis=0, keepdims=True))
            kept = jnp.exp(top - new_top)
            p = jnp.exp(s - new_top)
            total = total * kept + jnp.sum(p, axis=0, keepdims=True)
            acc = acc * kept + mm(values[feats, cols], p.astype(bf16), 1, 0)
            out.append((new_top, total, acc))
        return tuple(out)

    start = tuple(
        (
            jnp.full((1, BLK), big_negative, f32),
            jnp.zeros((1, BLK), f32),
            jnp.zeros((HEAD_DIM, BLK), f32),
        )
        for _ in range(heads)
    )
    done = lax.fori_loop(first, last + 1, step, start)
    for h in range(heads):
        top, total, acc = done[h]
        o_ref[pl.ds(h * HEAD_DIM, HEAD_DIM), :] = (acc / total).astype(bf16)
        lse_ref[pl.ds(h, 1), :] = top + jnp.log(total)


def attention_forward(first, q, k, v, left, lo, halo):
    feat, tokens = q.shape
    heads = feat // HEAD_DIM
    col = lambda i, *_: (0, i)
    whole = lambda shape: pl.BlockSpec(shape, lambda i, *_: (0, 0))
    q_spec = pl.BlockSpec((feat, BLK), col)
    return pl.pallas_call(
        functools.partial(attn_fwd_kernel, heads, halo),
        grid_spec=pltpu.PrefetchScalarGridSpec(
            num_scalar_prefetch=1,
            grid=(tokens // BLK,),
            in_specs=[q_spec, whole(k.shape), whole(v.shape), whole(left.shape), pl.BlockSpec((1, BLK), col)],
            out_specs=[q_spec, pl.BlockSpec((8, BLK), col)],
            scratch_shapes=[pltpu.VMEM((feat, halo + tokens), bf16)] * 2,
        ),
        out_shape=[shaped((feat, tokens), bf16), shaped((8, tokens), f32)],
        compiler_params=params(),
        cost_estimate=cost(16 * feat * tokens * 1024, 8 * feat * tokens, heads * tokens * 1024),
        name="attention_forward",
    )(first, q, k, v, left, lo)


def attn_bwd_step(heads, c, base, q_ref, k_ref, v_ref, do_ref, lse_ref, lo_row, hi_row, deltas, dq_ref, dk_ref, dv_ref):
    cols = pl.ds(pl.multiple_of((c - base) * BLK, BLK), BLK)
    ok = key_mask(c, lo_row, hi_row, (BLK, BLK))
    for h in range(heads):
        feats = pl.ds(h * HEAD_DIM, HEAD_DIM)
        s = mm(k_ref[feats, cols], q_ref[feats, :], 0, 0)
        p = jnp.exp(jnp.where(ok, s, big_negative) - lse_ref[pl.ds(h, 1), :])
        dp = mm(v_ref[feats, cols], do_ref[feats, :], 0, 0)
        ds = (p * (dp - deltas[h])).astype(bf16)
        dv_ref[feats, cols] += mm(do_ref[feats, :], p.astype(bf16), 1, 1)
        dk_ref[feats, cols] += mm(q_ref[feats, :], ds, 1, 1)
        dq_ref[feats, :] += mm(k_ref[feats, cols], ds, 1, 0)


def row_deltas(heads, o_ref, do_ref):
    deltas = []
    for h in range(heads):
        feats = pl.ds(h * HEAD_DIM, HEAD_DIM)
        prod = do_ref[feats, :].astype(f32) * o_ref[feats, :].astype(f32)
        deltas.append(jnp.sum(prod, axis=0, keepdims=True))
    return deltas


def halo_bwd_kernel(heads, halo, first_ref, q_ref, left_ref, lo_ref, o_ref, lse_ref, do_ref, dq_ref, back_ref, dk, dv):
    i = pl.program_id(0)
    feat = q_ref.shape[0]

    @pl.when(i == 0)
    def _():
        dk[...] = jnp.zeros_like(dk)
        dv[...] = jnp.zeros_like(dv)

    lo_row = lo_ref[...]
    hi_row = jnp.full((1, BLK), halo, jnp.int32)
    dq_ref[...] = jnp.zeros_like(dq_ref)
    deltas = row_deltas(heads, o_ref, do_ref)
    k_ref, v_ref = left_ref.at[:feat, :], left_ref.at[feat:, :]

    def step(c, carry):
        attn_bwd_step(
            heads, c, 0, q_ref, k_ref, v_ref, do_ref, lse_ref, lo_row, hi_row, deltas, dq_ref, dk, dv
        )
        return carry

    lax.fori_loop(first_ref[i], halo // BLK, step, 0)

    @pl.when(i == pl.num_programs(0) - 1)
    def _():
        back_ref[:feat, :] = dk[...].astype(bf16)
        back_ref[feat:, :] = dv[...].astype(bf16)


def own_bwd_kernel(
    heads, halo, first_ref, q_ref, k_ref, v_ref, lo_ref, o_ref, lse_ref, do_ref, part_ref, dq_ref, dk_ref, dv_ref
):
    i = pl.program_id(0)
    base = halo // BLK

    @pl.when(i == 0)
    def _():
        dk_ref[...] = jnp.zeros_like(dk_ref)
        dv_ref[...] = jnp.zeros_like(dv_ref)

    @pl.when(i < base)
    def _():
        dq_ref[...] = part_ref[...]

    @pl.when(i >= base)
    def _():
        dq_ref[...] = jnp.zeros_like(dq_ref)

    lo_row = lo_ref[...]
    hi_row = halo + i * BLK + lax.broadcasted_iota(jnp.int32, (1, BLK), 1)
    deltas = row_deltas(heads, o_ref, do_ref)

    def step(c, carry):
        attn_bwd_step(
            heads, c, base, q_ref, k_ref, v_ref, do_ref, lse_ref, lo_row, hi_row, deltas, dq_ref, dk_ref, dv_ref
        )
        return carry

    lax.fori_loop(jnp.maximum(first_ref[i], base), i + base + 1, step, 0)
    dq_ref[...] = dq_ref[...] * HEAD_DIM ** (-0.5)


def attention_backward(first, q, k, v, left, lo, o, lse, do, halo):
    feat, tokens = q.shape
    heads = feat // HEAD_DIM
    col = lambda i, *_: (0, i)
    whole = lambda shape: pl.BlockSpec(shape, lambda i, *_: (0, 0))
    q_spec = pl.BlockSpec((feat, BLK), col)
    lo_spec = pl.BlockSpec((1, BLK), col)
    lse_spec = pl.BlockSpec((8, BLK), col)
    dq_part, back = pl.pallas_call(
        functools.partial(halo_bwd_kernel, heads, halo),
        grid_spec=pltpu.PrefetchScalarGridSpec(
            num_scalar_prefetch=1,
            grid=(halo // BLK,),
            in_specs=[q_spec, whole(left.shape), lo_spec, q_spec, lse_spec, q_spec],
            out_specs=[q_spec, whole(left.shape)],
            scratch_shapes=[pltpu.VMEM((feat, halo), f32)] * 2,
        ),
        out_shape=[shaped((feat, halo), f32), shaped(left.shape, bf16)],
        compiler_params=params(),
        cost_estimate=cost(20 * feat * halo * 512, 20 * feat * halo, heads * halo * 512),
        name="attention_backward_left",
    )(first, q, left, lo, o, lse, do)
    back = passed_along(back, "dp", -1)
    part_spec = pl.BlockSpec((feat, BLK), lambda i, *_: (0, jnp.minimum(i, halo // BLK - 1)))
    dq, dk, dv = pl.pallas_call(
        functools.partial(own_bwd_kernel, heads, halo),
        grid_spec=pltpu.PrefetchScalarGridSpec(
            num_scalar_prefetch=1,
            grid=(tokens // BLK,),
            in_specs=[
                q_spec,
                whole(k.shape),
                whole(v.shape),
                lo_spec,
                q_spec,
                lse_spec,
                q_spec,
                part_spec,
            ],
            out_specs=[q_spec, whole(k.shape), whole(v.shape)],
        ),
        out_shape=[shaped((feat, tokens), f32)] * 3,
        compiler_params=params(),
        cost_estimate=cost(40 * feat * tokens * 1024, 20 * feat * tokens, heads * tokens * 1024),
        name="attention_backward_own",
    )(first, q, k, v, lo, o, lse, do, dq_part)
    return dq, dk, dv, back


def keep_send_specs(rows, dim):
    keep = pl.BlockSpec((rows, dim), lambda s, *_: (jnp.minimum(s, 1), 0))
    send = pl.BlockSpec((rows, dim), lambda s, *_: (jnp.maximum(s - 2, 0), 0))
    return keep, send


def put_rows(keep_ref, send_ref, value):
    s = pl.program_id(0)

    @pl.when(s < 2)
    def _():
        keep_ref[...] = value

    @pl.when(s >= 2)
    def _():
        send_ref[...] = value


def out_kernel(place_ref, o_ref, ff_ref, w_ref, keep_ref, send_ref):
    total = mm(o_ref[...], w_ref[...], 0, 0) + ff_ref[...].astype(f32)
    put_rows(keep_ref, send_ref, total.astype(bf16))


def branch_out(places, o, ff_out, out_w):
    feat, tokens = o.shape
    dim = out_w.shape[1]
    rows = tokens // 4
    keep, send = keep_send_specs(rows, dim)
    return pl.pallas_call(
        out_kernel,
        grid_spec=pltpu.PrefetchScalarGridSpec(
            num_scalar_prefetch=1,
            grid=(4,),
            in_specs=[
                pl.BlockSpec((feat, rows), lambda s, place: (0, place[s])),
                pl.BlockSpec((rows, dim), lambda s, *_: (s, 0)),
                pl.BlockSpec((feat, dim), lambda s, *_: (0, 0)),
            ],
            out_specs=[keep, send],
        ),
        out_shape=[shaped((tokens // 2, dim), bf16)] * 2,
        compiler_params=params(),
        cost_estimate=cost(2 * feat * tokens * dim, 4 * tokens * dim),
        name="branch_out",
    )(places, o, ff_out, out_w)


def tail_kernel(
    halo,
    place_ref,
    chunk_ref,
    dq_ref,
    dk_ref,
    dv_ref,
    back_ref,
    o_ref,
    x_ref,
    g_ref,
    n1_ref,
    u2_ref,
    wt_ref,
    vec_ref,
    cos_ref,
    sin_ref,
    keep_ref,
    send_ref,
    wkeep_ref,
    wsend_ref,
    small_ref,
    bias_ref,
    acc,
    late,
):
    s = pl.program_id(0)
    feat, rows = dq_ref.shape
    tokens = late.shape[1]

    @pl.when(s == 0)
    def _():
        late[:, : tokens - halo] = jnp.zeros((2 * feat, tokens - halo), bf16)
        late[:, tokens - halo :] = back_ref[...]
        acc[...] = jnp.zeros_like(acc)
        small_ref[...] = jnp.zeros_like(small_ref)
        bias_ref[...] = jnp.zeros_like(bias_ref)

    cols = pl.ds(pl.multiple_of(place_ref[s] * rows, rows), rows)
    cos_t, sin_t = cos_ref[...], -sin_ref[...]
    dq = turned(dq_ref[...], cos_t, sin_t)
    dk = turned(dk_ref[...] + late[:feat, cols].astype(f32), cos_t, sin_t)
    dv = dv_ref[...] + late[feat:, cols].astype(f32)
    grad = jnp.concatenate([dq, dk, dv], axis=0).astype(bf16)
    bias_ref[...] += jnp.sum(grad.astype(f32), axis=1, keepdims=True)
    one_grad = mm(grad, wt_ref[: 3 * feat, :], 0, 0)
    put_rows(keep_ref, send_ref, (one_grad * vec_ref[2:3, :] + u2_ref[...].astype(f32)).astype(bf16))
    acc[: 3 * feat, :] += mm(grad, n1_ref[...], 1, 0)
    acc[3 * feat :, :] += mm(o_ref[...], g_ref[...], 1, 0)
    normed = norm_rows(x_ref[...].astype(f32))
    small_ref[0:1, :] += jnp.sum(one_grad * normed, axis=0, keepdims=True)
    small_ref[1:2, :] += jnp.sum(one_grad, axis=0, keepdims=True)

    @pl.when(s == pl.num_programs(0) - 1)
    def _():
        acc_t = acc[...].T
        acc[...] = acc_t
        count = wkeep_ref.shape[0]
        parts = chunk_ref.shape[0] // 2
        size = count // parts
        for n in range(parts):
            at = pl.ds(pl.multiple_of(chunk_ref[n] * size, size), size)
            wkeep_ref[n * size : (n + 1) * size, :] = acc[at, :].astype(bf16)
            at = pl.ds(pl.multiple_of(chunk_ref[parts + n] * size, size), size)
            wsend_ref[n * size : (n + 1) * size, :] = acc[at, :].astype(bf16)


def tail(places, chunks, dq, dk, dv, back, o, x, g, n1, u2, wt, vec, cos_t, sin_t, halo):
    feat, tokens = dq.shape
    dim = x.shape[1]
    width = wt.shape[0]
    rows = tokens // 4
    spec = pl.BlockSpec((rows, dim), lambda s, *_: (s, 0))
    placed = lambda r: pl.BlockSpec((r, rows), lambda s, place, chunk: (0, place[s]))
    whole = lambda shape: pl.BlockSpec(shape, lambda s, *_: (0, 0))
    keep, send = keep_send_specs(rows, dim)
    return pl.pallas_call(
        functools.partial(tail_kernel, halo),
        grid_spec=pltpu.PrefetchScalarGridSpec(
            num_scalar_prefetch=2,
            grid=(4,),
            in_specs=[placed(feat)] * 3
            + [whole(back.shape), placed(feat), spec, spec, spec, spec, whole(wt.shape), whole(vec.shape)]
            + [placed(ROT // 2)] * 2,
            out_specs=[
                keep,
                send,
                whole((dim // 2, width)),
                whole((dim // 2, width)),
                whole((8, dim)),
                whole((3 * feat, 1)),
            ],
            scratch_shapes=[pltpu.VMEM((width, dim), f32), pltpu.VMEM((2 * feat, tokens), bf16)],
        ),
        out_shape=[shaped((tokens // 2, dim), bf16)] * 2
        + [shaped((dim // 2, width), bf16)] * 2
        + [shaped((8, dim), f32), shaped((3 * feat, 1), f32)],
        compiler_params=params(),
        cost_estimate=cost(14 * feat * tokens * dim, 14 * tokens * dim + 6 * dim * width),
        name="tail",
    )(places, chunks, dq, dk, dv, back, o, x, g, n1, u2, wt, vec, cos_t, sin_t)


def rope_tables(positions):
    freq_idx = jnp.arange(0, ROT, 2, dtype=f32)
    inverse = rope_base ** (-freq_idx / ROT)
    angles = inverse[:, None] * positions.astype(f32)[None, :]
    return jnp.cos(angles), jnp.sin(angles)


def late_chunks():
    n = lax.axis_size("dp")
    rank = lax.axis_index("dp")
    if n > 8:
        return jnp.arange(2, dtype=jnp.int32)
    mine = jnp.stack([rank ^ (2 * k) for k in range(n // 2)])
    return jnp.concatenate([mine, mine ^ 1]).astype(jnp.int32)


def late_scatter(keep, send):
    n = lax.axis_size("dp")
    if n > 8:
        whole = jnp.concatenate([keep, send], axis=0)
        return lax.psum_scatter(whole, "dp", scatter_dimension=0, tiled=True).astype(f32)
    size = keep.shape[0] * 2 // n
    total = keep.astype(f32) + swapped(send, "dp", 1).astype(f32)
    low = total.astype(bf16)
    own = total[:size]
    for k in range(1, n // 2):
        own = own + swapped(low[k * size : (k + 1) * size], "dp", 2 * k).astype(f32)
    return own


def body(
    hidden_in,
    w_qkv,
    b_qkv,
    w_out,
    b_out,
    w_fc,
    b_fc,
    w_fc2,
    b_fc2,
    ln1_gain,
    ln1_bias,
    ln2_gain,
    ln2_bias,
    segment_ids,
    positions,
    cotangent,
):
    local_dim = w_qkv.shape[2]
    ff = w_fc.shape[1]
    own_dims = w_fc.shape[0]
    seq_len = positions.shape[0]
    halo = seq_len * 3 // 8
    qkv_dim = 3 * local_dim
    rank = lax.axis_index("tensor")
    places = jnp.stack([rank ^ at for at in SLOTS]).astype(jnp.int32)

    vectors = jnp.stack([b_out, b_fc2, ln1_gain, ln1_bias, ln2_gain, ln2_bias], axis=1)
    vectors = jnp.pad(vectors, ((0, 0), (0, 122)))
    first_block = jnp.concatenate([w_fc, vectors], axis=1)
    third_block = jnp.concatenate(
        [jnp.transpose(w_qkv, (1, 0, 2)).reshape(own_dims, qkv_dim), w_out.T], axis=1
    )
    x_all = gather_rows(hidden_in)
    fc_pieces, owner = ring_gather(first_block, "dp")
    fc2_pieces, _ = ring_gather(w_fc2.T, "dp")
    g_all = gather_rows(cotangent)
    attn_pieces, _ = ring_gather(third_block, "dp")

    cos_t, sin_t = rope_tables(positions)
    lo = halo + jnp.arange(seq_len, dtype=jnp.int32) - positions
    first = lo[::BLK] // BLK
    lo_row = lo.reshape(1, seq_len)

    ff_out, u_two, ff_grads, vec, ff_small = feed_forward(
        owner, x_all, g_all, b_fc.astype(f32).reshape(1, ff), fc_pieces, fc2_pieces, ff
    )
    ff_own = lax.psum_scatter(ff_grads, "dp", scatter_dimension=0, tiled=True).astype(f32)

    normed_one, q, k, v, do, wt = project(
        owner, places, x_all, g_all, vec, b_qkv.astype(f32).reshape(qkv_dim, 1), cos_t, sin_t, attn_pieces, local_dim
    )
    left = passed_along(jnp.concatenate([k[:, -halo:], v[:, -halo:]], axis=0), "dp", 1)
    o, lse = attention_forward(first, q, k, v, left, lo_row, halo)
    summed = scatter_rows(*branch_out(places, o, ff_out, wt[qkv_dim:]))
    layer_out = (hidden_in.astype(f32) + summed + vec[0] + vec[1]).astype(bf16)

    dq, dk, dv, back = attention_backward(first, q, k, v, left, lo_row, o, lse, do, halo)
    u_keep, u_send, w_keep, w_send, one_small, qkv_bias = tail(
        places, late_chunks(), dq, dk, dv, back, o, x_all, g_all, normed_one, u_two, wt, vec, cos_t, sin_t, halo
    )
    late_own = late_scatter(w_keep, w_send)
    both = scatter_rows(u_keep, u_send)
    normed_own = hidden_in.astype(f32)
    normed_own = normed_own - jnp.mean(normed_own, axis=-1, keepdims=True)
    inv_own = lax.rsqrt(jnp.mean(normed_own * normed_own, axis=-1, keepdims=True) + norm_eps)
    normed_own = normed_own * inv_own
    input_grad = cotangent.astype(f32) + inv_own * (
        both
        - jnp.mean(both, axis=-1, keepdims=True)
        - normed_own * jnp.mean(both * normed_own, axis=-1, keepdims=True)
    )

    width = x_all.shape[1]
    dp_rank = lax.axis_index("dp")
    two_rows = summed_over(ff_small[:2], "tensor")
    early = summed_over(jnp.concatenate([two_rows, ff_small[2:4]], axis=0), "dp")
    one_rows = summed_over(one_small[:2], "tensor")
    qkv_rows = jnp.pad(qkv_bias[:, 0], (0, -qkv_dim % width)).reshape(-1, width)
    last = summed_over(jnp.concatenate([one_rows, qkv_rows], axis=0), "dp")
    own_early = lax.dynamic_slice_in_dim(early[:3], dp_rank * own_dims, own_dims, 1)
    own_late = lax.dynamic_slice_in_dim(last[:2], dp_rank * own_dims, own_dims, 1)
    qkv_b_total = last[2:].reshape(-1)[:qkv_dim].reshape(3, local_dim)
    return (
        layer_out,
        input_grad.astype(bf16),
        jnp.transpose(late_own[:, :qkv_dim].reshape(own_dims, 3, local_dim), (1, 0, 2)),
        qkv_b_total,
        late_own[:, qkv_dim:].T,
        own_early[2],
        ff_own[:, :ff],
        early[3],
        ff_own[:, ff:].T,
        own_early[2],
        own_late[0],
        own_late[1],
        own_early[0],
        own_early[1],
    )


def solution(mesh):
    in_specs = (
        P(("dp", "tensor"), None),
        P(None, "dp", "tensor"),
        P(None, "tensor"),
        P("tensor", "dp"),
        P("dp"),
        P("dp", "tensor"),
        P("tensor"),
        P("tensor", "dp"),
        P("dp"),
        P("dp"),
        P("dp"),
        P("dp"),
        P("dp"),
        P("dp"),
        P("dp"),
        P(("dp", "tensor"), None),
    )
    out_specs = (
        P(("dp", "tensor"), None),
        P(("dp", "tensor"), None),
        P(None, "dp", "tensor"),
        P(None, "tensor"),
        P("tensor", "dp"),
        P("dp"),
        P("dp", "tensor"),
        P("tensor"),
        P("tensor", "dp"),
        P("dp"),
        P("dp"),
        P("dp"),
        P("dp"),
        P("dp"),
    )
    return jax.shard_map(body, mesh=mesh, in_specs=in_specs, out_specs=out_specs, check_vma=False)
```

profile of v0, /device:TPU:16, one launch (start us, length us, event | category | flops | bytes accessed | tf_op | source)
XLA Modules:
  0.0 317.1 jit_solution(10313853205421204589)
XLA Ops:
  10.2 1.6 collective-permute-start.20
  12.2 1.5 collective-permute-start.3
  17.4 1.6 collective-permute-start.13
  19.5 1.6 collective-permute-start.6
  21.1 2.6 collective-permute-done.13.refs_9_
  25.7 4.0 %collective-permute-done.23.refs_4_ = bf16[96,768]{1,0:T(8,128)(2,1)S(1)} collective-permute-done((bf16[96,768]{1,0:T(8,128)(2,1)}, bf16[96,768]{1,0:T(8,128)(2,1)S(1)}, u32[]{:S(2)}, u32[]{:S(2)}) %collective-permute-start.23) | collective-permute-done | bytes 147488 | tf_op jit(solution)/shard_map/ppermute | solution.py:78
  29.7 1.6 collective-permute-start.22
  31.3 3.8 %collective-permute-done.22.refs_3_ = bf16[96,768]{1,0:T(8,128)(2,1)S(1)} collective-permute-done((bf16[96,768]{1,0:T(8,128)(2,1)}, bf16[96,768]{1,0:T(8,128)(2,1)S(1)}, u32[]{:S(2)}, u32[]{:S(2)}) %collective-permute-start.22) | collective-permute-done | bytes 147488 | tf_op jit(solution)/shard_map/ppermute | solution.py:75
  37.0 10.7 %collective-permute-done = bf16[512,768]{1,0:T(8,128)(2,1)S(1)} collective-permute-done((bf16[512,768]{1,0:T(8,128)(2,1)}, bf16[512,768]{1,0:T(8,128)(2,1)S(1)}, u32[]{:S(2)}, u32[]{:S(2)}) %collective-permute-start) | collective-permute-done | bytes 786464 | tf_op jit(solution)/shard_map/ppermute | solution.py:49
  48.9 1.6 collective-permute-start.15
  52.8 2.7 collective-permute-done.15.refs_11_
  55.5 1.6 collective-permute-start.8
  58.1 3.4 %collective-permute-done.8.refs_3_ = bf16[96,896]{1,0:T(8,128)(2,1)S(1)} collective-permute-done((bf16[96,896]{1,0:T(8,128)(2,1)S(1)}, bf16[96,896]{1,0:T(8,128)(2,1)S(1)}, u32[]{:S(2)}, u32[]{:S(2)}) %collective-permute-start.8) | collective-permute-done | bytes 172064 | tf_op jit(solution)/shard_map/ppermute | solution.py:75
  61.9 1.7 collective-permute-start.17
  63.6 1.6 collective-permute-start.10
  65.1 2.1 constant_dynamic-update-slice_fusion.5
  68.5 1.6 collective-permute-start.24
  71.0 2.2 collective-permute-start.11
  73.3 1.6 collective-permute-start.12
  74.8 2.1 constant_dynamic-update-slice_fusion.4.g_ref
  78.8 2.1 collective-permute-start.26
  82.5 22.9 %feed_forward.1 = (bf16[2048,768]{1,0:T(8,128)(2,1)}, bf16[2048,768]{1,0:T(8,128)(2,1)}, bf16[768,1536]{1,0:T(8,128)(2,1)}, f32[8,768]{1,0:T(8,128)}, f32[8,768]{1,0:T(8,128)}) custom-call(s32[8]{0:T(128)} %fusion.18.owner_ref, bf16[2048,768]{1,0:T(8,128)(2,1)} %copy-done.1, bf16[2048,768]{1,0:T(8,128)(2,1)} %constant_dynamic-update-slice_fusion.4.g_ref, ...), custom_call_target="tpu_custom_call" | custom-call | flops 14495514624 | bytes 17301504 | tf_op jit(solution)/shard_map/feed_forward/pallas_call | solution.py:166
  106.9 10.5 %project.1 = (bf16[2048,768]{1,0:T(8,128)(2,1)}, bf16[192,2048]{1,0:T(8,128)(2,1)}, bf16[192,2048]{1,0:T(8,128)(2,1)}, bf16[192,2048]{1,0:T(8,128)(2,1)}, bf16[1...) custom-call(s32[8]{0:T(128)} %fusion.18.owner_ref, s32[4]{0:T(128)} %pad_add_fusion.place_ref, bf16[2048,768]{1,0:T(8,128)(2,1)} %copy-done.1, ...), custom_call_target="tpu_custom_call" | custom-call | flops 2415919104 | bytes 11796480 | tf_op jit(solution)/shard_map/project/pallas_call | solution.py:231
  119.4 1.6 collective-permute-start.43
  121.0 5.1 %collective-permute-start.27 = (bf16[384,768]{1,0:T(8,128)(2,1)S(1)}, bf16[384,768]{1,0:T(8,128)(2,1)S(1)}, u32[]{:S(2)}, u32[]{:S(2)}) collective-permute-start(bf16[384,768]{1,0:T(8,128)(2,1)S(1)} %pad_maximum_fusion), channel_id=1, source_target_pairs={{0,4},{4,8},{8,12},{12,16},{16,20},{20,24},{24,28},{1,5},{5,9},{9,... | collective-permute-start | bytes 1769480 | tf_op jit(solution)/shard_map/ppermute | solution.py:44
  126.9 13.6 %collective-permute-done.44 = f32[4,768]{1,0:T(4,128)S(1)} collective-permute-done((f32[4,768]{1,0:T(4,128)S(1)}, f32[4,768]{1,0:T(4,128)S(1)}, u32[]{:S(2)}, u32[]{:S(2)}) %collective-permute-start.44) | collective-permute-done | bytes 12320 | tf_op jit(solution)/shard_map/ppermute | solution.py:49
  142.4 1.9 collective-permute-done.45
  145.2 26.1 %attention_forward.1 = (bf16[192,2048]{1,0:T(8,128)(2,1)}, f32[8,2048]{1,0:T(8,128)}) custom-call(s32[8]{0:T(128)} %and_select_fusion.first_ref, bf16[192,2048]{1,0:T(8,128)(2,1)} %get-tuple-element.41.q_ref, bf16[192,2048]{1,0:T(8,128)(2,1)} %get-tuple-element.42.k_ref, bf16[192,2048]{1,0:T(8,128)(2,1)} %get-tuple-element.43.v_ref, ...), custom_call_target="tpu_custom_call" | custom-call | flops 6442450944 | bytes 3145728 | tf_op jit(solution)/shard_map/attention_forward/pallas_call | solution.py:309
  171.2 7.0 %attention_backward_left.1 = (f32[192,768]{1,0:T(8,128)}, bf16[384,768]{1,0:T(8,128)(2,1)}) custom-call(s32[8]{0:T(128)} %and_select_fusion.first_ref, bf16[192,2048]{1,0:T(8,128)(2,1)} %get-tuple-element.41.q_ref, bf16[384,768]{1,0:T(8,128)(2,1)} %copy-done.21, s32[1,2048]{1,0:T(1,128)} %bitcast.45, bf16[192,2048]{1,0:T(8,128)(2,1)} %get-tuple-element.44.o_ref, ...), custom_call_target="tpu_custom_call" | custom-call | flops 1509949440 | bytes 2949120 | tf_op jit(solution)/shard_map/attention_backward_left/pallas_call | solution.py:418
  178.2 13.3 %collective-permute-start.30 = (bf16[384,768]{1,0:T(8,128)(2,1)}, bf16[384,768]{1,0:T(8,128)(2,1)S(1)}, u32[]{:S(2)}, u32[]{:S(2)}) collective-permute-start(bf16[384,768]{1,0:T(8,128)(2,1)} %get-tuple-element.55), channel_id=1, source_target_pairs={{4,0},{8,4},{12,8},{16,12},{20,16},{24,20},{28,24},{5,1},{9,5},{13... | collective-permute-start | bytes 1769480 | tf_op jit(solution)/shard_map/ppermute | solution.py:44
  191.4 23.4 %attention_backward_own.1 = (f32[192,2048]{1,0:T(8,128)}, f32[192,2048]{1,0:T(8,128)}, f32[192,2048]{1,0:T(8,128)}) custom-call(s32[8]{0:T(128)} %and_select_fusion.first_ref, bf16[192,2048]{1,0:T(8,128)(2,1)} %get-tuple-element.41.q_ref, bf16[192,2048]{1,0:T(8,128)(2,1)} %get-tuple-element.42.k_ref, bf16[192,2048]{1,0:T(8,128)(2,1)} %get-tuple-element.43.v_ref, ...), custom_call_target="tpu_custom_call" | custom-call | flops 16106127360 | bytes 7864320 | tf_op jit(solution)/shard_map/attention_backward_own/pallas_call | solution.py:434
  215.6 16.8 %tail.1 = (bf16[1024,768]{1,0:T(8,128)(2,1)}, bf16[1024,768]{1,0:T(8,128)(2,1)}, bf16[384,768]{1,0:T(8,128)(2,1)}, bf16[384,768]{1,0:T(8,128)(2,1)}, f32[8,768]{1,0:T(8,128)}, /*index=5*/f32[576,1]{1,0:T(8,128)}) custom-call(s32[4]{0:T(128)} %pad_add_fusion.place_ref, s32[8]{0:T(128)} %concatenate.30.chunk_ref, f32[192,2048]{1,0:T(8,128)} %get-tuple-element.52.dq_ref, ...), custom_call_target="tpu_custom_call" | custom-call | flops 4227858432 | bytes 25559040 | tf_op jit(solution)/shard_map/tail/pallas_call | solution.py:582
  234.0 1.7 slice.109.w_ref
  238.8 1.9 collective-permute-done.38
  240.8 6.4 %branch_out.1 = (bf16[1024,768]{1,0:T(8,128)(2,1)}, bf16[1024,768]{1,0:T(8,128)(2,1)}) custom-call(s32[4]{0:T(128)} %pad_add_fusion.place_ref, bf16[192,2048]{1,0:T(8,128)(2,1)} %get-tuple-element.44.o_ref, bf16[2048,768]{1,0:T(8,128)(2,1)} %get-tuple-element.45.ff_ref, bf16[192,768]{1,0:T(8,128)(2,1)} %slice.109.w_ref), custom_call_target="tpu_custom_call" | custom-call | flops 603979776 | bytes 6291456 | tf_op jit(solution)/shard_map/branch_out/pallas_call | solution.py:487
  247.1 2.1 collective-permute-start.33
  249.8 3.2 collective-permute-done.40
  253.6 4.0 %collective-permute-done.41 = f32[3,768]{1,0:T(4,128)S(1)} collective-permute-done((f32[3,768]{1,0:T(4,128)S(1)}, f32[3,768]{1,0:T(4,128)S(1)}, u32[]{:S(2)}, u32[]{:S(2)}) %collective-permute-start.41) | collective-permute-done | bytes 9248 | tf_op jit(solution)/shard_map/ppermute | solution.py:49
  258.9 4.6 %collective-permute-done.33 = bf16[384,768]{1,0:T(8,128)(2,1)} collective-permute-done((bf16[384,768]{1,0:T(8,128)(2,1)}, bf16[384,768]{1,0:T(8,128)(2,1)}, u32[]{:S(2)}, u32[]{:S(2)}) %collective-permute-start.33) | collective-permute-done | bytes 589856 | tf_op jit(solution)/shard_map/ppermute | solution.py:49
  264.9 2.3 add_convert_fusion
  267.9 4.3 %collective-permute-start.35 = (bf16[96,768]{1,0:T(8,128)(2,1)S(1)}, bf16[96,768]{1,0:T(8,128)(2,1)S(1)}, u32[]{:S(2)}, u32[]{:S(2)}) collective-permute-start(bf16[96,768]{1,0:T(8,128)(2,1)S(1)} %get-tuple-element.118), channel_id=1, source_target_pairs={{0,16},{4,20},{8,24},{12,28},{16,0},{20,4},{24,8},{28,12},{1,17},{... | collective-permute-start | bytes 442376 | tf_op jit(solution)/shard_map/ppermute | solution.py:49
  272.2 2.2 add_convert_fusion.1
  274.4 1.5 collective-permute-start.29
  275.9 5.1 %collective-permute-done.36 = bf16[96,768]{1,0:T(8,128)(2,1)S(1)} collective-permute-done((bf16[96,768]{1,0:T(8,128)(2,1)S(1)}, bf16[96,768]{1,0:T(8,128)(2,1)S(1)}, u32[]{:S(2)}, u32[]{:S(2)}) %collective-permute-start.36) | collective-permute-done | bytes 147488 | tf_op jit(solution)/shard_map/ppermute | solution.py:49
  284.6 3.4 %collective-permute-done.32 = bf16[512,768]{1,0:T(8,128)(2,1)} collective-permute-done((bf16[512,768]{1,0:T(8,128)(2,1)}, bf16[512,768]{1,0:T(8,128)(2,1)}, u32[]{:S(2)}, u32[]{:S(2)}) %collective-permute-start.32) | collective-permute-done | bytes 786464 | tf_op jit(solution)/shard_map/ppermute | solution.py:49
  287.9 2.1 fusion.17
  290.0 13.6 %collective-permute-done.29 = bf16[512,768]{1,0:T(8,128)(2,1)} collective-permute-done((bf16[512,768]{1,0:T(8,128)(2,1)}, bf16[512,768]{1,0:T(8,128)(2,1)}, u32[]{:S(2)}, u32[]{:S(2)}) %collective-permute-start.29) | collective-permute-done | bytes 786464 | tf_op jit(solution)/shard_map/ppermute | solution.py:49
  303.6 3.5 %fusion.8 = (bf16[512,768]{1,0:T(8,128)(2,1)}, bf16[512,768]{1,0:T(8,128)(2,1)}) fusion(bf16[512,768]{1,0:T(8,128)(2,1)S(1)} %copy-done, bf16[512,768]{1,0:T(8,128)(2,1)S(1)} %copy-done.3, f32[512]{0:T(512)S(1)} %get-tuple-element.130, f32[512]{0:T(512)S(1)} %get-tuple-element.131, f32[512]{0:T(512)S(1)} %add_rsqrt_fusion, ...), kind=kLoop, calls=%fused_computation.11 | loop fusion | flops 9437184 | bytes 7878656 | tf_op jit(solution)/shard_map/convert_element_type | solution.py:724
  (217 shorter events, 45.4 us)
Async XLA Ops:
  7.3 299.9 %reduce-scatter.2.cloned.1.call-start = ((), (), s32[]{:S(2)}) async-start(), calls=%async_computation.1 | async-start | bytes 2654208 | tf_op jit(solution)/shard_map/reduce_scatter | solution.py:686
  9.7 7.7 %collective-permute-start.21 = (bf16[96,768]{1,0:T(8,128)(2,1)S(1)}, bf16[96,768]{1,0:T(8,128)(2,1)}, u32[]{:S(2)}, u32[]{:S(2)}) collective-permute-start(bf16[96,768]{1,0:T(8,128)(2,1)S(1)} %pad_maximum_fusion.1.refs_0_), channel_id=1, source_target_pairs={{8,0},{16,8},{24,16},{28,24},{20,28},{12,20},{4,12},{0,4},{9,1},{1... | collective-permute-start | bytes 442376 | tf_op jit(solution)/shard_map/ppermute | solution.py:78
  10.2 8.8 %collective-permute-start.20 = (bf16[96,768]{1,0:T(8,128)(2,1)S(1)}, bf16[96,768]{1,0:T(8,128)(2,1)}, u32[]{:S(2)}, u32[]{:S(2)}) collective-permute-start(bf16[96,768]{1,0:T(8,128)(2,1)S(1)} %pad_maximum_fusion.1.refs_0_), channel_id=1, source_target_pairs={{0,8},{8,16},{16,24},{24,28},{28,20},{20,12},{12,4},{4,0},{1,9},{9... | collective-permute-start | bytes 442376 | tf_op jit(solution)/shard_map/ppermute | solution.py:75
  11.8 7.7 %collective-permute-start.14 = (bf16[96,768]{1,0:T(8,128)(2,1)}, bf16[96,768]{1,0:T(8,128)(2,1)}, u32[]{:S(2)}, u32[]{:S(2)}) collective-permute-start(bf16[96,768]{1,0:T(8,128)(2,1)} %bitcast.53), channel_id=1, source_target_pairs={{8,0},{16,8},{24,16},{28,24},{20,28},{12,20},{4,12},{0,4},{9,1},{1... | collective-permute-start | bytes 442376 | tf_op jit(solution)/shard_map/ppermute | solution.py:78
  12.2 24.8 %collective-permute-start.3 = (bf16[512,768]{1,0:T(8,128)(2,1)}, bf16[512,768]{1,0:T(8,128)(2,1)S(1)}, u32[]{:S(2)}, u32[]{:S(2)}) collective-permute-start(bf16[512,768]{1,0:T(8,128)(2,1)} %param.31), channel_id=1, source_target_pairs={{0,2},{1,3},{2,0},{3,1},{4,6},{5,7},{6,4},{7,5},{8,10},{9,11},{10,... | collective-permute-start | bytes 2359304 | tf_op jit(solution)/shard_map/ppermute | solution.py:49
  13.7 34.0 %collective-permute-start = (bf16[512,768]{1,0:T(8,128)(2,1)}, bf16[512,768]{1,0:T(8,128)(2,1)S(1)}, u32[]{:S(2)}, u32[]{:S(2)}) collective-permute-start(bf16[512,768]{1,0:T(8,128)(2,1)} %param.17), channel_id=1, source_target_pairs={{0,2},{1,3},{2,0},{3,1},{4,6},{5,7},{6,4},{7,5},{8,10},{9,11},{10,... | collective-permute-start | bytes 2359304 | tf_op jit(solution)/shard_map/ppermute | solution.py:49
  17.4 6.3 %collective-permute-start.13 = (bf16[96,768]{1,0:T(8,128)(2,1)}, bf16[96,768]{1,0:T(8,128)(2,1)S(1)}, u32[]{:S(2)}, u32[]{:S(2)}) collective-permute-start(bf16[96,768]{1,0:T(8,128)(2,1)} %bitcast.54), channel_id=1, source_target_pairs={{0,8},{8,16},{16,24},{24,28},{28,20},{20,12},{12,4},{4,0},{1,9},{9... | collective-permute-start | bytes 442376 | tf_op jit(solution)/shard_map/ppermute | solution.py:75
  19.0 6.0 %collective-permute-start.7 = (bf16[96,896]{1,0:T(8,128)(2,1)S(1)}, bf16[96,896]{1,0:T(8,128)(2,1)S(1)}, u32[]{:S(2)}, u32[]{:S(2)}) collective-permute-start(bf16[96,896]{1,0:T(8,128)(2,1)S(1)} %fusion.16.refs_0_), channel_id=1, source_target_pairs={{8,0},{16,8},{24,16},{28,24},{20,28},{12,20},{4,12},{0,4},{9,1},{1... | collective-permute-start | bytes 516104 | tf_op jit(solution)/shard_map/ppermute | solution.py:78
  19.5 6.1 %collective-permute-start.6 = (bf16[96,896]{1,0:T(8,128)(2,1)S(1)}, bf16[96,896]{1,0:T(8,128)(2,1)S(1)}, u32[]{:S(2)}, u32[]{:S(2)}) collective-permute-start(bf16[96,896]{1,0:T(8,128)(2,1)S(1)} %fusion.16.refs_0_), channel_id=1, source_target_pairs={{0,8},{8,16},{16,24},{24,28},{28,20},{20,12},{12,4},{4,0},{1,9},{9... | collective-permute-start | bytes 516104 | tf_op jit(solution)/shard_map/ppermute | solution.py:75
  24.3 5.4 %collective-permute-start.23 = (bf16[96,768]{1,0:T(8,128)(2,1)}, bf16[96,768]{1,0:T(8,128)(2,1)S(1)}, u32[]{:S(2)}, u32[]{:S(2)}) collective-permute-start(bf16[96,768]{1,0:T(8,128)(2,1)} %collective-permute-done.21.refs_2_), channel_id=1, source_target_pairs={{8,0},{16,8},{24,16},{28,24},{20,28},{12,20},{4,12},{0,4},{9,1},{1... | collective-permute-start | bytes 442376 | tf_op jit(solution)/shard_map/ppermute | solution.py:78
  25.1 36.8 %collective-permute-start.4 = (bf16[512,768]{1,0:T(8,128)(2,1)S(1)}, bf16[512,768]{1,0:T(8,128)(2,1)}, u32[]{:S(2)}, u32[]{:S(2)}) collective-permute-start(bf16[512,768]{1,0:T(8,128)(2,1)S(1)} %copy-done.3), channel_id=1, source_target_pairs={{0,1},{1,0},{2,3},{3,2},{4,5},{5,4},{6,7},{7,6},{8,9},{9,8},{10,11... | collective-permute-start | bytes 2359304 | tf_op jit(solution)/shard_map/ppermute | solution.py:49
  25.5 38.0 %collective-permute-start.1 = (bf16[512,768]{1,0:T(8,128)(2,1)S(1)}, bf16[512,768]{1,0:T(8,128)(2,1)}, u32[]{:S(2)}, u32[]{:S(2)}) collective-permute-start(bf16[512,768]{1,0:T(8,128)(2,1)S(1)} %copy-done), channel_id=1, source_target_pairs={{0,1},{1,0},{2,3},{3,2},{4,5},{5,4},{6,7},{7,6},{8,9},{9,8},{10,11... | collective-permute-start | bytes 2359304 | tf_op jit(solution)/shard_map/ppermute | solution.py:49
  29.7 5.4 %collective-permute-start.22 = (bf16[96,768]{1,0:T(8,128)(2,1)}, bf16[96,768]{1,0:T(8,128)(2,1)S(1)}, u32[]{:S(2)}, u32[]{:S(2)}) collective-permute-start(bf16[96,768]{1,0:T(8,128)(2,1)} %collective-permute-done.20.refs_1_), channel_id=1, source_target_pairs={{0,8},{8,16},{16,24},{24,28},{28,20},{20,12},{12,4},{4,0},{1,9},{9... | collective-permute-start | bytes 442376 | tf_op jit(solution)/shard_map/ppermute | solution.py:75
  35.7 13.2 %collective-permute-start.16 = (bf16[96,768]{1,0:T(8,128)(2,1)}, bf16[96,768]{1,0:T(8,128)(2,1)}, u32[]{:S(2)}, u32[]{:S(2)}) collective-permute-start(bf16[96,768]{1,0:T(8,128)(2,1)} %collective-permute-done.14.refs_10_), channel_id=1, source_target_pairs={{8,0},{16,8},{24,16},{28,24},{20,28},{12,20},{4,12},{0,4},{9,1},{1... | collective-permute-start | bytes 442376 | tf_op jit(solution)/shard_map/ppermute | solution.py:78
  37.0 36.2 %collective-permute-start.5 = (bf16[512,768]{1,0:T(8,128)(2,1)S(1)}, bf16[512,768]{1,0:T(8,128)(2,1)}, u32[]{:S(2)}, u32[]{:S(2)}) collective-permute-start(bf16[512,768]{1,0:T(8,128)(2,1)S(1)} %collective-permute-done.3), channel_id=1, source_target_pairs={{0,1},{1,0},{2,3},{3,2},{4,5},{5,4},{6,7},{7,6},{8,9},{9,8},{10,11... | collective-permute-start | bytes 2359304 | tf_op jit(solution)/shard_map/ppermute | solution.py:49
  47.7 25.5 %collective-permute-start.2 = (bf16[512,768]{1,0:T(8,128)(2,1)S(1)}, bf16[512,768]{1,0:T(8,128)(2,1)}, u32[]{:S(2)}, u32[]{:S(2)}) collective-permute-start(bf16[512,768]{1,0:T(8,128)(2,1)S(1)} %collective-permute-done), channel_id=1, source_target_pairs={{0,1},{1,0},{2,3},{3,2},{4,5},{5,4},{6,7},{7,6},{8,9},{9,8},{10,11... | collective-permute-start | bytes 2359304 | tf_op jit(solution)/shard_map/ppermute | solution.py:49
  48.9 6.6 %collective-permute-start.15 = (bf16[96,768]{1,0:T(8,128)(2,1)}, bf16[96,768]{1,0:T(8,128)(2,1)}, u32[]{:S(2)}, u32[]{:S(2)}) collective-permute-start(bf16[96,768]{1,0:T(8,128)(2,1)} %copy-done.33), channel_id=1, source_target_pairs={{0,8},{8,16},{16,24},{24,28},{28,20},{20,12},{12,4},{4,0},{1,9},{9... | collective-permute-start | bytes 442376 | tf_op jit(solution)/shard_map/ppermute | solution.py:75
  55.5 6.0 %collective-permute-start.8 = (bf16[96,896]{1,0:T(8,128)(2,1)S(1)}, bf16[96,896]{1,0:T(8,128)(2,1)S(1)}, u32[]{:S(2)}, u32[]{:S(2)}) collective-permute-start(bf16[96,896]{1,0:T(8,128)(2,1)S(1)} %copy-done.25), channel_id=1, source_target_pairs={{0,8},{8,16},{16,24},{24,28},{28,20},{20,12},{12,4},{4,0},{1,9},{9... | collective-permute-start | bytes 516104 | tf_op jit(solution)/shard_map/ppermute | solution.py:75
  61.5 6.9 %collective-permute-start.9 = (bf16[96,896]{1,0:T(8,128)(2,1)S(1)}, bf16[96,896]{1,0:T(8,128)(2,1)S(1)}, u32[]{:S(2)}, u32[]{:S(2)}) collective-permute-start(bf16[96,896]{1,0:T(8,128)(2,1)S(1)} %copy-done.23), channel_id=1, source_target_pairs={{8,0},{16,8},{24,16},{28,24},{20,28},{12,20},{4,12},{0,4},{9,1},{1... | collective-permute-start | bytes 516104 | tf_op jit(solution)/shard_map/ppermute | solution.py:78
  61.9 8.2 %collective-permute-start.17 = (bf16[96,768]{1,0:T(8,128)(2,1)}, bf16[96,768]{1,0:T(8,128)(2,1)S(1)}, u32[]{:S(2)}, u32[]{:S(2)}) collective-permute-start(bf16[96,768]{1,0:T(8,128)(2,1)} %collective-permute-done.15.refs_11_), channel_id=1, source_target_pairs={{0,8},{8,16},{16,24},{24,28},{28,20},{20,12},{12,4},{4,0},{1,9},{9... | collective-permute-start | bytes 442376 | tf_op jit(solution)/shard_map/ppermute | solution.py:75
  63.6 7.5 %collective-permute-start.10 = (bf16[96,896]{1,0:T(8,128)(2,1)S(1)}, bf16[96,896]{1,0:T(8,128)(2,1)S(1)}, u32[]{:S(2)}, u32[]{:S(2)}) collective-permute-start(bf16[96,896]{1,0:T(8,128)(2,1)S(1)} %collective-permute-done.8.refs_3_), channel_id=1, source_target_pairs={{0,8},{8,16},{16,24},{24,28},{28,20},{20,12},{12,4},{4,0},{1,9},{9... | collective-permute-start | bytes 516104 | tf_op jit(solution)/shard_map/ppermute | solution.py:75
  68.5 9.7 %collective-permute-start.24 = (bf16[96,768]{1,0:T(8,128)(2,1)S(1)}, bf16[96,768]{1,0:T(8,128)(2,1)S(1)}, u32[]{:S(2)}, u32[]{:S(2)}) collective-permute-start(bf16[96,768]{1,0:T(8,128)(2,1)S(1)} %copy-done.35), channel_id=1, source_target_pairs={{0,8},{8,16},{16,24},{24,28},{28,20},{20,12},{12,4},{4,0},{1,9},{9... | collective-permute-start | bytes 442376 | tf_op jit(solution)/shard_map/ppermute | solution.py:75
  70.1 8.7 %collective-permute-start.18 = (bf16[96,768]{1,0:T(8,128)(2,1)}, bf16[96,768]{1,0:T(8,128)(2,1)S(1)}, u32[]{:S(2)}, u32[]{:S(2)}) collective-permute-start(bf16[96,768]{1,0:T(8,128)(2,1)} %collective-permute-done.16.refs_12_), channel_id=1, source_target_pairs={{8,0},{16,8},{24,16},{28,24},{20,28},{12,20},{4,12},{0,4},{9,1},{1... | collective-permute-start | bytes 442376 | tf_op jit(solution)/shard_map/ppermute | solution.py:78
  71.0 9.9 %collective-permute-start.11 = (bf16[96,896]{1,0:T(8,128)(2,1)S(1)}, bf16[96,896]{1,0:T(8,128)(2,1)S(1)}, u32[]{:S(2)}, u32[]{:S(2)}) collective-permute-start(bf16[96,896]{1,0:T(8,128)(2,1)S(1)} %collective-permute-done.9.refs_4_), channel_id=1, source_target_pairs={{8,0},{16,8},{24,16},{28,24},{20,28},{12,20},{4,12},{0,4},{9,1},{1... | collective-permute-start | bytes 516104 | tf_op jit(solution)/shard_map/ppermute | solution.py:78
  73.3 7.6 %collective-permute-start.19 = (bf16[96,768]{1,0:T(8,128)(2,1)S(1)}, bf16[96,768]{1,0:T(8,128)(2,1)S(1)}, u32[]{:S(2)}, u32[]{:S(2)}) collective-permute-start(bf16[96,768]{1,0:T(8,128)(2,1)S(1)} %collective-permute-done.17.refs_13_), channel_id=1, source_target_pairs={{0,8},{8,16},{16,24},{24,28},{28,20},{20,12},{12,4},{4,0},{1,9},{9... | collective-permute-start | bytes 442376 | tf_op jit(solution)/shard_map/ppermute | solution.py:75
  73.3 8.6 %collective-permute-start.12 = (bf16[96,896]{1,0:T(8,128)(2,1)S(1)}, bf16[96,896]{1,0:T(8,128)(2,1)S(1)}, u32[]{:S(2)}, u32[]{:S(2)}) collective-permute-start(bf16[96,896]{1,0:T(8,128)(2,1)S(1)} %collective-permute-done.10.refs_5_), channel_id=1, source_target_pairs={{0,8},{8,16},{16,24},{24,28},{28,20},{20,12},{12,4},{4,0},{1,9},{9... | collective-permute-start | bytes 516104 | tf_op jit(solution)/shard_map/ppermute | solution.py:75
  78.2 28.0 %collective-permute-start.25 = (bf16[96,768]{1,0:T(8,128)(2,1)S(1)}, bf16[96,768]{1,0:T(8,128)(2,1)S(1)}, u32[]{:S(2)}, u32[]{:S(2)}) collective-permute-start(bf16[96,768]{1,0:T(8,128)(2,1)S(1)} %copy-done.32), channel_id=1, source_target_pairs={{8,0},{16,8},{24,16},{28,24},{20,28},{12,20},{4,12},{0,4},{9,1},{1... | collective-permute-start | bytes 442376 | tf_op jit(solution)/shard_map/ppermute | solution.py:78
  78.8 27.4 %collective-permute-start.26 = (bf16[96,768]{1,0:T(8,128)(2,1)S(1)}, bf16[96,768]{1,0:T(8,128)(2,1)S(1)}, u32[]{:S(2)}, u32[]{:S(2)}) collective-permute-start(bf16[96,768]{1,0:T(8,128)(2,1)S(1)} %collective-permute-done.24.refs_5_), channel_id=1, source_target_pairs={{0,8},{8,16},{16,24},{24,28},{28,20},{20,12},{12,4},{4,0},{1,9},{9... | collective-permute-start | bytes 442376 | tf_op jit(solution)/shard_map/ppermute | solution.py:75
  106.2 13.2 %collective-permute-start.42 = (f32[2,768]{1,0:T(2,128)S(1)}, f32[2,768]{1,0:T(2,128)S(1)}, u32[]{:S(2)}, u32[]{:S(2)}) collective-permute-start(f32[2,768]{1,0:T(2,128)S(1)} %slice.128), channel_id=1, source_target_pairs={{0,1},{1,0},{2,3},{3,2},{4,5},{5,4},{6,7},{7,6},{8,9},{9,8},{10,11... | collective-permute-start | bytes 18440 | tf_op jit(solution)/shard_map/ppermute | solution.py:49
  119.4 6.8 %collective-permute-start.43 = (f32[2,768]{1,0:T(2,128)S(1)}, f32[2,768]{1,0:T(2,128)S(1)}, u32[]{:S(2)}, u32[]{:S(2)}) collective-permute-start(f32[2,768]{1,0:T(2,128)S(1)} %get-tuple-element.119), channel_id=1, source_target_pairs={{0,2},{1,3},{2,0},{3,1},{4,6},{5,7},{6,4},{7,5},{8,10},{9,11},{10,... | collective-permute-start | bytes 18440 | tf_op jit(solution)/shard_map/ppermute | solution.py:49
  121.0 23.3 %collective-permute-start.27 = (bf16[384,768]{1,0:T(8,128)(2,1)S(1)}, bf16[384,768]{1,0:T(8,128)(2,1)S(1)}, u32[]{:S(2)}, u32[]{:S(2)}) collective-permute-start(bf16[384,768]{1,0:T(8,128)(2,1)S(1)} %pad_maximum_fusion), channel_id=1, source_target_pairs={{0,4},{4,8},{8,12},{12,16},{16,20},{20,24},{24,28},{1,5},{5,9},{9,... | collective-permute-start | bytes 1769480 | tf_op jit(solution)/shard_map/ppermute | solution.py:44
  126.2 14.3 %collective-permute-start.44 = (f32[4,768]{1,0:T(4,128)S(1)}, f32[4,768]{1,0:T(4,128)S(1)}, u32[]{:S(2)}, u32[]{:S(2)}) collective-permute-start(f32[4,768]{1,0:T(4,128)S(1)} %pad_maximum_fusion.3), channel_id=1, source_target_pairs={{0,4},{4,0},{8,12},{12,8},{16,20},{20,16},{24,28},{28,24},{1,5},{5... | collective-permute-start | bytes 36872 | tf_op jit(solution)/shard_map/ppermute | solution.py:49
  140.5 3.8 %collective-permute-start.45 = (f32[4,768]{1,0:T(4,128)S(1)}, f32[4,768]{1,0:T(4,128)S(1)}, u32[]{:S(2)}, u32[]{:S(2)}) collective-permute-start(f32[4,768]{1,0:T(4,128)S(1)} %fusion.20), channel_id=1, source_target_pairs={{0,8},{4,12},{8,0},{12,4},{16,24},{20,28},{24,16},{28,20},{1,9},{5... | collective-permute-start | bytes 36872 | tf_op jit(solution)/shard_map/ppermute | solution.py:49
  144.3 91.4 %collective-permute-start.46 = (f32[4,768]{1,0:T(4,128)S(1)}, f32[4,768]{1,0:T(4,128)S(1)}, u32[]{:S(2)}, u32[]{:S(2)}) collective-permute-start(f32[4,768]{1,0:T(4,128)S(1)} %add.148), channel_id=1, source_target_pairs={{0,16},{4,20},{8,24},{12,28},{16,0},{20,4},{24,8},{28,12},{1,17},{... | collective-permute-start | bytes 36872 | tf_op jit(solution)/shard_map/ppermute | solution.py:49
  178.2 36.6 %collective-permute-start.30 = (bf16[384,768]{1,0:T(8,128)(2,1)}, bf16[384,768]{1,0:T(8,128)(2,1)S(1)}, u32[]{:S(2)}, u32[]{:S(2)}) collective-permute-start(bf16[384,768]{1,0:T(8,128)(2,1)} %get-tuple-element.55), channel_id=1, source_target_pairs={{4,0},{8,4},{12,8},{16,12},{20,16},{24,20},{28,24},{5,1},{9,5},{13... | collective-permute-start | bytes 1769480 | tf_op jit(solution)/shard_map/ppermute | solution.py:44
  233.2 3.1 collective-permute-start.37
  235.7 29.1 %collective-permute-start.31 = (bf16[1024,768]{1,0:T(8,128)(2,1)}, bf16[1024,768]{1,0:T(8,128)(2,1)}, u32[]{:S(2)}, u32[]{:S(2)}) collective-permute-start(bf16[1024,768]{1,0:T(8,128)(2,1)} %get-tuple-element.59), channel_id=1, source_target_pairs={{0,1},{1,0},{2,3},{3,2},{4,5},{5,4},{6,7},{7,6},{8,9},{9,8},{10,11... | collective-permute-start | bytes 4718600 | tf_op jit(solution)/shard_map/ppermute | solution.py:49
  237.0 3.6 %collective-permute-start.38 = (f32[2,768]{1,0:T(2,128)S(1)}, f32[2,768]{1,0:T(2,128)S(1)}, u32[]{:S(2)}, u32[]{:S(2)}) collective-permute-start(f32[2,768]{1,0:T(2,128)S(1)} %slice_add_fusion.2), channel_id=1, source_target_pairs={{0,2},{1,3},{2,0},{3,1},{4,6},{5,7},{6,4},{7,5},{8,10},{9,11},{10,... | collective-permute-start | bytes 18440 | tf_op jit(solution)/shard_map/ppermute | solution.py:49
  240.7 8.5 %collective-permute-start.39 = (f32[3,768]{1,0:T(4,128)S(1)}, f32[3,768]{1,0:T(4,128)S(1)}, u32[]{:S(2)}, u32[]{:S(2)}) collective-permute-start(f32[3,768]{1,0:T(4,128)S(1)} %pad_maximum_fusion.2), channel_id=1, source_target_pairs={{0,4},{4,0},{8,12},{12,8},{16,20},{20,16},{24,28},{28,24},{1,5},{5... | collective-permute-start | bytes 27656 | tf_op jit(solution)/shard_map/ppermute | solution.py:49
  247.1 25.1 %collective-permute-start.28 = (bf16[1024,768]{1,0:T(8,128)(2,1)}, bf16[1024,768]{1,0:T(8,128)(2,1)}, u32[]{:S(2)}, u32[]{:S(2)}) collective-permute-start(bf16[1024,768]{1,0:T(8,128)(2,1)} %get-tuple-element.48), channel_id=1, source_target_pairs={{0,1},{1,0},{2,3},{3,2},{4,5},{5,4},{6,7},{7,6},{8,9},{9,8},{10,11... | collective-permute-start | bytes 4718600 | tf_op jit(solution)/shard_map/ppermute | solution.py:49
  247.1 16.3 %collective-permute-start.33 = (bf16[384,768]{1,0:T(8,128)(2,1)}, bf16[384,768]{1,0:T(8,128)(2,1)}, u32[]{:S(2)}, u32[]{:S(2)}) collective-permute-start(bf16[384,768]{1,0:T(8,128)(2,1)} %get-tuple-element.61), channel_id=1, source_target_pairs={{0,4},{4,0},{8,12},{12,8},{16,20},{20,16},{24,28},{28,24},{1,5},{5... | collective-permute-start | bytes 1769480 | tf_op jit(solution)/shard_map/ppermute | solution.py:49
  249.2 3.8 %collective-permute-start.40 = (f32[3,768]{1,0:T(4,128)S(1)}, f32[3,768]{1,0:T(4,128)S(1)}, u32[]{:S(2)}, u32[]{:S(2)}) collective-permute-start(f32[3,768]{1,0:T(4,128)S(1)} %fusion.19), channel_id=1, source_target_pairs={{0,8},{4,12},{8,0},{12,4},{16,24},{20,28},{24,16},{28,20},{1,9},{5... | collective-permute-start | bytes 27656 | tf_op jit(solution)/shard_map/ppermute | solution.py:49
  253.0 4.6 %collective-permute-start.41 = (f32[3,768]{1,0:T(4,128)S(1)}, f32[3,768]{1,0:T(4,128)S(1)}, u32[]{:S(2)}, u32[]{:S(2)}) collective-permute-start(f32[3,768]{1,0:T(4,128)S(1)} %add.143), channel_id=1, source_target_pairs={{0,16},{4,20},{8,24},{12,28},{16,0},{20,4},{24,8},{28,12},{1,17},{... | collective-permute-start | bytes 27656 | tf_op jit(solution)/shard_map/ppermute | solution.py:49
  267.2 20.7 %collective-permute-start.32 = (bf16[512,768]{1,0:T(8,128)(2,1)}, bf16[512,768]{1,0:T(8,128)(2,1)}, u32[]{:S(2)}, u32[]{:S(2)}) collective-permute-start(bf16[512,768]{1,0:T(8,128)(2,1)} %add_convert_fusion), channel_id=1, source_target_pairs={{0,2},{1,3},{2,0},{3,1},{4,6},{5,7},{6,4},{7,5},{8,10},{9,11},{10,... | collective-permute-start | bytes 2359304 | tf_op jit(solution)/shard_map/ppermute | solution.py:49
  267.7 8.2 %collective-permute-start.34 = (bf16[96,768]{1,0:T(8,128)(2,1)S(1)}, bf16[96,768]{1,0:T(8,128)(2,1)S(1)}, u32[]{:S(2)}, u32[]{:S(2)}) collective-permute-start(bf16[96,768]{1,0:T(8,128)(2,1)S(1)} %get-tuple-element.116), channel_id=1, source_target_pairs={{0,8},{4,12},{8,0},{12,4},{16,24},{20,28},{24,16},{28,20},{1,9},{5... | collective-permute-start | bytes 442376 | tf_op jit(solution)/shard_map/ppermute | solution.py:49
  267.8 13.2 %collective-permute-start.36 = (bf16[96,768]{1,0:T(8,128)(2,1)S(1)}, bf16[96,768]{1,0:T(8,128)(2,1)S(1)}, u32[]{:S(2)}, u32[]{:S(2)}) collective-permute-start(bf16[96,768]{1,0:T(8,128)(2,1)S(1)} %get-tuple-element.117), channel_id=1, source_target_pairs={{0,24},{4,28},{8,16},{12,20},{16,8},{20,12},{24,0},{28,4},{1,25},{... | collective-permute-start | bytes 442376 | tf_op jit(solution)/shard_map/ppermute | solution.py:49
  267.9 13.1 %collective-permute-start.35 = (bf16[96,768]{1,0:T(8,128)(2,1)S(1)}, bf16[96,768]{1,0:T(8,128)(2,1)S(1)}, u32[]{:S(2)}, u32[]{:S(2)}) collective-permute-start(bf16[96,768]{1,0:T(8,128)(2,1)S(1)} %get-tuple-element.118), channel_id=1, source_target_pairs={{0,16},{4,20},{8,24},{12,28},{16,0},{20,4},{24,8},{28,12},{1,17},{... | collective-permute-start | bytes 442376 | tf_op jit(solution)/shard_map/ppermute | solution.py:49
  274.4 29.2 %collective-permute-start.29 = (bf16[512,768]{1,0:T(8,128)(2,1)}, bf16[512,768]{1,0:T(8,128)(2,1)}, u32[]{:S(2)}, u32[]{:S(2)}) collective-permute-start(bf16[512,768]{1,0:T(8,128)(2,1)} %add_convert_fusion.1), channel_id=1, source_target_pairs={{0,2},{1,3},{2,0},{3,1},{4,6},{5,7},{6,4},{7,5},{8,10},{9,11},{10,... | collective-permute-start | bytes 2359304 | tf_op jit(solution)/shard_map/ppermute | solution.py:49
  (42 other events, 495.4 us)
Sparse Core Ops, SparseCore 0:
  142.5 78.9 reduce-scatter.1
where the time goes:
time: 319 us; the launch traced here: 317 us
  Pallas kernels  113 us (35%)
  waiting for transfers between devices  80.2 us (25%)
  starting transfers between devices  57.2 us (18%)
  local copies, waits for them, and re-layouts  32.8 us (10%)
  other arithmetic  19.1 us (6%)
  between operations  14.8 us (5%)
    ppermute x24, waiting for transfers between devices, swapped(): return lax.ppermute(block, axis, route)  61.8 us
    pallas_call x1, Pallas kernels, attention_forward(): pl.pallas_call(functools.partial(attn_fwd_kernel, heads, halo), grid_spec...  26.1 us
    pallas_call x1, Pallas kernels, attention_backward(): pl.pallas_call(functools.partial(own_bwd_kernel, heads, halo), grid_spec=...  23.4 us
    pallas_call x1, Pallas kernels, feed_forward(): pl.pallas_call(functools.partial(ff_kernel, len(fc_pieces)), grid_spec=pl...  22.9 us
    ppermute x2, starting transfers between devices, passed_along(): return lax.ppermute(block, axis, route)  18.4 us
    ppermute x12, starting transfers between devices, ring_gather(): from_left = lax.ppermute(from_left, axis, ahead)  18.1 us
    pallas_call x1, Pallas kernels, tail(): pl.pallas_call(functools.partial(tail_kernel, halo), grid_spec=pltpu.Pref...  16.8 us
    ppermute x24, starting transfers between devices, swapped(): return lax.ppermute(block, axis, route)  15 us
  transfers between devices with their start and end apart: 48, of which 18 were waited for; matrix products, arithmetic and copies ran while one was open for 13% of the time, Pallas kernels for 36%

commit v1 on v0

v1 whole, which is shorter than its diff:
```python
import functools

import jax
import jax.numpy as jnp
from jax import lax
from jax.experimental import pallas as pl
from jax.experimental.pallas import tpu as pltpu
from jax.sharding import PartitionSpec as P

HEAD_DIM = 64
ROT = 16
BLK = 256
SLOTS = (0, 2, 1, 3)

norm_eps = 1e-05
big_negative = -1e30
rope_base = 10000.0
inv_sqrt_two = 0.7071067811865476
inv_sqrt_two_pi = 0.3989422804014327

f32 = jnp.float32
bf16 = jnp.bfloat16


def mm(a, b, ca, cb):
    return lax.dot_general(a, b, (((ca,), (cb,)), ((), ())), preferred_element_type=f32)


def params(**kw):
    return pltpu.CompilerParams(vmem_limit_bytes=56 * 1024 * 1024, **kw)


def cost(flops, moved, exps=0):
    return pl.CostEstimate(flops=int(flops), bytes_accessed=int(moved), transcendentals=int(exps))


def shaped(shape, dtype):
    return jax.ShapeDtypeStruct(shape, dtype)


def passed_along(block, axis, distance):
    devices = range(lax.axis_size(axis))
    route = [(i - distance, i) for i in devices if i - distance in devices]
    return lax.ppermute(block, axis, route)


def swapped(block, axis, bit):
    route = [(i, i ^ bit) for i in range(lax.axis_size(axis))]
    return lax.ppermute(block, axis, route)


def ring_order(n):
    return list(range(0, n, 2)) + list(range(n - 1, 0, -2))


def ring_gather(block, axis):
    n = lax.axis_size(axis)
    rows = block.shape[0]
    if n > 8:
        return [lax.all_gather(block, axis, axis=0, tiled=True)], jnp.zeros((1,), jnp.int32)
    ring = ring_order(n)
    ahead = [(ring[r], ring[(r + 1) % n]) for r in range(n)]
    behind = [(b, a) for a, b in ahead]
    table = []
    for device in range(n):
        at = ring.index(device)
        row = [device * rows]
        for step in range(1, n // 2):
            row.append(ring[(at - step) % n] * rows)
            row.append(ring[(at + step) % n] * rows)
        row.append(ring[(at + n // 2) % n] * rows)
        row.append(ring[(at + n // 2) % n] * rows + rows // 2)
        table.append(row)
    pieces = [block]
    from_left = from_right = block
    for step in range(1, n // 2):
        from_left = lax.ppermute(from_left, axis, ahead)
        from_right = lax.ppermute(from_right, axis, behind)
        pieces += [from_left, from_right]
    pieces.append(lax.ppermute(from_left[: rows // 2], axis, ahead))
    pieces.append(lax.ppermute(from_right[rows // 2 :], axis, behind))
    return pieces, jnp.asarray(table, jnp.int32)[lax.axis_index(axis)]


def gather_rows(block):
    far = swapped(block, "tensor", 2)
    near = swapped(block, "tensor", 1)
    both = swapped(far, "tensor", 1)
    return jnp.concatenate([block, far, near, both], axis=0)


def scatter_near(keep, send):
    count = keep.shape[0] // 2
    came = swapped(send, "tensor", 1)
    other = (keep[count:].astype(f32) + came[count:].astype(f32)).astype(bf16)
    return keep[:count], came[:count], other


def scatter_far(own, came, other):
    return own.astype(f32) + came.astype(f32) + swapped(other, "tensor", 2).astype(f32)


def tied(*arrays):
    return lax.optimization_barrier(arrays)


def summed_over(vec, axis):
    n = lax.axis_size(axis)
    bit = 1
    while bit < n:
        vec = vec + swapped(vec, axis, bit)
        bit *= 2
    return vec


def assemble(piece_refs, start_ref, first, out_ref):
    columns = pl.ds(first, out_ref.shape[1])
    for n, ref in enumerate(piece_refs):
        rows = ref.shape[0]
        out_ref[pl.ds(pl.multiple_of(start_ref[n], rows), rows), :] = ref[:, columns]


def norm_rows(x):
    center = x - jnp.mean(x, axis=-1, keepdims=True)
    inv_std = lax.rsqrt(jnp.mean(center * center, axis=-1, keepdims=True) + norm_eps)
    return center * inv_std


def ff_kernel(pieces, start_ref, x_ref, g_ref, b_ref, vec_ref, *refs):
    w_refs = refs[:pieces]
    out_ref, u_ref, grads_ref, small_ref = refs[pieces : pieces + 4]
    fc_w, fc2_w, fc_acc, fc2_acc = refs[pieces + 4 :]
    step = pl.program_id(0)
    ff = fc2_w.shape[1]

    @pl.when(step == 0)
    def _():
        assemble(w_refs, start_ref, 0, fc_w)
        assemble(w_refs, start_ref, ff, fc2_w)
        fc_acc[...] = jnp.zeros_like(fc_acc)
        fc2_acc[...] = jnp.zeros_like(fc2_acc)
        small_ref[...] = jnp.zeros_like(small_ref)

    gain, shift = vec_ref[4:5, :], vec_ref[5:6, :]
    normed = norm_rows(x_ref[...].astype(f32))
    normed_two = (normed * gain + shift).astype(bf16)
    pre = mm(normed_two, fc_w[...], 1, 0) + b_ref[...]
    cdf = 0.5 + 0.5 * lax.erf(pre * inv_sqrt_two)
    act = (pre * cdf).astype(bf16)
    slope = cdf + pre * (jnp.exp(-0.5 * pre * pre) * inv_sqrt_two_pi)
    out_ref[...] = mm(act, fc2_w[...], 1, 1).astype(bf16)
    g = g_ref[...]
    pre_grad = (mm(g, fc2_w[...], 1, 0) * slope).astype(bf16)
    two_grad = mm(pre_grad, fc_w[...], 1, 1)
    u_ref[...] = (two_grad * gain).astype(bf16)
    fc_acc[...] += mm(normed_two, pre_grad, 0, 0)
    fc2_acc[...] += mm(g, act, 0, 0)
    small_ref[0:1, :] += jnp.sum(two_grad * normed, axis=0, keepdims=True)
    small_ref[1:2, :] += jnp.sum(two_grad, axis=0, keepdims=True)
    small_ref[2:3, :] += jnp.sum(g.astype(f32), axis=0, keepdims=True)
    small_ref[3:4, :] += jnp.sum(pre_grad.astype(f32), axis=0, keepdims=True)

    @pl.when(step == pl.num_programs(0) - 1)
    def _():
        grads_ref[:, :ff] = fc_acc[...].astype(bf16)
        grads_ref[:, ff:] = fc2_acc[...].astype(bf16)


def feed_forward(starts, x, g, b_fc, vec, pieces, ff):
    tokens, dim = x.shape
    rows = tokens // 4
    spec = pl.BlockSpec((rows, dim), lambda s, *_: (s, 0))
    whole = lambda shape: pl.BlockSpec(shape, lambda s, *_: (0, 0))
    return pl.pallas_call(
        functools.partial(ff_kernel, len(pieces)),
        grid_spec=pltpu.PrefetchScalarGridSpec(
            num_scalar_prefetch=1,
            grid=(4,),
            in_specs=[spec, spec, whole((1, ff)), whole(vec.shape)] + [whole(p.shape) for p in pieces],
            out_specs=[spec, spec, whole((dim, 2 * ff)), whole((8, dim))],
            scratch_shapes=[pltpu.VMEM((dim, ff), bf16)] * 2 + [pltpu.VMEM((dim, ff), f32)] * 2,
        ),
        out_shape=[
            shaped((tokens, dim), bf16),
            shaped((tokens, dim), bf16),
            shaped((dim, 2 * ff), bf16),
            shaped((8, dim), f32),
        ],
        compiler_params=params(),
        cost_estimate=cost(12 * tokens * dim * ff, 8 * tokens * dim + 8 * dim * ff, 2 * tokens * ff),
        name="feed_forward",
    )(starts, x, g, b_fc, vec, *pieces)


def turned(x, cos_t, sin_t):
    half = ROT // 2
    out = []
    for h in range(x.shape[0] // HEAD_DIM):
        a = x[h * HEAD_DIM : h * HEAD_DIM + half]
        b = x[h * HEAD_DIM + half : h * HEAD_DIM + ROT]
        out += [a * cos_t - b * sin_t, b * cos_t + a * sin_t, x[h * HEAD_DIM + ROT : (h + 1) * HEAD_DIM]]
    return jnp.concatenate(out, axis=0)


def project_kernel(pieces, first, start_ref, place_ref, x_ref, g_ref, b_ref, cos_ref, sin_ref, *refs):
    w_refs = refs[:pieces]
    q_ref, k_ref, v_ref, do_ref, wt_ref, vec_ref, packed = refs[pieces:]
    feat = q_ref.shape[0]
    width = wt_ref.shape[0]

    @pl.when(pl.program_id(0) == 0)
    def _():
        assemble(w_refs, start_ref, first, packed)
        wt_ref[...] = packed[:, :width].astype(f32).T.astype(bf16)
        vec_ref[...] = packed[:, width:].astype(f32).T[:8]

    normed = norm_rows(x_ref[...].astype(f32))
    normed_one = (normed * vec_ref[2:3, :] + vec_ref[3:4, :]).astype(bf16)
    proj = mm(wt_ref[: 3 * feat, :], normed_one, 1, 1) + b_ref[...]
    cos_t, sin_t = cos_ref[...], sin_ref[...]
    q_ref[...] = (turned(proj[:feat], cos_t, sin_t) * HEAD_DIM ** (-0.5)).astype(bf16)
    k_ref[...] = turned(proj[feat : 2 * feat], cos_t, sin_t).astype(bf16)
    v_ref[...] = proj[2 * feat :].astype(bf16)
    do_ref[...] = mm(wt_ref[3 * feat :, :], g_ref[...], 1, 1).astype(bf16)


def project(starts, places, x, g, b_col, cos_t, sin_t, pieces, first, feat):
    tokens, dim = x.shape
    rows = tokens // 4
    width = 4 * feat
    spec = pl.BlockSpec((rows, dim), lambda s, *_: (s, 0))
    placed = lambda r: pl.BlockSpec((r, rows), lambda s, start, place: (0, place[s]))
    whole = lambda shape: pl.BlockSpec(shape, lambda s, *_: (0, 0))
    return pl.pallas_call(
        functools.partial(project_kernel, len(pieces), first),
        grid_spec=pltpu.PrefetchScalarGridSpec(
            num_scalar_prefetch=2,
            grid=(4,),
            in_specs=[spec, spec, whole(b_col.shape), placed(ROT // 2), placed(ROT // 2)]
            + [whole(p.shape) for p in pieces],
            out_specs=[placed(feat)] * 4 + [whole((width, dim)), whole((8, dim))],
            scratch_shapes=[pltpu.VMEM((dim, width + 128), bf16)],
        ),
        out_shape=[shaped((feat, tokens), bf16)] * 4 + [shaped((width, dim), bf16), shaped((8, dim), f32)],
        compiler_params=params(),
        cost_estimate=cost(8 * tokens * dim * feat, 6 * tokens * dim + 4 * dim * width),
        name="project",
    )(starts, places, x, g, b_col, cos_t, sin_t, *pieces)


def key_mask(chunk, lo_row, hi_row):
    idx = chunk * BLK + lax.broadcasted_iota(jnp.int32, (BLK, BLK), 0)
    return jnp.where((idx >= lo_row) & (idx <= hi_row), 0.0, big_negative)


def attn_fwd_kernel(heads, halo, first_ref, q_ref, k_ref, v_ref, left_ref, lo_ref, o_ref, lse_ref, keys, values):
    i = pl.program_id(0)
    first = first_ref[i]
    last = i + halo // BLK
    feat = k_ref.shape[0]

    @pl.when(i == 0)
    def _():
        keys[:, :halo] = left_ref[:feat, :]
        keys[:, halo:] = k_ref[...]
        values[:, :halo] = left_ref[feat:, :]
        values[:, halo:] = v_ref[...]

    lo_row = lo_ref[...]
    hi_row = halo + i * BLK + lax.broadcasted_iota(jnp.int32, (1, BLK), 1)

    def step(c, carry):
        cols = pl.ds(pl.multiple_of(c * BLK, BLK), BLK)
        mask = key_mask(c, lo_row, hi_row)
        hs = range(heads)
        feats = [pl.ds(h * HEAD_DIM, HEAD_DIM) for h in hs]
        s = [mm(keys[feats[h], cols], q_ref[feats[h], :], 0, 0) + mask for h in hs]
        tops = [jnp.maximum(carry[h][0], jnp.max(s[h], axis=0, keepdims=True)) for h in hs]
        p = [jnp.exp(s[h] - tops[h]) for h in hs]
        pv = [mm(values[feats[h], cols], p[h].astype(bf16), 1, 0) for h in hs]
        kept = [jnp.exp(carry[h][0] - tops[h]) for h in hs]
        return tuple(
            (
                tops[h],
                carry[h][1] * kept[h] + jnp.sum(p[h], axis=0, keepdims=True),
                carry[h][2] * kept[h] + pv[h],
            )
            for h in hs
        )

    start = tuple(
        (
            jnp.full((1, BLK), big_negative, f32),
            jnp.zeros((1, BLK), f32),
            jnp.zeros((HEAD_DIM, BLK), f32),
        )
        for _ in range(heads)
    )
    done = lax.fori_loop(first, last + 1, step, start)
    for h in range(heads):
        top, total, acc = done[h]
        o_ref[pl.ds(h * HEAD_DIM, HEAD_DIM), :] = (acc / total).astype(bf16)
        lse_ref[pl.ds(h, 1), :] = top + jnp.log(total)


def attention_forward(first, q, k, v, left, lo, halo):
    feat, tokens = q.shape
    heads = feat // HEAD_DIM
    col = lambda i, *_: (0, i)
    whole = lambda shape: pl.BlockSpec(shape, lambda i, *_: (0, 0))
    q_spec = pl.BlockSpec((feat, BLK), col)
    return pl.pallas_call(
        functools.partial(attn_fwd_kernel, heads, halo),
        grid_spec=pltpu.PrefetchScalarGridSpec(
            num_scalar_prefetch=1,
            grid=(tokens // BLK,),
            in_specs=[q_spec, whole(k.shape), whole(v.shape), whole(left.shape), pl.BlockSpec((1, BLK), col)],
            out_specs=[q_spec, pl.BlockSpec((8, BLK), col)],
            scratch_shapes=[pltpu.VMEM((feat, halo + tokens), bf16)] * 2,
        ),
        out_shape=[shaped((feat, tokens), bf16), shaped((8, tokens), f32)],
        compiler_params=params(),
        cost_estimate=cost(16 * feat * tokens * 1024, 8 * feat * tokens, heads * tokens * 1024),
        name="attention_forward",
    )(first, q, k, v, left, lo)


def attn_bwd_step(heads, c, base, q_ref, k_ref, v_ref, do_ref, lse_ref, lo_row, hi_row, deltas, dq_ref, dk_ref, dv_ref):
    cols = pl.ds(pl.multiple_of((c - base) * BLK, BLK), BLK)
    mask = key_mask(c, lo_row, hi_row)
    hs = range(heads)
    feats = [pl.ds(h * HEAD_DIM, HEAD_DIM) for h in hs]
    s = [mm(k_ref[feats[h], cols], q_ref[feats[h], :], 0, 0) + mask for h in hs]
    dp = [mm(v_ref[feats[h], cols], do_ref[feats[h], :], 0, 0) for h in hs]
    p = [jnp.exp(s[h] - lse_ref[pl.ds(h, 1), :]) for h in hs]
    ds = [(p[h] * (dp[h] - deltas[h])).astype(bf16) for h in hs]
    dv = [mm(do_ref[feats[h], :], p[h].astype(bf16), 1, 1) for h in hs]
    dk = [mm(q_ref[feats[h], :], ds[h], 1, 1) for h in hs]
    dq = [mm(k_ref[feats[h], cols], ds[h], 1, 0) for h in hs]
    for h in hs:
        dv_ref[feats[h], cols] += dv[h]
        dk_ref[feats[h], cols] += dk[h]
        dq_ref[feats[h], :] += dq[h]


def row_deltas(heads, o_ref, do_ref):
    deltas = []
    for h in range(heads):
        feats = pl.ds(h * HEAD_DIM, HEAD_DIM)
        prod = do_ref[feats, :].astype(f32) * o_ref[feats, :].astype(f32)
        deltas.append(jnp.sum(prod, axis=0, keepdims=True))
    return deltas


def halo_bwd_kernel(heads, halo, first_ref, q_ref, left_ref, lo_ref, o_ref, lse_ref, do_ref, dq_ref, back_ref, dk, dv):
    i = pl.program_id(0)
    feat = q_ref.shape[0]

    @pl.when(i == 0)
    def _():
        dk[...] = jnp.zeros_like(dk)
        dv[...] = jnp.zeros_like(dv)

    lo_row = lo_ref[...]
    hi_row = jnp.full((1, BLK), halo, jnp.int32)
    dq_ref[...] = jnp.zeros_like(dq_ref)
    deltas = row_deltas(heads, o_ref, do_ref)
    k_ref, v_ref = left_ref.at[:feat, :], left_ref.at[feat:, :]

    def step(c, carry):
        attn_bwd_step(
            heads, c, 0, q_ref, k_ref, v_ref, do_ref, lse_ref, lo_row, hi_row, deltas, dq_ref, dk, dv
        )
        return carry

    lax.fori_loop(first_ref[i], halo // BLK, step, 0)

    @pl.when(i == pl.num_programs(0) - 1)
    def _():
        back_ref[:feat, :] = dk[...].astype(bf16)
        back_ref[feat:, :] = dv[...].astype(bf16)


def own_bwd_kernel(
    heads, halo, first_ref, q_ref, k_ref, v_ref, lo_ref, o_ref, lse_ref, do_ref, part_ref, dq_ref, dk_ref, dv_ref
):
    i = pl.program_id(0)
    base = halo // BLK

    @pl.when(i == 0)
    def _():
        dk_ref[...] = jnp.zeros_like(dk_ref)
        dv_ref[...] = jnp.zeros_like(dv_ref)

    @pl.when(i < base)
    def _():
        dq_ref[...] = part_ref[...]

    @pl.when(i >= base)
    def _():
        dq_ref[...] = jnp.zeros_like(dq_ref)

    lo_row = lo_ref[...]
    hi_row = halo + i * BLK + lax.broadcasted_iota(jnp.int32, (1, BLK), 1)
    deltas = row_deltas(heads, o_ref, do_ref)

    def step(c, carry):
        attn_bwd_step(
            heads, c, base, q_ref, k_ref, v_ref, do_ref, lse_ref, lo_row, hi_row, deltas, dq_ref, dk_ref, dv_ref
        )
        return carry

    lax.fori_loop(jnp.maximum(first_ref[i], base), i + base + 1, step, 0)
    dq_ref[...] = dq_ref[...] * HEAD_DIM ** (-0.5)


def backward_left(first, q, left, lo, o, lse, do, halo):
    feat, tokens = q.shape
    heads = feat // HEAD_DIM
    col = lambda i, *_: (0, i)
    whole = lambda shape: pl.BlockSpec(shape, lambda i, *_: (0, 0))
    q_spec = pl.BlockSpec((feat, BLK), col)
    return pl.pallas_call(
        functools.partial(halo_bwd_kernel, heads, halo),
        grid_spec=pltpu.PrefetchScalarGridSpec(
            num_scalar_prefetch=1,
            grid=(halo // BLK,),
            in_specs=[
                q_spec,
                whole(left.shape),
                pl.BlockSpec((1, BLK), col),
                q_spec,
                pl.BlockSpec((8, BLK), col),
                q_spec,
            ],
            out_specs=[q_spec, whole(left.shape)],
            scratch_shapes=[pltpu.VMEM((feat, halo), f32)] * 2,
        ),
        out_shape=[shaped((feat, halo), f32), shaped(left.shape, bf16)],
        compiler_params=params(),
        cost_estimate=cost(40 * feat * halo * 512, 20 * feat * halo, heads * halo * 512),
        name="attention_backward_left",
    )(first, q, left, lo, o, lse, do)


def backward_own(first, q, k, v, lo, o, lse, do, dq_part, halo):
    feat, tokens = q.shape
    heads = feat // HEAD_DIM
    col = lambda i, *_: (0, i)
    whole = lambda shape: pl.BlockSpec(shape, lambda i, *_: (0, 0))
    q_spec = pl.BlockSpec((feat, BLK), col)
    part_spec = pl.BlockSpec((feat, BLK), lambda i, *_: (0, jnp.minimum(i, halo // BLK - 1)))
    return pl.pallas_call(
        functools.partial(own_bwd_kernel, heads, halo),
        grid_spec=pltpu.PrefetchScalarGridSpec(
            num_scalar_prefetch=1,
            grid=(tokens // BLK,),
            in_specs=[
                q_spec,
                whole(k.shape),
                whole(v.shape),
                pl.BlockSpec((1, BLK), col),
                q_spec,
                pl.BlockSpec((8, BLK), col),
                q_spec,
                part_spec,
            ],
            out_specs=[q_spec, whole(k.shape), whole(v.shape)],
        ),
        out_shape=[shaped((feat, tokens), f32)] * 3,
        compiler_params=params(),
        cost_estimate=cost(40 * feat * tokens * 1024, 20 * feat * tokens, heads * tokens * 1024),
        name="attention_backward_own",
    )(first, q, k, v, lo, o, lse, do, dq_part)


def keep_send_specs(rows, dim):
    keep = pl.BlockSpec((rows, dim), lambda s, *_: (jnp.minimum(s, 1), 0))
    send = pl.BlockSpec((rows, dim), lambda s, *_: (jnp.maximum(s - 2, 0), 0))
    return keep, send


def put_rows(keep_ref, send_ref, value):
    s = pl.program_id(0)

    @pl.when(s < 2)
    def _():
        keep_ref[...] = value

    @pl.when(s >= 2)
    def _():
        send_ref[...] = value


def put_chunks(chunk_ref, keep_ref, send_ref, value):
    parts = chunk_ref.shape[0] // 2
    size = keep_ref.shape[0] // parts
    for half, ref in enumerate((keep_ref, send_ref)):
        for n in range(parts):
            at = pl.ds(pl.multiple_of(chunk_ref[half * parts + n] * size, size), size)
            ref[n * size : (n + 1) * size, :] = value[at, :].astype(bf16)


def out_kernel(place_ref, chunk_ref, o_ref, ff_ref, g_ref, w_ref, keep_ref, send_ref, wkeep_ref, wsend_ref, acc, acc_t):
    s = pl.program_id(0)

    @pl.when(s == 0)
    def _():
        acc[...] = jnp.zeros_like(acc)

    total = mm(o_ref[...], w_ref[...], 0, 0) + ff_ref[...].astype(f32)
    put_rows(keep_ref, send_ref, total.astype(bf16))
    acc[...] += mm(o_ref[...], g_ref[...], 1, 0)

    @pl.when(s == pl.num_programs(0) - 1)
    def _():
        acc_t[...] = acc[...].T
        put_chunks(chunk_ref, wkeep_ref, wsend_ref, acc_t)


def branch_out(places, chunks, o, ff_out, g, out_w):
    feat, tokens = o.shape
    dim = out_w.shape[1]
    rows = tokens // 4
    keep, send = keep_send_specs(rows, dim)
    spec = pl.BlockSpec((rows, dim), lambda s, *_: (s, 0))
    whole = lambda shape: pl.BlockSpec(shape, lambda s, *_: (0, 0))
    return pl.pallas_call(
        out_kernel,
        grid_spec=pltpu.PrefetchScalarGridSpec(
            num_scalar_prefetch=2,
            grid=(4,),
            in_specs=[
                pl.BlockSpec((feat, rows), lambda s, place, chunk: (0, place[s])),
                spec,
                spec,
                whole((feat, dim)),
            ],
            out_specs=[keep, send, whole((dim // 2, feat)), whole((dim // 2, feat))],
            scratch_shapes=[pltpu.VMEM((feat, dim), f32), pltpu.VMEM((dim, feat), f32)],
        ),
        out_shape=[shaped((tokens // 2, dim), bf16)] * 2 + [shaped((dim // 2, feat), bf16)] * 2,
        compiler_params=params(),
        cost_estimate=cost(4 * feat * tokens * dim, 6 * tokens * dim),
        name="branch_out",
    )(places, chunks, o, ff_out, g, out_w)


def input_grad_kernel(
    halo,
    place_ref,
    dq_ref,
    dk_ref,
    dv_ref,
    back_ref,
    x_ref,
    u2_ref,
    wt_ref,
    vec_ref,
    cos_ref,
    sin_ref,
    keep_ref,
    send_ref,
    grad_ref,
    small_ref,
    bias_ref,
    late,
):
    s = pl.program_id(0)
    feat, rows = dq_ref.shape
    tokens = late.shape[1]

    @pl.when(s == 0)
    def _():
        late[:, : tokens - halo] = jnp.zeros((2 * feat, tokens - halo), bf16)
        late[:, tokens - halo :] = back_ref[...]
        small_ref[...] = jnp.zeros_like(small_ref)
        bias_ref[...] = jnp.zeros_like(bias_ref)

    cols = pl.ds(pl.multiple_of(place_ref[s] * rows, rows), rows)
    cos_t, sin_t = cos_ref[...], -sin_ref[...]
    dq = turned(dq_ref[...], cos_t, sin_t)
    dk = turned(dk_ref[...] + late[:feat, cols].astype(f32), cos_t, sin_t)
    dv = dv_ref[...] + late[feat:, cols].astype(f32)
    grad = jnp.concatenate([dq, dk, dv], axis=0).astype(bf16)
    grad_ref[...] = grad
    bias_ref[...] += jnp.sum(grad.astype(f32), axis=1, keepdims=True)
    one_grad = mm(grad, wt_ref[: 3 * feat, :], 0, 0)
    put_rows(keep_ref, send_ref, (one_grad * vec_ref[2:3, :] + u2_ref[...].astype(f32)).astype(bf16))
    normed = norm_rows(x_ref[...].astype(f32))
    small_ref[0:1, :] += jnp.sum(one_grad * normed, axis=0, keepdims=True)
    small_ref[1:2, :] += jnp.sum(one_grad, axis=0, keepdims=True)


def input_gradient(places, dq, dk, dv, back, x, u2, wt, vec, cos_t, sin_t, halo):
    feat, tokens = dq.shape
    dim = x.shape[1]
    rows = tokens // 4
    spec = pl.BlockSpec((rows, dim), lambda s, *_: (s, 0))
    placed = lambda r: pl.BlockSpec((r, rows), lambda s, place: (0, place[s]))
    whole = lambda shape: pl.BlockSpec(shape, lambda s, *_: (0, 0))
    keep, send = keep_send_specs(rows, dim)
    return pl.pallas_call(
        functools.partial(input_grad_kernel, halo),
        grid_spec=pltpu.PrefetchScalarGridSpec(
            num_scalar_prefetch=1,
            grid=(4,),
            in_specs=[placed(feat)] * 3
            + [whole(back.shape), spec, spec, whole(wt.shape), whole(vec.shape)]
            + [placed(ROT // 2)] * 2,
            out_specs=[keep, send, placed(3 * feat), whole((8, dim)), whole((3 * feat, 1))],
            scratch_shapes=[pltpu.VMEM((2 * feat, tokens), bf16)],
        ),
        out_shape=[shaped((tokens // 2, dim), bf16)] * 2
        + [shaped((3 * feat, tokens), bf16), shaped((8, dim), f32), shaped((3 * feat, 1), f32)],
        compiler_params=params(),
        cost_estimate=cost(12 * feat * tokens * dim, 10 * tokens * dim),
        name="input_gradient",
    )(places, dq, dk, dv, back, x, u2, wt, vec, cos_t, sin_t)


def weight_grad_kernel(place_ref, chunk_ref, grad_ref, x_ref, vec_ref, wkeep_ref, wsend_ref, acc, acc_t):
    s = pl.program_id(0)

    @pl.when(s == 0)
    def _():
        acc[...] = jnp.zeros_like(acc)

    normed = norm_rows(x_ref[...].astype(f32))
    normed_one = (normed * vec_ref[2:3, :] + vec_ref[3:4, :]).astype(bf16)
    acc[...] += mm(grad_ref[...], normed_one, 1, 0)

    @pl.when(s == pl.num_programs(0) - 1)
    def _():
        acc_t[...] = acc[...].T
        put_chunks(chunk_ref, wkeep_ref, wsend_ref, acc_t)


def weight_gradient(places, chunks, grad, x, vec):
    width, tokens = grad.shape
    dim = x.shape[1]
    rows = tokens // 4
    whole = lambda shape: pl.BlockSpec(shape, lambda s, *_: (0, 0))
    return pl.pallas_call(
        weight_grad_kernel,
        grid_spec=pltpu.PrefetchScalarGridSpec(
            num_scalar_prefetch=2,
            grid=(4,),
            in_specs=[
                pl.BlockSpec((width, rows), lambda s, place, chunk: (0, place[s])),
                pl.BlockSpec((rows, dim), lambda s, *_: (s, 0)),
                whole(vec.shape),
            ],
            out_specs=[whole((dim // 2, width))] * 2,
            scratch_shapes=[pltpu.VMEM((width, dim), f32), pltpu.VMEM((dim, width), f32)],
        ),
        out_shape=[shaped((dim // 2, width), bf16)] * 2,
        compiler_params=params(),
        cost_estimate=cost(4 * width * tokens * dim, 4 * tokens * dim),
        name="weight_gradient",
    )(places, chunks, grad, x, vec)


def rope_tables(positions):
    freq_idx = jnp.arange(0, ROT, 2, dtype=f32)
    inverse = rope_base ** (-freq_idx / ROT)
    angles = inverse[:, None] * positions.astype(f32)[None, :]
    return jnp.cos(angles), jnp.sin(angles)


def late_chunks():
    n = lax.axis_size("dp")
    rank = lax.axis_index("dp")
    if n > 8:
        return jnp.arange(2, dtype=jnp.int32)
    mine = jnp.stack([rank ^ (2 * k) for k in range(n // 2)])
    return jnp.concatenate([mine, mine ^ 1]).astype(jnp.int32)


def late_near(keep, send):
    n = lax.axis_size("dp")
    if n > 8:
        whole = jnp.concatenate([keep, send], axis=0)
        return lax.psum_scatter(whole, "dp", scatter_dimension=0, tiled=True).astype(f32)
    return keep.astype(f32) + swapped(send, "dp", 1).astype(f32)


def late_far(total, dtype):
    n = lax.axis_size("dp")
    if n > 8:
        return total
    size = total.shape[0] * 2 // n
    low = total.astype(dtype)
    own = total[:size]
    for k in range(1, n // 2):
        own = own + swapped(low[k * size : (k + 1) * size], "dp", 2 * k).astype(f32)
    return own


def body(
    hidden_in,
    w_qkv,
    b_qkv,
    w_out,
    b_out,
    w_fc,
    b_fc,
    w_fc2,
    b_fc2,
    ln1_gain,
    ln1_bias,
    ln2_gain,
    ln2_bias,
    segment_ids,
    positions,
    cotangent,
):
    local_dim = w_qkv.shape[2]
    ff = w_fc.shape[1]
    own_dims = w_fc.shape[0]
    seq_len = positions.shape[0]
    halo = seq_len * 3 // 8
    qkv_dim = 3 * local_dim
    rank = lax.axis_index("tensor")
    places = jnp.stack([rank ^ at for at in SLOTS]).astype(jnp.int32)

    vectors = jnp.stack([b_out, b_fc2, ln1_gain, ln1_bias, ln2_gain, ln2_bias], axis=1)
    vectors = jnp.pad(vectors, ((0, 0), (0, 122)))
    block = jnp.concatenate(
        [
            w_fc,
            w_fc2.T,
            jnp.transpose(w_qkv, (1, 0, 2)).reshape(own_dims, qkv_dim),
            w_out.T,
            vectors,
        ],
        axis=1,
    )
    pieces, starts = ring_gather(block, "dp")
    x_all = gather_rows(hidden_in)
    g_all = gather_rows(cotangent)

    cos_t, sin_t = rope_tables(positions)
    lo = halo + jnp.arange(seq_len, dtype=jnp.int32) - positions
    first = lo[::BLK] // BLK
    lo_row = lo.reshape(1, seq_len)

    q, k, v, do, wt, vec = project(
        starts, places, x_all, g_all, b_qkv.astype(f32).reshape(qkv_dim, 1), cos_t, sin_t, pieces, 2 * ff, local_dim
    )
    left = passed_along(jnp.concatenate([k[:, -halo:], v[:, -halo:]], axis=0), "dp", 1)
    ff_out, u_two, ff_grads, ff_small = feed_forward(
        starts, x_all, g_all, b_fc.astype(f32).reshape(1, ff), vec, pieces, ff
    )
    ff_own = lax.psum_scatter(ff_grads, "dp", scatter_dimension=0, tiled=True).astype(f32)
    q, ff_out = tied(q, ff_out)

    o, lse = attention_forward(first, q, k, v, left, lo_row, halo)
    chunks = late_chunks()
    out_keep, out_send, ow_keep, ow_send = branch_out(places, chunks, o, ff_out, g_all, wt[qkv_dim:])
    own_o, came_o, other_o = scatter_near(out_keep, out_send)
    ow_near = late_near(ow_keep, ow_send)
    do, out_keep = tied(do, out_keep)
    dq_part, back = backward_left(first, q, left, lo_row, o, lse, do, halo)
    dq_part, back, other_o, ow_near = tied(dq_part, back, other_o, ow_near)
    far_o = swapped(other_o, "tensor", 2)
    back = passed_along(back, "dp", -1)
    ow_own = late_far(ow_near, bf16)
    dq, dk, dv = backward_own(first, q, k, v, lo_row, o, lse, do, dq_part, halo)
    back, dq, far_o, ow_own = tied(back, dq, far_o, ow_own)
    summed = own_o.astype(f32) + came_o.astype(f32) + far_o.astype(f32)
    layer_out = (hidden_in.astype(f32) + summed + vec[0] + vec[1]).astype(bf16)

    u_keep, u_send, proj_grad, one_small, qkv_bias = input_gradient(
        places, dq, dk, dv, back, x_all, u_two, wt, vec, cos_t, sin_t, halo
    )
    own_u, came_u, other_u = scatter_near(u_keep, u_send)
    w_keep, w_send = weight_gradient(places, chunks, proj_grad, x_all, vec)

    n = lax.axis_size("dp")
    dims = x_all.shape[1]
    mine = jnp.concatenate([one_small[:2], ff_small[:3]], axis=0).reshape(5, n, own_dims)
    mine = jnp.pad(jnp.transpose(mine, (1, 0, 2)), ((0, 0), (0, 0), (0, 128 - own_dims)))
    fc_rows = ff_small[3].reshape(-1, 128)
    qkv_rows = jnp.pad(qkv_bias[:, 0], (0, -qkv_dim % 128)).reshape(-1, 128)
    shared = jnp.concatenate([fc_rows, qkv_rows], axis=0)
    small = jnp.concatenate([mine, jnp.broadcast_to(shared, (n,) + shared.shape)], axis=1)
    w_send, small, _ = tied(w_send, small, other_u)
    w_near = late_near(w_keep, w_send)
    if n > 8:
        small_near = lax.psum_scatter(small, "dp", scatter_dimension=0, tiled=True)
    else:
        small = jnp.take(small, chunks, axis=0)
        small_near = late_near(small[: n // 2], small[n // 2 :])
    w_near, small_near = tied(w_near, small_near)
    both = scatter_far(own_u, came_u, other_u)
    small_own = late_far(small_near, f32)[0]
    late_own = late_far(w_near, bf16)
    late_own, ff_own = tied(late_own, ff_own)
    norm_grads = summed_over(small_own[:4], "tensor")[:, :own_dims]
    fc_count = fc_rows.shape[0]
    fc_b_total = small_own[5 : 5 + fc_count].reshape(-1)
    qkv_b_total = small_own[5 + fc_count :].reshape(-1)[:qkv_dim].reshape(3, local_dim)
    out_b_total = small_own[4, :own_dims]

    normed_own = hidden_in.astype(f32)
    normed_own = normed_own - jnp.mean(normed_own, axis=-1, keepdims=True)
    inv_own = lax.rsqrt(jnp.mean(normed_own * normed_own, axis=-1, keepdims=True) + norm_eps)
    normed_own = normed_own * inv_own
    input_grad = cotangent.astype(f32) + inv_own * (
        both
        - jnp.mean(both, axis=-1, keepdims=True)
        - normed_own * jnp.mean(both * normed_own, axis=-1, keepdims=True)
    )
    return (
        layer_out,
        input_grad.astype(bf16),
        jnp.transpose(late_own.reshape(own_dims, 3, local_dim), (1, 0, 2)),
        qkv_b_total,
        ow_own.T,
        out_b_total,
        ff_own[:, :ff],
        fc_b_total,
        ff_own[:, ff:].T,
        out_b_total,
        norm_grads[0],
        norm_grads[1],
        norm_grads[2],
        norm_grads[3],
    )


def solution(mesh):
    in_specs = (
        P(("dp", "tensor"), None),
        P(None, "dp", "tensor"),
        P(None, "tensor"),
        P("tensor", "dp"),
        P("dp"),
        P("dp", "tensor"),
        P("tensor"),
        P("tensor", "dp"),
        P("dp"),
        P("dp"),
        P("dp"),
        P("dp"),
        P("dp"),
        P("dp"),
        P("dp"),
        P(("dp", "tensor"), None),
    )
    out_specs = (
        P(("dp", "tensor"), None),
        P(("dp", "tensor"), None),
        P(None, "dp", "tensor"),
        P(None, "tensor"),
        P("tensor", "dp"),
        P("dp"),
        P("dp", "tensor"),
        P("tensor"),
        P("tensor", "dp"),
        P("dp"),
        P("dp"),
        P("dp"),
        P("dp"),
        P("dp"),
    )
    return jax.shard_map(body, mesh=mesh, in_specs=in_specs, out_specs=out_specs, check_vma=False)
```

time: 319 us -> 275 us (0.86)
  the two profiles are of different devices: /device:TPU:16 before, /device:TPU:0 now
where the time goes in v1:
time: 275 us; the launch traced here: 273 us
  Pallas kernels  97.9 us (36%)
  waiting for transfers between devices  57.4 us (21%)
  starting transfers between devices  52.5 us (19%)
  local copies, waits for them, and re-layouts  34 us (12%)
  other arithmetic  17 us (6%)
  between operations  14.6 us (5%)
    ppermute x24, starting transfers between devices, swapped(): return lax.ppermute(block, axis, route)  37.9 us
    ppermute x24, waiting for transfers between devices, swapped(): return lax.ppermute(block, axis, route)  37.8 us
    pallas_call x1, Pallas kernels, feed_forward(): pl.pallas_call(functools.partial(ff_kernel, len(pieces)), grid_spec=pltpu...  23.2 us
    pallas_call x1, Pallas kernels, backward_own(): pl.pallas_call(functools.partial(own_bwd_kernel, heads, halo), grid_spec=...  17 us
    unnamed x71, local copies, waits for them, and re-layouts  14.3 us
    pallas_call x1, Pallas kernels, attention_forward(): pl.pallas_call(functools.partial(attn_fwd_kernel, heads, halo), grid_spec...  14.1 us
    ppermute x3, waiting for transfers between devices, ring_gather(): from_right = lax.ppermute(from_right, axis, behind)  11.7 us
    pallas_call x1, Pallas kernels, input_gradient(): pl.pallas_call(functools.partial(input_grad_kernel, halo), grid_spec=pltp...  11.6 us
  transfers between devices with their start and end apart: 35, of which 14 were waited for; matrix products, arithmetic and copies ran while one was open for 12% of the time, Pallas kernels for 24%

profile of v1, /device:TPU:0, one launch (start us, length us, event | category | flops | bytes accessed | tf_op | source)
XLA Modules:
  0.0 273.4 jit_solution(8428701308971012671)
XLA Ops:
  11.5 3.0 %collective-permute-start.7 = (bf16[96,2432]{1,0:T(8,128)(2,1)S(1)}, bf16[96,2432]{1,0:T(8,128)(2,1)S(1)}, u32[]{:S(2)}, u32[]{:S(2)}) collective-permute-start(bf16[96,2432]{1,0:T(8,128)(2,1)S(1)} %concatenate.73.refs_0_), channel_id=1, source_target_pairs={{8,0},{16,8},{24,16},{28,24},{20,28},{12,20},{4,12},{0,4},{9,1},{1... | collective-permute-start | bytes 1400840 | tf_op jit(solution)/shard_map/ppermute | solution.py:78
  14.6 1.9 collective-permute-start.3
  17.4 1.3 dynamic-slice_bitcast_fusion.start_ref
  19.6 5.7 %collective-permute-done.7.refs_2_ = bf16[96,2432]{1,0:T(8,128)(2,1)S(1)} collective-permute-done((bf16[96,2432]{1,0:T(8,128)(2,1)S(1)}, bf16[96,2432]{1,0:T(8,128)(2,1)S(1)}, u32[]{:S(2)}, u32[]{:S(2)}) %collective-permute-start.7) | collective-permute-done | bytes 466976 | tf_op jit(solution)/shard_map/ppermute | solution.py:78
  25.3 1.5 collective-permute-done.6.refs_1_
  26.7 1.6 collective-permute-start.9
  31.6 3.5 %collective-permute-done.3 = bf16[512,768]{1,0:T(8,128)(2,1)} collective-permute-done((bf16[512,768]{1,0:T(8,128)(2,1)S(1)}, bf16[512,768]{1,0:T(8,128)(2,1)}, u32[]{:S(2)}, u32[]{:S(2)}) %collective-permute-start.3) | collective-permute-done | bytes 786464 | tf_op jit(solution)/shard_map/ppermute | solution.py:49
  35.2 16.4 %collective-permute-done = bf16[512,768]{1,0:T(8,128)(2,1)S(1)} collective-permute-done((bf16[512,768]{1,0:T(8,128)(2,1)S(1)}, bf16[512,768]{1,0:T(8,128)(2,1)S(1)}, u32[]{:S(2)}, u32[]{:S(2)}) %collective-permute-start) | collective-permute-done | bytes 786464 | tf_op jit(solution)/shard_map/ppermute | solution.py:49
  52.6 1.8 collective-permute-start.11
  54.7 1.2 constant_dynamic-update-slice_fusion.6
  56.8 1.2 constant_dynamic-update-slice_fusion.5
  58.0 2.1 constant_dynamic-update-slice_fusion.1
  60.0 6.0 %collective-permute-done.11.refs_6_ = bf16[96,2432]{1,0:T(8,128)(2,1)S(1)} collective-permute-done((bf16[96,2432]{1,0:T(8,128)(2,1)}, bf16[96,2432]{1,0:T(8,128)(2,1)S(1)}, u32[]{:S(2)}, u32[]{:S(2)}) %collective-permute-start.11) | collective-permute-done | bytes 466976 | tf_op jit(solution)/shard_map/ppermute | solution.py:78
  66.0 1.7 collective-permute-start.13
  69.4 4.1 %collective-permute-done.13.refs_8_ = bf16[48,2432]{1,0:T(8,128)(2,1)S(1)} collective-permute-done((bf16[48,2432]{1,0:T(8,128)(2,1)S(1)}, bf16[48,2432]{1,0:T(8,128)(2,1)S(1)}, u32[]{:S(2)}, u32[]{:S(2)}) %collective-permute-start.13) | collective-permute-done | bytes 233504 | tf_op jit(solution)/shard_map/ppermute | solution.py:81
  73.5 1.4 collective-permute-done.12.refs_7_
  75.6 10.5 %project.1 = (bf16[192,2048]{1,0:T(8,128)(2,1)}, bf16[192,2048]{1,0:T(8,128)(2,1)}, bf16[192,2048]{1,0:T(8,128)(2,1)}, bf16[192,2048]{1,0:T(8,128)(2,1)}, bf16[768,768]{1,0:T(8,128)(2,1)}, /*index=5*/f32[8,768]{1,0:T(8,128)}) custom-call(s32[9]{0:T(128)} %dynamic-slice_bitcast_fusion.start_ref, s32[4]{0:T(128)} %pad_add_fusion.place_ref, ...), custom_call_target="tpu_custom_call" | custom-call | flops 2415919104 | bytes 11796480 | tf_op jit(solution)/shard_map/project/pallas_call | solution.py:234
  88.1 3.7 %collective-permute-start.14 = (bf16[384,768]{1,0:T(8,128)(2,1)S(1)}, bf16[384,768]{1,0:T(8,128)(2,1)S(1)}, u32[]{:S(2)}, u32[]{:S(2)}) collective-permute-start(bf16[384,768]{1,0:T(8,128)(2,1)S(1)} %pad_maximum_fusion), channel_id=1, source_target_pairs={{0,4},{4,8},{8,12},{12,16},{16,20},{20,24},{24,28},{1,5},{5,9},{9,... | collective-permute-start | bytes 1769480 | tf_op jit(solution)/shard_map/ppermute | solution.py:44
  91.8 23.2 %feed_forward.1 = (bf16[2048,768]{1,0:T(8,128)(2,1)}, bf16[2048,768]{1,0:T(8,128)(2,1)}, bf16[768,1536]{1,0:T(8,128)(2,1)}, f32[8,768]{1,0:T(8,128)}) custom-call(s32[9]{0:T(128)} %dynamic-slice_bitcast_fusion.start_ref, bf16[2048,768]{1,0:T(8,128)(2,1)} %constant_dynamic-update-slice_fusion.x_ref, bf16[2048,768]{1,0:T(8,128)(2,1)} %copy-done.1, ...), custom_call_target="tpu_custom_call" | custom-call | flops 14495514624 | bytes 17301504 | tf_op jit(solution)/shard_map/feed_forward/pallas_call | solution.py:174
  115.1 1.7 slice.147.w_ref
  117.6 14.1 %attention_forward.1 = (bf16[192,2048]{1,0:T(8,128)(2,1)}, f32[8,2048]{1,0:T(8,128)}) custom-call(s32[8]{0:T(128)} %and_select_fusion.first_ref, bf16[192,2048]{1,0:T(8,128)(2,1)} %get-tuple-element.62.q_ref, bf16[192,2048]{1,0:T(8,128)(2,1)} %get-tuple-element.63.k_ref, bf16[192,2048]{1,0:T(8,128)(2,1)} %get-tuple-element.64.v_ref, ...), custom_call_target="tpu_custom_call" | custom-call | flops 6442450944 | bytes 3145728 | tf_op jit(solution)/shard_map/attention_forward/pallas_call | solution.py:312
  131.6 8.6 %branch_out.1 = (bf16[1024,768]{1,0:T(8,128)(2,1)}, bf16[1024,768]{1,0:T(8,128)(2,1)}, bf16[384,192]{1,0:T(8,128)(2,1)}, bf16[384,192]{1,0:T(8,128)(2,1)}) custom-call(s32[4]{0:T(128)} %pad_add_fusion.place_ref, s32[8]{0:T(128)} %concatenate.70.chunk_ref, bf16[192,2048]{1,0:T(8,128)(2,1)} %get-tuple-element.65.o_ref, ...), custom_call_target="tpu_custom_call" | custom-call | flops 1207959552 | bytes 9437184 | tf_op jit(solution)/shard_map/branch_out/pallas_call | solution.py:528
  141.4 5.5 %collective-permute-start.16 = (bf16[384,192]{1,0:T(8,128)(2,1)S(1)}, bf16[384,192]{1,0:T(8,128)(2,1)S(1)}, u32[]{:S(2)}, u32[]{:S(2)}) collective-permute-start(bf16[384,192]{1,0:T(8,128)(2,1)S(1)} %copy-done.28), channel_id=1, source_target_pairs={{0,4},{4,0},{8,12},{12,8},{16,20},{20,16},{24,28},{28,24},{1,5},{5... | collective-permute-start | bytes 442376 | tf_op jit(solution)/shard_map/ppermute | solution.py:49
  146.9 4.3 %attention_backward_left.1 = (f32[192,768]{1,0:T(8,128)}, bf16[384,768]{1,0:T(8,128)(2,1)}) custom-call(s32[8]{0:T(128)} %and_select_fusion.first_ref, bf16[192,2048]{1,0:T(8,128)(2,1)} %get-tuple-element.62.q_ref, bf16[384,768]{1,0:T(8,128)(2,1)} %copy-done.26, s32[1,2048]{1,0:T(1,128)} %bitcast.70, bf16[192,2048]{1,0:T(8,128)(2,1)} %get-tuple-element.65.o_ref, ...), custom_call_target="tpu_custom_call" | custom-call | flops 3019898880 | bytes 2949120 | tf_op jit(solution)/shard_map/attention_backward_left/pallas_call | solution.py:423
  151.2 1.2 collective-permute-done.16
  153.7 3.3 %collective-permute-start.19 = (bf16[96,192]{1,0:T(8,128)(2,1)S(1)}, bf16[96,192]{1,0:T(8,128)(2,1)S(1)}, u32[]{:S(2)}, u32[]{:S(2)}) collective-permute-start(bf16[96,192]{1,0:T(8,128)(2,1)S(1)} %get-tuple-element.157), channel_id=1, source_target_pairs={{0,8},{4,12},{8,0},{12,4},{16,24},{20,28},{24,16},{28,20},{1,9},{5... | collective-permute-start | bytes 110600 | tf_op jit(solution)/shard_map/ppermute | solution.py:49
  157.0 4.0 %collective-permute-start.21 = (bf16[96,192]{1,0:T(8,128)(2,1)S(1)}, bf16[96,192]{1,0:T(8,128)(2,1)S(1)}, u32[]{:S(2)}, u32[]{:S(2)}) collective-permute-start(bf16[96,192]{1,0:T(8,128)(2,1)S(1)} %get-tuple-element.158), channel_id=1, source_target_pairs={{0,24},{4,28},{8,16},{12,20},{16,8},{20,12},{24,0},{28,4},{1,25},{... | collective-permute-start | bytes 110600 | tf_op jit(solution)/shard_map/ppermute | solution.py:49
  161.1 1.5 collective-permute-start.17
  162.6 1.6 collective-permute-start.18
  164.2 17.0 %attention_backward_own.1 = (f32[192,2048]{1,0:T(8,128)}, f32[192,2048]{1,0:T(8,128)}, f32[192,2048]{1,0:T(8,128)}) custom-call(s32[8]{0:T(128)} %and_select_fusion.first_ref, bf16[192,2048]{1,0:T(8,128)(2,1)} %get-tuple-element.62.q_ref, bf16[192,2048]{1,0:T(8,128)(2,1)} %get-tuple-element.63.k_ref, bf16[192,2048]{1,0:T(8,128)(2,1)} %get-tuple-element.64.v_ref, ...), custom_call_target="tpu_custom_call" | custom-call | flops 16106127360 | bytes 7864320 | tf_op jit(solution)/shard_map/attention_backward_own/pallas_call | solution.py:453
  183.1 11.6 %input_gradient.1 = (bf16[1024,768]{1,0:T(8,128)(2,1)}, bf16[1024,768]{1,0:T(8,128)(2,1)}, bf16[576,2048]{1,0:T(8,128)(2,1)}, f32[8,768]{1,0:T(8,128)}, f32[576,1]{1,0:T(8,128)}) custom-call(s32[4]{0:T(128)} %pad_add_fusion.place_ref, f32[192,2048]{1,0:T(8,128)} %get-tuple-element.83.dq_ref, f32[192,2048]{1,0:T(8,128)} %get-tuple-element.84.dk_ref, ...), custom_call_target="tpu_custom_call" | custom-call | flops 3623878656 | bytes 15728640 | tf_op jit(solution)/shard_map/input_gradient/pallas_call | solution.py:603
  197.3 8.5 %weight_gradient.1 = (bf16[384,576]{1,0:T(8,128)(2,1)}, bf16[384,576]{1,0:T(8,128)(2,1)}) custom-call(s32[4]{0:T(128)} %pad_add_fusion.place_ref, s32[8]{0:T(128)} %concatenate.70.chunk_ref, bf16[576,2048]{1,0:T(8,128)(2,1)} %get-tuple-element.90.grad_ref, bf16[2048,768]{1,0:T(8,128)(2,1)} %constant_dynamic-update-slice_fusion.x_ref, ...), custom_call_target="tpu_custom_call" | custom-call | flops 3623878656 | bytes 6291456 | tf_op jit(solution)/shard_map/weight_gradient/pallas_call | solution.py:644
  205.8 2.2 add_convert_fusion
  208.0 9.8 %collective-permute-start.24 = (bf16[384,576]{1,0:T(8,128)(2,1)}, bf16[384,576]{1,0:T(8,128)(2,1)S(1)}, u32[]{:S(2)}, u32[]{:S(2)}) collective-permute-start(bf16[384,576]{1,0:T(8,128)(2,1)} %get-tuple-element.96), channel_id=1, source_target_pairs={{0,4},{4,0},{8,12},{12,8},{16,20},{20,16},{24,28},{28,24},{1,5},{5... | collective-permute-start | bytes 1327112 | tf_op jit(solution)/shard_map/ppermute | solution.py:49
  220.1 1.6 collective-permute-start.23
  221.7 9.0 %collective-permute-done.25 = f32[4,16,128]{2,1,0:T(8,128)S(1)} collective-permute-done((f32[4,16,128]{2,1,0:T(8,128)S(1)}, f32[4,16,128]{2,1,0:T(8,128)S(1)}, u32[]{:S(2)}, u32[]{:S(2)}) %collective-permute-start.25) | collective-permute-done | bytes 32800 | tf_op jit(solution)/shard_map/ppermute | solution.py:49
  230.7 1.8 convert_element_type.128
  233.4 1.3 convert_add_fusion.2
  234.6 2.4 collective-permute-start.29
  239.4 2.8 %collective-permute-start.26 = (bf16[96,576]{1,0:T(8,128)(2,1)}, bf16[96,576]{1,0:T(8,128)(2,1)S(1)}, u32[]{:S(2)}, u32[]{:S(2)}) collective-permute-start(bf16[96,576]{1,0:T(8,128)(2,1)} %get-tuple-element.154), channel_id=1, source_target_pairs={{0,8},{4,12},{8,0},{12,4},{16,24},{20,28},{24,16},{28,20},{1,9},{5... | collective-permute-start | bytes 331784 | tf_op jit(solution)/shard_map/ppermute | solution.py:49
  244.4 1.1 collective-permute-done.32
  245.6 1.5 collective-permute-start.33
  247.7 1.4 collective-permute-done.33
  250.3 4.4 %collective-permute-done.27 = bf16[96,576]{1,0:T(8,128)(2,1)} collective-permute-done((bf16[96,576]{1,0:T(8,128)(2,1)}, bf16[96,576]{1,0:T(8,128)(2,1)}, u32[]{:S(2)}, u32[]{:S(2)}) %collective-permute-start.27) | collective-permute-done | bytes 110624 | tf_op jit(solution)/shard_map/ppermute | solution.py:49
  254.7 1.7 convert_add_fusion.4
  258.4 2.0 slice_bitcast_fusion
  260.4 2.2 fusion.13
  262.7 3.3 %fusion.8 = (bf16[512,768]{1,0:T(8,128)(2,1)}, bf16[512,768]{1,0:T(8,128)(2,1)}) fusion(bf16[512,768]{1,0:T(8,128)(2,1)S(1)} %copy-done, bf16[512,768]{1,0:T(8,128)(2,1)S(1)} %copy-done.4, f32[512]{0:T(512)S(1)} %get-tuple-element.171, f32[512]{0:T(512)S(1)} %get-tuple-element.172, f32[512]{0:T(512)S(1)} %add_rsqrt_fusion, ...), kind=kLoop, calls=%fused_computation.12 | loop fusion | flops 9437184 | bytes 7878656 | tf_op jit(solution)/shard_map/convert_element_type | solution.py:817
  (177 shorter events, 35.4 us)
Async XLA Ops:
  7.2 9.3 %copy-start = (bf16[512,768]{1,0:T(8,128)(2,1)S(1)}, bf16[512,768]{1,0:T(8,128)(2,1)}, u32[]{:S(2)}) copy-start(bf16[512,768]{1,0:T(8,128)(2,1)} %param.17) | copy-start | bytes 2359300
  7.2 9.5 %copy-start.20 = (s32[2048]{0:T(1024)S(1)}, s32[2048]{0:T(1024)}, u32[]{:S(2)}) copy-start(s32[2048]{0:T(1024)} %param.30) | copy-start | bytes 24580
  7.2 22.3 %copy-start.24 = (bf16[768]{0:T(1024)(128)(2,1)S(1)}, bf16[768]{0:T(1024)(128)(2,1)}, u32[]{:S(2)}) copy-start(bf16[768]{0:T(1024)(128)(2,1)} %param.23) | copy-start | bytes 4612
  7.2 22.9 %copy-start.22 = (bf16[3,192]{1,0:T(4,128)(2,1)S(1)}, bf16[3,192]{1,0:T(4,128)(2,1)}, u32[]{:S(2)}) copy-start(bf16[3,192]{1,0:T(4,128)(2,1)} %param.19) | copy-start | bytes 3460
  7.2 223.4 %reduce-scatter.2.cloned.1.call-start = ((), (), s32[]{:S(2)}) async-start(), calls=%async_computation.1 | async-start | bytes 2654208 | tf_op jit(solution)/shard_map/reduce_scatter | solution.py:755
  11.5 41.1 %copy-start.5 = (bf16[96,2432]{1,0:T(8,128)(2,1)}, bf16[96,2432]{1,0:T(8,128)(2,1)S(1)}, u32[]{:S(2)}) copy-start(bf16[96,2432]{1,0:T(8,128)(2,1)S(1)} %concatenate.73.refs_0_) | copy-start | bytes 1400836
  11.5 13.8 %collective-permute-start.7 = (bf16[96,2432]{1,0:T(8,128)(2,1)S(1)}, bf16[96,2432]{1,0:T(8,128)(2,1)S(1)}, u32[]{:S(2)}, u32[]{:S(2)}) collective-permute-start(bf16[96,2432]{1,0:T(8,128)(2,1)S(1)} %concatenate.73.refs_0_), channel_id=1, source_target_pairs={{8,0},{16,8},{24,16},{28,24},{20,28},{12,20},{4,12},{0,4},{9,1},{1... | collective-permute-start | bytes 1400840 | tf_op jit(solution)/shard_map/ppermute | solution.py:78
  14.5 12.3 %collective-permute-start.6 = (bf16[96,2432]{1,0:T(8,128)(2,1)S(1)}, bf16[96,2432]{1,0:T(8,128)(2,1)}, u32[]{:S(2)}, u32[]{:S(2)}) collective-permute-start(bf16[96,2432]{1,0:T(8,128)(2,1)S(1)} %concatenate.73.refs_0_), channel_id=1, source_target_pairs={{0,8},{8,16},{16,24},{24,28},{28,20},{20,12},{12,4},{4,0},{1,9},{9... | collective-permute-start | bytes 1400840 | tf_op jit(solution)/shard_map/ppermute | solution.py:77
  14.6 13.7 %collective-permute-start.4 = (bf16[512,768]{1,0:T(8,128)(2,1)S(1)}, bf16[512,768]{1,0:T(8,128)(2,1)}, u32[]{:S(2)}, u32[]{:S(2)}) collective-permute-start(bf16[512,768]{1,0:T(8,128)(2,1)S(1)} %copy-done.3), channel_id=1, source_target_pairs={{0,1},{1,0},{2,3},{3,2},{4,5},{5,4},{6,7},{7,6},{8,9},{9,8},{10,11... | collective-permute-start | bytes 2359304 | tf_op jit(solution)/shard_map/ppermute | solution.py:49
  14.6 20.5 %collective-permute-start.3 = (bf16[512,768]{1,0:T(8,128)(2,1)S(1)}, bf16[512,768]{1,0:T(8,128)(2,1)}, u32[]{:S(2)}, u32[]{:S(2)}) collective-permute-start(bf16[512,768]{1,0:T(8,128)(2,1)S(1)} %copy-done.3), channel_id=1, source_target_pairs={{0,2},{1,3},{2,0},{3,1},{4,6},{5,7},{6,4},{7,5},{8,10},{9,11},{10,... | collective-permute-start | bytes 2359304 | tf_op jit(solution)/shard_map/ppermute | solution.py:49
  16.5 35.1 %collective-permute-start = (bf16[512,768]{1,0:T(8,128)(2,1)S(1)}, bf16[512,768]{1,0:T(8,128)(2,1)S(1)}, u32[]{:S(2)}, u32[]{:S(2)}) collective-permute-start(bf16[512,768]{1,0:T(8,128)(2,1)S(1)} %copy-done), channel_id=1, source_target_pairs={{0,2},{1,3},{2,0},{3,1},{4,6},{5,7},{6,4},{7,5},{8,10},{9,11},{10,... | collective-permute-start | bytes 2359304 | tf_op jit(solution)/shard_map/ppermute | solution.py:49
  16.7 35.8 %copy-start.21 = (s32[2048]{0:T(1024)}, s32[2048]{0:T(1024)S(1)}, u32[]{:S(2)}) copy-start(s32[2048]{0:T(1024)S(1)} %get-tuple-element.166) | copy-start | bytes 24580
  25.3 27.3 %copy-start.15 = (bf16[96,2432]{1,0:T(8,128)(2,1)}, bf16[96,2432]{1,0:T(8,128)(2,1)S(1)}, u32[]{:S(2)}) copy-start(bf16[96,2432]{1,0:T(8,128)(2,1)S(1)} %collective-permute-done.7.refs_2_) | copy-start | bytes 1400836
  25.3 32.7 %collective-permute-start.1 = (bf16[512,768]{1,0:T(8,128)(2,1)S(1)}, bf16[512,768]{1,0:T(8,128)(2,1)}, u32[]{:S(2)}, u32[]{:S(2)}) collective-permute-start(bf16[512,768]{1,0:T(8,128)(2,1)S(1)} %copy-done), channel_id=1, source_target_pairs={{0,1},{1,0},{2,3},{3,2},{4,5},{5,4},{6,7},{7,6},{8,9},{9,8},{10,11... | collective-permute-start | bytes 2359304 | tf_op jit(solution)/shard_map/ppermute | solution.py:49
  26.7 25.8 %collective-permute-start.9 = (bf16[96,2432]{1,0:T(8,128)(2,1)S(1)}, bf16[96,2432]{1,0:T(8,128)(2,1)}, u32[]{:S(2)}, u32[]{:S(2)}) collective-permute-start(bf16[96,2432]{1,0:T(8,128)(2,1)S(1)} %collective-permute-done.7.refs_2_), channel_id=1, source_target_pairs={{8,0},{16,8},{24,16},{28,24},{20,28},{12,20},{4,12},{0,4},{9,1},{1... | collective-permute-start | bytes 1400840 | tf_op jit(solution)/shard_map/ppermute | solution.py:78
  28.3 26.0 %collective-permute-start.8 = (bf16[96,2432]{1,0:T(8,128)(2,1)}, bf16[96,2432]{1,0:T(8,128)(2,1)}, u32[]{:S(2)}, u32[]{:S(2)}) collective-permute-start(bf16[96,2432]{1,0:T(8,128)(2,1)} %collective-permute-done.6.refs_1_), channel_id=1, source_target_pairs={{0,8},{8,16},{16,24},{24,28},{28,20},{20,12},{12,4},{4,0},{1,9},{9... | collective-permute-start | bytes 1400840 | tf_op jit(solution)/shard_map/ppermute | solution.py:77
  35.2 33.0 %collective-permute-start.5 = (bf16[512,768]{1,0:T(8,128)(2,1)}, bf16[512,768]{1,0:T(8,128)(2,1)S(1)}, u32[]{:S(2)}, u32[]{:S(2)}) collective-permute-start(bf16[512,768]{1,0:T(8,128)(2,1)} %collective-permute-done.3), channel_id=1, source_target_pairs={{0,1},{1,0},{2,3},{3,2},{4,5},{5,4},{6,7},{7,6},{8,9},{9,8},{10,11... | collective-permute-start | bytes 2359304 | tf_op jit(solution)/shard_map/ppermute | solution.py:49
  51.6 16.7 %collective-permute-start.2 = (bf16[512,768]{1,0:T(8,128)(2,1)S(1)}, bf16[512,768]{1,0:T(8,128)(2,1)S(1)}, u32[]{:S(2)}, u32[]{:S(2)}) collective-permute-start(bf16[512,768]{1,0:T(8,128)(2,1)S(1)} %collective-permute-done), channel_id=1, source_target_pairs={{0,1},{1,0},{2,3},{3,2},{4,5},{5,4},{6,7},{7,6},{8,9},{9,8},{10,11... | collective-permute-start | bytes 2359304 | tf_op jit(solution)/shard_map/ppermute | solution.py:49
  52.6 13.4 %collective-permute-start.11 = (bf16[96,2432]{1,0:T(8,128)(2,1)}, bf16[96,2432]{1,0:T(8,128)(2,1)S(1)}, u32[]{:S(2)}, u32[]{:S(2)}) collective-permute-start(bf16[96,2432]{1,0:T(8,128)(2,1)} %collective-permute-done.9.refs_4_), channel_id=1, source_target_pairs={{8,0},{16,8},{24,16},{28,24},{20,28},{12,20},{4,12},{0,4},{9,1},{1... | collective-permute-start | bytes 1400840 | tf_op jit(solution)/shard_map/ppermute | solution.py:78
  54.4 13.4 %collective-permute-start.10 = (bf16[96,2432]{1,0:T(8,128)(2,1)}, bf16[96,2432]{1,0:T(8,128)(2,1)S(1)}, u32[]{:S(2)}, u32[]{:S(2)}) collective-permute-start(bf16[96,2432]{1,0:T(8,128)(2,1)} %collective-permute-done.8.refs_3_), channel_id=1, source_target_pairs={{0,8},{8,16},{16,24},{24,28},{28,20},{20,12},{12,4},{4,0},{1,9},{9... | collective-permute-start | bytes 1400840 | tf_op jit(solution)/shard_map/ppermute | solution.py:77
  66.0 7.4 %collective-permute-start.13 = (bf16[48,2432]{1,0:T(8,128)(2,1)S(1)}, bf16[48,2432]{1,0:T(8,128)(2,1)S(1)}, u32[]{:S(2)}, u32[]{:S(2)}) collective-permute-start(bf16[48,2432]{1,0:T(8,128)(2,1)S(1)} %slice.190), channel_id=1, source_target_pairs={{8,0},{16,8},{24,16},{28,24},{20,28},{12,20},{4,12},{0,4},{9,1},{1... | collective-permute-start | bytes 700424 | tf_op jit(solution)/shard_map/ppermute | solution.py:81
  67.8 7.1 %collective-permute-start.12 = (bf16[48,2432]{1,0:T(8,128)(2,1)S(1)}, bf16[48,2432]{1,0:T(8,128)(2,1)S(1)}, u32[]{:S(2)}, u32[]{:S(2)}) collective-permute-start(bf16[48,2432]{1,0:T(8,128)(2,1)S(1)} %slice.189), channel_id=1, source_target_pairs={{0,8},{8,16},{16,24},{24,28},{28,20},{20,12},{12,4},{4,0},{1,9},{9... | collective-permute-start | bytes 700424 | tf_op jit(solution)/shard_map/ppermute | solution.py:80
  88.1 28.6 %collective-permute-start.14 = (bf16[384,768]{1,0:T(8,128)(2,1)S(1)}, bf16[384,768]{1,0:T(8,128)(2,1)S(1)}, u32[]{:S(2)}, u32[]{:S(2)}) collective-permute-start(bf16[384,768]{1,0:T(8,128)(2,1)S(1)} %pad_maximum_fusion), channel_id=1, source_target_pairs={{0,4},{4,8},{8,12},{12,16},{16,20},{20,24},{24,28},{1,5},{5,9},{9,... | collective-permute-start | bytes 1769480 | tf_op jit(solution)/shard_map/ppermute | solution.py:44
  140.2 12.3 %collective-permute-start.15 = (bf16[1024,768]{1,0:T(8,128)(2,1)}, bf16[1024,768]{1,0:T(8,128)(2,1)S(1)}, u32[]{:S(2)}, u32[]{:S(2)}) collective-permute-start(bf16[1024,768]{1,0:T(8,128)(2,1)} %get-tuple-element.69), channel_id=1, source_target_pairs={{0,1},{1,0},{2,3},{3,2},{4,5},{5,4},{6,7},{7,6},{8,9},{9,8},{10,11... | collective-permute-start | bytes 4718600 | tf_op jit(solution)/shard_map/ppermute | solution.py:49
  141.4 11.0 %collective-permute-start.16 = (bf16[384,192]{1,0:T(8,128)(2,1)S(1)}, bf16[384,192]{1,0:T(8,128)(2,1)S(1)}, u32[]{:S(2)}, u32[]{:S(2)}) collective-permute-start(bf16[384,192]{1,0:T(8,128)(2,1)S(1)} %copy-done.28), channel_id=1, source_target_pairs={{0,4},{4,0},{8,12},{12,8},{16,20},{20,16},{24,28},{28,24},{1,5},{5... | collective-permute-start | bytes 442376 | tf_op jit(solution)/shard_map/ppermute | solution.py:49
  152.5 8.6 %copy-start.25 = (bf16[384,768]{1,0:T(8,128)(2,1)S(1)}, bf16[384,768]{1,0:T(8,128)(2,1)}, u32[]{:S(2)}) copy-start(bf16[384,768]{1,0:T(8,128)(2,1)} %get-tuple-element.77) | copy-start | bytes 1769476
  153.7 27.5 %collective-permute-start.19 = (bf16[96,192]{1,0:T(8,128)(2,1)S(1)}, bf16[96,192]{1,0:T(8,128)(2,1)S(1)}, u32[]{:S(2)}, u32[]{:S(2)}) collective-permute-start(bf16[96,192]{1,0:T(8,128)(2,1)S(1)} %get-tuple-element.157), channel_id=1, source_target_pairs={{0,8},{4,12},{8,0},{12,4},{16,24},{20,28},{24,16},{28,20},{1,9},{5... | collective-permute-start | bytes 110600 | tf_op jit(solution)/shard_map/ppermute | solution.py:49
  157.0 24.2 %collective-permute-start.21 = (bf16[96,192]{1,0:T(8,128)(2,1)S(1)}, bf16[96,192]{1,0:T(8,128)(2,1)S(1)}, u32[]{:S(2)}, u32[]{:S(2)}) collective-permute-start(bf16[96,192]{1,0:T(8,128)(2,1)S(1)} %get-tuple-element.158), channel_id=1, source_target_pairs={{0,24},{4,28},{8,16},{12,20},{16,8},{20,12},{24,0},{28,4},{1,25},{... | collective-permute-start | bytes 110600 | tf_op jit(solution)/shard_map/ppermute | solution.py:49
  161.1 20.2 %collective-permute-start.20 = (bf16[96,192]{1,0:T(8,128)(2,1)S(1)}, bf16[96,192]{1,0:T(8,128)(2,1)S(1)}, u32[]{:S(2)}, u32[]{:S(2)}) collective-permute-start(bf16[96,192]{1,0:T(8,128)(2,1)S(1)} %get-tuple-element.159), channel_id=1, source_target_pairs={{0,16},{4,20},{8,24},{12,28},{16,0},{20,4},{24,8},{28,12},{1,17},{... | collective-permute-start | bytes 110600 | tf_op jit(solution)/shard_map/ppermute | solution.py:49
  161.1 21.2 %collective-permute-start.17 = (bf16[384,768]{1,0:T(8,128)(2,1)S(1)}, bf16[384,768]{1,0:T(8,128)(2,1)S(1)}, u32[]{:S(2)}, u32[]{:S(2)}) collective-permute-start(bf16[384,768]{1,0:T(8,128)(2,1)S(1)} %copy-done.25), channel_id=1, source_target_pairs={{4,0},{8,4},{12,8},{16,12},{20,16},{24,20},{28,24},{5,1},{9,5},{13... | collective-permute-start | bytes 1769480 | tf_op jit(solution)/shard_map/ppermute | solution.py:44
  162.6 19.7 %collective-permute-start.18 = (bf16[512,768]{1,0:T(8,128)(2,1)S(1)}, bf16[512,768]{1,0:T(8,128)(2,1)S(1)}, u32[]{:S(2)}, u32[]{:S(2)}) collective-permute-start(bf16[512,768]{1,0:T(8,128)(2,1)S(1)} %add_convert_fusion.1), channel_id=1, source_target_pairs={{0,2},{1,3},{2,0},{3,1},{4,6},{5,7},{6,4},{7,5},{8,10},{9,11},{10,... | collective-permute-start | bytes 2359304 | tf_op jit(solution)/shard_map/ppermute | solution.py:49
  182.3 12.4 %copy-start.12 = (bf16[512,768]{1,0:T(8,128)(2,1)}, bf16[512,768]{1,0:T(8,128)(2,1)S(1)}, u32[]{:S(2)}) copy-start(bf16[512,768]{1,0:T(8,128)(2,1)S(1)} %collective-permute-done.18) | copy-start | bytes 2359300
  183.1 12.1 %copy-start.23 = (s32[8]{0:T(128)S(1)}, s32[8]{0:T(128)}, u32[]{:S(2)}) copy-start(s32[8]{0:T(128)} %concatenate.70.chunk_ref) | copy-start | bytes 100
  183.1 12.1 %copy-start.19 = (f32[8,768]{1,0:T(8,128)S(1)}, f32[8,768]{1,0:T(8,128)}, u32[]{:S(2)}) copy-start(f32[8,768]{1,0:T(8,128)} %get-tuple-element.94) | copy-start | bytes 73732
  194.7 11.1 %collective-permute-start.22 = (bf16[1024,768]{1,0:T(8,128)(2,1)}, bf16[1024,768]{1,0:T(8,128)(2,1)}, u32[]{:S(2)}, u32[]{:S(2)}) collective-permute-start(bf16[1024,768]{1,0:T(8,128)(2,1)} %get-tuple-element.89), channel_id=1, source_target_pairs={{0,1},{1,0},{2,3},{3,2},{4,5},{5,4},{6,7},{7,6},{8,9},{9,8},{10,11... | collective-permute-start | bytes 4718600 | tf_op jit(solution)/shard_map/ppermute | solution.py:49
  197.3 8.5 %copy-start.2 = (bf16[1024,768]{1,0:T(8,128)(2,1)S(1)}, bf16[1024,768]{1,0:T(8,128)(2,1)}, u32[]{:S(2)}) copy-start(bf16[1024,768]{1,0:T(8,128)(2,1)} %get-tuple-element.88) | copy-start | bytes 4718596
  208.0 24.5 %collective-permute-start.24 = (bf16[384,576]{1,0:T(8,128)(2,1)}, bf16[384,576]{1,0:T(8,128)(2,1)S(1)}, u32[]{:S(2)}, u32[]{:S(2)}) collective-permute-start(bf16[384,576]{1,0:T(8,128)(2,1)} %get-tuple-element.96), channel_id=1, source_target_pairs={{0,4},{4,0},{8,12},{12,8},{16,20},{20,16},{24,28},{28,24},{1,5},{5... | collective-permute-start | bytes 1327112 | tf_op jit(solution)/shard_map/ppermute | solution.py:49
  218.5 12.2 %collective-permute-start.25 = (f32[4,16,128]{2,1,0:T(8,128)S(1)}, f32[4,16,128]{2,1,0:T(8,128)S(1)}, u32[]{:S(2)}, u32[]{:S(2)}) collective-permute-start(f32[4,16,128]{2,1,0:T(8,128)S(1)} %slice.199), channel_id=1, source_target_pairs={{0,4},{4,0},{8,12},{12,8},{16,20},{20,16},{24,28},{28,24},{1,5},{5... | collective-permute-start | bytes 98312 | tf_op jit(solution)/shard_map/ppermute | solution.py:49
  220.1 40.3 %collective-permute-start.23 = (bf16[512,768]{1,0:T(8,128)(2,1)}, bf16[512,768]{1,0:T(8,128)(2,1)}, u32[]{:S(2)}, u32[]{:S(2)}) collective-permute-start(bf16[512,768]{1,0:T(8,128)(2,1)} %add_convert_fusion), channel_id=1, source_target_pairs={{0,2},{1,3},{2,0},{3,1},{4,6},{5,7},{6,4},{7,5},{8,10},{9,11},{10,... | collective-permute-start | bytes 2359304 | tf_op jit(solution)/shard_map/ppermute | solution.py:49
  234.6 7.6 %collective-permute-start.29 = (f32[1,16,128]{2,1,0:T(8,128)S(1)}, f32[1,16,128]{2,1,0:T(8,128)S(1)}, u32[]{:S(2)}, u32[]{:S(2)}) collective-permute-start(f32[1,16,128]{2,1,0:T(8,128)S(1)} %get-tuple-element.160), channel_id=1, source_target_pairs={{0,8},{4,12},{8,0},{12,4},{16,24},{20,28},{24,16},{28,20},{1,9},{5... | collective-permute-start | bytes 24584 | tf_op jit(solution)/shard_map/ppermute | solution.py:49
  237.1 6.1 %collective-permute-start.31 = (f32[1,16,128]{2,1,0:T(8,128)S(1)}, f32[1,16,128]{2,1,0:T(8,128)S(1)}, u32[]{:S(2)}, u32[]{:S(2)}) collective-permute-start(f32[1,16,128]{2,1,0:T(8,128)S(1)} %get-tuple-element.161), channel_id=1, source_target_pairs={{0,24},{4,28},{8,16},{12,20},{16,8},{20,12},{24,0},{28,4},{1,25},{... | collective-permute-start | bytes 24584 | tf_op jit(solution)/shard_map/ppermute | solution.py:49
  237.9 5.8 %collective-permute-start.30 = (f32[1,16,128]{2,1,0:T(8,128)S(1)}, f32[1,16,128]{2,1,0:T(8,128)S(1)}, u32[]{:S(2)}, u32[]{:S(2)}) collective-permute-start(f32[1,16,128]{2,1,0:T(8,128)S(1)} %get-tuple-element.162), channel_id=1, source_target_pairs={{0,16},{4,20},{8,24},{12,28},{16,0},{20,4},{24,8},{28,12},{1,17},{... | collective-permute-start | bytes 24584 | tf_op jit(solution)/shard_map/ppermute | solution.py:49
  239.4 10.3 %collective-permute-start.26 = (bf16[96,576]{1,0:T(8,128)(2,1)}, bf16[96,576]{1,0:T(8,128)(2,1)S(1)}, u32[]{:S(2)}, u32[]{:S(2)}) collective-permute-start(bf16[96,576]{1,0:T(8,128)(2,1)} %get-tuple-element.154), channel_id=1, source_target_pairs={{0,8},{4,12},{8,0},{12,4},{16,24},{20,28},{24,16},{28,20},{1,9},{5... | collective-permute-start | bytes 331784 | tf_op jit(solution)/shard_map/ppermute | solution.py:49
  242.3 8.0 %collective-permute-start.28 = (bf16[96,576]{1,0:T(8,128)(2,1)}, bf16[96,576]{1,0:T(8,128)(2,1)}, u32[]{:S(2)}, u32[]{:S(2)}) collective-permute-start(bf16[96,576]{1,0:T(8,128)(2,1)} %get-tuple-element.155), channel_id=1, source_target_pairs={{0,24},{4,28},{8,16},{12,20},{16,8},{20,12},{24,0},{28,4},{1,25},{... | collective-permute-start | bytes 331784 | tf_op jit(solution)/shard_map/ppermute | solution.py:49
  243.1 11.5 %collective-permute-start.27 = (bf16[96,576]{1,0:T(8,128)(2,1)}, bf16[96,576]{1,0:T(8,128)(2,1)}, u32[]{:S(2)}, u32[]{:S(2)}) collective-permute-start(bf16[96,576]{1,0:T(8,128)(2,1)} %get-tuple-element.156), channel_id=1, source_target_pairs={{0,16},{4,20},{8,24},{12,28},{16,0},{20,4},{24,8},{28,12},{1,17},{... | collective-permute-start | bytes 331784 | tf_op jit(solution)/shard_map/ppermute | solution.py:49
  244.4 1.2 collective-permute-start.32
  245.6 3.6 %collective-permute-start.33 = (f32[4,128]{1,0:T(4,128)S(1)}, f32[4,128]{1,0:T(4,128)S(1)}, u32[]{:S(2)}, u32[]{:S(2)}) collective-permute-start(f32[4,128]{1,0:T(4,128)S(1)} %fusion.15), channel_id=1, source_target_pairs={{0,2},{1,3},{2,0},{3,1},{4,6},{5,7},{6,4},{7,5},{8,10},{9,11},{10,... | collective-permute-start | bytes 6152 | tf_op jit(solution)/shard_map/ppermute | solution.py:49
  247.0 19.0 %copy-start.29 = (f32[96]{0:T(128)}, f32[96]{0:T(128)S(1)}, u32[]{:S(2)}) copy-start(f32[96]{0:T(128)S(1)} %slice_bitcast_fusion.4) | copy-start | bytes 1156
  (17 other events, 50.9 us)
Sparse Core Ops, SparseCore 0:
  140.8 85.2 reduce-scatter.1

commit v2 on v1

--- a/solution.py
+++ b/solution.py
@@ -53,11 +53,11 @@
     return list(range(0, n, 2)) + list(range(n - 1, 0, -2))
 
 
-def ring_gather(block, axis):
+def ring_gather(block, axis, early, late):
     n = lax.axis_size(axis)
     rows = block.shape[0]
     if n > 8:
-        return [lax.all_gather(block, axis, axis=0, tiled=True)], jnp.zeros((1,), jnp.int32)
+        return [lax.all_gather(block, axis, axis=0, tiled=True)], jnp.zeros((1,), jnp.int32), early, late
     ring = ring_order(n)
     ahead = [(ring[r], ring[(r + 1) % n]) for r in range(n)]
     behind = [(b, a) for a, b in ahead]
@@ -76,17 +76,20 @@
     for step in range(1, n // 2):
         from_left = lax.ppermute(from_left, axis, ahead)
         from_right = lax.ppermute(from_right, axis, behind)
+        if step == n // 2 - 1:
+            from_left, from_right, early = tied(from_left, from_right, early)
+        else:
+            from_left, from_right = tied(from_left, from_right)
         pieces += [from_left, from_right]
-    pieces.append(lax.ppermute(from_left[: rows // 2], axis, ahead))
-    pieces.append(lax.ppermute(from_right[rows // 2 :], axis, behind))
-    return pieces, jnp.asarray(table, jnp.int32)[lax.axis_index(axis)]
-
-
-def gather_rows(block):
-    far = swapped(block, "tensor", 2)
-    near = swapped(block, "tensor", 1)
-    both = swapped(far, "tensor", 1)
-    return jnp.concatenate([block, far, near, both], axis=0)
+    from_left = lax.ppermute(from_left[: rows // 2], axis, ahead)
+    from_right = lax.ppermute(from_right[rows // 2 :], axis, behind)
+    from_left, from_right, late = tied(from_left, from_right, late)
+    pieces += [from_left, from_right]
+    return pieces, jnp.asarray(table, jnp.int32)[lax.axis_index(axis)], early, late
+
+
+def gather_rows(block, near, far):
+    return jnp.concatenate([block, far, near, swapped(far, "tensor", 1)], axis=0)
 
 
 def scatter_near(keep, send):
@@ -94,10 +97,6 @@
     came = swapped(send, "tensor", 1)
     other = (keep[count:].astype(f32) + came[count:].astype(f32)).astype(bf16)
     return keep[:count], came[:count], other
-
-
-def scatter_far(own, came, other):
-    return own.astype(f32) + came.astype(f32) + swapped(other, "tensor", 2).astype(f32)
 
 
 def tied(*arrays):
@@ -120,29 +119,32 @@
         out_ref[pl.ds(pl.multiple_of(start_ref[n], rows), rows), :] = ref[:, columns]
 
 
-def norm_rows(x):
-    center = x - jnp.mean(x, axis=-1, keepdims=True)
-    inv_std = lax.rsqrt(jnp.mean(center * center, axis=-1, keepdims=True) + norm_eps)
-    return center * inv_std
-
-
-def ff_kernel(pieces, start_ref, x_ref, g_ref, b_ref, vec_ref, *refs):
+def row_stats(x):
+    mean = jnp.mean(x, axis=-1, keepdims=True)
+    center = x - mean
+    return mean, lax.rsqrt(jnp.mean(center * center, axis=-1, keepdims=True) + norm_eps)
+
+
+def normed_from(x_ref, stats_ref):
+    return (x_ref[...].astype(f32) - stats_ref[:, 0:1]) * stats_ref[:, 1:2]
+
+
+def ff_kernel(pieces, start_ref, x_ref, g_ref, stats_ref, b_ref, vec_ref, fc2_w, *refs):
     w_refs = refs[:pieces]
     out_ref, u_ref, grads_ref, small_ref = refs[pieces : pieces + 4]
-    fc_w, fc2_w, fc_acc, fc2_acc = refs[pieces + 4 :]
+    fc_w, fc_acc, fc2_acc = refs[pieces + 4 :]
     step = pl.program_id(0)
     ff = fc2_w.shape[1]
 
     @pl.when(step == 0)
     def _():
         assemble(w_refs, start_ref, 0, fc_w)
-        assemble(w_refs, start_ref, ff, fc2_w)
         fc_acc[...] = jnp.zeros_like(fc_acc)
         fc2_acc[...] = jnp.zeros_like(fc2_acc)
         small_ref[...] = jnp.zeros_like(small_ref)
 
     gain, shift = vec_ref[4:5, :], vec_ref[5:6, :]
-    normed = norm_rows(x_ref[...].astype(f32))
+    normed = normed_from(x_ref, stats_ref)
     normed_two = (normed * gain + shift).astype(bf16)
     pre = mm(normed_two, fc_w[...], 1, 0) + b_ref[...]
     cdf = 0.5 + 0.5 * lax.erf(pre * inv_sqrt_two)
@@ -166,7 +168,7 @@
         grads_ref[:, ff:] = fc2_acc[...].astype(bf16)
 
 
-def feed_forward(starts, x, g, b_fc, vec, pieces, ff):
+def feed_forward(starts, x, g, stats, b_fc, vec, fc2_w, pieces, ff):
     tokens, dim = x.shape
     rows = tokens // 4
     spec = pl.BlockSpec((rows, dim), lambda s, *_: (s, 0))
@@ -176,9 +178,17 @@
         grid_spec=pltpu.PrefetchScalarGridSpec(
             num_scalar_prefetch=1,
             grid=(4,),
-            in_specs=[spec, spec, whole((1, ff)), whole(vec.shape)] + [whole(p.shape) for p in pieces],
+            in_specs=[
+                spec,
+                spec,
+                pl.BlockSpec((rows, 128), lambda s, *_: (s, 0)),
+                whole((1, ff)),
+                whole(vec.shape),
+                whole(fc2_w.shape),
+            ]
+            + [whole(p.shape) for p in pieces],
             out_specs=[spec, spec, whole((dim, 2 * ff)), whole((8, dim))],
-            scratch_shapes=[pltpu.VMEM((dim, ff), bf16)] * 2 + [pltpu.VMEM((dim, ff), f32)] * 2,
+            scratch_shapes=[pltpu.VMEM((dim, ff), bf16)] + [pltpu.VMEM((dim, ff), f32)] * 2,
         ),
         out_shape=[
             shaped((tokens, dim), bf16),
@@ -189,7 +199,7 @@
         compiler_params=params(),
         cost_estimate=cost(12 * tokens * dim * ff, 8 * tokens * dim + 8 * dim * ff, 2 * tokens * ff),
         name="feed_forward",
-    )(starts, x, g, b_fc, vec, *pieces)
+    )(starts, x, g, stats, b_fc, vec, fc2_w, *pieces)
 
 
 def turned(x, cos_t, sin_t):
@@ -202,9 +212,9 @@
     return jnp.concatenate(out, axis=0)
 
 
-def project_kernel(pieces, first, start_ref, place_ref, x_ref, g_ref, b_ref, cos_ref, sin_ref, *refs):
+def project_kernel(pieces, first, start_ref, place_ref, x_ref, b_ref, cos_ref, sin_ref, *refs):
     w_refs = refs[:pieces]
-    q_ref, k_ref, v_ref, do_ref, wt_ref, vec_ref, packed = refs[pieces:]
+    q_ref, k_ref, v_ref, halo_ref, normed_ref, stats_ref, wt_ref, vec_ref, packed = refs[pieces:]
     feat = q_ref.shape[0]
     width = wt_ref.shape[0]
 
@@ -214,17 +224,32 @@
         wt_ref[...] = packed[:, :width].astype(f32).T.astype(bf16)
         vec_ref[...] = packed[:, width:].astype(f32).T[:8]
 
-    normed = norm_rows(x_ref[...].astype(f32))
-    normed_one = (normed * vec_ref[2:3, :] + vec_ref[3:4, :]).astype(bf16)
+    x = x_ref[...].astype(f32)
+    mean, inv_std = row_stats(x)
+    lane = lax.broadcasted_iota(jnp.int32, stats_ref.shape, 1)
+    stats_ref[...] = jnp.where(lane == 0, mean, inv_std)
+    normed_one = ((x - mean) * inv_std * vec_ref[2:3, :] + vec_ref[3:4, :]).astype(bf16)
+    normed_ref[...] = normed_one
     proj = mm(wt_ref[: 3 * feat, :], normed_one, 1, 1) + b_ref[...]
     cos_t, sin_t = cos_ref[...], sin_ref[...]
     q_ref[...] = (turned(proj[:feat], cos_t, sin_t) * HEAD_DIM ** (-0.5)).astype(bf16)
     k_ref[...] = turned(proj[feat : 2 * feat], cos_t, sin_t).astype(bf16)
     v_ref[...] = proj[2 * feat :].astype(bf16)
-    do_ref[...] = mm(wt_ref[3 * feat :, :], g_ref[...], 1, 1).astype(bf16)
-
-
-def project(starts, places, x, g, b_col, cos_t, sin_t, pieces, first, feat):
+    rows = k_ref.shape[1]
+    halo = halo_ref.shape[1]
+    place = place_ref[pl.program_id(0)]
+    for n in range(4):
+        begin = max(0, 4 * rows - halo - n * rows)
+        if begin < rows:
+            to = n * rows + begin - (4 * rows - halo)
+
+            @pl.when(place == n)
+            def _():
+                halo_ref[:feat, to : to + rows - begin] = k_ref[:, begin:]
+                halo_ref[feat:, to : to + rows - begin] = v_ref[:, begin:]
+
+
+def project(starts, places, x, b_col, cos_t, sin_t, pieces, first, feat, halo):
     tokens, dim = x.shape
     rows = tokens // 4
     width = 4 * feat
@@ -236,16 +261,30 @@
         grid_spec=pltpu.PrefetchScalarGridSpec(
             num_scalar_prefetch=2,
             grid=(4,),
-            in_specs=[spec, spec, whole(b_col.shape), placed(ROT // 2), placed(ROT // 2)]
+            in_specs=[spec, whole(b_col.shape), placed(ROT // 2), placed(ROT // 2)]
             + [whole(p.shape) for p in pieces],
-            out_specs=[placed(feat)] * 4 + [whole((width, dim)), whole((8, dim))],
+            out_specs=[placed(feat)] * 3
+            + [
+                whole((2 * feat, halo)),
+                spec,
+                pl.BlockSpec((rows, 128), lambda s, *_: (s, 0)),
+                whole((width, dim)),
+                whole((8, dim)),
+            ],
             scratch_shapes=[pltpu.VMEM((dim, width + 128), bf16)],
         ),
-        out_shape=[shaped((feat, tokens), bf16)] * 4 + [shaped((width, dim), bf16), shaped((8, dim), f32)],
+        out_shape=[shaped((feat, tokens), bf16)] * 3
+        + [
+            shaped((2 * feat, halo), bf16),
+            shaped((tokens, dim), bf16),
+            shaped((tokens, 128), f32),
+            shaped((width, dim), bf16),
+            shaped((8, dim), f32),
+        ],
         compiler_params=params(),
-        cost_estimate=cost(8 * tokens * dim * feat, 6 * tokens * dim + 4 * dim * width),
+        cost_estimate=cost(6 * tokens * dim * feat, 6 * tokens * dim + 4 * dim * width),
         name="project",
-    )(starts, places, x, g, b_col, cos_t, sin_t, *pieces)
+    )(starts, places, x, b_col, cos_t, sin_t, *pieces)
 
 
 def key_mask(chunk, lo_row, hi_row):
@@ -501,7 +540,9 @@
             ref[n * size : (n + 1) * size, :] = value[at, :].astype(bf16)
 
 
-def out_kernel(place_ref, chunk_ref, o_ref, ff_ref, g_ref, w_ref, keep_ref, send_ref, wkeep_ref, wsend_ref, acc, acc_t):
+def out_kernel(
+    place_ref, chunk_ref, o_ref, ff_ref, g_ref, w_ref, keep_ref, send_ref, wkeep_ref, wsend_ref, do_ref, acc, acc_t
+):
     s = pl.program_id(0)
 
     @pl.when(s == 0)
@@ -511,6 +552,7 @@
     total = mm(o_ref[...], w_ref[...], 0, 0) + ff_ref[...].astype(f32)
     put_rows(keep_ref, send_ref, total.astype(bf16))
     acc[...] += mm(o_ref[...], g_ref[...], 1, 0)
+    do_ref[...] = mm(w_ref[...], g_ref[...], 1, 1).astype(bf16)
 
     @pl.when(s == pl.num_programs(0) - 1)
     def _():
@@ -518,32 +560,30 @@
         put_chunks(chunk_ref, wkeep_ref, wsend_ref, acc_t)
 
 
-def branch_out(places, chunks, o, ff_out, g, out_w):
+def branch_out(places, chunks, o, ff_out, g, wt):
     feat, tokens = o.shape
-    dim = out_w.shape[1]
+    dim = wt.shape[1]
     rows = tokens // 4
     keep, send = keep_send_specs(rows, dim)
     spec = pl.BlockSpec((rows, dim), lambda s, *_: (s, 0))
+    placed = pl.BlockSpec((feat, rows), lambda s, place, chunk: (0, place[s]))
     whole = lambda shape: pl.BlockSpec(shape, lambda s, *_: (0, 0))
     return pl.pallas_call(
         out_kernel,
         grid_spec=pltpu.PrefetchScalarGridSpec(
             num_scalar_prefetch=2,
             grid=(4,),
-            in_specs=[
-                pl.BlockSpec((feat, rows), lambda s, place, chunk: (0, place[s])),
-                spec,
-                spec,
-                whole((feat, dim)),
-            ],
-            out_specs=[keep, send, whole((dim // 2, feat)), whole((dim // 2, feat))],
+            in_specs=[placed, spec, spec, pl.BlockSpec((feat, dim), lambda s, *_: (3, 0))],
+            out_specs=[keep, send, whole((dim // 2, feat)), whole((dim // 2, feat)), placed],
             scratch_shapes=[pltpu.VMEM((feat, dim), f32), pltpu.VMEM((dim, feat), f32)],
         ),
-        out_shape=[shaped((tokens // 2, dim), bf16)] * 2 + [shaped((dim // 2, feat), bf16)] * 2,
+        out_shape=[shaped((tokens // 2, dim), bf16)] * 2
+        + [shaped((dim // 2, feat), bf16)] * 2
+        + [shaped((feat, tokens), bf16)],
         compiler_params=params(),
         cost_estimate=cost(4 * feat * tokens * dim, 6 * tokens * dim),
         name="branch_out",
-    )(places, chunks, o, ff_out, g, out_w)
+    )(places, chunks, o, ff_out, g, wt)
 
 
 def input_grad_kernel(
@@ -554,6 +594,7 @@
     dv_ref,
     back_ref,
     x_ref,
+    stats_ref,
     u2_ref,
     wt_ref,
     vec_ref,
@@ -587,12 +628,12 @@
     bias_ref[...] += jnp.sum(grad.astype(f32), axis=1, keepdims=True)
     one_grad = mm(grad, wt_ref[: 3 * feat, :], 0, 0)
     put_rows(keep_ref, send_ref, (one_grad * vec_ref[2:3, :] + u2_ref[...].astype(f32)).astype(bf16))
-    normed = norm_rows(x_ref[...].astype(f32))
+    normed = normed_from(x_ref, stats_ref)
     small_ref[0:1, :] += jnp.sum(one_grad * normed, axis=0, keepdims=True)
     small_ref[1:2, :] += jnp.sum(one_grad, axis=0, keepdims=True)
 
 
-def input_gradient(places, dq, dk, dv, back, x, u2, wt, vec, cos_t, sin_t, halo):
+def input_gradient(places, dq, dk, dv, back, x, stats, u2, wt, vec, cos_t, sin_t, halo):
     feat, tokens = dq.shape
     dim = x.shape[1]
     rows = tokens // 4
@@ -606,7 +647,8 @@
             num_scalar_prefetch=1,
             grid=(4,),
             in_specs=[placed(feat)] * 3
-            + [whole(back.shape), spec, spec, whole(wt.shape), whole(vec.shape)]
+            + [whole(back.shape), spec, pl.BlockSpec((rows, 128), lambda s, *_: (s, 0)), spec, whole(wt.shape)]
+            + [whole(vec.shape)]
             + [placed(ROT // 2)] * 2,
             out_specs=[keep, send, placed(3 * feat), whole((8, dim)), whole((3 * feat, 1))],
             scratch_shapes=[pltpu.VMEM((2 * feat, tokens), bf16)],
@@ -616,19 +658,17 @@
         compiler_params=params(),
         cost_estimate=cost(12 * feat * tokens * dim, 10 * tokens * dim),
         name="input_gradient",
-    )(places, dq, dk, dv, back, x, u2, wt, vec, cos_t, sin_t)
-
-
-def weight_grad_kernel(place_ref, chunk_ref, grad_ref, x_ref, vec_ref, wkeep_ref, wsend_ref, acc, acc_t):
+    )(places, dq, dk, dv, back, x, stats, u2, wt, vec, cos_t, sin_t)
+
+
+def weight_grad_kernel(place_ref, chunk_ref, grad_ref, normed_ref, wkeep_ref, wsend_ref, acc, acc_t):
     s = pl.program_id(0)
 
     @pl.when(s == 0)
     def _():
         acc[...] = jnp.zeros_like(acc)
 
-    normed = norm_rows(x_ref[...].astype(f32))
-    normed_one = (normed * vec_ref[2:3, :] + vec_ref[3:4, :]).astype(bf16)
-    acc[...] += mm(grad_ref[...], normed_one, 1, 0)
+    acc[...] += mm(grad_ref[...], normed_ref[...], 1, 0)
 
     @pl.when(s == pl.num_programs(0) - 1)
     def _():
@@ -636,9 +676,10 @@
         put_chunks(chunk_ref, wkeep_ref, wsend_ref, acc_t)
 
 
-def weight_gradient(places, chunks, grad, x, vec):
+def weight_gradient(places, chunks, grad, normed, part, parts):
     width, tokens = grad.shape
-    dim = x.shape[1]
+    width = width // parts
+    dim = normed.shape[1]
     rows = tokens // 4
     whole = lambda shape: pl.BlockSpec(shape, lambda s, *_: (0, 0))
     return pl.pallas_call(
@@ -647,9 +688,8 @@
             num_scalar_prefetch=2,
             grid=(4,),
             in_specs=[
-                pl.BlockSpec((width, rows), lambda s, place, chunk: (0, place[s])),
+                pl.BlockSpec((width, rows), lambda s, place, chunk: (part, place[s])),
                 pl.BlockSpec((rows, dim), lambda s, *_: (s, 0)),
-                whole(vec.shape),
             ],
             out_specs=[whole((dim // 2, width))] * 2,
             scratch_shapes=[pltpu.VMEM((width, dim), f32), pltpu.VMEM((dim, width), f32)],
@@ -658,7 +698,32 @@
         compiler_params=params(),
         cost_estimate=cost(4 * width * tokens * dim, 4 * tokens * dim),
         name="weight_gradient",
-    )(places, chunks, grad, x, vec)
+    )(places, chunks, grad, normed)
+
+
+def norm_back_kernel(own_ref, came_ref, far_ref, x_ref, stats_ref, g_ref, out_ref):
+    both = own_ref[...].astype(f32) + came_ref[...].astype(f32) + far_ref[...].astype(f32)
+    normed = normed_from(x_ref, stats_ref)
+    inv_std = stats_ref[:, 1:2]
+    grad = both - jnp.mean(both, axis=-1, keepdims=True)
+    grad = grad - normed * jnp.mean(both * normed, axis=-1, keepdims=True)
+    out_ref[...] = (g_ref[...].astype(f32) + inv_std * grad).astype(bf16)
+
+
+def norm_back(own, came, far, x, stats, g):
+    count, dim = x.shape
+    rows = count // 2
+    spec = pl.BlockSpec((rows, dim), lambda s: (s, 0))
+    return pl.pallas_call(
+        norm_back_kernel,
+        grid=(2,),
+        in_specs=[spec] * 4 + [pl.BlockSpec((rows, 128), lambda s: (s, 0)), spec],
+        out_specs=spec,
+        out_shape=shaped((count, dim), bf16),
+        compiler_params=params(),
+        cost_estimate=cost(20 * count * dim, 12 * count * dim),
+        name="norm_back",
+    )(own, came, far, x, stats, g)
 
 
 def rope_tables(positions):
@@ -677,12 +742,20 @@
     return jnp.concatenate([mine, mine ^ 1]).astype(jnp.int32)
 
 
-def late_near(keep, send):
+def late_sent(keep, send):
     n = lax.axis_size("dp")
     if n > 8:
         whole = jnp.concatenate([keep, send], axis=0)
-        return lax.psum_scatter(whole, "dp", scatter_dimension=0, tiled=True).astype(f32)
-    return keep.astype(f32) + swapped(send, "dp", 1).astype(f32)
+        return None, lax.psum_scatter(whole, "dp", scatter_dimension=0, tiled=True).astype(f32)
+    return keep, swapped(send, "dp", 1)
+
+
+def late_sum(keep, came):
+    return came if keep is None else keep.astype(f32) + came.astype(f32)
+
+
+def late_near(keep, send):
+    return late_sum(*late_sent(keep, send))
 
 
 def late_far(total, dtype):
@@ -729,38 +802,48 @@
     block = jnp.concatenate(
         [
             w_fc,
-            w_fc2.T,
             jnp.transpose(w_qkv, (1, 0, 2)).reshape(own_dims, qkv_dim),
             w_out.T,
             vectors,
         ],
         axis=1,
     )
-    pieces, starts = ring_gather(block, "dp")
-    x_all = gather_rows(hidden_in)
-    g_all = gather_rows(cotangent)
+    x_far, g_far = swapped(hidden_in, "tensor", 2), swapped(cotangent, "tensor", 2)
+    x_near, g_near = swapped(hidden_in, "tensor", 1), swapped(cotangent, "tensor", 1)
+    pieces, starts, x_far, g_far = ring_gather(block, "dp", x_far, g_far)
+    fc2_w = lax.all_gather(w_fc2.T, "dp", axis=0, tiled=True)
+    x_all = gather_rows(hidden_in, x_near, x_far)
+    g_all = gather_rows(cotangent, g_near, g_far)
 
     cos_t, sin_t = rope_tables(positions)
     lo = halo + jnp.arange(seq_len, dtype=jnp.int32) - positions
     first = lo[::BLK] // BLK
     lo_row = lo.reshape(1, seq_len)
 
-    q, k, v, do, wt, vec = project(
-        starts, places, x_all, g_all, b_qkv.astype(f32).reshape(qkv_dim, 1), cos_t, sin_t, pieces, 2 * ff, local_dim
+    q, k, v, right, normed_one, stats, wt, vec = project(
+        starts,
+        places,
+        x_all,
+        b_qkv.astype(f32).reshape(qkv_dim, 1),
+        cos_t,
+        sin_t,
+        pieces,
+        ff,
+        local_dim,
+        halo,
     )
-    left = passed_along(jnp.concatenate([k[:, -halo:], v[:, -halo:]], axis=0), "dp", 1)
+    left = passed_along(right, "dp", 1)
     ff_out, u_two, ff_grads, ff_small = feed_forward(
-        starts, x_all, g_all, b_fc.astype(f32).reshape(1, ff), vec, pieces, ff
+        starts, x_all, g_all, stats, b_fc.astype(f32).reshape(1, ff), vec, fc2_w, pieces, ff
     )
     ff_own = lax.psum_scatter(ff_grads, "dp", scatter_dimension=0, tiled=True).astype(f32)
     q, ff_out = tied(q, ff_out)
 
     o, lse = attention_forward(first, q, k, v, left, lo_row, halo)
     chunks = late_chunks()
-    out_keep, out_send, ow_keep, ow_send = branch_out(places, chunks, o, ff_out, g_all, wt[qkv_dim:])
+    out_keep, out_send, ow_keep, ow_send, do = branch_out(places, chunks, o, ff_out, g_all, wt)
     own_o, came_o, other_o = scatter_near(out_keep, out_send)
     ow_near = late_near(ow_keep, ow_send)
-    do, out_keep = tied(do, out_keep)
     dq_part, back = backward_left(first, q, left, lo_row, o, lse, do, halo)
     dq_part, back, other_o, ow_near = tied(dq_part, back, other_o, ow_near)
     far_o = swapped(other_o, "tensor", 2)
@@ -772,10 +855,13 @@
     layer_out = (hidden_in.astype(f32) + summed + vec[0] + vec[1]).astype(bf16)
 
     u_keep, u_send, proj_grad, one_small, qkv_bias = input_gradient(
-        places, dq, dk, dv, back, x_all, u_two, wt, vec, cos_t, sin_t, halo
+        places, dq, dk, dv, back, x_all, stats, u_two, wt, vec, cos_t, sin_t, halo
     )
     own_u, came_u, other_u = scatter_near(u_keep, u_send)
-    w_keep, w_send = weight_gradient(places, chunks, proj_grad, x_all, vec)
+    keep_a, send_a = weight_gradient(places, chunks, proj_grad, normed_one, 0, 2)
+    proj_grad, other_u, send_a = tied(proj_grad, other_u, send_a)
+    keep_a, came_a = late_sent(keep_a, send_a)
+    keep_b, send_b = weight_gradient(places, chunks, proj_grad, normed_one, 1, 2)
 
     n = lax.axis_size("dp")
     dims = x_all.shape[1]
@@ -785,17 +871,20 @@
     qkv_rows = jnp.pad(qkv_bias[:, 0], (0, -qkv_dim % 128)).reshape(-1, 128)
     shared = jnp.concatenate([fc_rows, qkv_rows], axis=0)
     small = jnp.concatenate([mine, jnp.broadcast_to(shared, (n,) + shared.shape)], axis=1)
-    w_send, small, _ = tied(w_send, small, other_u)
-    w_near = late_near(w_keep, w_send)
+    send_b, small, came_a = tied(send_b, small, came_a)
+    near_a = late_sum(keep_a, came_a)
+    near_b = late_near(keep_b, send_b)
     if n > 8:
         small_near = lax.psum_scatter(small, "dp", scatter_dimension=0, tiled=True)
     else:
         small = jnp.take(small, chunks, axis=0)
         small_near = late_near(small[: n // 2], small[n // 2 :])
-    w_near, small_near = tied(w_near, small_near)
-    both = scatter_far(own_u, came_u, other_u)
+    far_u = swapped(other_u, "tensor", 2)
+    late_a, far_u = tied(late_far(near_a, bf16), far_u)
+    near_b, small_near = tied(near_b, small_near)
+    late_b = late_far(near_b, bf16)
     small_own = late_far(small_near, f32)[0]
-    late_own = late_far(w_near, bf16)
+    late_own = jnp.concatenate([late_a, late_b], axis=1)
     late_own, ff_own = tied(late_own, ff_own)
     norm_grads = summed_over(small_own[:4], "tensor")[:, :own_dims]
     fc_count = fc_rows.shape[0]
@@ -803,18 +892,10 @@
     qkv_b_total = small_own[5 + fc_count :].reshape(-1)[:qkv_dim].reshape(3, local_dim)
     out_b_total = small_own[4, :own_dims]
 
-    normed_own = hidden_in.astype(f32)
-    normed_own = normed_own - jnp.mean(normed_own, axis=-1, keepdims=True)
-    inv_own = lax.rsqrt(jnp.mean(normed_own * normed_own, axis=-1, keepdims=True) + norm_eps)
-    normed_own = normed_own * inv_own
-    input_grad = cotangent.astype(f32) + inv_own * (
-        both
-        - jnp.mean(both, axis=-1, keepdims=True)
-        - normed_own * jnp.mean(both * normed_own, axis=-1, keepdims=True)
-    )
+    input_grad = norm_back(own_u, came_u, far_u, hidden_in, stats[: hidden_in.shape[0]], cotangent)
     return (
         layer_out,
-        input_grad.astype(bf16),
+        input_grad,
         jnp.transpose(late_own.reshape(own_dims, 3, local_dim), (1, 0, 2)),
         qkv_b_total,
         ow_own.T,

time: 275 us -> 278 us (1.011)
  Pallas kernels: 97.9 us -> 105 us
  other arithmetic: 17 us -> 9.91 us
  waiting for transfers between devices: 57.4 us -> 60.2 us
    ppermute x24 -> x28, waiting for transfers between devices: 37.8 us -> 19.3 us  [swapped(): return lax.ppermute(block, axis, route)]
    reduce_scatter x1, waiting for transfers between devices: 0.01 us -> 15.6 us  [body(): lax.psum_scatter(ff_grads, 'dp', scatter_dimension=0, tiled=True)]
    ppermute x3, waiting for transfers between devices: 1.48 us -> 11.9 us  [ring_gather(): from_left = lax.ppermute(from_left, axis, ahead)]
    pallas_call x1 -> x2, Pallas kernels: 8.51 us -> 12 us  [weight_gradient(): pl.pallas_call(weight_grad_kernel, grid_spec=pltpu.PrefetchScalarGridSpec...]
    pallas_call x0 -> x1, Pallas kernels: none -> 3.39 us  [norm_back(): pl.pallas_call(norm_back_kernel, grid=(2,), in_specs=[spec] * 4 + [pl.Blo...]
    slice x5, local copies, waits for them, and re-layouts: 3.7 us -> 6.8 us  [the longest x2 1.94 us: scatter_near(): return (keep[:count], came[:count], other)]
    ppermute x3, waiting for transfers between devices: 11.7 us -> 8.71 us  [ring_gather(): from_right = lax.ppermute(from_right, axis, behind)]
    unnamed x71 -> x65, local copies, waits for them, and re-layouts: 14.3 us -> 12.3 us
  transfers between devices with their start and end apart: 35 -> 40, of which waited for: 14 -> 19; matrix products, arithmetic and copies ran while one was open for 12% -> 13% of each run, Pallas kernels for 24% -> 24%
where the time goes in v2:
time: 278 us; the launch traced here: 277 us
  Pallas kernels  105 us (38%)
  waiting for transfers between devices  60.2 us (22%)
  starting transfers between devices  51.2 us (18%)
  local copies, waits for them, and re-layouts  36.5 us (13%)
  between operations  14.6 us (5%)
  other arithmetic  9.91 us (4%)
    ppermute x28, starting transfers between devices, swapped(): return lax.ppermute(block, axis, route)  36.5 us
    pallas_call x1, Pallas kernels, feed_forward(): pl.pallas_call(functools.partial(ff_kernel, len(pieces)), grid_spec=pltpu...  22.7 us
    ppermute x28, waiting for transfers between devices, swapped(): return lax.ppermute(block, axis, route)  19.3 us
    pallas_call x1, Pallas kernels, backward_own(): pl.pallas_call(functools.partial(own_bwd_kernel, heads, halo), grid_spec=...  17 us
    reduce_scatter x1, waiting for transfers between devices, body(): lax.psum_scatter(ff_grads, 'dp', scatter_dimension=0, tiled=True)  15.6 us
    pallas_call x1, Pallas kernels, attention_forward(): pl.pallas_call(functools.partial(attn_fwd_kernel, heads, halo), grid_spec...  14.1 us
    unnamed x65, local copies, waits for them, and re-layouts  12.3 us
    pallas_call x2, Pallas kernels, weight_gradient(): pl.pallas_call(weight_grad_kernel, grid_spec=pltpu.PrefetchScalarGridSpec...  12 us
  transfers between devices with their start and end apart: 40, of which 19 were waited for; matrix products, arithmetic and copies ran while one was open for 13% of the time, Pallas kernels for 24%

profile of v2, /device:TPU:0, one launch (start us, length us, event | category | flops | bytes accessed | tf_op | source)
XLA Modules:
  0.0 276.9 jit_solution(262814941343886204)
XLA Ops:
  11.4 3.0 %collective-permute-start.1 = (bf16[96,1664]{1,0:T(8,128)(2,1)S(1)}, bf16[96,1664]{1,0:T(8,128)(2,1)}, u32[]{:S(2)}, u32[]{:S(2)}) collective-permute-start(bf16[96,1664]{1,0:T(8,128)(2,1)S(1)} %concatenate.71.refs_0_), channel_id=1, source_target_pairs={{8,0},{16,8},{24,16},{28,24},{20,28},{12,20},{4,12},{0,4},{9,1},{1... | collective-permute-start | bytes 958472 | tf_op jit(solution)/shard_map/ppermute | solution.py:78
  14.6 1.9 collective-permute-start.6
  17.8 4.3 %collective-permute-done.1.refs_2_ = bf16[96,1664]{1,0:T(8,128)(2,1)} collective-permute-done((bf16[96,1664]{1,0:T(8,128)(2,1)S(1)}, bf16[96,1664]{1,0:T(8,128)(2,1)}, u32[]{:S(2)}, u32[]{:S(2)}) %collective-permute-start.1) | collective-permute-done | bytes 319520 | tf_op jit(solution)/shard_map/ppermute | solution.py:78
  22.1 1.4 collective-permute-done.refs_1_
  23.9 1.6 collective-permute-start.3
  26.5 7.0 %collective-permute-done.2.refs_3_ = bf16[96,1664]{1,0:T(8,128)(2,1)} collective-permute-done((bf16[96,1664]{1,0:T(8,128)(2,1)}, bf16[96,1664]{1,0:T(8,128)(2,1)}, u32[]{:S(2)}, u32[]{:S(2)}) %collective-permute-start.2) | collective-permute-done | bytes 319520 | tf_op jit(solution)/shard_map/ppermute | solution.py:77
  33.5 2.1 collective-permute-done.3.refs_4_
  35.6 2.0 collective-permute-start.4
  39.4 3.5 %collective-permute-done.4.refs_5_ = bf16[96,1664]{1,0:T(8,128)(2,1)} collective-permute-done((bf16[96,1664]{1,0:T(8,128)(2,1)}, bf16[96,1664]{1,0:T(8,128)(2,1)}, u32[]{:S(2)}, u32[]{:S(2)}) %collective-permute-start.4) | collective-permute-done | bytes 319520 | tf_op jit(solution)/shard_map/ppermute | solution.py:77
  42.9 2.3 collective-permute-done.5.refs_6_
  45.8 1.6 slice.149
  47.4 1.6 slice.150
  49.3 2.4 collective-permute-done.11
  51.7 1.8 collective-permute-start.9
  55.8 4.6 %collective-permute-done.10.refs_8_ = bf16[48,1664]{1,0:T(8,128)(2,1)} collective-permute-done((bf16[48,1664]{1,0:T(8,128)(2,1)}, bf16[48,1664]{1,0:T(8,128)(2,1)}, u32[]{:S(2)}, u32[]{:S(2)}) %collective-permute-start.10) | collective-permute-done | bytes 159776 | tf_op jit(solution)/shard_map/ppermute | solution.py:85
  62.8 2.1 constant_dynamic-update-slice_fusion.5
  66.1 1.7 copy-done.1
  67.8 10.2 %project.1 = (bf16[192,2048]{1,0:T(8,128)(2,1)}, bf16[192,2048]{1,0:T(8,128)(2,1)}, bf16[192,2048]{1,0:T(8,128)(2,1)}, bf16[384,768]{1,0:T(8,128)(2,1)}, bf16[20...) custom-call(s32[9]{0:T(128)} %dynamic-slice_bitcast_fusion.start_ref, ...), custom_call_target="tpu_custom_call" | custom-call | flops 1811939328 | bytes 11796480 | tf_op jit(solution)/shard_map/project/pallas_call | solution.py:259
  78.0 3.7 %collective-permute-start.14 = (bf16[384,768]{1,0:T(8,128)(2,1)}, bf16[384,768]{1,0:T(8,128)(2,1)S(1)}, u32[]{:S(2)}, u32[]{:S(2)}) collective-permute-start(bf16[384,768]{1,0:T(8,128)(2,1)} %get-tuple-element.96), channel_id=1, source_target_pairs={{0,4},{4,8},{8,12},{12,16},{16,20},{20,24},{24,28},{1,5},{5,9},{9,... | collective-permute-start | bytes 1769480 | tf_op jit(solution)/shard_map/ppermute | solution.py:44
  82.7 22.7 %feed_forward.1 = (bf16[2048,768]{1,0:T(8,128)(2,1)}, bf16[2048,768]{1,0:T(8,128)(2,1)}, bf16[768,1536]{1,0:T(8,128)(2,1)}, f32[8,768]{1,0:T(8,128)}) custom-call(s32[9]{0:T(128)} %dynamic-slice_bitcast_fusion.start_ref, bf16[2048,768]{1,0:T(8,128)(2,1)} %copy-done.1, bf16[2048,768]{1,0:T(8,128)(2,1)} %constant_dynamic-update-slice_fusion.4.g_ref, ...), custom_call_target="tpu_custom_call" | custom-call | flops 14495514624 | bytes 17301504 | tf_op jit(solution)/shard_map/feed_forward/pallas_call | solution.py:176
  106.3 14.1 %attention_forward.1 = (bf16[192,2048]{1,0:T(8,128)(2,1)}, f32[8,2048]{1,0:T(8,128)}) custom-call(s32[8]{0:T(128)} %and_select_fusion.first_ref, bf16[192,2048]{1,0:T(8,128)(2,1)} %get-tuple-element.93.q_ref, bf16[192,2048]{1,0:T(8,128)(2,1)} %get-tuple-element.94.k_ref, bf16[192,2048]{1,0:T(8,128)(2,1)} %get-tuple-element.95.v_ref, ...), custom_call_target="tpu_custom_call" | custom-call | flops 6442450944 | bytes 3145728 | tf_op jit(solution)/shard_map/attention_forward/pallas_call | solution.py:351
  120.3 9.4 %branch_out.1 = (bf16[1024,768]{1,0:T(8,128)(2,1)}, bf16[1024,768]{1,0:T(8,128)(2,1)}, bf16[384,192]{1,0:T(8,128)(2,1)}, bf16[384,192]{1,0:T(8,128)(2,1)}, bf16[192,2048]{1,0:T(8,128)(2,1)}) custom-call(s32[4]{0:T(128)} %pad_add_fusion.place_ref, s32[8]{0:T(128)} %concatenate.70.chunk_ref, bf16[192,2048]{1,0:T(8,128)(2,1)} %get-tuple-element.97.o_ref, ...), custom_call_target="tpu_custom_call" | custom-call | flops 1207959552 | bytes 9437184 | tf_op jit(solution)/shard_map/branch_out/pallas_call | solution.py:571
  130.2 5.2 %collective-permute-start.16 = (bf16[384,192]{1,0:T(8,128)(2,1)}, bf16[384,192]{1,0:T(8,128)(2,1)S(1)}, u32[]{:S(2)}, u32[]{:S(2)}) collective-permute-start(bf16[384,192]{1,0:T(8,128)(2,1)} %get-tuple-element.107), channel_id=1, source_target_pairs={{0,4},{4,0},{8,12},{12,8},{16,20},{20,16},{24,28},{28,24},{1,5},{5... | collective-permute-start | bytes 442376 | tf_op jit(solution)/shard_map/ppermute | solution.py:49
  135.4 4.4 %attention_backward_left.1 = (f32[192,768]{1,0:T(8,128)}, bf16[384,768]{1,0:T(8,128)(2,1)}) custom-call(s32[8]{0:T(128)} %and_select_fusion.first_ref, bf16[192,2048]{1,0:T(8,128)(2,1)} %get-tuple-element.93.q_ref, bf16[384,768]{1,0:T(8,128)(2,1)} %copy-done.23, s32[1,2048]{1,0:T(1,128)} %bitcast.70, bf16[192,2048]{1,0:T(8,128)(2,1)} %get-tuple-element.97.o_ref, ...), custom_call_target="tpu_custom_call" | custom-call | flops 3019898880 | bytes 2949120 | tf_op jit(solution)/shard_map/attention_backward_left/pallas_call | solution.py:462
  143.0 7.8 %collective-permute-start.21 = (bf16[96,192]{1,0:T(8,128)(2,1)S(1)}, bf16[96,192]{1,0:T(8,128)(2,1)S(1)}, u32[]{:S(2)}, u32[]{:S(2)}) collective-permute-start(bf16[96,192]{1,0:T(8,128)(2,1)S(1)} %get-tuple-element.199), channel_id=1, source_target_pairs={{0,24},{4,28},{8,16},{12,20},{16,8},{20,12},{24,0},{28,4},{1,25},{... | collective-permute-start | bytes 110600 | tf_op jit(solution)/shard_map/ppermute | solution.py:49
  150.8 1.5 collective-permute-start.17
  152.3 1.5 collective-permute-start.18
  153.8 17.0 %attention_backward_own.1 = (f32[192,2048]{1,0:T(8,128)}, f32[192,2048]{1,0:T(8,128)}, f32[192,2048]{1,0:T(8,128)}) custom-call(s32[8]{0:T(128)} %and_select_fusion.first_ref, bf16[192,2048]{1,0:T(8,128)(2,1)} %get-tuple-element.93.q_ref, bf16[192,2048]{1,0:T(8,128)(2,1)} %get-tuple-element.94.k_ref, bf16[192,2048]{1,0:T(8,128)(2,1)} %get-tuple-element.95.v_ref, ...), custom_call_target="tpu_custom_call" | custom-call | flops 16106127360 | bytes 7864320 | tf_op jit(solution)/shard_map/attention_backward_own/pallas_call | solution.py:492
  171.7 11.4 %input_gradient.1 = (bf16[1024,768]{1,0:T(8,128)(2,1)}, bf16[1024,768]{1,0:T(8,128)(2,1)}, bf16[576,2048]{1,0:T(8,128)(2,1)}, f32[8,768]{1,0:T(8,128)}, f32[576,1]{1,0:T(8,128)}) custom-call(s32[4]{0:T(128)} %pad_add_fusion.place_ref, f32[192,2048]{1,0:T(8,128)} %get-tuple-element.114.dq_ref, f32[192,2048]{1,0:T(8,128)} %get-tuple-element.115.dk_ref, ...), custom_call_target="tpu_custom_call" | custom-call | flops 3623878656 | bytes 15728640 | tf_op jit(solution)/shard_map/input_gradient/pallas_call | solution.py:644
  184.3 1.7 slice.172.stats_ref
  186.0 1.4 slice_reduce_fusion.2
  188.2 1.3 slice_reduce_fusion
  191.8 6.1 %weight_gradient.2 = (bf16[384,288]{1,0:T(8,128)(2,1)}, bf16[384,288]{1,0:T(8,128)(2,1)}) custom-call(s32[4]{0:T(128)} %pad_add_fusion.place_ref, s32[8]{0:T(128)} %concatenate.70.chunk_ref, bf16[576,2048]{1,0:T(8,128)(2,1)} %get-tuple-element.125.grad_ref, bf16[2048,768]{1,0:T(8,128)(2,1)} %get-tuple-element.122.normed_ref), custom_call_target="tpu_custom_call" | custom-call | flops 1811939328 | bytes 6291456 | tf_op jit(solution)/shard_map/weight_gradient/pallas_call | solution.py:685
  198.0 2.9 %add_convert_fusion.1 = bf16[512,768]{1,0:T(8,128)(2,1)} fusion(bf16[512,768]{1,0:T(8,128)(2,1)S(1)} %collective-permute-done.18, bf16[512,768]{1,0:T(8,128)(2,1)S(1)} %copy-done, bf16[1024,768]{1,0:T(8,128)(2,1)} %copy-done.5, f32[768]{0:T(1024)S(1)} %copy-done.15, f32[768]{0:T(1024)S(1)} %copy-done.14, bf16[1024,768]{1,0:T(8,128)(2,1)} %get-tuple-element.100), kind=kLoop, calls=%fused_computation.2 | loop fusion | flops 3932160 | bytes 3938304 | tf_op jit(solution)/shard_map/convert_element_type | solution.py:855
  201.9 3.1 %collective-permute-start.23 = (bf16[384,288]{1,0:T(8,128)(2,1)S(1)}, bf16[384,288]{1,0:T(8,128)(2,1)S(1)}, u32[]{:S(2)}, u32[]{:S(2)}) collective-permute-start(bf16[384,288]{1,0:T(8,128)(2,1)S(1)} %copy-done.25), channel_id=1, source_target_pairs={{0,4},{4,0},{8,12},{12,8},{16,20},{20,16},{24,28},{28,24},{1,5},{5... | collective-permute-start | bytes 663560 | tf_op jit(solution)/shard_map/ppermute | solution.py:49
  208.4 5.9 %weight_gradient.3 = (bf16[384,288]{1,0:T(8,128)(2,1)}, bf16[384,288]{1,0:T(8,128)(2,1)}) custom-call(s32[4]{0:T(128)} %pad_add_fusion.place_ref, s32[8]{0:T(128)} %concatenate.70.chunk_ref, bf16[576,2048]{1,0:T(8,128)(2,1)} %get-tuple-element.125.grad_ref, bf16[2048,768]{1,0:T(8,128)(2,1)} %get-tuple-element.122.normed_ref), custom_call_target="tpu_custom_call" | custom-call | flops 1811939328 | bytes 6291456 | tf_op jit(solution)/shard_map/weight_gradient/pallas_call | solution.py:685
  214.3 1.5 collective-permute-done.23
  216.6 1.9 collective-permute-start.29
  219.0 3.4 %collective-permute-start.26 = (bf16[96,288]{1,0:T(8,128)(2,1)S(1)}, bf16[96,288]{1,0:T(8,128)(2,1)S(1)}, u32[]{:S(2)}, u32[]{:S(2)}) collective-permute-start(bf16[96,288]{1,0:T(8,128)(2,1)S(1)} %get-tuple-element.196), channel_id=1, source_target_pairs={{0,24},{4,28},{8,16},{12,20},{16,8},{20,12},{24,0},{28,4},{1,25},{... | collective-permute-start | bytes 165896 | tf_op jit(solution)/shard_map/ppermute | solution.py:49
  223.4 3.9 %collective-permute-done.26 = bf16[96,288]{1,0:T(8,128)(2,1)S(1)} collective-permute-done((bf16[96,288]{1,0:T(8,128)(2,1)S(1)}, bf16[96,288]{1,0:T(8,128)(2,1)S(1)}, u32[]{:S(2)}, u32[]{:S(2)}) %collective-permute-start.26) | collective-permute-done | bytes 55328 | tf_op jit(solution)/shard_map/ppermute | solution.py:49
  227.3 2.1 collective-permute-done.25
  229.5 3.8 %collective-permute-done.28 = bf16[384,288]{1,0:T(8,128)(2,1)S(1)} collective-permute-done((bf16[384,288]{1,0:T(8,128)(2,1)S(1)}, bf16[384,288]{1,0:T(8,128)(2,1)S(1)}, u32[]{:S(2)}, u32[]{:S(2)}) %collective-permute-start.28) | collective-permute-done | bytes 221216 | tf_op jit(solution)/shard_map/ppermute | solution.py:49
  234.2 2.8 %collective-permute-start.35 = (f32[1,16,128]{2,1,0:T(8,128)S(1)}, f32[1,16,128]{2,1,0:T(8,128)S(1)}, u32[]{:S(2)}, u32[]{:S(2)}) collective-permute-start(f32[1,16,128]{2,1,0:T(8,128)S(1)} %get-tuple-element.202), channel_id=1, source_target_pairs={{0,24},{4,28},{8,16},{12,20},{16,8},{20,12},{24,0},{28,4},{1,25},{... | collective-permute-start | bytes 24584 | tf_op jit(solution)/shard_map/ppermute | solution.py:49
  237.1 1.6 collective-permute-start.30
  238.7 2.8 %collective-permute-start.32 = (bf16[96,288]{1,0:T(8,128)(2,1)S(1)}, bf16[96,288]{1,0:T(8,128)(2,1)S(1)}, u32[]{:S(2)}, u32[]{:S(2)}) collective-permute-start(bf16[96,288]{1,0:T(8,128)(2,1)S(1)} %get-tuple-element.193), channel_id=1, source_target_pairs={{0,24},{4,28},{8,16},{12,20},{16,8},{20,12},{24,0},{28,4},{1,25},{... | collective-permute-start | bytes 165896 | tf_op jit(solution)/shard_map/ppermute | solution.py:49
  244.5 2.5 collective-permute-done.37
  247.6 15.6 %reduce-scatter.2.cloned.1.call-done = bf16[96,1536]{1,0:T(8,128)(2,1)} async-done(((bf16[768,1536]{1,0:T(8,128)(2,1)}), bf16[96,1536]{1,0:T(8,128)(2,1)}) %reduce-scatter.2.cloned.1.call-update) | async-done | bytes 294928 | tf_op jit(solution)/shard_map/reduce_scatter | solution.py:839
  266.2 3.4 %norm_back.1 = bf16[512,768]{1,0:T(8,128)(2,1)} custom-call(bf16[512,768]{1,0:T(8,128)(2,1)} %slice.161.own_ref, bf16[512,768]{1,0:T(8,128)(2,1)} %slice.202.came_ref, bf16[512,768]{1,0:T(8,128)(2,1)} %copy-done.6, bf16[512,768]{1,0:T(8,128)(2,1)} %x_ref.1, f32[512,128]{1,0:T(8,128)} %slice.172.stats_ref, bf16[512,768]{1,0:T(8,128)(2,1)} %g_ref.1), custom_call_target="tpu_custom_call" | custom-call | flops 7864320 | bytes 4718592 | tf_op jit(solution)/shard_map/norm_back/pallas_call | solution.py:717
  (181 shorter events, 40.7 us)
Async XLA Ops:
  7.2 75.5 %all-gather.2.cloned.1.call-start = ((), (), s32[]{:S(2)}) async-start(), calls=%async_computation.1 | async-start | bytes 1327104 | tf_op jit(solution)/shard_map/all_gather | solution.py:814
  10.3 43.9 %copy-start.20 = (bf16[768]{0:T(1024)(128)(2,1)S(1)}, bf16[768]{0:T(1024)(128)(2,1)}, u32[]{:S(2)}) copy-start(bf16[768]{0:T(1024)(128)(2,1)} %param.23) | copy-start | bytes 4612
  10.4 44.5 %copy-start.18 = (bf16[3,192]{1,0:T(4,128)(2,1)S(1)}, bf16[3,192]{1,0:T(4,128)(2,1)}, u32[]{:S(2)}) copy-start(bf16[3,192]{1,0:T(4,128)(2,1)} %param.19) | copy-start | bytes 3460
  11.4 44.4 %copy-start.8 = (bf16[96,1664]{1,0:T(8,128)(2,1)}, bf16[96,1664]{1,0:T(8,128)(2,1)S(1)}, u32[]{:S(2)}) copy-start(bf16[96,1664]{1,0:T(8,128)(2,1)S(1)} %concatenate.71.refs_0_) | copy-start | bytes 958468
  11.4 44.3 %copy-start = (bf16[512,768]{1,0:T(8,128)(2,1)S(1)}, bf16[512,768]{1,0:T(8,128)(2,1)}, u32[]{:S(2)}) copy-start(bf16[512,768]{1,0:T(8,128)(2,1)} %x_ref.1) | copy-start | bytes 2359300
  11.4 10.7 %collective-permute-start.1 = (bf16[96,1664]{1,0:T(8,128)(2,1)S(1)}, bf16[96,1664]{1,0:T(8,128)(2,1)}, u32[]{:S(2)}, u32[]{:S(2)}) collective-permute-start(bf16[96,1664]{1,0:T(8,128)(2,1)S(1)} %concatenate.71.refs_0_), channel_id=1, source_target_pairs={{8,0},{16,8},{24,16},{28,24},{20,28},{12,20},{4,12},{0,4},{9,1},{1... | collective-permute-start | bytes 958472 | tf_op jit(solution)/shard_map/ppermute | solution.py:78
  14.4 9.1 %collective-permute-start = (bf16[96,1664]{1,0:T(8,128)(2,1)S(1)}, bf16[96,1664]{1,0:T(8,128)(2,1)}, u32[]{:S(2)}, u32[]{:S(2)}) collective-permute-start(bf16[96,1664]{1,0:T(8,128)(2,1)S(1)} %concatenate.71.refs_0_), channel_id=1, source_target_pairs={{0,8},{8,16},{16,24},{24,28},{28,20},{20,12},{12,4},{4,0},{1,9},{9... | collective-permute-start | bytes 958472 | tf_op jit(solution)/shard_map/ppermute | solution.py:77
  14.6 46.1 %collective-permute-start.7 = (bf16[512,768]{1,0:T(8,128)(2,1)}, bf16[512,768]{1,0:T(8,128)(2,1)}, u32[]{:S(2)}, u32[]{:S(2)}) collective-permute-start(bf16[512,768]{1,0:T(8,128)(2,1)} %x_ref.1), channel_id=1, source_target_pairs={{0,1},{1,0},{2,3},{3,2},{4,5},{5,4},{6,7},{7,6},{8,9},{9,8},{10,11... | collective-permute-start | bytes 2359304 | tf_op jit(solution)/shard_map/ppermute | solution.py:49
  14.6 23.6 %collective-permute-start.6 = (bf16[512,768]{1,0:T(8,128)(2,1)}, bf16[512,768]{1,0:T(8,128)(2,1)S(1)}, u32[]{:S(2)}, u32[]{:S(2)}) collective-permute-start(bf16[512,768]{1,0:T(8,128)(2,1)} %x_ref.1), channel_id=1, source_target_pairs={{0,2},{1,3},{2,0},{3,1},{4,6},{5,7},{6,4},{7,5},{8,10},{9,11},{10,... | collective-permute-start | bytes 2359304 | tf_op jit(solution)/shard_map/ppermute | solution.py:49
  16.5 246.7 %reduce-scatter.2.cloned.1.call-start = ((), (), s32[]{:S(2)}) async-start(), calls=%async_computation.2 | async-start | bytes 2654208 | tf_op jit(solution)/shard_map/reduce_scatter | solution.py:839
  16.5 35.2 %collective-permute-start.11 = (bf16[512,768]{1,0:T(8,128)(2,1)S(1)}, bf16[512,768]{1,0:T(8,128)(2,1)S(1)}, u32[]{:S(2)}, u32[]{:S(2)}) collective-permute-start(bf16[512,768]{1,0:T(8,128)(2,1)S(1)} %copy-done.2), channel_id=1, source_target_pairs={{0,2},{1,3},{2,0},{3,1},{4,6},{5,7},{6,4},{7,5},{8,10},{9,11},{10,... | collective-permute-start | bytes 2359304 | tf_op jit(solution)/shard_map/ppermute | solution.py:49
  16.8 39.0 %copy-start.17 = (s32[2048]{0:T(1024)}, s32[2048]{0:T(1024)S(1)}, u32[]{:S(2)}) copy-start(s32[2048]{0:T(1024)S(1)} %get-tuple-element.207) | copy-start | bytes 24580
  23.5 10.0 %collective-permute-start.2 = (bf16[96,1664]{1,0:T(8,128)(2,1)}, bf16[96,1664]{1,0:T(8,128)(2,1)}, u32[]{:S(2)}, u32[]{:S(2)}) collective-permute-start(bf16[96,1664]{1,0:T(8,128)(2,1)} %collective-permute-done.refs_1_), channel_id=1, source_target_pairs={{0,8},{8,16},{16,24},{24,28},{28,20},{20,12},{12,4},{4,0},{1,9},{9... | collective-permute-start | bytes 958472 | tf_op jit(solution)/shard_map/ppermute | solution.py:77
  23.9 11.7 %collective-permute-start.3 = (bf16[96,1664]{1,0:T(8,128)(2,1)}, bf16[96,1664]{1,0:T(8,128)(2,1)}, u32[]{:S(2)}, u32[]{:S(2)}) collective-permute-start(bf16[96,1664]{1,0:T(8,128)(2,1)} %collective-permute-done.1.refs_2_), channel_id=1, source_target_pairs={{8,0},{16,8},{24,16},{28,24},{20,28},{12,20},{4,12},{0,4},{9,1},{1... | collective-permute-start | bytes 958472 | tf_op jit(solution)/shard_map/ppermute | solution.py:78
  35.6 7.3 %collective-permute-start.4 = (bf16[96,1664]{1,0:T(8,128)(2,1)}, bf16[96,1664]{1,0:T(8,128)(2,1)}, u32[]{:S(2)}, u32[]{:S(2)}) collective-permute-start(bf16[96,1664]{1,0:T(8,128)(2,1)} %collective-permute-done.2.refs_3_), channel_id=1, source_target_pairs={{0,8},{8,16},{16,24},{24,28},{28,20},{20,12},{12,4},{4,0},{1,9},{9... | collective-permute-start | bytes 958472 | tf_op jit(solution)/shard_map/ppermute | solution.py:77
  37.6 7.5 %collective-permute-start.5 = (bf16[96,1664]{1,0:T(8,128)(2,1)}, bf16[96,1664]{1,0:T(8,128)(2,1)}, u32[]{:S(2)}, u32[]{:S(2)}) collective-permute-start(bf16[96,1664]{1,0:T(8,128)(2,1)} %collective-permute-done.3.refs_4_), channel_id=1, source_target_pairs={{8,0},{16,8},{24,16},{28,24},{20,28},{12,20},{4,12},{0,4},{9,1},{1... | collective-permute-start | bytes 958472 | tf_op jit(solution)/shard_map/ppermute | solution.py:78
  38.2 24.6 %collective-permute-start.12 = (bf16[512,768]{1,0:T(8,128)(2,1)S(1)}, bf16[512,768]{1,0:T(8,128)(2,1)}, u32[]{:S(2)}, u32[]{:S(2)}) collective-permute-start(bf16[512,768]{1,0:T(8,128)(2,1)S(1)} %copy-done.2), channel_id=1, source_target_pairs={{0,1},{1,0},{2,3},{3,2},{4,5},{5,4},{6,7},{7,6},{8,9},{9,8},{10,11... | collective-permute-start | bytes 2359304 | tf_op jit(solution)/shard_map/ppermute | solution.py:49
  45.2 19.7 %collective-permute-start.8 = (bf16[512,768]{1,0:T(8,128)(2,1)S(1)}, bf16[512,768]{1,0:T(8,128)(2,1)}, u32[]{:S(2)}, u32[]{:S(2)}) collective-permute-start(bf16[512,768]{1,0:T(8,128)(2,1)S(1)} %collective-permute-done.6), channel_id=1, source_target_pairs={{0,1},{1,0},{2,3},{3,2},{4,5},{5,4},{6,7},{7,6},{8,9},{9,8},{10,11... | collective-permute-start | bytes 2359304 | tf_op jit(solution)/shard_map/ppermute | solution.py:49
  49.0 11.5 %collective-permute-start.10 = (bf16[48,1664]{1,0:T(8,128)(2,1)}, bf16[48,1664]{1,0:T(8,128)(2,1)}, u32[]{:S(2)}, u32[]{:S(2)}) collective-permute-start(bf16[48,1664]{1,0:T(8,128)(2,1)} %slice.150), channel_id=1, source_target_pairs={{8,0},{16,8},{24,16},{28,24},{20,28},{12,20},{4,12},{0,4},{9,1},{1... | collective-permute-start | bytes 479240 | tf_op jit(solution)/shard_map/ppermute | solution.py:85
  51.7 8.7 %collective-permute-start.9 = (bf16[48,1664]{1,0:T(8,128)(2,1)}, bf16[48,1664]{1,0:T(8,128)(2,1)}, u32[]{:S(2)}, u32[]{:S(2)}) collective-permute-start(bf16[48,1664]{1,0:T(8,128)(2,1)} %slice.149), channel_id=1, source_target_pairs={{0,8},{8,16},{16,24},{24,28},{28,20},{20,12},{12,4},{4,0},{1,9},{9... | collective-permute-start | bytes 479240 | tf_op jit(solution)/shard_map/ppermute | solution.py:84
  60.5 21.3 %collective-permute-start.13 = (bf16[512,768]{1,0:T(8,128)(2,1)S(1)}, bf16[512,768]{1,0:T(8,128)(2,1)S(1)}, u32[]{:S(2)}, u32[]{:S(2)}) collective-permute-start(bf16[512,768]{1,0:T(8,128)(2,1)S(1)} %collective-permute-done.11), channel_id=1, source_target_pairs={{0,1},{1,0},{2,3},{3,2},{4,5},{5,4},{6,7},{7,6},{8,9},{9,8},{10,11... | collective-permute-start | bytes 2359304 | tf_op jit(solution)/shard_map/ppermute | solution.py:49
  78.0 27.4 %collective-permute-start.14 = (bf16[384,768]{1,0:T(8,128)(2,1)}, bf16[384,768]{1,0:T(8,128)(2,1)S(1)}, u32[]{:S(2)}, u32[]{:S(2)}) collective-permute-start(bf16[384,768]{1,0:T(8,128)(2,1)} %get-tuple-element.96), channel_id=1, source_target_pairs={{0,4},{4,8},{8,12},{12,16},{16,20},{20,24},{24,28},{1,5},{5,9},{9,... | collective-permute-start | bytes 1769480 | tf_op jit(solution)/shard_map/ppermute | solution.py:44
  129.8 11.2 %collective-permute-start.15 = (bf16[1024,768]{1,0:T(8,128)(2,1)}, bf16[1024,768]{1,0:T(8,128)(2,1)S(1)}, u32[]{:S(2)}, u32[]{:S(2)}) collective-permute-start(bf16[1024,768]{1,0:T(8,128)(2,1)} %get-tuple-element.101), channel_id=1, source_target_pairs={{0,1},{1,0},{2,3},{3,2},{4,5},{5,4},{6,7},{7,6},{8,9},{9,8},{10,11... | collective-permute-start | bytes 4718600 | tf_op jit(solution)/shard_map/ppermute | solution.py:49
  130.2 10.7 %collective-permute-start.16 = (bf16[384,192]{1,0:T(8,128)(2,1)}, bf16[384,192]{1,0:T(8,128)(2,1)S(1)}, u32[]{:S(2)}, u32[]{:S(2)}) collective-permute-start(bf16[384,192]{1,0:T(8,128)(2,1)} %get-tuple-element.107), channel_id=1, source_target_pairs={{0,4},{4,0},{8,12},{12,8},{16,20},{20,16},{24,28},{28,24},{1,5},{5... | collective-permute-start | bytes 442376 | tf_op jit(solution)/shard_map/ppermute | solution.py:49
  142.1 28.7 %collective-permute-start.19 = (bf16[96,192]{1,0:T(8,128)(2,1)S(1)}, bf16[96,192]{1,0:T(8,128)(2,1)S(1)}, u32[]{:S(2)}, u32[]{:S(2)}) collective-permute-start(bf16[96,192]{1,0:T(8,128)(2,1)S(1)} %get-tuple-element.198), channel_id=1, source_target_pairs={{0,8},{4,12},{8,0},{12,4},{16,24},{20,28},{24,16},{28,20},{1,9},{5... | collective-permute-start | bytes 110600 | tf_op jit(solution)/shard_map/ppermute | solution.py:49
  143.0 27.8 %collective-permute-start.21 = (bf16[96,192]{1,0:T(8,128)(2,1)S(1)}, bf16[96,192]{1,0:T(8,128)(2,1)S(1)}, u32[]{:S(2)}, u32[]{:S(2)}) collective-permute-start(bf16[96,192]{1,0:T(8,128)(2,1)S(1)} %get-tuple-element.199), channel_id=1, source_target_pairs={{0,24},{4,28},{8,16},{12,20},{16,8},{20,12},{24,0},{28,4},{1,25},{... | collective-permute-start | bytes 110600 | tf_op jit(solution)/shard_map/ppermute | solution.py:49
  150.8 20.0 %collective-permute-start.20 = (bf16[96,192]{1,0:T(8,128)(2,1)S(1)}, bf16[96,192]{1,0:T(8,128)(2,1)S(1)}, u32[]{:S(2)}, u32[]{:S(2)}) collective-permute-start(bf16[96,192]{1,0:T(8,128)(2,1)S(1)} %get-tuple-element.200), channel_id=1, source_target_pairs={{0,16},{4,20},{8,24},{12,28},{16,0},{20,4},{24,8},{28,12},{1,17},{... | collective-permute-start | bytes 110600 | tf_op jit(solution)/shard_map/ppermute | solution.py:49
  150.8 20.1 %collective-permute-start.17 = (bf16[384,768]{1,0:T(8,128)(2,1)S(1)}, bf16[384,768]{1,0:T(8,128)(2,1)S(1)}, u32[]{:S(2)}, u32[]{:S(2)}) collective-permute-start(bf16[384,768]{1,0:T(8,128)(2,1)S(1)} %copy-done.22), channel_id=1, source_target_pairs={{4,0},{8,4},{12,8},{16,12},{20,16},{24,20},{28,24},{5,1},{9,5},{13... | collective-permute-start | bytes 1769480 | tf_op jit(solution)/shard_map/ppermute | solution.py:44
  152.3 18.9 %collective-permute-start.18 = (bf16[512,768]{1,0:T(8,128)(2,1)S(1)}, bf16[512,768]{1,0:T(8,128)(2,1)S(1)}, u32[]{:S(2)}, u32[]{:S(2)}) collective-permute-start(bf16[512,768]{1,0:T(8,128)(2,1)S(1)} %add_convert_fusion.2), channel_id=1, source_target_pairs={{0,2},{1,3},{2,0},{3,1},{4,6},{5,7},{6,4},{7,5},{8,10},{9,11},{10,... | collective-permute-start | bytes 2359304 | tf_op jit(solution)/shard_map/ppermute | solution.py:49
  171.7 12.1 %copy-start.19 = (s32[8]{0:T(128)S(1)}, s32[8]{0:T(128)}, u32[]{:S(2)}) copy-start(s32[8]{0:T(128)} %concatenate.70.chunk_ref) | copy-start | bytes 100
  183.1 17.7 %collective-permute-start.22 = (bf16[1024,768]{1,0:T(8,128)(2,1)}, bf16[1024,768]{1,0:T(8,128)(2,1)S(1)}, u32[]{:S(2)}, u32[]{:S(2)}) collective-permute-start(bf16[1024,768]{1,0:T(8,128)(2,1)} %get-tuple-element.120), channel_id=1, source_target_pairs={{0,1},{1,0},{2,3},{3,2},{4,5},{5,4},{6,7},{7,6},{8,9},{9,8},{10,11... | collective-permute-start | bytes 4718600 | tf_op jit(solution)/shard_map/ppermute | solution.py:49
  201.9 13.9 %collective-permute-start.23 = (bf16[384,288]{1,0:T(8,128)(2,1)S(1)}, bf16[384,288]{1,0:T(8,128)(2,1)S(1)}, u32[]{:S(2)}, u32[]{:S(2)}) collective-permute-start(bf16[384,288]{1,0:T(8,128)(2,1)S(1)} %copy-done.25), channel_id=1, source_target_pairs={{0,4},{4,0},{8,12},{12,8},{16,20},{20,16},{24,28},{28,24},{1,5},{5... | collective-permute-start | bytes 663560 | tf_op jit(solution)/shard_map/ppermute | solution.py:49
  206.8 57.4 %collective-permute-start.27 = (bf16[512,768]{1,0:T(8,128)(2,1)}, bf16[512,768]{1,0:T(8,128)(2,1)S(1)}, u32[]{:S(2)}, u32[]{:S(2)}) collective-permute-start(bf16[512,768]{1,0:T(8,128)(2,1)} %add_convert_fusion), channel_id=1, source_target_pairs={{0,2},{1,3},{2,0},{3,1},{4,6},{5,7},{6,4},{7,5},{8,10},{9,11},{10,... | collective-permute-start | bytes 2359304 | tf_op jit(solution)/shard_map/ppermute | solution.py:49
  214.3 18.9 %copy-start.10 = (bf16[384,288]{1,0:T(8,128)(2,1)S(1)}, bf16[384,288]{1,0:T(8,128)(2,1)}, u32[]{:S(2)}) copy-start(bf16[384,288]{1,0:T(8,128)(2,1)} %get-tuple-element.135) | copy-start | bytes 663556
  216.6 5.8 %collective-permute-start.29 = (f32[4,16,128]{2,1,0:T(8,128)S(1)}, f32[4,16,128]{2,1,0:T(8,128)S(1)}, u32[]{:S(2)}, u32[]{:S(2)}) collective-permute-start(f32[4,16,128]{2,1,0:T(8,128)S(1)} %slice.209), channel_id=1, source_target_pairs={{0,4},{4,0},{8,12},{12,8},{16,20},{20,16},{24,28},{28,24},{1,5},{5... | collective-permute-start | bytes 98312 | tf_op jit(solution)/shard_map/ppermute | solution.py:49
  218.6 4.8 %collective-permute-start.24 = (bf16[96,288]{1,0:T(8,128)(2,1)S(1)}, bf16[96,288]{1,0:T(8,128)(2,1)S(1)}, u32[]{:S(2)}, u32[]{:S(2)}) collective-permute-start(bf16[96,288]{1,0:T(8,128)(2,1)S(1)} %get-tuple-element.195), channel_id=1, source_target_pairs={{0,8},{4,12},{8,0},{12,4},{16,24},{20,28},{24,16},{28,20},{1,9},{5... | collective-permute-start | bytes 165896 | tf_op jit(solution)/shard_map/ppermute | solution.py:49
  219.0 8.3 %collective-permute-start.26 = (bf16[96,288]{1,0:T(8,128)(2,1)S(1)}, bf16[96,288]{1,0:T(8,128)(2,1)S(1)}, u32[]{:S(2)}, u32[]{:S(2)}) collective-permute-start(bf16[96,288]{1,0:T(8,128)(2,1)S(1)} %get-tuple-element.196), channel_id=1, source_target_pairs={{0,24},{4,28},{8,16},{12,20},{16,8},{20,12},{24,0},{28,4},{1,25},{... | collective-permute-start | bytes 165896 | tf_op jit(solution)/shard_map/ppermute | solution.py:49
  222.4 7.0 %collective-permute-start.25 = (bf16[96,288]{1,0:T(8,128)(2,1)S(1)}, bf16[96,288]{1,0:T(8,128)(2,1)S(1)}, u32[]{:S(2)}, u32[]{:S(2)}) collective-permute-start(bf16[96,288]{1,0:T(8,128)(2,1)S(1)} %get-tuple-element.197), channel_id=1, source_target_pairs={{0,16},{4,20},{8,24},{12,28},{16,0},{20,4},{24,8},{28,12},{1,17},{... | collective-permute-start | bytes 165896 | tf_op jit(solution)/shard_map/ppermute | solution.py:49
  222.4 10.8 %collective-permute-start.28 = (bf16[384,288]{1,0:T(8,128)(2,1)S(1)}, bf16[384,288]{1,0:T(8,128)(2,1)S(1)}, u32[]{:S(2)}, u32[]{:S(2)}) collective-permute-start(bf16[384,288]{1,0:T(8,128)(2,1)S(1)} %copy-done.24), channel_id=1, source_target_pairs={{0,4},{4,0},{8,12},{12,8},{16,20},{20,16},{24,28},{28,24},{1,5},{5... | collective-permute-start | bytes 663560 | tf_op jit(solution)/shard_map/ppermute | solution.py:49
  233.3 5.4 %collective-permute-start.33 = (f32[1,16,128]{2,1,0:T(8,128)S(1)}, f32[1,16,128]{2,1,0:T(8,128)S(1)}, u32[]{:S(2)}, u32[]{:S(2)}) collective-permute-start(f32[1,16,128]{2,1,0:T(8,128)S(1)} %get-tuple-element.201), channel_id=1, source_target_pairs={{0,8},{4,12},{8,0},{12,4},{16,24},{20,28},{24,16},{28,20},{1,9},{5... | collective-permute-start | bytes 24584 | tf_op jit(solution)/shard_map/ppermute | solution.py:49
  234.2 7.3 %collective-permute-start.35 = (f32[1,16,128]{2,1,0:T(8,128)S(1)}, f32[1,16,128]{2,1,0:T(8,128)S(1)}, u32[]{:S(2)}, u32[]{:S(2)}) collective-permute-start(f32[1,16,128]{2,1,0:T(8,128)S(1)} %get-tuple-element.202), channel_id=1, source_target_pairs={{0,24},{4,28},{8,16},{12,20},{16,8},{20,12},{24,0},{28,4},{1,25},{... | collective-permute-start | bytes 24584 | tf_op jit(solution)/shard_map/ppermute | solution.py:49
  237.0 5.2 %collective-permute-start.34 = (f32[1,16,128]{2,1,0:T(8,128)S(1)}, f32[1,16,128]{2,1,0:T(8,128)S(1)}, u32[]{:S(2)}, u32[]{:S(2)}) collective-permute-start(f32[1,16,128]{2,1,0:T(8,128)S(1)} %get-tuple-element.203), channel_id=1, source_target_pairs={{0,16},{4,20},{8,24},{12,28},{16,0},{20,4},{24,8},{28,12},{1,17},{... | collective-permute-start | bytes 24584 | tf_op jit(solution)/shard_map/ppermute | solution.py:49
  237.1 10.5 %collective-permute-start.30 = (bf16[96,288]{1,0:T(8,128)(2,1)S(1)}, bf16[96,288]{1,0:T(8,128)(2,1)S(1)}, u32[]{:S(2)}, u32[]{:S(2)}) collective-permute-start(bf16[96,288]{1,0:T(8,128)(2,1)S(1)} %get-tuple-element.192), channel_id=1, source_target_pairs={{0,8},{4,12},{8,0},{12,4},{16,24},{20,28},{24,16},{28,20},{1,9},{5... | collective-permute-start | bytes 165896 | tf_op jit(solution)/shard_map/ppermute | solution.py:49
  238.7 8.8 %collective-permute-start.32 = (bf16[96,288]{1,0:T(8,128)(2,1)S(1)}, bf16[96,288]{1,0:T(8,128)(2,1)S(1)}, u32[]{:S(2)}, u32[]{:S(2)}) collective-permute-start(bf16[96,288]{1,0:T(8,128)(2,1)S(1)} %get-tuple-element.193), channel_id=1, source_target_pairs={{0,24},{4,28},{8,16},{12,20},{16,8},{20,12},{24,0},{28,4},{1,25},{... | collective-permute-start | bytes 165896 | tf_op jit(solution)/shard_map/ppermute | solution.py:49
  241.5 6.0 %collective-permute-start.31 = (bf16[96,288]{1,0:T(8,128)(2,1)S(1)}, bf16[96,288]{1,0:T(8,128)(2,1)S(1)}, u32[]{:S(2)}, u32[]{:S(2)}) collective-permute-start(bf16[96,288]{1,0:T(8,128)(2,1)S(1)} %get-tuple-element.194), channel_id=1, source_target_pairs={{0,16},{4,20},{8,24},{12,28},{16,0},{20,4},{24,8},{28,12},{1,17},{... | collective-permute-start | bytes 165896 | tf_op jit(solution)/shard_map/ppermute | solution.py:49
  242.3 1.2 collective-permute-start.36
  243.4 3.6 %collective-permute-start.37 = (f32[4,128]{1,0:T(4,128)S(1)}, f32[4,128]{1,0:T(4,128)S(1)}, u32[]{:S(2)}, u32[]{:S(2)}) collective-permute-start(f32[4,128]{1,0:T(4,128)S(1)} %fusion.3), channel_id=1, source_target_pairs={{0,2},{1,3},{2,0},{3,1},{4,6},{5,7},{6,4},{7,5},{8,10},{9,11},{10,... | collective-permute-start | bytes 6152 | tf_op jit(solution)/shard_map/ppermute | solution.py:49
  243.8 25.8 %copy-start.26 = (f32[96]{0:T(128)}, f32[96]{0:T(128)S(1)}, u32[]{:S(2)}) copy-start(f32[96]{0:T(128)S(1)} %slice_bitcast_fusion.4) | copy-start | bytes 1156
  (19 other events, 103.0 us)
Sparse Core Ops, SparseCore 0:
  16.6 44.3 all-gather.1
  187.6 75.5 reduce-scatter.1

commit v3 on v2

--- a/solution.py
+++ b/solution.py
@@ -69,7 +69,6 @@
             row.append(ring[(at - step) % n] * rows)
             row.append(ring[(at + step) % n] * rows)
         row.append(ring[(at + n // 2) % n] * rows)
-        row.append(ring[(at + n // 2) % n] * rows + rows // 2)
         table.append(row)
     pieces = [block]
     from_left = from_right = block
@@ -81,22 +80,20 @@
         else:
             from_left, from_right = tied(from_left, from_right)
         pieces += [from_left, from_right]
-    from_left = lax.ppermute(from_left[: rows // 2], axis, ahead)
-    from_right = lax.ppermute(from_right[rows // 2 :], axis, behind)
-    from_left, from_right, late = tied(from_left, from_right, late)
-    pieces += [from_left, from_right]
+    from_left, late = tied(lax.ppermute(from_left, axis, ahead), late)
+    pieces.append(from_left)
     return pieces, jnp.asarray(table, jnp.int32)[lax.axis_index(axis)], early, late
 
 
 def gather_rows(block, near, far):
-    return jnp.concatenate([block, far, near, swapped(far, "tensor", 1)], axis=0)
+    return [block, far, near, swapped(far, "tensor", 1)]
 
 
 def scatter_near(keep, send):
     count = keep.shape[0] // 2
     came = swapped(send, "tensor", 1)
     other = (keep[count:].astype(f32) + came[count:].astype(f32)).astype(bf16)
-    return keep[:count], came[:count], other
+    return keep, came, other
 
 
 def tied(*arrays):
@@ -119,6 +116,14 @@
         out_ref[pl.ds(pl.multiple_of(start_ref[n], rows), rows), :] = ref[:, columns]
 
 
+def take_rows(block_refs, out_ref):
+    for n, ref in enumerate(block_refs):
+
+        @pl.when(pl.program_id(0) == n)
+        def _():
+            out_ref[...] = ref[...]
+
+
 def row_stats(x):
     mean = jnp.mean(x, axis=-1, keepdims=True)
     center = x - mean
@@ -129,10 +134,10 @@
     return (x_ref[...].astype(f32) - stats_ref[:, 0:1]) * stats_ref[:, 1:2]
 
 
-def ff_kernel(pieces, start_ref, x_ref, g_ref, stats_ref, b_ref, vec_ref, fc2_w, *refs):
-    w_refs = refs[:pieces]
-    out_ref, u_ref, grads_ref, small_ref = refs[pieces : pieces + 4]
-    fc_w, fc_acc, fc2_acc = refs[pieces + 4 :]
+def ff_kernel(pieces, start_ref, x_ref, stats_ref, b_ref, vec_ref, fc2_w, *refs):
+    g_refs, w_refs = refs[:4], refs[4 : 4 + pieces]
+    out_ref, u_ref, g_ref, grads_ref, small_ref, fc_w, fc_acc, fc2_acc = refs[4 + pieces :]
+    take_rows(g_refs, g_ref)
     step = pl.program_id(0)
     ff = fc2_w.shape[1]
 
@@ -180,17 +185,17 @@
             grid=(4,),
             in_specs=[
                 spec,
-                spec,
                 pl.BlockSpec((rows, 128), lambda s, *_: (s, 0)),
                 whole((1, ff)),
                 whole(vec.shape),
                 whole(fc2_w.shape),
             ]
-            + [whole(p.shape) for p in pieces],
-            out_specs=[spec, spec, whole((dim, 2 * ff)), whole((8, dim))],
+            + [whole(p.shape) for p in g + pieces],
+            out_specs=[spec, spec, spec, whole((dim, 2 * ff)), whole((8, dim))],
             scratch_shapes=[pltpu.VMEM((dim, ff), bf16)] + [pltpu.VMEM((dim, ff), f32)] * 2,
         ),
         out_shape=[
+            shaped((tokens, dim), bf16),
             shaped((tokens, dim), bf16),
             shaped((tokens, dim), bf16),
             shaped((dim, 2 * ff), bf16),
@@ -199,7 +204,7 @@
         compiler_params=params(),
         cost_estimate=cost(12 * tokens * dim * ff, 8 * tokens * dim + 8 * dim * ff, 2 * tokens * ff),
         name="feed_forward",
-    )(starts, x, g, stats, b_fc, vec, fc2_w, *pieces)
+    )(starts, x, stats, b_fc, vec, fc2_w, *g, *pieces)
 
 
 def turned(x, cos_t, sin_t):
@@ -212,9 +217,10 @@
     return jnp.concatenate(out, axis=0)
 
 
-def project_kernel(pieces, first, start_ref, place_ref, x_ref, b_ref, cos_ref, sin_ref, *refs):
-    w_refs = refs[:pieces]
-    q_ref, k_ref, v_ref, halo_ref, normed_ref, stats_ref, wt_ref, vec_ref, packed = refs[pieces:]
+def project_kernel(pieces, first, start_ref, place_ref, b_ref, cos_ref, sin_ref, *refs):
+    x_refs, w_refs = refs[:4], refs[4 : 4 + pieces]
+    (q_ref, k_ref, v_ref, halo_ref, x_ref, normed_ref, stats_ref, wt_ref, vec_ref, packed) = refs[4 + pieces :]
+    take_rows(x_refs, x_ref)
     feat = q_ref.shape[0]
     width = wt_ref.shape[0]
 
@@ -250,8 +256,8 @@
 
 
 def project(starts, places, x, b_col, cos_t, sin_t, pieces, first, feat, halo):
-    tokens, dim = x.shape
-    rows = tokens // 4
+    rows, dim = x[0].shape
+    tokens = 4 * rows
     width = 4 * feat
     spec = pl.BlockSpec((rows, dim), lambda s, *_: (s, 0))
     placed = lambda r: pl.BlockSpec((r, rows), lambda s, start, place: (0, place[s]))
@@ -261,11 +267,12 @@
         grid_spec=pltpu.PrefetchScalarGridSpec(
             num_scalar_prefetch=2,
             grid=(4,),
-            in_specs=[spec, whole(b_col.shape), placed(ROT // 2), placed(ROT // 2)]
-            + [whole(p.shape) for p in pieces],
+            in_specs=[whole(b_col.shape), placed(ROT // 2), placed(ROT // 2)]
+            + [whole(p.shape) for p in x + pieces],
             out_specs=[placed(feat)] * 3
             + [
                 whole((2 * feat, halo)),
+                spec,
                 spec,
                 pl.BlockSpec((rows, 128), lambda s, *_: (s, 0)),
                 whole((width, dim)),
@@ -277,6 +284,7 @@
         + [
             shaped((2 * feat, halo), bf16),
             shaped((tokens, dim), bf16),
+            shaped((tokens, dim), bf16),
             shaped((tokens, 128), f32),
             shaped((width, dim), bf16),
             shaped((8, dim), f32),
@@ -284,7 +292,7 @@
         compiler_params=params(),
         cost_estimate=cost(6 * tokens * dim * feat, 6 * tokens * dim + 4 * dim * width),
         name="project",
-    )(starts, places, x, b_col, cos_t, sin_t, *pieces)
+    )(starts, places, b_col, cos_t, sin_t, *x, *pieces)
 
 
 def key_mask(chunk, lo_row, hi_row):
@@ -661,44 +669,64 @@
     )(places, dq, dk, dv, back, x, stats, u2, wt, vec, cos_t, sin_t)
 
 
-def weight_grad_kernel(place_ref, chunk_ref, grad_ref, normed_ref, wkeep_ref, wsend_ref, acc, acc_t):
+def weight_grad_kernel(own_dims, place_ref, chunk_ref, grad_ref, normed_ref, *refs):
+    small_refs, (wkeep_ref, wsend_ref, acc, acc_t) = refs[:-4], refs[-4:]
     s = pl.program_id(0)
 
     @pl.when(s == 0)
     def _():
         acc[...] = jnp.zeros_like(acc)
 
-    acc[...] += mm(grad_ref[...], normed_ref[...], 1, 0)
+    width = grad_ref.shape[0]
+    acc[:width, :] += mm(grad_ref[...], normed_ref[...], 1, 0)
 
     @pl.when(s == pl.num_programs(0) - 1)
     def _():
+        if small_refs:
+            one_ref, ff_ref, bias_ref = small_refs
+            acc[256:258, :] = one_ref[0:2, :]
+            acc[258:262, :] = ff_ref[0:4, :]
         acc_t[...] = acc[...].T
+        if small_refs:
+            columns = acc_t[:, 256:]
+            lane = lax.broadcasted_iota(jnp.int32, (own_dims, 128), 1)
+            shared = jnp.zeros((own_dims, 128), f32)
+            count = columns.shape[0] // own_dims
+            for n in range(count):
+                part = columns[n * own_dims : (n + 1) * own_dims, 5:6]
+                shared = jnp.where(lane == 8 + n, part, shared)
+            for n in range(bias_ref.shape[0] // own_dims):
+                part = bias_ref[n * own_dims : (n + 1) * own_dims, 0:1]
+                shared = jnp.where(lane == 8 + count + n, part, shared)
+            lane = lax.broadcasted_iota(jnp.int32, columns.shape, 1)
+            acc_t[:, 256:] = jnp.where(lane < 5, columns, jnp.concatenate([shared] * count, axis=0))
         put_chunks(chunk_ref, wkeep_ref, wsend_ref, acc_t)
 
 
-def weight_gradient(places, chunks, grad, normed, part, parts):
-    width, tokens = grad.shape
-    width = width // parts
+def weight_gradient(places, chunks, grad, normed, width, part, own_dims, small=()):
+    tokens = grad.shape[1]
     dim = normed.shape[1]
     rows = tokens // 4
+    out_width = 384 if small else width
     whole = lambda shape: pl.BlockSpec(shape, lambda s, *_: (0, 0))
     return pl.pallas_call(
-        weight_grad_kernel,
+        functools.partial(weight_grad_kernel, own_dims),
         grid_spec=pltpu.PrefetchScalarGridSpec(
             num_scalar_prefetch=2,
             grid=(4,),
             in_specs=[
                 pl.BlockSpec((width, rows), lambda s, place, chunk: (part, place[s])),
                 pl.BlockSpec((rows, dim), lambda s, *_: (s, 0)),
-            ],
-            out_specs=[whole((dim // 2, width))] * 2,
-            scratch_shapes=[pltpu.VMEM((width, dim), f32), pltpu.VMEM((dim, width), f32)],
+            ]
+            + [whole(a.shape) for a in small],
+            out_specs=[whole((dim // 2, out_width))] * 2,
+            scratch_shapes=[pltpu.VMEM((out_width, dim), f32), pltpu.VMEM((dim, out_width), f32)],
         ),
-        out_shape=[shaped((dim // 2, width), bf16)] * 2,
+        out_shape=[shaped((dim // 2, out_width), bf16)] * 2,
         compiler_params=params(),
         cost_estimate=cost(4 * width * tokens * dim, 4 * tokens * dim),
         name="weight_gradient",
-    )(places, chunks, grad, normed)
+    )(places, chunks, grad, normed, *small)
 
 
 def norm_back_kernel(own_ref, came_ref, far_ref, x_ref, stats_ref, g_ref, out_ref):
@@ -717,7 +745,7 @@
     return pl.pallas_call(
         norm_back_kernel,
         grid=(2,),
-        in_specs=[spec] * 4 + [pl.BlockSpec((rows, 128), lambda s: (s, 0)), spec],
+        in_specs=[spec, spec, spec, spec, pl.BlockSpec((rows, 128), lambda s: (s, 0)), spec],
         out_specs=spec,
         out_shape=shaped((count, dim), bf16),
         compiler_params=params(),
@@ -812,18 +840,18 @@
     x_near, g_near = swapped(hidden_in, "tensor", 1), swapped(cotangent, "tensor", 1)
     pieces, starts, x_far, g_far = ring_gather(block, "dp", x_far, g_far)
     fc2_w = lax.all_gather(w_fc2.T, "dp", axis=0, tiled=True)
-    x_all = gather_rows(hidden_in, x_near, x_far)
-    g_all = gather_rows(cotangent, g_near, g_far)
+    x_blocks = gather_rows(hidden_in, x_near, x_far)
+    g_blocks = gather_rows(cotangent, g_near, g_far)
 
     cos_t, sin_t = rope_tables(positions)
     lo = halo + jnp.arange(seq_len, dtype=jnp.int32) - positions
     first = lo[::BLK] // BLK
     lo_row = lo.reshape(1, seq_len)
 
-    q, k, v, right, normed_one, stats, wt, vec = project(
+    q, k, v, right, x_all, normed_one, stats, wt, vec = project(
         starts,
         places,
-        x_all,
+        x_blocks,
         b_qkv.astype(f32).reshape(qkv_dim, 1),
         cos_t,
         sin_t,
@@ -833,8 +861,8 @@
         halo,
     )
     left = passed_along(right, "dp", 1)
-    ff_out, u_two, ff_grads, ff_small = feed_forward(
-        starts, x_all, g_all, stats, b_fc.astype(f32).reshape(1, ff), vec, fc2_w, pieces, ff
+    ff_out, u_two, g_all, ff_grads, ff_small = feed_forward(
+        starts, x_all, g_blocks, stats, b_fc.astype(f32).reshape(1, ff), vec, fc2_w, pieces, ff
     )
     ff_own = lax.psum_scatter(ff_grads, "dp", scatter_dimension=0, tiled=True).astype(f32)
     q, ff_out = tied(q, ff_out)
@@ -850,49 +878,37 @@
     back = passed_along(back, "dp", -1)
     ow_own = late_far(ow_near, bf16)
     dq, dk, dv = backward_own(first, q, k, v, lo_row, o, lse, do, dq_part, halo)
-    back, dq, far_o, ow_own = tied(back, dq, far_o, ow_own)
-    summed = own_o.astype(f32) + came_o.astype(f32) + far_o.astype(f32)
+    back, dq, far_o, ow_own, ff_own = tied(back, dq, far_o, ow_own, ff_own)
+    count = hidden_in.shape[0]
+    summed = own_o[:count].astype(f32) + came_o[:count].astype(f32) + far_o.astype(f32)
     layer_out = (hidden_in.astype(f32) + summed + vec[0] + vec[1]).astype(bf16)
 
     u_keep, u_send, proj_grad, one_small, qkv_bias = input_gradient(
         places, dq, dk, dv, back, x_all, stats, u_two, wt, vec, cos_t, sin_t, halo
     )
     own_u, came_u, other_u = scatter_near(u_keep, u_send)
-    keep_a, send_a = weight_gradient(places, chunks, proj_grad, normed_one, 0, 2)
+    keep_a, send_a = weight_gradient(places, chunks, proj_grad, normed_one, 2 * local_dim, 0, own_dims)
     proj_grad, other_u, send_a = tied(proj_grad, other_u, send_a)
     keep_a, came_a = late_sent(keep_a, send_a)
-    keep_b, send_b = weight_gradient(places, chunks, proj_grad, normed_one, 1, 2)
-
-    n = lax.axis_size("dp")
-    dims = x_all.shape[1]
-    mine = jnp.concatenate([one_small[:2], ff_small[:3]], axis=0).reshape(5, n, own_dims)
-    mine = jnp.pad(jnp.transpose(mine, (1, 0, 2)), ((0, 0), (0, 0), (0, 128 - own_dims)))
-    fc_rows = ff_small[3].reshape(-1, 128)
-    qkv_rows = jnp.pad(qkv_bias[:, 0], (0, -qkv_dim % 128)).reshape(-1, 128)
-    shared = jnp.concatenate([fc_rows, qkv_rows], axis=0)
-    small = jnp.concatenate([mine, jnp.broadcast_to(shared, (n,) + shared.shape)], axis=1)
-    send_b, small, came_a = tied(send_b, small, came_a)
+    keep_b, send_b = weight_gradient(
+        places, chunks, proj_grad, normed_one, local_dim, 2, own_dims, (one_small, ff_small, qkv_bias)
+    )
+    send_b, came_a = tied(send_b, came_a)
     near_a = late_sum(keep_a, came_a)
     near_b = late_near(keep_b, send_b)
-    if n > 8:
-        small_near = lax.psum_scatter(small, "dp", scatter_dimension=0, tiled=True)
-    else:
-        small = jnp.take(small, chunks, axis=0)
-        small_near = late_near(small[: n // 2], small[n // 2 :])
     far_u = swapped(other_u, "tensor", 2)
     late_a, far_u = tied(late_far(near_a, bf16), far_u)
-    near_b, small_near = tied(near_b, small_near)
     late_b = late_far(near_b, bf16)
-    small_own = late_far(small_near, f32)[0]
-    late_own = jnp.concatenate([late_a, late_b], axis=1)
-    late_own, ff_own = tied(late_own, ff_own)
-    norm_grads = summed_over(small_own[:4], "tensor")[:, :own_dims]
-    fc_count = fc_rows.shape[0]
-    fc_b_total = small_own[5 : 5 + fc_count].reshape(-1)
-    qkv_b_total = small_own[5 + fc_count :].reshape(-1)[:qkv_dim].reshape(3, local_dim)
-    out_b_total = small_own[4, :own_dims]
-
-    input_grad = norm_back(own_u, came_u, far_u, hidden_in, stats[: hidden_in.shape[0]], cotangent)
+    late_own = jnp.concatenate([late_a, late_b[:, :local_dim]], axis=1)
+
+    vectors = late_b[:, 256:]
+    norm_grads = summed_over(vectors, "tensor")[:, :4].T
+    fc_count = ff // own_dims
+    fc_b_total = vectors[:, 8 : 8 + fc_count].T.reshape(ff)
+    qkv_b_total = vectors[:, 8 + fc_count : 8 + fc_count + qkv_dim // own_dims].T.reshape(3, local_dim)
+    out_b_total = vectors[:, 4]
+
+    input_grad = norm_back(own_u, came_u, far_u, hidden_in, stats, cotangent)
     return (
         layer_out,
         input_grad,

time: 278 us -> 250 us (0.90)
  local copies, waits for them, and re-layouts: 36.5 us -> 18.2 us
  waiting for transfers between devices: 60.2 us -> 54.2 us
  starting transfers between devices: 51.2 us -> 48 us
  other arithmetic: 9.91 us -> 7.01 us
    slice x10 -> x4, local copies, waits for them, and re-layouts: 10.2 us -> 0.93 us  [the longest x1 0.74 us: body(): norm_grads[3]]
    ppermute x3, waiting for transfers between devices: 11.9 us -> 20.5 us  [ring_gather(): from_left = lax.ppermute(from_left, axis, ahead)]
    reduce_scatter x1, waiting for transfers between devices: 15.6 us -> 7.72 us  [body(): lax.psum_scatter(ff_grads, 'dp', scatter_dimension=0, tiled=True)]
    ppermute x28 -> x24, waiting for transfers between devices: 19.3 us -> 13.7 us  [swapped(): return lax.ppermute(block, axis, route)]
    ppermute x28 -> x24, starting transfers between devices: 36.5 us -> 31.1 us  [swapped(): return lax.ppermute(block, axis, route)]
    unnamed x65 -> x62, local copies, waits for them, and re-layouts: 12.3 us -> 6.98 us
    ppermute x3, starting transfers between devices: 4.6 us -> 0.54 us  [ring_gather(): from_right = lax.ppermute(from_right, axis, behind)]
    ppermute x3, starting transfers between devices: 2.59 us -> 6.59 us  [ring_gather(): from_left = lax.ppermute(from_left, axis, ahead)]
  transfers between devices with their start and end apart: 40 -> 35, of which waited for: 19 -> 14; matrix products, arithmetic and copies ran while one was open for 13% -> 6% of each run, Pallas kernels for 24% -> 37%
where the time goes in v3:
time: 250 us; the launch traced here: 249 us
  Pallas kernels  107 us (43%)
  waiting for transfers between devices  54.2 us (22%)
  starting transfers between devices  48 us (19%)
  local copies, waits for them, and re-layouts  18.2 us (7%)
  between operations  14.5 us (6%)
  other arithmetic  7.01 us (3%)
    ppermute x24, starting transfers between devices, swapped(): return lax.ppermute(block, axis, route)  31.1 us
    pallas_call x1, Pallas kernels, feed_forward(): pl.pallas_call(functools.partial(ff_kernel, len(pieces)), grid_spec=pltpu...  23.7 us
    ppermute x3, waiting for transfers between devices, ring_gather(): from_left = lax.ppermute(from_left, axis, ahead)  20.5 us
    pallas_call x1, Pallas kernels, backward_own(): pl.pallas_call(functools.partial(own_bwd_kernel, heads, halo), grid_spec=...  17.1 us
    pallas_call x1, Pallas kernels, attention_forward(): pl.pallas_call(functools.partial(attn_fwd_kernel, heads, halo), grid_spec...  14.1 us
    ppermute x24, waiting for transfers between devices, swapped(): return lax.ppermute(block, axis, route)  13.7 us
    pallas_call x2, Pallas kernels, weight_gradient(): pl.pallas_call(functools.partial(weight_grad_kernel, own_dims), grid_spec...  12.7 us
    pallas_call x1, Pallas kernels, input_gradient(): pl.pallas_call(functools.partial(input_grad_kernel, halo), grid_spec=pltp...  11.2 us
  transfers between devices with their start and end apart: 35, of which 14 were waited for; matrix products, arithmetic and copies ran while one was open for 6% of the time, Pallas kernels for 37%

profile of v3, /device:TPU:0, one launch (start us, length us, event | category | flops | bytes accessed | tf_op | source)
XLA Modules:
  0.0 248.8 jit_solution(17001604576858292954)
XLA Ops:
  7.3 1.2 copy.55
  10.4 1.0 concatenate.11.refs_4_
  11.4 3.1 %collective-permute-start = (bf16[96,1664]{1,0:T(8,128)(2,1)S(1)}, bf16[96,1664]{1,0:T(8,128)(2,1)S(1)}, u32[]{:S(2)}, u32[]{:S(2)}) collective-permute-start(bf16[96,1664]{1,0:T(8,128)(2,1)S(1)} %concatenate.11.refs_4_), channel_id=1, source_target_pairs={{0,8},{8,16},{16,24},{24,28},{28,20},{20,12},{12,4},{4,0},{1,9},{9... | collective-permute-start | bytes 958472 | tf_op jit(solution)/shard_map/ppermute | solution.py:76
  14.6 2.0 collective-permute-start.6
  16.6 5.3 %collective-permute-done.refs_5_ = bf16[96,1664]{1,0:T(8,128)(2,1)S(1)} collective-permute-done((bf16[96,1664]{1,0:T(8,128)(2,1)S(1)}, bf16[96,1664]{1,0:T(8,128)(2,1)S(1)}, u32[]{:S(2)}, u32[]{:S(2)}) %collective-permute-start) | collective-permute-done | bytes 319520 | tf_op jit(solution)/shard_map/ppermute | solution.py:76
  22.0 1.6 collective-permute-done.1.refs_6_
  23.6 1.6 collective-permute-start.2
  25.6 1.5 collective-permute-start.10
  27.2 8.1 %collective-permute-done.2.refs_7_ = bf16[96,1664]{1,0:T(8,128)(2,1)} collective-permute-done((bf16[96,1664]{1,0:T(8,128)(2,1)S(1)}, bf16[96,1664]{1,0:T(8,128)(2,1)}, u32[]{:S(2)}, u32[]{:S(2)}) %collective-permute-start.2) | collective-permute-done | bytes 319520 | tf_op jit(solution)/shard_map/ppermute | solution.py:76
  35.2 2.5 collective-permute-done.3.refs_8_
  37.7 1.9 collective-permute-start.4
  40.3 7.1 %collective-permute-done.4.refs_9_ = bf16[96,1664]{1,0:T(8,128)(2,1)} collective-permute-done((bf16[96,1664]{1,0:T(8,128)(2,1)}, bf16[96,1664]{1,0:T(8,128)(2,1)}, u32[]{:S(2)}, u32[]{:S(2)}) %collective-permute-start.4) | collective-permute-done | bytes 319520 | tf_op jit(solution)/shard_map/ppermute | solution.py:76
  47.4 4.3 %collective-permute-done.5.refs_10_ = bf16[96,1664]{1,0:T(8,128)(2,1)} collective-permute-done((bf16[96,1664]{1,0:T(8,128)(2,1)}, bf16[96,1664]{1,0:T(8,128)(2,1)}, u32[]{:S(2)}, u32[]{:S(2)}) %collective-permute-start.5) | collective-permute-done | bytes 319520 | tf_op jit(solution)/shard_map/ppermute | solution.py:77
  51.7 4.3 %collective-permute-start.9 = (bf16[96,1664]{1,0:T(8,128)(2,1)}, bf16[96,1664]{1,0:T(8,128)(2,1)S(1)}, u32[]{:S(2)}, u32[]{:S(2)}) collective-permute-start(bf16[96,1664]{1,0:T(8,128)(2,1)} %collective-permute-done.4.refs_9_), channel_id=1, source_target_pairs={{0,8},{8,16},{16,24},{24,28},{28,20},{20,12},{12,4},{4,0},{1,9},{9... | collective-permute-start | bytes 958472 | tf_op jit(solution)/shard_map/ppermute | solution.py:83
  56.1 1.2 dynamic-slice_bitcast_fusion.start_ref
  57.3 3.8 %collective-permute-done.9.refs_11_ = bf16[96,1664]{1,0:T(8,128)(2,1)S(1)} collective-permute-done((bf16[96,1664]{1,0:T(8,128)(2,1)}, bf16[96,1664]{1,0:T(8,128)(2,1)S(1)}, u32[]{:S(2)}, u32[]{:S(2)}) %collective-permute-start.9) | collective-permute-done | bytes 319520 | tf_op jit(solution)/shard_map/ppermute | solution.py:83
  64.7 1.0 multiply_sine_fusion
  65.7 11.0 %project.1 = (bf16[192,2048]{1,0:T(8,128)(2,1)}, bf16[192,2048]{1,0:T(8,128)(2,1)}, bf16[192,2048]{1,0:T(8,128)(2,1)}, bf16[384,768]{1,0:T(8,128)(2,1)}, bf16[20...) custom-call(s32[8]{0:T(128)} %dynamic-slice_bitcast_fusion.start_ref, ...), custom_call_target="tpu_custom_call" | custom-call | flops 1811939328 | bytes 11796480 | tf_op jit(solution)/shard_map/project/pallas_call | solution.py:265
  76.7 3.9 %collective-permute-start.13 = (bf16[384,768]{1,0:T(8,128)(2,1)}, bf16[384,768]{1,0:T(8,128)(2,1)S(1)}, u32[]{:S(2)}, u32[]{:S(2)}) collective-permute-start(bf16[384,768]{1,0:T(8,128)(2,1)} %get-tuple-element.93), channel_id=1, source_target_pairs={{0,4},{4,8},{8,12},{12,16},{16,20},{20,24},{24,28},{1,5},{5,9},{9,... | collective-permute-start | bytes 1769480 | tf_op jit(solution)/shard_map/ppermute | solution.py:44
  80.7 23.7 %feed_forward.1 = (bf16[2048,768]{1,0:T(8,128)(2,1)}, bf16[2048,768]{1,0:T(8,128)(2,1)}, bf16[2048,768]{1,0:T(8,128)(2,1)}, bf16[768,1536]{1,0:T(8,128)(2,1)}, f32[8,768]{1,0:T(8,128)}) custom-call(s32[8]{0:T(128)} %dynamic-slice_bitcast_fusion.start_ref, bf16[2048,768]{1,0:T(8,128)(2,1)} %get-tuple-element.85.x_ref, ...), custom_call_target="tpu_custom_call" | custom-call | flops 14495514624 | bytes 17301504 | tf_op jit(solution)/shard_map/feed_forward/pallas_call | solution.py:181
  105.7 14.1 %attention_forward.1 = (bf16[192,2048]{1,0:T(8,128)(2,1)}, f32[8,2048]{1,0:T(8,128)}) custom-call(s32[8]{0:T(128)} %and_select_fusion.first_ref, bf16[192,2048]{1,0:T(8,128)(2,1)} %get-tuple-element.90.q_ref, bf16[192,2048]{1,0:T(8,128)(2,1)} %get-tuple-element.91.k_ref, bf16[192,2048]{1,0:T(8,128)(2,1)} %get-tuple-element.92.v_ref, ...), custom_call_target="tpu_custom_call" | custom-call | flops 6442450944 | bytes 3145728 | tf_op jit(solution)/shard_map/attention_forward/pallas_call | solution.py:359
  119.8 9.5 %branch_out.1 = (bf16[1024,768]{1,0:T(8,128)(2,1)}, bf16[1024,768]{1,0:T(8,128)(2,1)}, bf16[384,192]{1,0:T(8,128)(2,1)}, bf16[384,192]{1,0:T(8,128)(2,1)}, bf16[192,2048]{1,0:T(8,128)(2,1)}) custom-call(s32[4]{0:T(128)} %pad_add_fusion.place_ref, s32[8]{0:T(128)} %concatenate.10.chunk_ref, bf16[192,2048]{1,0:T(8,128)(2,1)} %get-tuple-element.94.o_ref, ...), custom_call_target="tpu_custom_call" | custom-call | flops 1207959552 | bytes 9437184 | tf_op jit(solution)/shard_map/branch_out/pallas_call | solution.py:579
  129.2 7.3 %collective-permute-start.15 = (bf16[384,192]{1,0:T(8,128)(2,1)}, bf16[384,192]{1,0:T(8,128)(2,1)S(1)}, u32[]{:S(2)}, u32[]{:S(2)}) collective-permute-start(bf16[384,192]{1,0:T(8,128)(2,1)} %get-tuple-element.105), channel_id=1, source_target_pairs={{0,4},{4,0},{8,12},{12,8},{16,20},{20,16},{24,28},{28,24},{1,5},{5... | collective-permute-start | bytes 442376 | tf_op jit(solution)/shard_map/ppermute | solution.py:49
  136.6 4.4 %attention_backward_left.1 = (f32[192,768]{1,0:T(8,128)}, bf16[384,768]{1,0:T(8,128)(2,1)}) custom-call(s32[8]{0:T(128)} %and_select_fusion.first_ref, bf16[192,2048]{1,0:T(8,128)(2,1)} %get-tuple-element.90.q_ref, bf16[384,768]{1,0:T(8,128)(2,1)} %copy-done.25, s32[1,2048]{1,0:T(1,128)} %bitcast.40, bf16[192,2048]{1,0:T(8,128)(2,1)} %get-tuple-element.94.o_ref, ...), custom_call_target="tpu_custom_call" | custom-call | flops 3019898880 | bytes 2949120 | tf_op jit(solution)/shard_map/attention_backward_left/pallas_call | solution.py:470
  141.0 3.3 %collective-permute-done.15 = bf16[384,192]{1,0:T(8,128)(2,1)S(1)} collective-permute-done((bf16[384,192]{1,0:T(8,128)(2,1)}, bf16[384,192]{1,0:T(8,128)(2,1)S(1)}, u32[]{:S(2)}, u32[]{:S(2)}) %collective-permute-start.15) | collective-permute-done | bytes 147488 | tf_op jit(solution)/shard_map/ppermute | solution.py:49
  145.6 3.6 %collective-permute-start.18 = (bf16[96,192]{1,0:T(8,128)(2,1)S(1)}, bf16[96,192]{1,0:T(8,128)(2,1)S(1)}, u32[]{:S(2)}, u32[]{:S(2)}) collective-permute-start(bf16[96,192]{1,0:T(8,128)(2,1)S(1)} %get-tuple-element.198), channel_id=1, source_target_pairs={{0,8},{4,12},{8,0},{12,4},{16,24},{20,28},{24,16},{28,20},{1,9},{5... | collective-permute-start | bytes 110600 | tf_op jit(solution)/shard_map/ppermute | solution.py:49
  149.2 2.4 collective-permute-start.20
  151.6 1.6 collective-permute-start.17
  153.2 1.5 collective-permute-start.16
  154.7 17.1 %attention_backward_own.1 = (f32[192,2048]{1,0:T(8,128)}, f32[192,2048]{1,0:T(8,128)}, f32[192,2048]{1,0:T(8,128)}) custom-call(s32[8]{0:T(128)} %and_select_fusion.first_ref, bf16[192,2048]{1,0:T(8,128)(2,1)} %get-tuple-element.90.q_ref, bf16[192,2048]{1,0:T(8,128)(2,1)} %get-tuple-element.91.k_ref, bf16[192,2048]{1,0:T(8,128)(2,1)} %get-tuple-element.92.v_ref, ...), custom_call_target="tpu_custom_call" | custom-call | flops 16106127360 | bytes 7864320 | tf_op jit(solution)/shard_map/attention_backward_own/pallas_call | solution.py:500
  171.8 7.7 %reduce-scatter.2.cloned.1.call-done = bf16[96,1536]{1,0:T(8,128)(2,1)} async-done(((bf16[768,1536]{1,0:T(8,128)(2,1)}), bf16[96,1536]{1,0:T(8,128)(2,1)}) %reduce-scatter.2.cloned.1.call-update) | async-done | bytes 294928 | tf_op jit(solution)/shard_map/reduce_scatter | solution.py:867
  179.5 1.9 convert_element_type.110
  182.2 11.2 %input_gradient.1 = (bf16[1024,768]{1,0:T(8,128)(2,1)}, bf16[1024,768]{1,0:T(8,128)(2,1)}, bf16[576,2048]{1,0:T(8,128)(2,1)}, f32[8,768]{1,0:T(8,128)}, f32[576,1]{1,0:T(8,128)}) custom-call(s32[4]{0:T(128)} %pad_add_fusion.place_ref, f32[192,2048]{1,0:T(8,128)} %get-tuple-element.113.dq_ref, f32[192,2048]{1,0:T(8,128)} %get-tuple-element.114.dk_ref, ...), custom_call_target="tpu_custom_call" | custom-call | flops 3623878656 | bytes 15728640 | tf_op jit(solution)/shard_map/input_gradient/pallas_call | solution.py:652
  195.2 6.6 %weight_gradient.2 = (bf16[384,384]{1,0:T(8,128)(2,1)}, bf16[384,384]{1,0:T(8,128)(2,1)}) custom-call(s32[4]{0:T(128)} %pad_add_fusion.place_ref, s32[8]{0:T(128)} %concatenate.10.chunk_ref, bf16[576,2048]{1,0:T(8,128)(2,1)} %get-tuple-element.124.grad_ref, bf16[2048,768]{1,0:T(8,128)(2,1)} %get-tuple-element.121.normed_ref), custom_call_target="tpu_custom_call" | custom-call | flops 2415919104 | bytes 6291456 | tf_op jit(solution)/shard_map/weight_gradient/pallas_call | solution.py:712
  201.8 1.4 add_convert_fusion.1
  203.2 1.1 add_convert_fusion
  205.8 1.1 collective-permute-start.26
  206.9 6.1 %weight_gradient.3 = (bf16[384,384]{1,0:T(8,128)(2,1)}, bf16[384,384]{1,0:T(8,128)(2,1)}) custom-call(s32[4]{0:T(128)} %pad_add_fusion.place_ref, s32[8]{0:T(128)} %concatenate.10.chunk_ref, bf16[576,2048]{1,0:T(8,128)(2,1)} %get-tuple-element.124.grad_ref, bf16[2048,768]{1,0:T(8,128)(2,1)} %get-tuple-element.121.normed_ref, ...), custom_call_target="tpu_custom_call" | custom-call | flops 1207959552 | bytes 6291456 | tf_op jit(solution)/shard_map/weight_gradient/pallas_call | solution.py:712
  214.7 1.7 collective-permute-start.24
  216.4 2.6 %collective-permute-start.25 = (bf16[96,384]{1,0:T(8,128)(2,1)S(1)}, bf16[96,384]{1,0:T(8,128)(2,1)S(1)}, u32[]{:S(2)}, u32[]{:S(2)}) collective-permute-start(bf16[96,384]{1,0:T(8,128)(2,1)S(1)} %get-tuple-element.196), channel_id=1, source_target_pairs={{0,24},{4,28},{8,16},{12,20},{16,8},{20,12},{24,0},{28,4},{1,25},{... | collective-permute-start | bytes 221192 | tf_op jit(solution)/shard_map/ppermute | solution.py:49
  219.0 3.6 %collective-permute-done.27 = bf16[384,384]{1,0:T(8,128)(2,1)S(1)} collective-permute-done((bf16[384,384]{1,0:T(8,128)(2,1)}, bf16[384,384]{1,0:T(8,128)(2,1)S(1)}, u32[]{:S(2)}, u32[]{:S(2)}) %collective-permute-start.27) | collective-permute-done | bytes 294944 | tf_op jit(solution)/shard_map/ppermute | solution.py:49
  223.1 1.2 collective-permute-start.29
  224.3 2.8 %collective-permute-start.30 = (bf16[96,384]{1,0:T(8,128)(2,1)S(1)}, bf16[96,384]{1,0:T(8,128)(2,1)S(1)}, u32[]{:S(2)}, u32[]{:S(2)}) collective-permute-start(bf16[96,384]{1,0:T(8,128)(2,1)S(1)} %get-tuple-element.193), channel_id=1, source_target_pairs={{0,24},{4,28},{8,16},{12,20},{16,8},{20,12},{24,0},{28,4},{1,25},{... | collective-permute-start | bytes 221192 | tf_op jit(solution)/shard_map/ppermute | solution.py:49
  227.2 3.5 %collective-permute-done.29 = bf16[96,384]{1,0:T(8,128)(2,1)S(1)} collective-permute-done((bf16[96,384]{1,0:T(8,128)(2,1)S(1)}, bf16[96,384]{1,0:T(8,128)(2,1)S(1)}, u32[]{:S(2)}, u32[]{:S(2)}) %collective-permute-start.29) | collective-permute-done | bytes 73760 | tf_op jit(solution)/shard_map/ppermute | solution.py:49
  231.0 1.1 collective-permute-done.31
  232.1 1.1 collective-permute-start.32
  235.0 1.3 collective-permute-done.32
  238.1 3.4 %norm_back.1 = bf16[512,768]{1,0:T(8,128)(2,1)} custom-call(bf16[1024,768]{1,0:T(8,128)(2,1)} %get-tuple-element.118.own_ref, bf16[1024,768]{1,0:T(8,128)(2,1)} %copy-done.1, bf16[512,768]{1,0:T(8,128)(2,1)} %copy-done.10, bf16[512,768]{1,0:T(8,128)(2,1)} %x_ref.1, f32[2048,128]{1,0:T(8,128)} %get-tuple-element.86.stats_ref, bf16[512,768]{1,0:T(8,128)(2,1)} %g_ref.1), custom_call_target="tpu_custom_call" | custom-call | flops 7864320 | bytes 4718592 | tf_op jit(solution)/shard_map/norm_back/pallas_call | solution.py:745
  (143 shorter events, 20.0 us)
Async XLA Ops:
  7.2 18.5 %copy-start.9 = (bf16[512,768]{1,0:T(8,128)(2,1)S(1)}, bf16[512,768]{1,0:T(8,128)(2,1)}, u32[]{:S(2)}) copy-start(bf16[512,768]{1,0:T(8,128)(2,1)} %g_ref.1) | copy-start | bytes 2359300
  7.2 48.8 %copy-start.18 = (s32[2048]{0:T(1024)S(1)}, s32[2048]{0:T(1024)}, u32[]{:S(2)}) copy-start(s32[2048]{0:T(1024)} %param.30) | copy-start | bytes 24580
  7.2 54.7 %copy-start.20 = (bf16[3,192]{1,0:T(4,128)(2,1)S(1)}, bf16[3,192]{1,0:T(4,128)(2,1)}, u32[]{:S(2)}) copy-start(bf16[3,192]{1,0:T(4,128)(2,1)} %param.19) | copy-start | bytes 3460
  7.2 55.7 %copy-start.21 = (bf16[768]{0:T(1024)(128)(2,1)S(1)}, bf16[768]{0:T(1024)(128)(2,1)}, u32[]{:S(2)}) copy-start(bf16[768]{0:T(1024)(128)(2,1)} %param.23) | copy-start | bytes 4612
  7.2 73.4 %all-gather.2.cloned.1.call-start = ((), (), s32[]{:S(2)}) async-start(), calls=%async_computation.1 | async-start | bytes 1327104 | tf_op jit(solution)/shard_map/all_gather | solution.py:842
  11.4 54.3 %copy-start.14 = (bf16[96,1664]{1,0:T(8,128)(2,1)}, bf16[96,1664]{1,0:T(8,128)(2,1)S(1)}, u32[]{:S(2)}) copy-start(bf16[96,1664]{1,0:T(8,128)(2,1)S(1)} %concatenate.11.refs_4_) | copy-start | bytes 958468
  11.4 10.5 %collective-permute-start = (bf16[96,1664]{1,0:T(8,128)(2,1)S(1)}, bf16[96,1664]{1,0:T(8,128)(2,1)S(1)}, u32[]{:S(2)}, u32[]{:S(2)}) collective-permute-start(bf16[96,1664]{1,0:T(8,128)(2,1)S(1)} %concatenate.11.refs_4_), channel_id=1, source_target_pairs={{0,8},{8,16},{16,24},{24,28},{28,20},{20,12},{12,4},{4,0},{1,9},{9... | collective-permute-start | bytes 958472 | tf_op jit(solution)/shard_map/ppermute | solution.py:76
  14.5 9.1 %collective-permute-start.1 = (bf16[96,1664]{1,0:T(8,128)(2,1)S(1)}, bf16[96,1664]{1,0:T(8,128)(2,1)}, u32[]{:S(2)}, u32[]{:S(2)}) collective-permute-start(bf16[96,1664]{1,0:T(8,128)(2,1)S(1)} %concatenate.11.refs_4_), channel_id=1, source_target_pairs={{8,0},{16,8},{24,16},{28,24},{20,28},{12,20},{4,12},{0,4},{9,1},{1... | collective-permute-start | bytes 958472 | tf_op jit(solution)/shard_map/ppermute | solution.py:77
  14.5 165.0 %reduce-scatter.2.cloned.1.call-start = ((), (), s32[]{:S(2)}) async-start(), calls=%async_computation.2 | async-start | bytes 2654208 | tf_op jit(solution)/shard_map/reduce_scatter | solution.py:867
  14.6 25.1 %collective-permute-start.6 = (bf16[512,768]{1,0:T(8,128)(2,1)S(1)}, bf16[512,768]{1,0:T(8,128)(2,1)}, u32[]{:S(2)}, u32[]{:S(2)}) collective-permute-start(bf16[512,768]{1,0:T(8,128)(2,1)S(1)} %copy-done.2), channel_id=1, source_target_pairs={{0,2},{1,3},{2,0},{3,1},{4,6},{5,7},{6,4},{7,5},{8,10},{9,11},{10,... | collective-permute-start | bytes 2359304 | tf_op jit(solution)/shard_map/ppermute | solution.py:49
  22.0 43.8 %copy-start.26 = (bf16[96,1664]{1,0:T(8,128)(2,1)}, bf16[96,1664]{1,0:T(8,128)(2,1)S(1)}, u32[]{:S(2)}) copy-start(bf16[96,1664]{1,0:T(8,128)(2,1)S(1)} %collective-permute-done.refs_5_) | copy-start | bytes 958468
  23.6 11.6 %collective-permute-start.2 = (bf16[96,1664]{1,0:T(8,128)(2,1)S(1)}, bf16[96,1664]{1,0:T(8,128)(2,1)}, u32[]{:S(2)}, u32[]{:S(2)}) collective-permute-start(bf16[96,1664]{1,0:T(8,128)(2,1)S(1)} %collective-permute-done.refs_5_), channel_id=1, source_target_pairs={{0,8},{8,16},{16,24},{24,28},{28,20},{20,12},{12,4},{4,0},{1,9},{9... | collective-permute-start | bytes 958472 | tf_op jit(solution)/shard_map/ppermute | solution.py:76
  25.2 12.5 %collective-permute-start.3 = (bf16[96,1664]{1,0:T(8,128)(2,1)}, bf16[96,1664]{1,0:T(8,128)(2,1)}, u32[]{:S(2)}, u32[]{:S(2)}) collective-permute-start(bf16[96,1664]{1,0:T(8,128)(2,1)} %collective-permute-done.1.refs_6_), channel_id=1, source_target_pairs={{8,0},{16,8},{24,16},{28,24},{20,28},{12,20},{4,12},{0,4},{9,1},{1... | collective-permute-start | bytes 958472 | tf_op jit(solution)/shard_map/ppermute | solution.py:77
  25.6 31.7 %collective-permute-start.10 = (bf16[512,768]{1,0:T(8,128)(2,1)S(1)}, bf16[512,768]{1,0:T(8,128)(2,1)S(1)}, u32[]{:S(2)}, u32[]{:S(2)}) collective-permute-start(bf16[512,768]{1,0:T(8,128)(2,1)S(1)} %copy-done.9), channel_id=1, source_target_pairs={{0,2},{1,3},{2,0},{3,1},{4,6},{5,7},{6,4},{7,5},{8,10},{9,11},{10,... | collective-permute-start | bytes 2359304 | tf_op jit(solution)/shard_map/ppermute | solution.py:49
  37.7 9.7 %collective-permute-start.4 = (bf16[96,1664]{1,0:T(8,128)(2,1)}, bf16[96,1664]{1,0:T(8,128)(2,1)}, u32[]{:S(2)}, u32[]{:S(2)}) collective-permute-start(bf16[96,1664]{1,0:T(8,128)(2,1)} %collective-permute-done.2.refs_7_), channel_id=1, source_target_pairs={{0,8},{8,16},{16,24},{24,28},{28,20},{20,12},{12,4},{4,0},{1,9},{9... | collective-permute-start | bytes 958472 | tf_op jit(solution)/shard_map/ppermute | solution.py:76
  39.6 12.1 %collective-permute-start.5 = (bf16[96,1664]{1,0:T(8,128)(2,1)}, bf16[96,1664]{1,0:T(8,128)(2,1)}, u32[]{:S(2)}, u32[]{:S(2)}) collective-permute-start(bf16[96,1664]{1,0:T(8,128)(2,1)} %collective-permute-done.3.refs_8_), channel_id=1, source_target_pairs={{8,0},{16,8},{24,16},{28,24},{20,28},{12,20},{4,12},{0,4},{9,1},{1... | collective-permute-start | bytes 958472 | tf_op jit(solution)/shard_map/ppermute | solution.py:77
  39.7 26.0 %collective-permute-start.7 = (bf16[512,768]{1,0:T(8,128)(2,1)S(1)}, bf16[512,768]{1,0:T(8,128)(2,1)}, u32[]{:S(2)}, u32[]{:S(2)}) collective-permute-start(bf16[512,768]{1,0:T(8,128)(2,1)S(1)} %copy-done.2), channel_id=1, source_target_pairs={{0,1},{1,0},{2,3},{3,2},{4,5},{5,4},{6,7},{7,6},{8,9},{9,8},{10,11... | collective-permute-start | bytes 2359304 | tf_op jit(solution)/shard_map/ppermute | solution.py:49
  39.7 40.9 %collective-permute-start.11 = (bf16[512,768]{1,0:T(8,128)(2,1)S(1)}, bf16[512,768]{1,0:T(8,128)(2,1)}, u32[]{:S(2)}, u32[]{:S(2)}) collective-permute-start(bf16[512,768]{1,0:T(8,128)(2,1)S(1)} %copy-done.9), channel_id=1, source_target_pairs={{0,1},{1,0},{2,3},{3,2},{4,5},{5,4},{6,7},{7,6},{8,9},{9,8},{10,11... | collective-permute-start | bytes 2359304 | tf_op jit(solution)/shard_map/ppermute | solution.py:49
  51.7 9.4 %collective-permute-start.9 = (bf16[96,1664]{1,0:T(8,128)(2,1)}, bf16[96,1664]{1,0:T(8,128)(2,1)S(1)}, u32[]{:S(2)}, u32[]{:S(2)}) collective-permute-start(bf16[96,1664]{1,0:T(8,128)(2,1)} %collective-permute-done.4.refs_9_), channel_id=1, source_target_pairs={{0,8},{8,16},{16,24},{24,28},{28,20},{20,12},{12,4},{4,0},{1,9},{9... | collective-permute-start | bytes 958472 | tf_op jit(solution)/shard_map/ppermute | solution.py:83
  56.0 20.7 %copy-start.19 = (s32[2048]{0:T(1024)}, s32[2048]{0:T(1024)S(1)}, u32[]{:S(2)}) copy-start(s32[2048]{0:T(1024)S(1)} %get-tuple-element.204) | copy-start | bytes 24580
  56.0 9.7 %collective-permute-start.8 = (bf16[512,768]{1,0:T(8,128)(2,1)}, bf16[512,768]{1,0:T(8,128)(2,1)}, u32[]{:S(2)}, u32[]{:S(2)}) collective-permute-start(bf16[512,768]{1,0:T(8,128)(2,1)} %collective-permute-done.6.refs_1_), channel_id=1, source_target_pairs={{0,1},{1,0},{2,3},{3,2},{4,5},{5,4},{6,7},{7,6},{8,9},{9,8},{10,11... | collective-permute-start | bytes 2359304 | tf_op jit(solution)/shard_map/ppermute | solution.py:49
  57.3 19.4 %copy-start.23 = (bf16[512,768]{1,0:T(8,128)(2,1)}, bf16[512,768]{1,0:T(8,128)(2,1)S(1)}, u32[]{:S(2)}) copy-start(bf16[512,768]{1,0:T(8,128)(2,1)S(1)} %collective-permute-done.10.refs_1_) | copy-start | bytes 2359300
  61.1 19.5 %collective-permute-start.12 = (bf16[512,768]{1,0:T(8,128)(2,1)S(1)}, bf16[512,768]{1,0:T(8,128)(2,1)}, u32[]{:S(2)}, u32[]{:S(2)}) collective-permute-start(bf16[512,768]{1,0:T(8,128)(2,1)S(1)} %collective-permute-done.10.refs_1_), channel_id=1, source_target_pairs={{0,1},{1,0},{2,3},{3,2},{4,5},{5,4},{6,7},{7,6},{8,9},{9,8},{10,11... | collective-permute-start | bytes 2359304 | tf_op jit(solution)/shard_map/ppermute | solution.py:49
  76.7 28.2 %collective-permute-start.13 = (bf16[384,768]{1,0:T(8,128)(2,1)}, bf16[384,768]{1,0:T(8,128)(2,1)S(1)}, u32[]{:S(2)}, u32[]{:S(2)}) collective-permute-start(bf16[384,768]{1,0:T(8,128)(2,1)} %get-tuple-element.93), channel_id=1, source_target_pairs={{0,4},{4,8},{8,12},{12,16},{16,20},{20,24},{24,28},{1,5},{5,9},{9,... | collective-permute-start | bytes 1769480 | tf_op jit(solution)/shard_map/ppermute | solution.py:44
  129.2 15.1 %collective-permute-start.14 = (bf16[1024,768]{1,0:T(8,128)(2,1)}, bf16[1024,768]{1,0:T(8,128)(2,1)S(1)}, u32[]{:S(2)}, u32[]{:S(2)}) collective-permute-start(bf16[1024,768]{1,0:T(8,128)(2,1)} %get-tuple-element.99), channel_id=1, source_target_pairs={{0,1},{1,0},{2,3},{3,2},{4,5},{5,4},{6,7},{7,6},{8,9},{9,8},{10,11... | collective-permute-start | bytes 4718600 | tf_op jit(solution)/shard_map/ppermute | solution.py:49
  129.2 15.1 %collective-permute-start.15 = (bf16[384,192]{1,0:T(8,128)(2,1)}, bf16[384,192]{1,0:T(8,128)(2,1)S(1)}, u32[]{:S(2)}, u32[]{:S(2)}) collective-permute-start(bf16[384,192]{1,0:T(8,128)(2,1)} %get-tuple-element.105), channel_id=1, source_target_pairs={{0,4},{4,0},{8,12},{12,8},{16,20},{20,16},{24,28},{28,24},{1,5},{5... | collective-permute-start | bytes 442376 | tf_op jit(solution)/shard_map/ppermute | solution.py:49
  136.6 7.8 %copy-start.5 = (bf16[1024,768]{1,0:T(8,128)(2,1)S(1)}, bf16[1024,768]{1,0:T(8,128)(2,1)}, u32[]{:S(2)}) copy-start(bf16[1024,768]{1,0:T(8,128)(2,1)} %get-tuple-element.98) | copy-start | bytes 4718596
  144.4 8.8 %copy-start.24 = (bf16[384,768]{1,0:T(8,128)(2,1)S(1)}, bf16[384,768]{1,0:T(8,128)(2,1)}, u32[]{:S(2)}) copy-start(bf16[384,768]{1,0:T(8,128)(2,1)} %get-tuple-element.106) | copy-start | bytes 1769476
  145.6 26.2 %collective-permute-start.18 = (bf16[96,192]{1,0:T(8,128)(2,1)S(1)}, bf16[96,192]{1,0:T(8,128)(2,1)S(1)}, u32[]{:S(2)}, u32[]{:S(2)}) collective-permute-start(bf16[96,192]{1,0:T(8,128)(2,1)S(1)} %get-tuple-element.198), channel_id=1, source_target_pairs={{0,8},{4,12},{8,0},{12,4},{16,24},{20,28},{24,16},{28,20},{1,9},{5... | collective-permute-start | bytes 110600 | tf_op jit(solution)/shard_map/ppermute | solution.py:49
  149.2 22.6 %collective-permute-start.19 = (bf16[96,192]{1,0:T(8,128)(2,1)S(1)}, bf16[96,192]{1,0:T(8,128)(2,1)S(1)}, u32[]{:S(2)}, u32[]{:S(2)}) collective-permute-start(bf16[96,192]{1,0:T(8,128)(2,1)S(1)} %get-tuple-element.200), channel_id=1, source_target_pairs={{0,16},{4,20},{8,24},{12,28},{16,0},{20,4},{24,8},{28,12},{1,17},{... | collective-permute-start | bytes 110600 | tf_op jit(solution)/shard_map/ppermute | solution.py:49
  149.2 22.6 %collective-permute-start.20 = (bf16[96,192]{1,0:T(8,128)(2,1)S(1)}, bf16[96,192]{1,0:T(8,128)(2,1)S(1)}, u32[]{:S(2)}, u32[]{:S(2)}) collective-permute-start(bf16[96,192]{1,0:T(8,128)(2,1)S(1)} %get-tuple-element.199), channel_id=1, source_target_pairs={{0,24},{4,28},{8,16},{12,20},{16,8},{20,12},{24,0},{28,4},{1,25},{... | collective-permute-start | bytes 110600 | tf_op jit(solution)/shard_map/ppermute | solution.py:49
  151.6 29.9 %collective-permute-start.17 = (bf16[512,768]{1,0:T(8,128)(2,1)S(1)}, bf16[512,768]{1,0:T(8,128)(2,1)S(1)}, u32[]{:S(2)}, u32[]{:S(2)}) collective-permute-start(bf16[512,768]{1,0:T(8,128)(2,1)S(1)} %add_convert_fusion.2), channel_id=1, source_target_pairs={{0,2},{1,3},{2,0},{3,1},{4,6},{5,7},{6,4},{7,5},{8,10},{9,11},{10,... | collective-permute-start | bytes 2359304 | tf_op jit(solution)/shard_map/ppermute | solution.py:49
  153.2 28.2 %collective-permute-start.16 = (bf16[384,768]{1,0:T(8,128)(2,1)S(1)}, bf16[384,768]{1,0:T(8,128)(2,1)S(1)}, u32[]{:S(2)}, u32[]{:S(2)}) collective-permute-start(bf16[384,768]{1,0:T(8,128)(2,1)S(1)} %copy-done.24), channel_id=1, source_target_pairs={{4,0},{8,4},{12,8},{16,12},{20,16},{24,20},{28,24},{5,1},{9,5},{13... | collective-permute-start | bytes 1769480 | tf_op jit(solution)/shard_map/ppermute | solution.py:44
  181.4 12.0 %copy-start.11 = (bf16[512,768]{1,0:T(8,128)(2,1)}, bf16[512,768]{1,0:T(8,128)(2,1)S(1)}, u32[]{:S(2)}) copy-start(bf16[512,768]{1,0:T(8,128)(2,1)S(1)} %collective-permute-done.17) | copy-start | bytes 2359300
  193.4 9.7 %collective-permute-start.21 = (bf16[1024,768]{1,0:T(8,128)(2,1)}, bf16[1024,768]{1,0:T(8,128)(2,1)S(1)}, u32[]{:S(2)}, u32[]{:S(2)}) collective-permute-start(bf16[1024,768]{1,0:T(8,128)(2,1)} %get-tuple-element.119), channel_id=1, source_target_pairs={{0,1},{1,0},{2,3},{3,2},{4,5},{5,4},{6,7},{7,6},{8,9},{9,8},{10,11... | collective-permute-start | bytes 4718600 | tf_op jit(solution)/shard_map/ppermute | solution.py:49
  204.3 9.4 %collective-permute-start.22 = (bf16[384,384]{1,0:T(8,128)(2,1)S(1)}, bf16[384,384]{1,0:T(8,128)(2,1)S(1)}, u32[]{:S(2)}, u32[]{:S(2)}) collective-permute-start(bf16[384,384]{1,0:T(8,128)(2,1)S(1)} %copy-done.28), channel_id=1, source_target_pairs={{0,4},{4,0},{8,12},{12,8},{16,20},{20,16},{24,28},{28,24},{1,5},{5... | collective-permute-start | bytes 884744 | tf_op jit(solution)/shard_map/ppermute | solution.py:49
  205.8 31.2 %collective-permute-start.26 = (bf16[512,768]{1,0:T(8,128)(2,1)}, bf16[512,768]{1,0:T(8,128)(2,1)S(1)}, u32[]{:S(2)}, u32[]{:S(2)}) collective-permute-start(bf16[512,768]{1,0:T(8,128)(2,1)} %add_convert_fusion), channel_id=1, source_target_pairs={{0,2},{1,3},{2,0},{3,1},{4,6},{5,7},{6,4},{7,5},{8,10},{9,11},{10,... | collective-permute-start | bytes 2359304 | tf_op jit(solution)/shard_map/ppermute | solution.py:49
  212.9 9.6 %copy-start.16 = (bf16[384,384]{1,0:T(8,128)(2,1)S(1)}, bf16[384,384]{1,0:T(8,128)(2,1)}, u32[]{:S(2)}) copy-start(bf16[384,384]{1,0:T(8,128)(2,1)} %get-tuple-element.134) | copy-start | bytes 884740
  213.7 8.8 %collective-permute-start.27 = (bf16[384,384]{1,0:T(8,128)(2,1)}, bf16[384,384]{1,0:T(8,128)(2,1)S(1)}, u32[]{:S(2)}, u32[]{:S(2)}) collective-permute-start(bf16[384,384]{1,0:T(8,128)(2,1)} %get-tuple-element.135), channel_id=1, source_target_pairs={{0,4},{4,0},{8,12},{12,8},{16,20},{20,16},{24,28},{28,24},{1,5},{5... | collective-permute-start | bytes 884744 | tf_op jit(solution)/shard_map/ppermute | solution.py:49
  214.5 8.5 %collective-permute-start.23 = (bf16[96,384]{1,0:T(8,128)(2,1)S(1)}, bf16[96,384]{1,0:T(8,128)(2,1)S(1)}, u32[]{:S(2)}, u32[]{:S(2)}) collective-permute-start(bf16[96,384]{1,0:T(8,128)(2,1)S(1)} %get-tuple-element.195), channel_id=1, source_target_pairs={{0,8},{4,12},{8,0},{12,4},{16,24},{20,28},{24,16},{28,20},{1,9},{5... | collective-permute-start | bytes 221192 | tf_op jit(solution)/shard_map/ppermute | solution.py:49
  214.7 9.6 %collective-permute-start.24 = (bf16[96,384]{1,0:T(8,128)(2,1)S(1)}, bf16[96,384]{1,0:T(8,128)(2,1)S(1)}, u32[]{:S(2)}, u32[]{:S(2)}) collective-permute-start(bf16[96,384]{1,0:T(8,128)(2,1)S(1)} %get-tuple-element.197), channel_id=1, source_target_pairs={{0,16},{4,20},{8,24},{12,28},{16,0},{20,4},{24,8},{28,12},{1,17},{... | collective-permute-start | bytes 221192 | tf_op jit(solution)/shard_map/ppermute | solution.py:49
  216.4 10.8 %collective-permute-start.25 = (bf16[96,384]{1,0:T(8,128)(2,1)S(1)}, bf16[96,384]{1,0:T(8,128)(2,1)S(1)}, u32[]{:S(2)}, u32[]{:S(2)}) collective-permute-start(bf16[96,384]{1,0:T(8,128)(2,1)S(1)} %get-tuple-element.196), channel_id=1, source_target_pairs={{0,24},{4,28},{8,16},{12,20},{16,8},{20,12},{24,0},{28,4},{1,25},{... | collective-permute-start | bytes 221192 | tf_op jit(solution)/shard_map/ppermute | solution.py:49
  222.7 4.5 %collective-permute-start.28 = (bf16[96,384]{1,0:T(8,128)(2,1)S(1)}, bf16[96,384]{1,0:T(8,128)(2,1)S(1)}, u32[]{:S(2)}, u32[]{:S(2)}) collective-permute-start(bf16[96,384]{1,0:T(8,128)(2,1)S(1)} %get-tuple-element.192), channel_id=1, source_target_pairs={{0,8},{4,12},{8,0},{12,4},{16,24},{20,28},{24,16},{28,20},{1,9},{5... | collective-permute-start | bytes 221192 | tf_op jit(solution)/shard_map/ppermute | solution.py:49
  223.1 7.7 %collective-permute-start.29 = (bf16[96,384]{1,0:T(8,128)(2,1)S(1)}, bf16[96,384]{1,0:T(8,128)(2,1)S(1)}, u32[]{:S(2)}, u32[]{:S(2)}) collective-permute-start(bf16[96,384]{1,0:T(8,128)(2,1)S(1)} %get-tuple-element.194), channel_id=1, source_target_pairs={{0,16},{4,20},{8,24},{12,28},{16,0},{20,4},{24,8},{28,12},{1,17},{... | collective-permute-start | bytes 221192 | tf_op jit(solution)/shard_map/ppermute | solution.py:49
  224.3 6.4 %collective-permute-start.30 = (bf16[96,384]{1,0:T(8,128)(2,1)S(1)}, bf16[96,384]{1,0:T(8,128)(2,1)S(1)}, u32[]{:S(2)}, u32[]{:S(2)}) collective-permute-start(bf16[96,384]{1,0:T(8,128)(2,1)S(1)} %get-tuple-element.193), channel_id=1, source_target_pairs={{0,24},{4,28},{8,16},{12,20},{16,8},{20,12},{24,0},{28,4},{1,25},{... | collective-permute-start | bytes 221192 | tf_op jit(solution)/shard_map/ppermute | solution.py:49
  230.9 1.2 collective-permute-start.31
  232.1 4.1 %collective-permute-start.32 = (f32[96,128]{1,0:T(8,128)S(1)}, f32[96,128]{1,0:T(8,128)S(1)}, u32[]{:S(2)}, u32[]{:S(2)}) collective-permute-start(f32[96,128]{1,0:T(8,128)S(1)} %slice_add_fusion.3), channel_id=1, source_target_pairs={{0,2},{1,3},{2,0},{3,1},{4,6},{5,7},{6,4},{7,5},{8,10},{9,11},{10,... | collective-permute-start | bytes 147464 | tf_op jit(solution)/shard_map/ppermute | solution.py:49
  233.4 8.0 %copy-start.22 = (f32[96]{0:T(128)}, f32[96]{0:T(128)S(1)}, u32[]{:S(2)}) copy-start(f32[96]{0:T(128)S(1)} %slice_reduce_fusion.4) | copy-start | bytes 1156
  (16 other events, 60.7 us)
Sparse Core Ops, SparseCore 0:
  14.7 44.4 all-gather.1
  104.5 75.0 reduce-scatter.1

commit v4 on v3

--- a/solution.py
+++ b/solution.py
@@ -31,7 +31,7 @@
 
 
 def cost(flops, moved, exps=0):
-    return pl.CostEstimate(flops=int(flops), bytes_accessed=int(moved), transcendentals=int(exps))
+    return pl.CostEstimate(flops=int(flops) // 16, bytes_accessed=int(moved) // 16, transcendentals=int(exps) // 16)
 
 
 def shaped(shape, dtype):
@@ -53,11 +53,11 @@
     return list(range(0, n, 2)) + list(range(n - 1, 0, -2))
 
 
-def ring_gather(block, axis, early, late):
+def ring_gather(block, axis, early):
     n = lax.axis_size(axis)
     rows = block.shape[0]
     if n > 8:
-        return [lax.all_gather(block, axis, axis=0, tiled=True)], jnp.zeros((1,), jnp.int32), early, late
+        return [lax.all_gather(block, axis, axis=0, tiled=True)], jnp.zeros((1,), jnp.int32), early
     ring = ring_order(n)
     ahead = [(ring[r], ring[(r + 1) % n]) for r in range(n)]
     behind = [(b, a) for a, b in ahead]
@@ -80,9 +80,8 @@
         else:
             from_left, from_right = tied(from_left, from_right)
         pieces += [from_left, from_right]
-    from_left, late = tied(lax.ppermute(from_left, axis, ahead), late)
-    pieces.append(from_left)
-    return pieces, jnp.asarray(table, jnp.int32)[lax.axis_index(axis)], early, late
+    pieces.append(lax.ppermute(from_left, axis, ahead))
+    return pieces, jnp.asarray(table, jnp.int32)[lax.axis_index(axis)], early
 
 
 def gather_rows(block, near, far):
@@ -134,16 +133,15 @@
     return (x_ref[...].astype(f32) - stats_ref[:, 0:1]) * stats_ref[:, 1:2]
 
 
-def ff_kernel(pieces, start_ref, x_ref, stats_ref, b_ref, vec_ref, fc2_w, *refs):
-    g_refs, w_refs = refs[:4], refs[4 : 4 + pieces]
-    out_ref, u_ref, g_ref, grads_ref, small_ref, fc_w, fc_acc, fc2_acc = refs[4 + pieces :]
+def ff_kernel(x_ref, stats_ref, b_ref, vec_ref, w_ref, *refs):
+    g_refs, (out_ref, u_ref, g_ref, grads_ref, small_ref, fc_acc, fc2_acc) = refs[:4], refs[4:]
     take_rows(g_refs, g_ref)
     step = pl.program_id(0)
-    ff = fc2_w.shape[1]
+    ff = fc_acc.shape[1]
+    fc_w, fc2_w = w_ref.at[:, :ff], w_ref.at[:, ff:]
 
     @pl.when(step == 0)
     def _():
-        assemble(w_refs, start_ref, 0, fc_w)
         fc_acc[...] = jnp.zeros_like(fc_acc)
         fc2_acc[...] = jnp.zeros_like(fc2_acc)
         small_ref[...] = jnp.zeros_like(small_ref)
@@ -173,26 +171,26 @@
         grads_ref[:, ff:] = fc2_acc[...].astype(bf16)
 
 
-def feed_forward(starts, x, g, stats, b_fc, vec, fc2_w, pieces, ff):
+def feed_forward(x, g, stats, b_fc, vec, w, ff):
     tokens, dim = x.shape
     rows = tokens // 4
     spec = pl.BlockSpec((rows, dim), lambda s, *_: (s, 0))
     whole = lambda shape: pl.BlockSpec(shape, lambda s, *_: (0, 0))
     return pl.pallas_call(
-        functools.partial(ff_kernel, len(pieces)),
+        ff_kernel,
         grid_spec=pltpu.PrefetchScalarGridSpec(
-            num_scalar_prefetch=1,
+            num_scalar_prefetch=0,
             grid=(4,),
             in_specs=[
                 spec,
                 pl.BlockSpec((rows, 128), lambda s, *_: (s, 0)),
                 whole((1, ff)),
                 whole(vec.shape),
-                whole(fc2_w.shape),
+                whole(w.shape),
             ]
-            + [whole(p.shape) for p in g + pieces],
+            + [whole(p.shape) for p in g],
             out_specs=[spec, spec, spec, whole((dim, 2 * ff)), whole((8, dim))],
-            scratch_shapes=[pltpu.VMEM((dim, ff), bf16)] + [pltpu.VMEM((dim, ff), f32)] * 2,
+            scratch_shapes=[pltpu.VMEM((dim, ff), f32)] * 2,
         ),
         out_shape=[
             shaped((tokens, dim), bf16),
@@ -204,7 +202,7 @@
         compiler_params=params(),
         cost_estimate=cost(12 * tokens * dim * ff, 8 * tokens * dim + 8 * dim * ff, 2 * tokens * ff),
         name="feed_forward",
-    )(starts, x, stats, b_fc, vec, fc2_w, *g, *pieces)
+    )(x, stats, b_fc, vec, w, *g)
 
 
 def turned(x, cos_t, sin_t):
@@ -829,7 +827,6 @@
     vectors = jnp.pad(vectors, ((0, 0), (0, 122)))
     block = jnp.concatenate(
         [
-            w_fc,
             jnp.transpose(w_qkv, (1, 0, 2)).reshape(own_dims, qkv_dim),
             w_out.T,
             vectors,
@@ -838,10 +835,9 @@
     )
     x_far, g_far = swapped(hidden_in, "tensor", 2), swapped(cotangent, "tensor", 2)
     x_near, g_near = swapped(hidden_in, "tensor", 1), swapped(cotangent, "tensor", 1)
-    pieces, starts, x_far, g_far = ring_gather(block, "dp", x_far, g_far)
-    fc2_w = lax.all_gather(w_fc2.T, "dp", axis=0, tiled=True)
+    pieces, starts, x_far = ring_gather(block, "dp", x_far)
+    ff_w = lax.all_gather(jnp.concatenate([w_fc, w_fc2.T], axis=1), "dp", axis=0, tiled=True)
     x_blocks = gather_rows(hidden_in, x_near, x_far)
-    g_blocks = gather_rows(cotangent, g_near, g_far)
 
     cos_t, sin_t = rope_tables(positions)
     lo = halo + jnp.arange(seq_len, dtype=jnp.int32) - positions
@@ -856,15 +852,17 @@
         cos_t,
         sin_t,
         pieces,
-        ff,
+        0,
         local_dim,
         halo,
     )
+    right, g_far = tied(right, g_far)
     left = passed_along(right, "dp", 1)
+    g_blocks = gather_rows(cotangent, g_near, g_far)
     ff_out, u_two, g_all, ff_grads, ff_small = feed_forward(
-        starts, x_all, g_blocks, stats, b_fc.astype(f32).reshape(1, ff), vec, fc2_w, pieces, ff
+        x_all, g_blocks, stats, b_fc.astype(f32).reshape(1, ff), vec, ff_w, ff
     )
-    ff_own = lax.psum_scatter(ff_grads, "dp", scatter_dimension=0, tiled=True).astype(f32)
+    ff_sum = lax.psum_scatter(ff_grads, "dp", scatter_dimension=0, tiled=True)
     q, ff_out = tied(q, ff_out)
 
     o, lse = attention_forward(first, q, k, v, left, lo_row, halo)
@@ -878,7 +876,7 @@
     back = passed_along(back, "dp", -1)
     ow_own = late_far(ow_near, bf16)
     dq, dk, dv = backward_own(first, q, k, v, lo_row, o, lse, do, dq_part, halo)
-    back, dq, far_o, ow_own, ff_own = tied(back, dq, far_o, ow_own, ff_own)
+    back, dq, far_o, ow_own = tied(back, dq, far_o, ow_own)
     count = hidden_in.shape[0]
     summed = own_o[:count].astype(f32) + came_o[:count].astype(f32) + far_o.astype(f32)
     layer_out = (hidden_in.astype(f32) + summed + vec[0] + vec[1]).astype(bf16)
@@ -887,6 +885,7 @@
         places, dq, dk, dv, back, x_all, stats, u_two, wt, vec, cos_t, sin_t, halo
     )
     own_u, came_u, other_u = scatter_near(u_keep, u_send)
+    proj_grad, ff_sum = tied(proj_grad, ff_sum)
     keep_a, send_a = weight_gradient(places, chunks, proj_grad, normed_one, 2 * local_dim, 0, own_dims)
     proj_grad, other_u, send_a = tied(proj_grad, other_u, send_a)
     keep_a, came_a = late_sent(keep_a, send_a)
@@ -901,6 +900,8 @@
     late_b = late_far(near_b, bf16)
     late_own = jnp.concatenate([late_a, late_b[:, :local_dim]], axis=1)
 
+    late_b, ff_sum = tied(late_b, ff_sum)
+    ff_own = ff_sum.astype(f32)
     vectors = late_b[:, 256:]
     norm_grads = summed_over(vectors, "tensor")[:, :4].T
     fc_count = ff // own_dims

time: 250 us -> 241 us (0.964); the launches traced: 249 us -> 236 us
  waiting for transfers between devices: 54.2 us -> 41 us
    ppermute x3, waiting for transfers between devices: 20.5 us -> 9.68 us  [ring_gather(): from_left = lax.ppermute(from_left, axis, ahead)]
    reduce_scatter x1, waiting for transfers between devices: 7.72 us -> 0.02 us  [body(): ff_sum = lax.psum_scatter(ff_grads, 'dp', scatter_dimension=0, tiled=True)]
    ppermute x3, starting transfers between devices: 6.59 us -> 2.42 us  [ring_gather(): from_left = lax.ppermute(from_left, axis, ahead)]
    ppermute x2, starting transfers between devices: 5.37 us -> 8.57 us  [passed_along(): return lax.ppermute(block, axis, route)]
    ppermute x3, starting transfers between devices: 0.54 us -> 3.71 us  [ring_gather(): from_right = lax.ppermute(from_right, axis, behind)]
    ppermute x1, waiting for transfers between devices: 3.81 us -> 6.88 us  [ring_gather(): pieces.append(lax.ppermute(from_left, axis, ahead))]
    ppermute x1, starting transfers between devices: 4.32 us -> 1.67 us  [ring_gather(): pieces.append(lax.ppermute(from_left, axis, ahead))]
    ppermute x24, starting transfers between devices: 31.1 us -> 33.6 us  [swapped(): return lax.ppermute(block, axis, route)]
  transfers between devices with their start and end apart: 35 -> 35, of which waited for: 14 -> 15; matrix products, arithmetic and copies ran while one was open for 6% -> 8% of each run, Pallas kernels for 37% -> 40%
where the time goes in v4:
time: 241 us; the launch traced here: 236 us
  Pallas kernels  106 us (44%)
  starting transfers between devices  50.1 us (21%)
  waiting for transfers between devices  41 us (17%)
  local copies, waits for them, and re-layouts  17.1 us (7%)
  between operations  14.6 us (6%)
  other arithmetic  7.9 us (3%)
    ppermute x24, starting transfers between devices, swapped(): return lax.ppermute(block, axis, route)  33.6 us
    pallas_call x1, Pallas kernels, feed_forward(): pl.pallas_call(ff_kernel, grid_spec=pltpu.PrefetchScalarGridSpec(num_scal...  22.5 us
    pallas_call x1, Pallas kernels, backward_own(): pl.pallas_call(functools.partial(own_bwd_kernel, heads, halo), grid_spec=...  17 us
    ppermute x24, waiting for transfers between devices, swapped(): return lax.ppermute(block, axis, route)  15.7 us
    pallas_call x1, Pallas kernels, attention_forward(): pl.pallas_call(functools.partial(attn_fwd_kernel, heads, halo), grid_spec...  14.1 us
    pallas_call x2, Pallas kernels, weight_gradient(): pl.pallas_call(functools.partial(weight_grad_kernel, own_dims), grid_spec...  12.7 us
    pallas_call x1, Pallas kernels, input_gradient(): pl.pallas_call(functools.partial(input_grad_kernel, halo), grid_spec=pltp...  11.2 us
    pallas_call x1, Pallas kernels, project(): pl.pallas_call(functools.partial(project_kernel, len(pieces), first), gri...  10.9 us
  transfers between devices with their start and end apart: 35, of which 15 were waited for; matrix products, arithmetic and copies ran while one was open for 8% of the time, Pallas kernels for 40%

profile of v4, /device:TPU:0, one launch (start us, length us, event | category | flops | bytes accessed | tf_op | source)
XLA Modules:
  0.0 236.4 jit_solution(14488153117009988861)
XLA Ops:
  7.3 1.8 pad_maximum_fusion
  9.2 3.0 %collective-permute-start.6 = (bf16[512,768]{1,0:T(8,128)(2,1)}, bf16[512,768]{1,0:T(8,128)(2,1)}, u32[]{:S(2)}, u32[]{:S(2)}) collective-permute-start(bf16[512,768]{1,0:T(8,128)(2,1)} %x_ref.1), channel_id=1, source_target_pairs={{0,2},{1,3},{2,0},{3,1},{4,6},{5,7},{6,4},{7,5},{8,10},{9,11},{10,... | collective-permute-start | bytes 2359304 | tf_op jit(solution)/shard_map/ppermute | solution.py:49
  13.1 0.9 copy.56
  14.0 1.1 copy.55
  15.3 1.5 collective-permute-start.1
  17.4 3.8 %collective-permute-done.1.refs_6_ = bf16[96,896]{1,0:T(8,128)(2,1)S(1)} collective-permute-done((bf16[96,896]{1,0:T(8,128)(2,1)S(1)}, bf16[96,896]{1,0:T(8,128)(2,1)S(1)}, u32[]{:S(2)}, u32[]{:S(2)}) %collective-permute-start.1) | collective-permute-done | bytes 172064 | tf_op jit(solution)/shard_map/ppermute | solution.py:77
  21.2 1.3 collective-permute-done.refs_5_
  23.1 1.5 collective-permute-start.3
  25.1 0.9 reshape.74.b_ref
  26.0 4.8 %collective-permute-done.2.refs_7_ = bf16[96,896]{1,0:T(8,128)(2,1)} collective-permute-done((bf16[96,896]{1,0:T(8,128)(2,1)}, bf16[96,896]{1,0:T(8,128)(2,1)}, u32[]{:S(2)}, u32[]{:S(2)}) %collective-permute-start.2) | collective-permute-done | bytes 172064 | tf_op jit(solution)/shard_map/ppermute | solution.py:76
  30.8 2.4 %collective-permute-done.3.refs_8_ = bf16[96,896]{1,0:T(8,128)(2,1)} collective-permute-done((bf16[96,896]{1,0:T(8,128)(2,1)S(1)}, bf16[96,896]{1,0:T(8,128)(2,1)}, u32[]{:S(2)}, u32[]{:S(2)}) %collective-permute-start.3) | collective-permute-done | bytes 172064 | tf_op jit(solution)/shard_map/ppermute | solution.py:77
  33.2 1.4 collective-permute-start.4
  35.2 3.6 %collective-permute-done.4.refs_9_ = bf16[96,896]{1,0:T(8,128)(2,1)S(1)} collective-permute-done((bf16[96,896]{1,0:T(8,128)(2,1)}, bf16[96,896]{1,0:T(8,128)(2,1)S(1)}, u32[]{:S(2)}, u32[]{:S(2)}) %collective-permute-start.4) | collective-permute-done | bytes 172064 | tf_op jit(solution)/shard_map/ppermute | solution.py:76
  38.8 2.5 %collective-permute-done.5.refs_10_ = bf16[96,896]{1,0:T(8,128)(2,1)S(1)} collective-permute-done((bf16[96,896]{1,0:T(8,128)(2,1)}, bf16[96,896]{1,0:T(8,128)(2,1)S(1)}, u32[]{:S(2)}, u32[]{:S(2)}) %collective-permute-start.5) | collective-permute-done | bytes 172064 | tf_op jit(solution)/shard_map/ppermute | solution.py:77
  41.3 1.0 multiply_sine_fusion
  42.3 1.7 collective-permute-start.9
  44.0 1.2 dynamic-slice_bitcast_fusion.start_ref
  45.8 6.9 %collective-permute-done.9.refs_11_ = bf16[96,896]{1,0:T(8,128)(2,1)S(1)} collective-permute-done((bf16[96,896]{1,0:T(8,128)(2,1)S(1)}, bf16[96,896]{1,0:T(8,128)(2,1)S(1)}, u32[]{:S(2)}, u32[]{:S(2)}) %collective-permute-start.9) | collective-permute-done | bytes 172064 | tf_op jit(solution)/shard_map/ppermute | solution.py:83
  53.6 10.9 %project.1 = (bf16[192,2048]{1,0:T(8,128)(2,1)}, bf16[192,2048]{1,0:T(8,128)(2,1)}, bf16[192,2048]{1,0:T(8,128)(2,1)}, bf16[384,768]{1,0:T(8,128)(2,1)}, bf16[20...) custom-call(s32[8]{0:T(128)} %dynamic-slice_bitcast_fusion.start_ref, ...), custom_call_target="tpu_custom_call" | custom-call | flops 113246208 | bytes 737280 | tf_op jit(solution)/shard_map/project/pallas_call | solution.py:263
  64.6 7.1 %collective-permute-start.13 = (bf16[384,768]{1,0:T(8,128)(2,1)}, bf16[384,768]{1,0:T(8,128)(2,1)S(1)}, u32[]{:S(2)}, u32[]{:S(2)}) collective-permute-start(bf16[384,768]{1,0:T(8,128)(2,1)} %get-tuple-element.96), channel_id=1, source_target_pairs={{0,4},{4,8},{8,12},{12,16},{16,20},{20,24},{24,28},{1,5},{5,9},{9,... | collective-permute-start | bytes 1769480 | tf_op jit(solution)/shard_map/ppermute | solution.py:44
  73.9 22.5 %feed_forward.1 = (bf16[2048,768]{1,0:T(8,128)(2,1)}, bf16[2048,768]{1,0:T(8,128)(2,1)}, bf16[2048,768]{1,0:T(8,128)(2,1)}, bf16[768,1536]{1,0:T(8,128)(2,1)}, f32[8,768]{1,0:T(8,128)}) custom-call(bf16[2048,768]{1,0:T(8,128)(2,1)} %get-tuple-element.87.x_ref, f32[2048,128]{1,0:T(8,128)} %get-tuple-element.88.stats_ref, f32[1,768]{1,0:T(1,128)} %reshape.73.b_ref, ...), custom_call_target="tpu_custom_call" | custom-call | flops 905969664 | bytes 1081344 | tf_op jit(solution)/shard_map/feed_forward/pallas_call | solution.py:179
  97.8 14.1 %attention_forward.1 = (bf16[192,2048]{1,0:T(8,128)(2,1)}, f32[8,2048]{1,0:T(8,128)}) custom-call(s32[8]{0:T(128)} %and_select_fusion.first_ref, bf16[192,2048]{1,0:T(8,128)(2,1)} %get-tuple-element.93.q_ref, bf16[192,2048]{1,0:T(8,128)(2,1)} %get-tuple-element.94.k_ref, bf16[192,2048]{1,0:T(8,128)(2,1)} %get-tuple-element.95.v_ref, ...), custom_call_target="tpu_custom_call" | custom-call | flops 402653184 | bytes 196608 | tf_op jit(solution)/shard_map/attention_forward/pallas_call | solution.py:357
  111.9 9.5 %branch_out.1 = (bf16[1024,768]{1,0:T(8,128)(2,1)}, bf16[1024,768]{1,0:T(8,128)(2,1)}, bf16[384,192]{1,0:T(8,128)(2,1)}, bf16[384,192]{1,0:T(8,128)(2,1)}, bf16[192,2048]{1,0:T(8,128)(2,1)}) custom-call(s32[4]{0:T(128)} %pad_add_fusion.place_ref, s32[8]{0:T(128)} %concatenate.13.chunk_ref, bf16[192,2048]{1,0:T(8,128)(2,1)} %get-tuple-element.97.o_ref, ...), custom_call_target="tpu_custom_call" | custom-call | flops 75497472 | bytes 589824 | tf_op jit(solution)/shard_map/branch_out/pallas_call | solution.py:577
  121.6 7.8 %collective-permute-start.15 = (bf16[384,192]{1,0:T(8,128)(2,1)}, bf16[384,192]{1,0:T(8,128)(2,1)S(1)}, u32[]{:S(2)}, u32[]{:S(2)}) collective-permute-start(bf16[384,192]{1,0:T(8,128)(2,1)} %get-tuple-element.108), channel_id=1, source_target_pairs={{0,4},{4,0},{8,12},{12,8},{16,20},{20,16},{24,28},{28,24},{1,5},{5... | collective-permute-start | bytes 442376 | tf_op jit(solution)/shard_map/ppermute | solution.py:49
  129.4 4.4 %attention_backward_left.1 = (f32[192,768]{1,0:T(8,128)}, bf16[384,768]{1,0:T(8,128)(2,1)}) custom-call(s32[8]{0:T(128)} %and_select_fusion.first_ref, bf16[192,2048]{1,0:T(8,128)(2,1)} %get-tuple-element.93.q_ref, bf16[384,768]{1,0:T(8,128)(2,1)} %copy-done.4, s32[1,2048]{1,0:T(1,128)} %bitcast.40, bf16[192,2048]{1,0:T(8,128)(2,1)} %get-tuple-element.97.o_ref, ...), custom_call_target="tpu_custom_call" | custom-call | flops 188743680 | bytes 184320 | tf_op jit(solution)/shard_map/attention_backward_left/pallas_call | solution.py:468
  133.8 3.3 %collective-permute-done.15 = bf16[384,192]{1,0:T(8,128)(2,1)S(1)} collective-permute-done((bf16[384,192]{1,0:T(8,128)(2,1)}, bf16[384,192]{1,0:T(8,128)(2,1)S(1)}, u32[]{:S(2)}, u32[]{:S(2)}) %collective-permute-start.15) | collective-permute-done | bytes 147488 | tf_op jit(solution)/shard_map/ppermute | solution.py:49
  137.4 1.9 collective-permute-start.17
  139.3 1.5 collective-permute-start.16
  140.9 4.3 %collective-permute-start.18 = (bf16[96,192]{1,0:T(8,128)(2,1)S(1)}, bf16[96,192]{1,0:T(8,128)(2,1)S(1)}, u32[]{:S(2)}, u32[]{:S(2)}) collective-permute-start(bf16[96,192]{1,0:T(8,128)(2,1)S(1)} %get-tuple-element.202), channel_id=1, source_target_pairs={{0,8},{4,12},{8,0},{12,4},{16,24},{20,28},{24,16},{28,20},{1,9},{5... | collective-permute-start | bytes 110600 | tf_op jit(solution)/shard_map/ppermute | solution.py:49
  145.2 3.1 %collective-permute-start.20 = (bf16[96,192]{1,0:T(8,128)(2,1)S(1)}, bf16[96,192]{1,0:T(8,128)(2,1)S(1)}, u32[]{:S(2)}, u32[]{:S(2)}) collective-permute-start(bf16[96,192]{1,0:T(8,128)(2,1)S(1)} %get-tuple-element.203), channel_id=1, source_target_pairs={{0,24},{4,28},{8,16},{12,20},{16,8},{20,12},{24,0},{28,4},{1,25},{... | collective-permute-start | bytes 110600 | tf_op jit(solution)/shard_map/ppermute | solution.py:49
  148.3 17.0 %attention_backward_own.1 = (f32[192,2048]{1,0:T(8,128)}, f32[192,2048]{1,0:T(8,128)}, f32[192,2048]{1,0:T(8,128)}) custom-call(s32[8]{0:T(128)} %and_select_fusion.first_ref, bf16[192,2048]{1,0:T(8,128)(2,1)} %get-tuple-element.93.q_ref, bf16[192,2048]{1,0:T(8,128)(2,1)} %get-tuple-element.94.k_ref, bf16[192,2048]{1,0:T(8,128)(2,1)} %get-tuple-element.95.v_ref, ...), custom_call_target="tpu_custom_call" | custom-call | flops 1006632960 | bytes 491520 | tf_op jit(solution)/shard_map/attention_backward_own/pallas_call | solution.py:498
  166.3 11.2 %input_gradient.1 = (bf16[1024,768]{1,0:T(8,128)(2,1)}, bf16[1024,768]{1,0:T(8,128)(2,1)}, bf16[576,2048]{1,0:T(8,128)(2,1)}, f32[8,768]{1,0:T(8,128)}, f32[576,1]{1,0:T(8,128)}) custom-call(s32[4]{0:T(128)} %pad_add_fusion.place_ref, f32[192,2048]{1,0:T(8,128)} %get-tuple-element.115.dq_ref, f32[192,2048]{1,0:T(8,128)} %get-tuple-element.116.dk_ref, ...), custom_call_target="tpu_custom_call" | custom-call | flops 226492416 | bytes 983040 | tf_op jit(solution)/shard_map/input_gradient/pallas_call | solution.py:650
  179.2 2.0 collective-permute-done.21.came_ref
  181.2 1.9 add_convert_fusion
  183.2 6.7 %weight_gradient.2 = (bf16[384,384]{1,0:T(8,128)(2,1)}, bf16[384,384]{1,0:T(8,128)(2,1)}) custom-call(s32[4]{0:T(128)} %pad_add_fusion.place_ref, s32[8]{0:T(128)} %concatenate.13.chunk_ref, bf16[576,2048]{1,0:T(8,128)(2,1)} %get-tuple-element.128.grad_ref, bf16[2048,768]{1,0:T(8,128)(2,1)} %get-tuple-element.125.normed_ref), custom_call_target="tpu_custom_call" | custom-call | flops 150994944 | bytes 393216 | tf_op jit(solution)/shard_map/weight_gradient/pallas_call | solution.py:710
  189.8 1.9 collective-permute-start.22
  191.7 1.4 add_convert_fusion.1
  193.1 1.0 collective-permute-start.26
  194.0 6.0 %weight_gradient.3 = (bf16[384,384]{1,0:T(8,128)(2,1)}, bf16[384,384]{1,0:T(8,128)(2,1)}) custom-call(s32[4]{0:T(128)} %pad_add_fusion.place_ref, s32[8]{0:T(128)} %concatenate.13.chunk_ref, bf16[576,2048]{1,0:T(8,128)(2,1)} %get-tuple-element.128.grad_ref, bf16[2048,768]{1,0:T(8,128)(2,1)} %get-tuple-element.125.normed_ref, ...), custom_call_target="tpu_custom_call" | custom-call | flops 75497472 | bytes 393216 | tf_op jit(solution)/shard_map/weight_gradient/pallas_call | solution.py:710
  201.8 3.1 %collective-permute-start.25 = (bf16[96,384]{1,0:T(8,128)(2,1)S(1)}, bf16[96,384]{1,0:T(8,128)(2,1)S(1)}, u32[]{:S(2)}, u32[]{:S(2)}) collective-permute-start(bf16[96,384]{1,0:T(8,128)(2,1)S(1)} %get-tuple-element.200), channel_id=1, source_target_pairs={{0,24},{4,28},{8,16},{12,20},{16,8},{20,12},{24,0},{28,4},{1,25},{... | collective-permute-start | bytes 221192 | tf_op jit(solution)/shard_map/ppermute | solution.py:49
  204.9 3.9 %collective-permute-done.27 = bf16[384,384]{1,0:T(8,128)(2,1)S(1)} collective-permute-done((bf16[384,384]{1,0:T(8,128)(2,1)}, bf16[384,384]{1,0:T(8,128)(2,1)S(1)}, u32[]{:S(2)}, u32[]{:S(2)}) %collective-permute-start.27) | collective-permute-done | bytes 294944 | tf_op jit(solution)/shard_map/ppermute | solution.py:49
  209.7 3.0 %collective-permute-start.30 = (bf16[96,384]{1,0:T(8,128)(2,1)S(1)}, bf16[96,384]{1,0:T(8,128)(2,1)S(1)}, u32[]{:S(2)}, u32[]{:S(2)}) collective-permute-start(bf16[96,384]{1,0:T(8,128)(2,1)S(1)} %get-tuple-element.197), channel_id=1, source_target_pairs={{0,24},{4,28},{8,16},{12,20},{16,8},{20,12},{24,0},{28,4},{1,25},{... | collective-permute-start | bytes 221192 | tf_op jit(solution)/shard_map/ppermute | solution.py:49
  212.8 1.4 collective-permute-done.28
  214.2 1.8 collective-permute-done.30
  216.0 2.3 collective-permute-done.29
  219.7 1.1 collective-permute-start.32
  224.7 0.9 copy.63
  225.6 3.4 %norm_back.1 = bf16[512,768]{1,0:T(8,128)(2,1)} custom-call(bf16[1024,768]{1,0:T(8,128)(2,1)} %get-tuple-element.120.own_ref, bf16[1024,768]{1,0:T(8,128)(2,1)} %copy-done.2, bf16[512,768]{1,0:T(8,128)(2,1)} %copy-done.10, bf16[512,768]{1,0:T(8,128)(2,1)} %x_ref.1, f32[2048,128]{1,0:T(8,128)} %get-tuple-element.88.stats_ref, bf16[512,768]{1,0:T(8,128)(2,1)} %g_ref.1), custom_call_target="tpu_custom_call" | custom-call | flops 491520 | bytes 294912 | tf_op jit(solution)/shard_map/norm_back/pallas_call | solution.py:743
  (150 shorter events, 20.1 us)
Async XLA Ops:
  7.2 31.6 %copy-start = (bf16[512,768]{1,0:T(8,128)(2,1)S(1)}, bf16[512,768]{1,0:T(8,128)(2,1)}, u32[]{:S(2)}) copy-start(bf16[512,768]{1,0:T(8,128)(2,1)} %x_ref.1) | copy-start | bytes 2359300
  7.2 17.4 %copy-start.3 = (bf16[512,768]{1,0:T(8,128)(2,1)S(1)}, bf16[512,768]{1,0:T(8,128)(2,1)}, u32[]{:S(2)}) copy-start(bf16[512,768]{1,0:T(8,128)(2,1)} %g_ref.1) | copy-start | bytes 2359300
  7.2 17.9 %copy-start.28 = (bf16[3,192]{1,0:T(4,128)(2,1)S(1)}, bf16[3,192]{1,0:T(4,128)(2,1)}, u32[]{:S(2)}) copy-start(bf16[3,192]{1,0:T(4,128)(2,1)} %param.19) | copy-start | bytes 3460
  7.2 28.0 %copy-start.27 = (s32[2048]{0:T(1024)S(1)}, s32[2048]{0:T(1024)}, u32[]{:S(2)}) copy-start(s32[2048]{0:T(1024)} %param.30) | copy-start | bytes 24580
  7.2 65.8 %all-gather.2.cloned.1.call-start = ((), (), s32[]{:S(2)}) async-start(), calls=%async_computation.1 | async-start | bytes 2654208 | tf_op jit(solution)/shard_map/all_gather | solution.py:839
  9.1 174.0 %reduce-scatter.2.cloned.1.call-start = ((), (), s32[]{:S(2)}) async-start(), calls=%async_computation.2 | async-start | bytes 2654208 | tf_op jit(solution)/shard_map/reduce_scatter | solution.py:865
  9.2 32.1 %collective-permute-start.6 = (bf16[512,768]{1,0:T(8,128)(2,1)}, bf16[512,768]{1,0:T(8,128)(2,1)}, u32[]{:S(2)}, u32[]{:S(2)}) collective-permute-start(bf16[512,768]{1,0:T(8,128)(2,1)} %x_ref.1), channel_id=1, source_target_pairs={{0,2},{1,3},{2,0},{3,1},{4,6},{5,7},{6,4},{7,5},{8,10},{9,11},{10,... | collective-permute-start | bytes 2359304 | tf_op jit(solution)/shard_map/ppermute | solution.py:49
  15.3 37.4 %copy-start.17 = (bf16[96,896]{1,0:T(8,128)(2,1)}, bf16[96,896]{1,0:T(8,128)(2,1)S(1)}, u32[]{:S(2)}) copy-start(bf16[96,896]{1,0:T(8,128)(2,1)S(1)} %fusion.1.refs_4_) | copy-start | bytes 516100
  15.3 5.9 %collective-permute-start.1 = (bf16[96,896]{1,0:T(8,128)(2,1)S(1)}, bf16[96,896]{1,0:T(8,128)(2,1)S(1)}, u32[]{:S(2)}, u32[]{:S(2)}) collective-permute-start(bf16[96,896]{1,0:T(8,128)(2,1)S(1)} %fusion.1.refs_4_), channel_id=1, source_target_pairs={{8,0},{16,8},{24,16},{28,24},{20,28},{12,20},{4,12},{0,4},{9,1},{1... | collective-permute-start | bytes 516104 | tf_op jit(solution)/shard_map/ppermute | solution.py:77
  16.9 5.7 %collective-permute-start = (bf16[96,896]{1,0:T(8,128)(2,1)S(1)}, bf16[96,896]{1,0:T(8,128)(2,1)}, u32[]{:S(2)}, u32[]{:S(2)}) collective-permute-start(bf16[96,896]{1,0:T(8,128)(2,1)S(1)} %fusion.1.refs_4_), channel_id=1, source_target_pairs={{0,8},{8,16},{16,24},{24,28},{28,20},{20,12},{12,4},{4,0},{1,9},{9... | collective-permute-start | bytes 516104 | tf_op jit(solution)/shard_map/ppermute | solution.py:76
  21.2 31.5 %copy-start.22 = (bf16[96,896]{1,0:T(8,128)(2,1)}, bf16[96,896]{1,0:T(8,128)(2,1)S(1)}, u32[]{:S(2)}) copy-start(bf16[96,896]{1,0:T(8,128)(2,1)S(1)} %collective-permute-done.1.refs_6_) | copy-start | bytes 516100
  22.5 8.3 %collective-permute-start.2 = (bf16[96,896]{1,0:T(8,128)(2,1)}, bf16[96,896]{1,0:T(8,128)(2,1)}, u32[]{:S(2)}, u32[]{:S(2)}) collective-permute-start(bf16[96,896]{1,0:T(8,128)(2,1)} %collective-permute-done.refs_5_), channel_id=1, source_target_pairs={{0,8},{8,16},{16,24},{24,28},{28,20},{20,12},{12,4},{4,0},{1,9},{9... | collective-permute-start | bytes 516104 | tf_op jit(solution)/shard_map/ppermute | solution.py:76
  23.1 10.1 %collective-permute-start.3 = (bf16[96,896]{1,0:T(8,128)(2,1)S(1)}, bf16[96,896]{1,0:T(8,128)(2,1)}, u32[]{:S(2)}, u32[]{:S(2)}) collective-permute-start(bf16[96,896]{1,0:T(8,128)(2,1)S(1)} %collective-permute-done.1.refs_6_), channel_id=1, source_target_pairs={{8,0},{16,8},{24,16},{28,24},{20,28},{12,20},{4,12},{0,4},{9,1},{1... | collective-permute-start | bytes 516104 | tf_op jit(solution)/shard_map/ppermute | solution.py:77
  24.6 48.5 %collective-permute-start.11 = (bf16[512,768]{1,0:T(8,128)(2,1)S(1)}, bf16[512,768]{1,0:T(8,128)(2,1)S(1)}, u32[]{:S(2)}, u32[]{:S(2)}) collective-permute-start(bf16[512,768]{1,0:T(8,128)(2,1)S(1)} %copy-done.3), channel_id=1, source_target_pairs={{0,1},{1,0},{2,3},{3,2},{4,5},{5,4},{6,7},{7,6},{8,9},{9,8},{10,11... | collective-permute-start | bytes 2359304 | tf_op jit(solution)/shard_map/ppermute | solution.py:49
  24.6 39.9 %collective-permute-start.10 = (bf16[512,768]{1,0:T(8,128)(2,1)S(1)}, bf16[512,768]{1,0:T(8,128)(2,1)S(1)}, u32[]{:S(2)}, u32[]{:S(2)}) collective-permute-start(bf16[512,768]{1,0:T(8,128)(2,1)S(1)} %copy-done.3), channel_id=1, source_target_pairs={{0,2},{1,3},{2,0},{3,1},{4,6},{5,7},{6,4},{7,5},{8,10},{9,11},{10,... | collective-permute-start | bytes 2359304 | tf_op jit(solution)/shard_map/ppermute | solution.py:49
  33.2 5.6 %collective-permute-start.4 = (bf16[96,896]{1,0:T(8,128)(2,1)}, bf16[96,896]{1,0:T(8,128)(2,1)S(1)}, u32[]{:S(2)}, u32[]{:S(2)}) collective-permute-start(bf16[96,896]{1,0:T(8,128)(2,1)} %collective-permute-done.2.refs_7_), channel_id=1, source_target_pairs={{0,8},{8,16},{16,24},{24,28},{28,20},{20,12},{12,4},{4,0},{1,9},{9... | collective-permute-start | bytes 516104 | tf_op jit(solution)/shard_map/ppermute | solution.py:76
  34.6 6.8 %collective-permute-start.5 = (bf16[96,896]{1,0:T(8,128)(2,1)}, bf16[96,896]{1,0:T(8,128)(2,1)S(1)}, u32[]{:S(2)}, u32[]{:S(2)}) collective-permute-start(bf16[96,896]{1,0:T(8,128)(2,1)} %collective-permute-done.3.refs_8_), channel_id=1, source_target_pairs={{8,0},{16,8},{24,16},{28,24},{20,28},{12,20},{4,12},{0,4},{9,1},{1... | collective-permute-start | bytes 516104 | tf_op jit(solution)/shard_map/ppermute | solution.py:77
  35.2 37.7 %copy-start.26 = (s32[2048]{0:T(1024)}, s32[2048]{0:T(1024)S(1)}, u32[]{:S(2)}) copy-start(s32[2048]{0:T(1024)S(1)} %get-tuple-element.208) | copy-start | bytes 24580
  38.8 13.9 %copy-start.23 = (bf16[96,896]{1,0:T(8,128)(2,1)}, bf16[96,896]{1,0:T(8,128)(2,1)S(1)}, u32[]{:S(2)}) copy-start(bf16[96,896]{1,0:T(8,128)(2,1)S(1)} %collective-permute-done.4.refs_9_) | copy-start | bytes 516100
  38.8 6.9 %collective-permute-start.7 = (bf16[512,768]{1,0:T(8,128)(2,1)S(1)}, bf16[512,768]{1,0:T(8,128)(2,1)S(1)}, u32[]{:S(2)}, u32[]{:S(2)}) collective-permute-start(bf16[512,768]{1,0:T(8,128)(2,1)S(1)} %copy-done), channel_id=1, source_target_pairs={{0,1},{1,0},{2,3},{3,2},{4,5},{5,4},{6,7},{7,6},{8,9},{9,8},{10,11... | collective-permute-start | bytes 2359304 | tf_op jit(solution)/shard_map/ppermute | solution.py:49
  41.3 11.4 %copy-start.24 = (bf16[96,896]{1,0:T(8,128)(2,1)}, bf16[96,896]{1,0:T(8,128)(2,1)S(1)}, u32[]{:S(2)}) copy-start(bf16[96,896]{1,0:T(8,128)(2,1)S(1)} %collective-permute-done.5.refs_10_) | copy-start | bytes 516100
  41.3 11.4 %collective-permute-start.8 = (bf16[512,768]{1,0:T(8,128)(2,1)}, bf16[512,768]{1,0:T(8,128)(2,1)S(1)}, u32[]{:S(2)}, u32[]{:S(2)}) collective-permute-start(bf16[512,768]{1,0:T(8,128)(2,1)} %collective-permute-done.6.refs_1_), channel_id=1, source_target_pairs={{0,1},{1,0},{2,3},{3,2},{4,5},{5,4},{6,7},{7,6},{8,9},{9,8},{10,11... | collective-permute-start | bytes 2359304 | tf_op jit(solution)/shard_map/ppermute | solution.py:49
  42.3 10.4 %collective-permute-start.9 = (bf16[96,896]{1,0:T(8,128)(2,1)S(1)}, bf16[96,896]{1,0:T(8,128)(2,1)S(1)}, u32[]{:S(2)}, u32[]{:S(2)}) collective-permute-start(bf16[96,896]{1,0:T(8,128)(2,1)S(1)} %collective-permute-done.4.refs_9_), channel_id=1, source_target_pairs={{0,8},{8,16},{16,24},{24,28},{28,20},{20,12},{12,4},{4,0},{1,9},{9... | collective-permute-start | bytes 516104 | tf_op jit(solution)/shard_map/ppermute | solution.py:83
  53.6 18.8 %copy-start.29 = (bf16[768]{0:T(1024)(128)(2,1)S(1)}, bf16[768]{0:T(1024)(128)(2,1)}, u32[]{:S(2)}) copy-start(bf16[768]{0:T(1024)(128)(2,1)} %param.23) | copy-start | bytes 4612
  64.5 8.5 %collective-permute-start.12 = (bf16[512,768]{1,0:T(8,128)(2,1)S(1)}, bf16[512,768]{1,0:T(8,128)(2,1)}, u32[]{:S(2)}, u32[]{:S(2)}) collective-permute-start(bf16[512,768]{1,0:T(8,128)(2,1)S(1)} %collective-permute-done.10.refs_1_), channel_id=1, source_target_pairs={{0,1},{1,0},{2,3},{3,2},{4,5},{5,4},{6,7},{7,6},{8,9},{9,8},{10,11... | collective-permute-start | bytes 2359304 | tf_op jit(solution)/shard_map/ppermute | solution.py:49
  64.6 32.4 %collective-permute-start.13 = (bf16[384,768]{1,0:T(8,128)(2,1)}, bf16[384,768]{1,0:T(8,128)(2,1)S(1)}, u32[]{:S(2)}, u32[]{:S(2)}) collective-permute-start(bf16[384,768]{1,0:T(8,128)(2,1)} %get-tuple-element.96), channel_id=1, source_target_pairs={{0,4},{4,8},{8,12},{12,16},{16,20},{20,24},{24,28},{1,5},{5,9},{9,... | collective-permute-start | bytes 1769480 | tf_op jit(solution)/shard_map/ppermute | solution.py:44
  121.4 15.8 %copy-start.21 = (bf16[384,192]{1,0:T(8,128)(2,1)S(1)}, bf16[384,192]{1,0:T(8,128)(2,1)}, u32[]{:S(2)}) copy-start(bf16[384,192]{1,0:T(8,128)(2,1)} %get-tuple-element.107) | copy-start | bytes 442372
  121.4 15.8 %collective-permute-start.14 = (bf16[1024,768]{1,0:T(8,128)(2,1)}, bf16[1024,768]{1,0:T(8,128)(2,1)S(1)}, u32[]{:S(2)}, u32[]{:S(2)}) collective-permute-start(bf16[1024,768]{1,0:T(8,128)(2,1)} %get-tuple-element.102), channel_id=1, source_target_pairs={{0,1},{1,0},{2,3},{3,2},{4,5},{5,4},{6,7},{7,6},{8,9},{9,8},{10,11... | collective-permute-start | bytes 4718600 | tf_op jit(solution)/shard_map/ppermute | solution.py:49
  121.6 15.5 %collective-permute-start.15 = (bf16[384,192]{1,0:T(8,128)(2,1)}, bf16[384,192]{1,0:T(8,128)(2,1)S(1)}, u32[]{:S(2)}, u32[]{:S(2)}) collective-permute-start(bf16[384,192]{1,0:T(8,128)(2,1)} %get-tuple-element.108), channel_id=1, source_target_pairs={{0,4},{4,0},{8,12},{12,8},{16,20},{20,16},{24,28},{28,24},{1,5},{5... | collective-permute-start | bytes 442376 | tf_op jit(solution)/shard_map/ppermute | solution.py:49
  137.4 28.1 %collective-permute-start.17 = (bf16[512,768]{1,0:T(8,128)(2,1)S(1)}, bf16[512,768]{1,0:T(8,128)(2,1)S(1)}, u32[]{:S(2)}, u32[]{:S(2)}) collective-permute-start(bf16[512,768]{1,0:T(8,128)(2,1)S(1)} %add_convert_fusion.2), channel_id=1, source_target_pairs={{0,2},{1,3},{2,0},{3,1},{4,6},{5,7},{6,4},{7,5},{8,10},{9,11},{10,... | collective-permute-start | bytes 2359304 | tf_op jit(solution)/shard_map/ppermute | solution.py:49
  139.3 26.1 %collective-permute-start.16 = (bf16[384,768]{1,0:T(8,128)(2,1)S(1)}, bf16[384,768]{1,0:T(8,128)(2,1)S(1)}, u32[]{:S(2)}, u32[]{:S(2)}) collective-permute-start(bf16[384,768]{1,0:T(8,128)(2,1)S(1)} %copy-done.31), channel_id=1, source_target_pairs={{4,0},{8,4},{12,8},{16,12},{20,16},{24,20},{28,24},{5,1},{9,5},{13... | collective-permute-start | bytes 1769480 | tf_op jit(solution)/shard_map/ppermute | solution.py:44
  140.9 24.5 %collective-permute-start.18 = (bf16[96,192]{1,0:T(8,128)(2,1)S(1)}, bf16[96,192]{1,0:T(8,128)(2,1)S(1)}, u32[]{:S(2)}, u32[]{:S(2)}) collective-permute-start(bf16[96,192]{1,0:T(8,128)(2,1)S(1)} %get-tuple-element.202), channel_id=1, source_target_pairs={{0,8},{4,12},{8,0},{12,4},{16,24},{20,28},{24,16},{28,20},{1,9},{5... | collective-permute-start | bytes 110600 | tf_op jit(solution)/shard_map/ppermute | solution.py:49
  145.2 20.2 %collective-permute-start.20 = (bf16[96,192]{1,0:T(8,128)(2,1)S(1)}, bf16[96,192]{1,0:T(8,128)(2,1)S(1)}, u32[]{:S(2)}, u32[]{:S(2)}) collective-permute-start(bf16[96,192]{1,0:T(8,128)(2,1)S(1)} %get-tuple-element.203), channel_id=1, source_target_pairs={{0,24},{4,28},{8,16},{12,20},{16,8},{20,12},{24,0},{28,4},{1,25},{... | collective-permute-start | bytes 110600 | tf_op jit(solution)/shard_map/ppermute | solution.py:49
  148.3 17.1 %collective-permute-start.19 = (bf16[96,192]{1,0:T(8,128)(2,1)S(1)}, bf16[96,192]{1,0:T(8,128)(2,1)S(1)}, u32[]{:S(2)}, u32[]{:S(2)}) collective-permute-start(bf16[96,192]{1,0:T(8,128)(2,1)S(1)} %get-tuple-element.204), channel_id=1, source_target_pairs={{0,16},{4,20},{8,24},{12,28},{16,0},{20,4},{24,8},{28,12},{1,17},{... | collective-permute-start | bytes 110600 | tf_op jit(solution)/shard_map/ppermute | solution.py:49
  165.5 12.0 %copy-start.13 = (bf16[512,768]{1,0:T(8,128)(2,1)}, bf16[512,768]{1,0:T(8,128)(2,1)S(1)}, u32[]{:S(2)}) copy-start(bf16[512,768]{1,0:T(8,128)(2,1)S(1)} %collective-permute-done.17) | copy-start | bytes 2359300
  177.5 3.7 %collective-permute-start.21 = (bf16[1024,768]{1,0:T(8,128)(2,1)}, bf16[1024,768]{1,0:T(8,128)(2,1)S(1)}, u32[]{:S(2)}, u32[]{:S(2)}) collective-permute-start(bf16[1024,768]{1,0:T(8,128)(2,1)} %get-tuple-element.121), channel_id=1, source_target_pairs={{0,1},{1,0},{2,3},{3,2},{4,5},{5,4},{6,7},{7,6},{8,9},{9,8},{10,11... | collective-permute-start | bytes 4718600 | tf_op jit(solution)/shard_map/ppermute | solution.py:49
  189.8 10.3 %collective-permute-start.22 = (bf16[384,384]{1,0:T(8,128)(2,1)}, bf16[384,384]{1,0:T(8,128)(2,1)S(1)}, u32[]{:S(2)}, u32[]{:S(2)}) collective-permute-start(bf16[384,384]{1,0:T(8,128)(2,1)} %get-tuple-element.133), channel_id=1, source_target_pairs={{0,4},{4,0},{8,12},{12,8},{16,20},{20,16},{24,28},{28,24},{1,5},{5... | collective-permute-start | bytes 884744 | tf_op jit(solution)/shard_map/ppermute | solution.py:49
  193.1 31.5 %collective-permute-start.26 = (bf16[512,768]{1,0:T(8,128)(2,1)S(1)}, bf16[512,768]{1,0:T(8,128)(2,1)S(1)}, u32[]{:S(2)}, u32[]{:S(2)}) collective-permute-start(bf16[512,768]{1,0:T(8,128)(2,1)S(1)} %add_convert_fusion), channel_id=1, source_target_pairs={{0,2},{1,3},{2,0},{3,1},{4,6},{5,7},{6,4},{7,5},{8,10},{9,11},{10,... | collective-permute-start | bytes 2359304 | tf_op jit(solution)/shard_map/ppermute | solution.py:49
  200.1 8.8 %collective-permute-start.27 = (bf16[384,384]{1,0:T(8,128)(2,1)}, bf16[384,384]{1,0:T(8,128)(2,1)S(1)}, u32[]{:S(2)}, u32[]{:S(2)}) collective-permute-start(bf16[384,384]{1,0:T(8,128)(2,1)} %get-tuple-element.139), channel_id=1, source_target_pairs={{0,4},{4,0},{8,12},{12,8},{16,20},{20,16},{24,28},{28,24},{1,5},{5... | collective-permute-start | bytes 884744 | tf_op jit(solution)/shard_map/ppermute | solution.py:49
  201.1 8.6 %collective-permute-start.23 = (bf16[96,384]{1,0:T(8,128)(2,1)S(1)}, bf16[96,384]{1,0:T(8,128)(2,1)S(1)}, u32[]{:S(2)}, u32[]{:S(2)}) collective-permute-start(bf16[96,384]{1,0:T(8,128)(2,1)S(1)} %get-tuple-element.199), channel_id=1, source_target_pairs={{0,8},{4,12},{8,0},{12,4},{16,24},{20,28},{24,16},{28,20},{1,9},{5... | collective-permute-start | bytes 221192 | tf_op jit(solution)/shard_map/ppermute | solution.py:49
  201.8 10.9 %collective-permute-start.25 = (bf16[96,384]{1,0:T(8,128)(2,1)S(1)}, bf16[96,384]{1,0:T(8,128)(2,1)S(1)}, u32[]{:S(2)}, u32[]{:S(2)}) collective-permute-start(bf16[96,384]{1,0:T(8,128)(2,1)S(1)} %get-tuple-element.200), channel_id=1, source_target_pairs={{0,24},{4,28},{8,16},{12,20},{16,8},{20,12},{24,0},{28,4},{1,25},{... | collective-permute-start | bytes 221192 | tf_op jit(solution)/shard_map/ppermute | solution.py:49
  204.9 7.8 %collective-permute-start.24 = (bf16[96,384]{1,0:T(8,128)(2,1)S(1)}, bf16[96,384]{1,0:T(8,128)(2,1)S(1)}, u32[]{:S(2)}, u32[]{:S(2)}) collective-permute-start(bf16[96,384]{1,0:T(8,128)(2,1)S(1)} %get-tuple-element.201), channel_id=1, source_target_pairs={{0,16},{4,20},{8,24},{12,28},{16,0},{20,4},{24,8},{28,12},{1,17},{... | collective-permute-start | bytes 221192 | tf_op jit(solution)/shard_map/ppermute | solution.py:49
  208.9 9.6 %copy-start.9 = (bf16[96,1536]{1,0:T(8,128)(2,1)S(1)}, bf16[96,1536]{1,0:T(8,128)(2,1)}, u32[]{:S(2)}) copy-start(bf16[96,1536]{1,0:T(8,128)(2,1)} %reduce-scatter.2.cloned.1.call-done) | copy-start | bytes 884740
  209.0 5.2 %collective-permute-start.28 = (bf16[96,384]{1,0:T(8,128)(2,1)S(1)}, bf16[96,384]{1,0:T(8,128)(2,1)S(1)}, u32[]{:S(2)}, u32[]{:S(2)}) collective-permute-start(bf16[96,384]{1,0:T(8,128)(2,1)S(1)} %get-tuple-element.196), channel_id=1, source_target_pairs={{0,8},{4,12},{8,0},{12,4},{16,24},{20,28},{24,16},{28,20},{1,9},{5... | collective-permute-start | bytes 221192 | tf_op jit(solution)/shard_map/ppermute | solution.py:49
  209.7 6.3 %collective-permute-start.30 = (bf16[96,384]{1,0:T(8,128)(2,1)S(1)}, bf16[96,384]{1,0:T(8,128)(2,1)S(1)}, u32[]{:S(2)}, u32[]{:S(2)}) collective-permute-start(bf16[96,384]{1,0:T(8,128)(2,1)S(1)} %get-tuple-element.197), channel_id=1, source_target_pairs={{0,24},{4,28},{8,16},{12,20},{16,8},{20,12},{24,0},{28,4},{1,25},{... | collective-permute-start | bytes 221192 | tf_op jit(solution)/shard_map/ppermute | solution.py:49
  212.7 5.5 %collective-permute-start.29 = (bf16[96,384]{1,0:T(8,128)(2,1)S(1)}, bf16[96,384]{1,0:T(8,128)(2,1)S(1)}, u32[]{:S(2)}, u32[]{:S(2)}) collective-permute-start(bf16[96,384]{1,0:T(8,128)(2,1)S(1)} %get-tuple-element.198), channel_id=1, source_target_pairs={{0,16},{4,20},{8,24},{12,28},{16,0},{20,4},{24,8},{28,12},{1,17},{... | collective-permute-start | bytes 221192 | tf_op jit(solution)/shard_map/ppermute | solution.py:49
  218.4 1.2 collective-permute-start.31
  219.7 4.1 %collective-permute-start.32 = (f32[96,128]{1,0:T(8,128)S(1)}, f32[96,128]{1,0:T(8,128)S(1)}, u32[]{:S(2)}, u32[]{:S(2)}) collective-permute-start(f32[96,128]{1,0:T(8,128)S(1)} %slice_add_fusion.3), channel_id=1, source_target_pairs={{0,2},{1,3},{2,0},{3,1},{4,6},{5,7},{6,4},{7,5},{8,10},{9,11},{10,... | collective-permute-start | bytes 147464 | tf_op jit(solution)/shard_map/ppermute | solution.py:49
  (19 other events, 101.0 us)
Sparse Core Ops, SparseCore 0:
  10.8 58.2 all-gather.1
  96.6 83.2 reduce-scatter.1

commit v5 on v4

--- a/solution.py
+++ b/solution.py
@@ -546,50 +546,32 @@
             ref[n * size : (n + 1) * size, :] = value[at, :].astype(bf16)
 
 
-def out_kernel(
-    place_ref, chunk_ref, o_ref, ff_ref, g_ref, w_ref, keep_ref, send_ref, wkeep_ref, wsend_ref, do_ref, acc, acc_t
-):
-    s = pl.program_id(0)
-
-    @pl.when(s == 0)
-    def _():
-        acc[...] = jnp.zeros_like(acc)
-
+def out_kernel(place_ref, o_ref, ff_ref, g_ref, w_ref, keep_ref, send_ref, do_ref):
     total = mm(o_ref[...], w_ref[...], 0, 0) + ff_ref[...].astype(f32)
     put_rows(keep_ref, send_ref, total.astype(bf16))
-    acc[...] += mm(o_ref[...], g_ref[...], 1, 0)
     do_ref[...] = mm(w_ref[...], g_ref[...], 1, 1).astype(bf16)
 
-    @pl.when(s == pl.num_programs(0) - 1)
-    def _():
-        acc_t[...] = acc[...].T
-        put_chunks(chunk_ref, wkeep_ref, wsend_ref, acc_t)
-
-
-def branch_out(places, chunks, o, ff_out, g, wt):
+
+def branch_out(places, o, ff_out, g, wt):
     feat, tokens = o.shape
     dim = wt.shape[1]
     rows = tokens // 4
     keep, send = keep_send_specs(rows, dim)
     spec = pl.BlockSpec((rows, dim), lambda s, *_: (s, 0))
-    placed = pl.BlockSpec((feat, rows), lambda s, place, chunk: (0, place[s]))
-    whole = lambda shape: pl.BlockSpec(shape, lambda s, *_: (0, 0))
+    placed = pl.BlockSpec((feat, rows), lambda s, place: (0, place[s]))
     return pl.pallas_call(
         out_kernel,
         grid_spec=pltpu.PrefetchScalarGridSpec(
-            num_scalar_prefetch=2,
+            num_scalar_prefetch=1,
             grid=(4,),
             in_specs=[placed, spec, spec, pl.BlockSpec((feat, dim), lambda s, *_: (3, 0))],
-            out_specs=[keep, send, whole((dim // 2, feat)), whole((dim // 2, feat)), placed],
-            scratch_shapes=[pltpu.VMEM((feat, dim), f32), pltpu.VMEM((dim, feat), f32)],
+            out_specs=[keep, send, placed],
         ),
-        out_shape=[shaped((tokens // 2, dim), bf16)] * 2
-        + [shaped((dim // 2, feat), bf16)] * 2
-        + [shaped((feat, tokens), bf16)],
+        out_shape=[shaped((tokens // 2, dim), bf16)] * 2 + [shaped((feat, tokens), bf16)],
         compiler_params=params(),
         cost_estimate=cost(4 * feat * tokens * dim, 6 * tokens * dim),
         name="branch_out",
-    )(places, chunks, o, ff_out, g, wt)
+    )(places, o, ff_out, g, wt)
 
 
 def input_grad_kernel(
@@ -668,7 +650,7 @@
 
 
 def weight_grad_kernel(own_dims, place_ref, chunk_ref, grad_ref, normed_ref, *refs):
-    small_refs, (wkeep_ref, wsend_ref, acc, acc_t) = refs[:-4], refs[-4:]
+    more_refs, (wkeep_ref, wsend_ref, acc, acc_t) = refs[:-4], refs[-4:]
     s = pl.program_id(0)
 
     @pl.when(s == 0)
@@ -676,17 +658,20 @@
         acc[...] = jnp.zeros_like(acc)
 
     width = grad_ref.shape[0]
+    base = 2 * width
     acc[:width, :] += mm(grad_ref[...], normed_ref[...], 1, 0)
+    if more_refs:
+        o_ref, g_ref, one_ref, ff_ref, bias_ref = more_refs
+        acc[width:base, :] += mm(o_ref[...], g_ref[...], 1, 0)
 
     @pl.when(s == pl.num_programs(0) - 1)
     def _():
-        if small_refs:
-            one_ref, ff_ref, bias_ref = small_refs
-            acc[256:258, :] = one_ref[0:2, :]
-            acc[258:262, :] = ff_ref[0:4, :]
+        if more_refs:
+            acc[base : base + 2, :] = one_ref[0:2, :]
+            acc[base + 2 : base + 6, :] = ff_ref[0:4, :]
         acc_t[...] = acc[...].T
-        if small_refs:
-            columns = acc_t[:, 256:]
+        if more_refs:
+            columns = acc_t[:, base:]
             lane = lax.broadcasted_iota(jnp.int32, (own_dims, 128), 1)
             shared = jnp.zeros((own_dims, 128), f32)
             count = columns.shape[0] // own_dims
@@ -697,25 +682,26 @@
                 part = bias_ref[n * own_dims : (n + 1) * own_dims, 0:1]
                 shared = jnp.where(lane == 8 + count + n, part, shared)
             lane = lax.broadcasted_iota(jnp.int32, columns.shape, 1)
-            acc_t[:, 256:] = jnp.where(lane < 5, columns, jnp.concatenate([shared] * count, axis=0))
+            acc_t[:, base:] = jnp.where(lane < 5, columns, jnp.concatenate([shared] * count, axis=0))
         put_chunks(chunk_ref, wkeep_ref, wsend_ref, acc_t)
 
 
-def weight_gradient(places, chunks, grad, normed, width, part, own_dims, small=()):
+def weight_gradient(places, chunks, grad, normed, width, part, own_dims, o=None, g=None, small=()):
     tokens = grad.shape[1]
     dim = normed.shape[1]
     rows = tokens // 4
-    out_width = 384 if small else width
+    out_width = 2 * width + 128 if small else width
+    column = lambda part: pl.BlockSpec((width, rows), lambda s, place, chunk: (part, place[s]))
+    spec = pl.BlockSpec((rows, dim), lambda s, *_: (s, 0))
+    more = (o, g, *small) if small else ()
     whole = lambda shape: pl.BlockSpec(shape, lambda s, *_: (0, 0))
     return pl.pallas_call(
         functools.partial(weight_grad_kernel, own_dims),
         grid_spec=pltpu.PrefetchScalarGridSpec(
             num_scalar_prefetch=2,
             grid=(4,),
-            in_specs=[
-                pl.BlockSpec((width, rows), lambda s, place, chunk: (part, place[s])),
-                pl.BlockSpec((rows, dim), lambda s, *_: (s, 0)),
-            ]
+            in_specs=[column(part), spec]
+            + ([column(0), spec] if small else [])
             + [whole(a.shape) for a in small],
             out_specs=[whole((dim // 2, out_width))] * 2,
             scratch_shapes=[pltpu.VMEM((out_width, dim), f32), pltpu.VMEM((dim, out_width), f32)],
@@ -724,7 +710,7 @@
         compiler_params=params(),
         cost_estimate=cost(4 * width * tokens * dim, 4 * tokens * dim),
         name="weight_gradient",
-    )(places, chunks, grad, normed, *small)
+    )(places, chunks, grad, normed, *more)
 
 
 def norm_back_kernel(own_ref, came_ref, far_ref, x_ref, stats_ref, g_ref, out_ref):
@@ -867,16 +853,14 @@
 
     o, lse = attention_forward(first, q, k, v, left, lo_row, halo)
     chunks = late_chunks()
-    out_keep, out_send, ow_keep, ow_send, do = branch_out(places, chunks, o, ff_out, g_all, wt)
+    out_keep, out_send, do = branch_out(places, o, ff_out, g_all, wt)
     own_o, came_o, other_o = scatter_near(out_keep, out_send)
-    ow_near = late_near(ow_keep, ow_send)
     dq_part, back = backward_left(first, q, left, lo_row, o, lse, do, halo)
-    dq_part, back, other_o, ow_near = tied(dq_part, back, other_o, ow_near)
+    dq_part, back, other_o = tied(dq_part, back, other_o)
     far_o = swapped(other_o, "tensor", 2)
     back = passed_along(back, "dp", -1)
-    ow_own = late_far(ow_near, bf16)
     dq, dk, dv = backward_own(first, q, k, v, lo_row, o, lse, do, dq_part, halo)
-    back, dq, far_o, ow_own = tied(back, dq, far_o, ow_own)
+    back, dq, far_o = tied(back, dq, far_o)
     count = hidden_in.shape[0]
     summed = own_o[:count].astype(f32) + came_o[:count].astype(f32) + far_o.astype(f32)
     layer_out = (hidden_in.astype(f32) + summed + vec[0] + vec[1]).astype(bf16)
@@ -890,7 +874,16 @@
     proj_grad, other_u, send_a = tied(proj_grad, other_u, send_a)
     keep_a, came_a = late_sent(keep_a, send_a)
     keep_b, send_b = weight_gradient(
-        places, chunks, proj_grad, normed_one, local_dim, 2, own_dims, (one_small, ff_small, qkv_bias)
+        places,
+        chunks,
+        proj_grad,
+        normed_one,
+        local_dim,
+        2,
+        own_dims,
+        o,
+        g_all,
+        (one_small, ff_small, qkv_bias),
     )
     send_b, came_a = tied(send_b, came_a)
     near_a = late_sum(keep_a, came_a)
@@ -900,22 +893,22 @@
     late_b = late_far(near_b, bf16)
     late_own = jnp.concatenate([late_a, late_b[:, :local_dim]], axis=1)
 
-    late_b, ff_sum = tied(late_b, ff_sum)
+    input_grad = norm_back(own_u, came_u, far_u, hidden_in, stats, cotangent)
+    late_b, ff_sum, input_grad = tied(late_b, ff_sum, input_grad)
     ff_own = ff_sum.astype(f32)
-    vectors = late_b[:, 256:]
+    vectors = late_b[:, 2 * local_dim :]
     norm_grads = summed_over(vectors, "tensor")[:, :4].T
     fc_count = ff // own_dims
     fc_b_total = vectors[:, 8 : 8 + fc_count].T.reshape(ff)
     qkv_b_total = vectors[:, 8 + fc_count : 8 + fc_count + qkv_dim // own_dims].T.reshape(3, local_dim)
     out_b_total = vectors[:, 4]
 
-    input_grad = norm_back(own_u, came_u, far_u, hidden_in, stats, cotangent)
     return (
         layer_out,
         input_grad,
         jnp.transpose(late_own.reshape(own_dims, 3, local_dim), (1, 0, 2)),
         qkv_b_total,
-        ow_own.T,
+        late_b[:, local_dim : 2 * local_dim].T,
         out_b_total,
         ff_own[:, :ff],
         fc_b_total,

time: 241 us -> 236 us (0.979); the launches traced: 236 us -> 236 us
  starting transfers between devices: 50.1 us -> 32.6 us
  waiting for transfers between devices: 41 us -> 54.8 us
    ppermute x24 -> x20, starting transfers between devices: 33.6 us -> 16.3 us  [swapped(): return lax.ppermute(block, axis, route)]
    reduce_scatter x1, waiting for transfers between devices: 0.02 us -> 9.28 us  [body(): ff_sum = lax.psum_scatter(ff_grads, 'dp', scatter_dimension=0, tiled=True)]
    ppermute x2, waiting for transfers between devices: 0.01 us -> 6.05 us  [passed_along(): return lax.ppermute(block, axis, route)]
    unnamed x68 -> x66, local copies, waits for them, and re-layouts: 6.49 us -> 8.52 us
    ppermute x24 -> x20, waiting for transfers between devices: 15.7 us -> 14.1 us  [swapped(): return lax.ppermute(block, axis, route)]
  transfers between devices with their start and end apart: 35 -> 31, of which waited for: 15 -> 15; matrix products, arithmetic and copies ran while one was open for 8% -> 8% of each run, Pallas kernels for 40% -> 41%
where the time goes in v5:
time: 236 us
  Pallas kernels  106 us (45%)
  waiting for transfers between devices  54.8 us (23%)
  starting transfers between devices  32.6 us (14%)
  local copies, waits for them, and re-layouts  19.2 us (8%)
  between operations  14.5 us (6%)
  other arithmetic  8.75 us (4%)
    pallas_call x1, Pallas kernels, feed_forward(): pl.pallas_call(ff_kernel, grid_spec=pltpu.PrefetchScalarGridSpec(num_scal...  22.5 us
    pallas_call x1, Pallas kernels, backward_own(): pl.pallas_call(functools.partial(own_bwd_kernel, heads, halo), grid_spec=...  17.7 us
    ppermute x20, starting transfers between devices, swapped(): return lax.ppermute(block, axis, route)  16.3 us
    pallas_call x1, Pallas kernels, attention_forward(): pl.pallas_call(functools.partial(attn_fwd_kernel, heads, halo), grid_spec...  14.6 us
    ppermute x20, waiting for transfers between devices, swapped(): return lax.ppermute(block, axis, route)  14.1 us
    pallas_call x2, Pallas kernels, weight_gradient(): pl.pallas_call(functools.partial(weight_grad_kernel, own_dims), grid_spec...  13.9 us
    pallas_call x1, Pallas kernels, input_gradient(): pl.pallas_call(functools.partial(input_grad_kernel, halo), grid_spec=pltp...  11.2 us
    pallas_call x1, Pallas kernels, project(): pl.pallas_call(functools.partial(project_kernel, len(pieces), first), gri...  10.9 us
  transfers between devices with their start and end apart: 31, of which 15 were waited for; matrix products, arithmetic and copies ran while one was open for 8% of the time, Pallas kernels for 41%

profile of v5, /device:TPU:0, one launch (start us, length us, event | category | flops | bytes accessed | tf_op | source)
XLA Modules:
  0.0 236.1 jit_solution(18170179502619745832)
XLA Ops:
  7.3 1.8 pad_maximum_fusion
  9.2 3.0 %collective-permute-start.6 = (bf16[512,768]{1,0:T(8,128)(2,1)}, bf16[512,768]{1,0:T(8,128)(2,1)}, u32[]{:S(2)}, u32[]{:S(2)}) collective-permute-start(bf16[512,768]{1,0:T(8,128)(2,1)} %x_ref.1), channel_id=1, source_target_pairs={{0,2},{1,3},{2,0},{3,1},{4,6},{5,7},{6,4},{7,5},{8,10},{9,11},{10,... | collective-permute-start | bytes 2359304 | tf_op jit(solution)/shard_map/ppermute | solution.py:49
  13.1 0.9 copy.56
  14.0 1.1 copy.55
  15.3 1.5 collective-permute-start.1
  17.4 3.8 %collective-permute-done.1.refs_6_ = bf16[96,896]{1,0:T(8,128)(2,1)S(1)} collective-permute-done((bf16[96,896]{1,0:T(8,128)(2,1)S(1)}, bf16[96,896]{1,0:T(8,128)(2,1)S(1)}, u32[]{:S(2)}, u32[]{:S(2)}) %collective-permute-start.1) | collective-permute-done | bytes 172064 | tf_op jit(solution)/shard_map/ppermute | solution.py:77
  21.2 1.3 collective-permute-done.refs_5_
  23.1 1.5 collective-permute-start.3
  25.1 0.9 reshape.74.b_ref
  26.0 4.8 %collective-permute-done.2.refs_7_ = bf16[96,896]{1,0:T(8,128)(2,1)} collective-permute-done((bf16[96,896]{1,0:T(8,128)(2,1)}, bf16[96,896]{1,0:T(8,128)(2,1)}, u32[]{:S(2)}, u32[]{:S(2)}) %collective-permute-start.2) | collective-permute-done | bytes 172064 | tf_op jit(solution)/shard_map/ppermute | solution.py:76
  30.8 2.4 %collective-permute-done.3.refs_8_ = bf16[96,896]{1,0:T(8,128)(2,1)} collective-permute-done((bf16[96,896]{1,0:T(8,128)(2,1)S(1)}, bf16[96,896]{1,0:T(8,128)(2,1)}, u32[]{:S(2)}, u32[]{:S(2)}) %collective-permute-start.3) | collective-permute-done | bytes 172064 | tf_op jit(solution)/shard_map/ppermute | solution.py:77
  33.2 1.4 collective-permute-start.4
  35.2 3.6 %collective-permute-done.4.refs_9_ = bf16[96,896]{1,0:T(8,128)(2,1)S(1)} collective-permute-done((bf16[96,896]{1,0:T(8,128)(2,1)}, bf16[96,896]{1,0:T(8,128)(2,1)S(1)}, u32[]{:S(2)}, u32[]{:S(2)}) %collective-permute-start.4) | collective-permute-done | bytes 172064 | tf_op jit(solution)/shard_map/ppermute | solution.py:76
  38.8 2.5 %collective-permute-done.5.refs_10_ = bf16[96,896]{1,0:T(8,128)(2,1)S(1)} collective-permute-done((bf16[96,896]{1,0:T(8,128)(2,1)}, bf16[96,896]{1,0:T(8,128)(2,1)S(1)}, u32[]{:S(2)}, u32[]{:S(2)}) %collective-permute-start.5) | collective-permute-done | bytes 172064 | tf_op jit(solution)/shard_map/ppermute | solution.py:77
  41.3 1.0 multiply_sine_fusion
  42.3 1.7 collective-permute-start.9
  44.0 1.2 dynamic-slice_bitcast_fusion.start_ref
  45.8 6.9 %collective-permute-done.9.refs_11_ = bf16[96,896]{1,0:T(8,128)(2,1)S(1)} collective-permute-done((bf16[96,896]{1,0:T(8,128)(2,1)S(1)}, bf16[96,896]{1,0:T(8,128)(2,1)S(1)}, u32[]{:S(2)}, u32[]{:S(2)}) %collective-permute-start.9) | collective-permute-done | bytes 172064 | tf_op jit(solution)/shard_map/ppermute | solution.py:83
  53.6 10.9 %project.1 = (bf16[192,2048]{1,0:T(8,128)(2,1)}, bf16[192,2048]{1,0:T(8,128)(2,1)}, bf16[192,2048]{1,0:T(8,128)(2,1)}, bf16[384,768]{1,0:T(8,128)(2,1)}, bf16[20...) custom-call(s32[8]{0:T(128)} %dynamic-slice_bitcast_fusion.start_ref, ...), custom_call_target="tpu_custom_call" | custom-call | flops 113246208 | bytes 737280 | tf_op jit(solution)/shard_map/project/pallas_call | solution.py:263
  64.5 6.9 %collective-permute-start.13 = (bf16[384,768]{1,0:T(8,128)(2,1)}, bf16[384,768]{1,0:T(8,128)(2,1)S(1)}, u32[]{:S(2)}, u32[]{:S(2)}) collective-permute-start(bf16[384,768]{1,0:T(8,128)(2,1)} %get-tuple-element.93), channel_id=1, source_target_pairs={{0,4},{4,8},{8,12},{12,16},{16,20},{20,24},{24,28},{1,5},{5,9},{9,... | collective-permute-start | bytes 1769480 | tf_op jit(solution)/shard_map/ppermute | solution.py:44
  73.0 22.5 %feed_forward.1 = (bf16[2048,768]{1,0:T(8,128)(2,1)}, bf16[2048,768]{1,0:T(8,128)(2,1)}, bf16[2048,768]{1,0:T(8,128)(2,1)}, bf16[768,1536]{1,0:T(8,128)(2,1)}, f32[8,768]{1,0:T(8,128)}) custom-call(bf16[2048,768]{1,0:T(8,128)(2,1)} %get-tuple-element.84.x_ref, f32[2048,128]{1,0:T(8,128)} %get-tuple-element.85.stats_ref, f32[1,768]{1,0:T(1,128)} %reshape.73.b_ref, ...), custom_call_target="tpu_custom_call" | custom-call | flops 905969664 | bytes 1081344 | tf_op jit(solution)/shard_map/feed_forward/pallas_call | solution.py:179
  96.9 14.6 %attention_forward.1 = (bf16[192,2048]{1,0:T(8,128)(2,1)}, f32[8,2048]{1,0:T(8,128)}) custom-call(s32[8]{0:T(128)} %and_select_fusion.first_ref, bf16[192,2048]{1,0:T(8,128)(2,1)} %get-tuple-element.90.q_ref, bf16[192,2048]{1,0:T(8,128)(2,1)} %get-tuple-element.91.k_ref, bf16[192,2048]{1,0:T(8,128)(2,1)} %get-tuple-element.92.v_ref, ...), custom_call_target="tpu_custom_call" | custom-call | flops 402653184 | bytes 196608 | tf_op jit(solution)/shard_map/attention_forward/pallas_call | solution.py:357
  111.5 7.6 %branch_out.1 = (bf16[1024,768]{1,0:T(8,128)(2,1)}, bf16[1024,768]{1,0:T(8,128)(2,1)}, bf16[192,2048]{1,0:T(8,128)(2,1)}) custom-call(s32[4]{0:T(128)} %pad_add_fusion.place_ref, bf16[192,2048]{1,0:T(8,128)(2,1)} %get-tuple-element.94.o_ref.refs_0_, bf16[2048,768]{1,0:T(8,128)(2,1)} %get-tuple-element.95.ff_ref, ...), custom_call_target="tpu_custom_call" | custom-call | flops 75497472 | bytes 589824 | tf_op jit(solution)/shard_map/branch_out/pallas_call | solution.py:562
  119.4 4.4 %attention_backward_left.1 = (f32[192,768]{1,0:T(8,128)}, bf16[384,768]{1,0:T(8,128)(2,1)}) custom-call(s32[8]{0:T(128)} %and_select_fusion.first_ref, bf16[192,2048]{1,0:T(8,128)(2,1)} %get-tuple-element.90.q_ref, bf16[384,768]{1,0:T(8,128)(2,1)} %copy-done.4, s32[1,2048]{1,0:T(1,128)} %bitcast.40, bf16[192,2048]{1,0:T(8,128)(2,1)} %get-tuple-element.94.o_ref.refs_0_, ...), custom_call_target="tpu_custom_call" | custom-call | flops 188743680 | bytes 184320 | tf_op jit(solution)/shard_map/attention_backward_left/pallas_call | solution.py:468
  124.1 1.1 copy-done.30
  125.2 1.5 collective-permute-start.15
  126.7 17.7 %attention_backward_own.1 = (f32[192,2048]{1,0:T(8,128)}, f32[192,2048]{1,0:T(8,128)}, f32[192,2048]{1,0:T(8,128)}) custom-call(s32[8]{0:T(128)} %and_select_fusion.first_ref, bf16[192,2048]{1,0:T(8,128)(2,1)} %get-tuple-element.90.q_ref, bf16[192,2048]{1,0:T(8,128)(2,1)} %get-tuple-element.91.k_ref, bf16[192,2048]{1,0:T(8,128)(2,1)} %get-tuple-element.92.v_ref, ...), custom_call_target="tpu_custom_call" | custom-call | flops 1006632960 | bytes 491520 | tf_op jit(solution)/shard_map/attention_backward_own/pallas_call | solution.py:498
  144.4 6.1 %collective-permute-done.15.back_ref = bf16[384,768]{1,0:T(8,128)(2,1)S(1)} collective-permute-done((bf16[384,768]{1,0:T(8,128)(2,1)S(1)}, bf16[384,768]{1,0:T(8,128)(2,1)S(1)}, u32[]{:S(2)}, u32[]{:S(2)}) %collective-permute-start.15) | collective-permute-done | bytes 589856 | tf_op jit(solution)/shard_map/ppermute | solution.py:44
  151.3 11.2 %input_gradient.1 = (bf16[1024,768]{1,0:T(8,128)(2,1)}, bf16[1024,768]{1,0:T(8,128)(2,1)}, bf16[576,2048]{1,0:T(8,128)(2,1)}, f32[8,768]{1,0:T(8,128)}, f32[576,1]{1,0:T(8,128)}) custom-call(s32[4]{0:T(128)} %pad_add_fusion.place_ref, f32[192,2048]{1,0:T(8,128)} %get-tuple-element.109.dq_ref, f32[192,2048]{1,0:T(8,128)} %get-tuple-element.110.dk_ref, ...), custom_call_target="tpu_custom_call" | custom-call | flops 226492416 | bytes 983040 | tf_op jit(solution)/shard_map/input_gradient/pallas_call | solution.py:632
  164.1 2.1 collective-permute-done.17.came_ref
  166.2 2.8 %add_convert_fusion = bf16[512,768]{1,0:T(8,128)(2,1)} fusion(bf16[1024,768]{1,0:T(8,128)(2,1)S(1)} %collective-permute-done.17.came_ref, bf16[1024,768]{1,0:T(8,128)(2,1)} %get-tuple-element.117.own_ref), kind=kLoop, calls=%fused_computation | loop fusion | flops 1572864 | bytes 2359296 | tf_op jit(solution)/shard_map/convert_element_type | solution.py:94
  169.0 9.3 %reduce-scatter.2.cloned.1.call-done = bf16[96,1536]{1,0:T(8,128)(2,1)} async-done(((bf16[768,1536]{1,0:T(8,128)(2,1)}), bf16[96,1536]{1,0:T(8,128)(2,1)}) %reduce-scatter.2.cloned.1.call-update) | async-done | bytes 294928 | tf_op jit(solution)/shard_map/reduce_scatter | solution.py:851
  178.3 6.3 %weight_gradient.2 = (bf16[384,384]{1,0:T(8,128)(2,1)}, bf16[384,384]{1,0:T(8,128)(2,1)}) custom-call(s32[4]{0:T(128)} %pad_add_fusion.place_ref, s32[8]{0:T(128)} %concatenate.15.chunk_ref, bf16[576,2048]{1,0:T(8,128)(2,1)} %get-tuple-element.121.grad_ref, bf16[2048,768]{1,0:T(8,128)(2,1)} %get-tuple-element.119.normed_ref), custom_call_target="tpu_custom_call" | custom-call | flops 150994944 | bytes 393216 | tf_op jit(solution)/shard_map/weight_gradient/pallas_call | solution.py:698
  185.3 1.4 add_convert_fusion.1
  186.6 1.5 collective-permute-start.26
  188.1 7.6 %weight_gradient.3 = (bf16[384,512]{1,0:T(8,128)(2,1)}, bf16[384,512]{1,0:T(8,128)(2,1)}) custom-call(s32[4]{0:T(128)} %pad_add_fusion.place_ref, s32[8]{0:T(128)} %concatenate.15.chunk_ref, bf16[576,2048]{1,0:T(8,128)(2,1)} %get-tuple-element.121.grad_ref, bf16[2048,768]{1,0:T(8,128)(2,1)} %get-tuple-element.119.normed_ref, ...), custom_call_target="tpu_custom_call" | custom-call | flops 75497472 | bytes 393216 | tf_op jit(solution)/shard_map/weight_gradient/pallas_call | solution.py:698
  195.7 1.4 collective-permute-start.19
  197.2 0.9 collective-permute-start.23
  198.2 2.1 collective-permute-start.25
  200.8 4.8 %collective-permute-done.19 = bf16[384,512]{1,0:T(8,128)(2,1)S(1)} collective-permute-done((bf16[384,512]{1,0:T(8,128)(2,1)}, bf16[384,512]{1,0:T(8,128)(2,1)S(1)}, u32[]{:S(2)}, u32[]{:S(2)}) %collective-permute-start.19) | collective-permute-done | bytes 393248 | tf_op jit(solution)/shard_map/ppermute | solution.py:49
  206.3 3.4 %collective-permute-start.22 = (bf16[96,512]{1,0:T(8,128)(2,1)S(1)}, bf16[96,512]{1,0:T(8,128)(2,1)S(1)}, u32[]{:S(2)}, u32[]{:S(2)}) collective-permute-start(bf16[96,512]{1,0:T(8,128)(2,1)S(1)} %get-tuple-element.191), channel_id=1, source_target_pairs={{0,24},{4,28},{8,16},{12,20},{16,8},{20,12},{24,0},{28,4},{1,25},{... | collective-permute-start | bytes 294920 | tf_op jit(solution)/shard_map/ppermute | solution.py:49
  209.8 1.6 collective-permute-done.20
  211.4 2.1 collective-permute-done.22
  213.6 3.1 %collective-permute-done.21 = bf16[96,512]{1,0:T(8,128)(2,1)S(1)} collective-permute-done((bf16[96,512]{1,0:T(8,128)(2,1)S(1)}, bf16[96,512]{1,0:T(8,128)(2,1)S(1)}, u32[]{:S(2)}, u32[]{:S(2)}) %collective-permute-start.21) | collective-permute-done | bytes 98336 | tf_op jit(solution)/shard_map/ppermute | solution.py:49
  216.7 0.9 copy-done.11
  217.6 3.4 %norm_back.1 = bf16[512,768]{1,0:T(8,128)(2,1)} custom-call(bf16[1024,768]{1,0:T(8,128)(2,1)} %get-tuple-element.117.own_ref, bf16[1024,768]{1,0:T(8,128)(2,1)} %copy-done.2, bf16[512,768]{1,0:T(8,128)(2,1)} %copy-done.11, bf16[512,768]{1,0:T(8,128)(2,1)} %x_ref.1, f32[2048,128]{1,0:T(8,128)} %get-tuple-element.85.stats_ref, bf16[512,768]{1,0:T(8,128)(2,1)} %g_ref.1), custom_call_target="tpu_custom_call" | custom-call | flops 491520 | bytes 294912 | tf_op jit(solution)/shard_map/norm_back/pallas_call | solution.py:729
  222.5 1.2 collective-permute-start.28
  227.1 0.9 copy.63
  (137 shorter events, 19.2 us)
Async XLA Ops:
  7.2 31.6 %copy-start = (bf16[512,768]{1,0:T(8,128)(2,1)S(1)}, bf16[512,768]{1,0:T(8,128)(2,1)}, u32[]{:S(2)}) copy-start(bf16[512,768]{1,0:T(8,128)(2,1)} %x_ref.1) | copy-start | bytes 2359300
  7.2 17.4 %copy-start.3 = (bf16[512,768]{1,0:T(8,128)(2,1)S(1)}, bf16[512,768]{1,0:T(8,128)(2,1)}, u32[]{:S(2)}) copy-start(bf16[512,768]{1,0:T(8,128)(2,1)} %g_ref.1) | copy-start | bytes 2359300
  7.2 17.9 %copy-start.27 = (bf16[3,192]{1,0:T(4,128)(2,1)S(1)}, bf16[3,192]{1,0:T(4,128)(2,1)}, u32[]{:S(2)}) copy-start(bf16[3,192]{1,0:T(4,128)(2,1)} %param.19) | copy-start | bytes 3460
  7.2 28.0 %copy-start.26 = (s32[2048]{0:T(1024)S(1)}, s32[2048]{0:T(1024)}, u32[]{:S(2)}) copy-start(s32[2048]{0:T(1024)} %param.30) | copy-start | bytes 24580
  7.2 65.0 %all-gather.2.cloned.1.call-start = ((), (), s32[]{:S(2)}) async-start(), calls=%async_computation.1 | async-start | bytes 2654208 | tf_op jit(solution)/shard_map/all_gather | solution.py:825
  9.1 169.1 %reduce-scatter.2.cloned.1.call-start = ((), (), s32[]{:S(2)}) async-start(), calls=%async_computation.2 | async-start | bytes 2654208 | tf_op jit(solution)/shard_map/reduce_scatter | solution.py:851
  9.2 32.1 %collective-permute-start.6 = (bf16[512,768]{1,0:T(8,128)(2,1)}, bf16[512,768]{1,0:T(8,128)(2,1)}, u32[]{:S(2)}, u32[]{:S(2)}) collective-permute-start(bf16[512,768]{1,0:T(8,128)(2,1)} %x_ref.1), channel_id=1, source_target_pairs={{0,2},{1,3},{2,0},{3,1},{4,6},{5,7},{6,4},{7,5},{8,10},{9,11},{10,... | collective-permute-start | bytes 2359304 | tf_op jit(solution)/shard_map/ppermute | solution.py:49
  15.3 37.3 %copy-start.17 = (bf16[96,896]{1,0:T(8,128)(2,1)}, bf16[96,896]{1,0:T(8,128)(2,1)S(1)}, u32[]{:S(2)}) copy-start(bf16[96,896]{1,0:T(8,128)(2,1)S(1)} %fusion.3.refs_4_) | copy-start | bytes 516100
  15.3 5.9 %collective-permute-start.1 = (bf16[96,896]{1,0:T(8,128)(2,1)S(1)}, bf16[96,896]{1,0:T(8,128)(2,1)S(1)}, u32[]{:S(2)}, u32[]{:S(2)}) collective-permute-start(bf16[96,896]{1,0:T(8,128)(2,1)S(1)} %fusion.3.refs_4_), channel_id=1, source_target_pairs={{8,0},{16,8},{24,16},{28,24},{20,28},{12,20},{4,12},{0,4},{9,1},{1... | collective-permute-start | bytes 516104 | tf_op jit(solution)/shard_map/ppermute | solution.py:77
  16.9 5.7 %collective-permute-start = (bf16[96,896]{1,0:T(8,128)(2,1)S(1)}, bf16[96,896]{1,0:T(8,128)(2,1)}, u32[]{:S(2)}, u32[]{:S(2)}) collective-permute-start(bf16[96,896]{1,0:T(8,128)(2,1)S(1)} %fusion.3.refs_4_), channel_id=1, source_target_pairs={{0,8},{8,16},{16,24},{24,28},{28,20},{20,12},{12,4},{4,0},{1,9},{9... | collective-permute-start | bytes 516104 | tf_op jit(solution)/shard_map/ppermute | solution.py:76
  21.2 31.4 %copy-start.21 = (bf16[96,896]{1,0:T(8,128)(2,1)}, bf16[96,896]{1,0:T(8,128)(2,1)S(1)}, u32[]{:S(2)}) copy-start(bf16[96,896]{1,0:T(8,128)(2,1)S(1)} %collective-permute-done.1.refs_6_) | copy-start | bytes 516100
  22.5 8.3 %collective-permute-start.2 = (bf16[96,896]{1,0:T(8,128)(2,1)}, bf16[96,896]{1,0:T(8,128)(2,1)}, u32[]{:S(2)}, u32[]{:S(2)}) collective-permute-start(bf16[96,896]{1,0:T(8,128)(2,1)} %collective-permute-done.refs_5_), channel_id=1, source_target_pairs={{0,8},{8,16},{16,24},{24,28},{28,20},{20,12},{12,4},{4,0},{1,9},{9... | collective-permute-start | bytes 516104 | tf_op jit(solution)/shard_map/ppermute | solution.py:76
  23.1 10.1 %collective-permute-start.3 = (bf16[96,896]{1,0:T(8,128)(2,1)S(1)}, bf16[96,896]{1,0:T(8,128)(2,1)}, u32[]{:S(2)}, u32[]{:S(2)}) collective-permute-start(bf16[96,896]{1,0:T(8,128)(2,1)S(1)} %collective-permute-done.1.refs_6_), channel_id=1, source_target_pairs={{8,0},{16,8},{24,16},{28,24},{20,28},{12,20},{4,12},{0,4},{9,1},{1... | collective-permute-start | bytes 516104 | tf_op jit(solution)/shard_map/ppermute | solution.py:77
  24.6 47.6 %collective-permute-start.11 = (bf16[512,768]{1,0:T(8,128)(2,1)S(1)}, bf16[512,768]{1,0:T(8,128)(2,1)S(1)}, u32[]{:S(2)}, u32[]{:S(2)}) collective-permute-start(bf16[512,768]{1,0:T(8,128)(2,1)S(1)} %copy-done.3), channel_id=1, source_target_pairs={{0,1},{1,0},{2,3},{3,2},{4,5},{5,4},{6,7},{7,6},{8,9},{9,8},{10,11... | collective-permute-start | bytes 2359304 | tf_op jit(solution)/shard_map/ppermute | solution.py:49
  24.6 39.9 %collective-permute-start.10 = (bf16[512,768]{1,0:T(8,128)(2,1)S(1)}, bf16[512,768]{1,0:T(8,128)(2,1)S(1)}, u32[]{:S(2)}, u32[]{:S(2)}) collective-permute-start(bf16[512,768]{1,0:T(8,128)(2,1)S(1)} %copy-done.3), channel_id=1, source_target_pairs={{0,2},{1,3},{2,0},{3,1},{4,6},{5,7},{6,4},{7,5},{8,10},{9,11},{10,... | collective-permute-start | bytes 2359304 | tf_op jit(solution)/shard_map/ppermute | solution.py:49
  33.2 5.6 %collective-permute-start.4 = (bf16[96,896]{1,0:T(8,128)(2,1)}, bf16[96,896]{1,0:T(8,128)(2,1)S(1)}, u32[]{:S(2)}, u32[]{:S(2)}) collective-permute-start(bf16[96,896]{1,0:T(8,128)(2,1)} %collective-permute-done.2.refs_7_), channel_id=1, source_target_pairs={{0,8},{8,16},{16,24},{24,28},{28,20},{20,12},{12,4},{4,0},{1,9},{9... | collective-permute-start | bytes 516104 | tf_op jit(solution)/shard_map/ppermute | solution.py:76
  34.6 6.8 %collective-permute-start.5 = (bf16[96,896]{1,0:T(8,128)(2,1)}, bf16[96,896]{1,0:T(8,128)(2,1)S(1)}, u32[]{:S(2)}, u32[]{:S(2)}) collective-permute-start(bf16[96,896]{1,0:T(8,128)(2,1)} %collective-permute-done.3.refs_8_), channel_id=1, source_target_pairs={{8,0},{16,8},{24,16},{28,24},{20,28},{12,20},{4,12},{0,4},{9,1},{1... | collective-permute-start | bytes 516104 | tf_op jit(solution)/shard_map/ppermute | solution.py:77
  35.2 36.8 %copy-start.25 = (s32[2048]{0:T(1024)}, s32[2048]{0:T(1024)S(1)}, u32[]{:S(2)}) copy-start(s32[2048]{0:T(1024)S(1)} %get-tuple-element.199) | copy-start | bytes 24580
  38.8 13.8 %copy-start.22 = (bf16[96,896]{1,0:T(8,128)(2,1)}, bf16[96,896]{1,0:T(8,128)(2,1)S(1)}, u32[]{:S(2)}) copy-start(bf16[96,896]{1,0:T(8,128)(2,1)S(1)} %collective-permute-done.4.refs_9_) | copy-start | bytes 516100
  38.8 6.9 %collective-permute-start.7 = (bf16[512,768]{1,0:T(8,128)(2,1)S(1)}, bf16[512,768]{1,0:T(8,128)(2,1)S(1)}, u32[]{:S(2)}, u32[]{:S(2)}) collective-permute-start(bf16[512,768]{1,0:T(8,128)(2,1)S(1)} %copy-done), channel_id=1, source_target_pairs={{0,1},{1,0},{2,3},{3,2},{4,5},{5,4},{6,7},{7,6},{8,9},{9,8},{10,11... | collective-permute-start | bytes 2359304 | tf_op jit(solution)/shard_map/ppermute | solution.py:49
  41.3 11.4 %copy-start.23 = (bf16[96,896]{1,0:T(8,128)(2,1)}, bf16[96,896]{1,0:T(8,128)(2,1)S(1)}, u32[]{:S(2)}) copy-start(bf16[96,896]{1,0:T(8,128)(2,1)S(1)} %collective-permute-done.5.refs_10_) | copy-start | bytes 516100
  41.3 11.3 %collective-permute-start.8 = (bf16[512,768]{1,0:T(8,128)(2,1)}, bf16[512,768]{1,0:T(8,128)(2,1)S(1)}, u32[]{:S(2)}, u32[]{:S(2)}) collective-permute-start(bf16[512,768]{1,0:T(8,128)(2,1)} %collective-permute-done.6.refs_1_), channel_id=1, source_target_pairs={{0,1},{1,0},{2,3},{3,2},{4,5},{5,4},{6,7},{7,6},{8,9},{9,8},{10,11... | collective-permute-start | bytes 2359304 | tf_op jit(solution)/shard_map/ppermute | solution.py:49
  42.3 10.3 %collective-permute-start.9 = (bf16[96,896]{1,0:T(8,128)(2,1)S(1)}, bf16[96,896]{1,0:T(8,128)(2,1)S(1)}, u32[]{:S(2)}, u32[]{:S(2)}) collective-permute-start(bf16[96,896]{1,0:T(8,128)(2,1)S(1)} %collective-permute-done.4.refs_9_), channel_id=1, source_target_pairs={{0,8},{8,16},{16,24},{24,28},{28,20},{20,12},{12,4},{4,0},{1,9},{9... | collective-permute-start | bytes 516104 | tf_op jit(solution)/shard_map/ppermute | solution.py:83
  53.6 17.9 %copy-start.28 = (bf16[768]{0:T(1024)(128)(2,1)S(1)}, bf16[768]{0:T(1024)(128)(2,1)}, u32[]{:S(2)}) copy-start(bf16[768]{0:T(1024)(128)(2,1)} %param.23) | copy-start | bytes 4612
  64.4 7.7 %copy-start.10 = (bf16[512,768]{1,0:T(8,128)(2,1)}, bf16[512,768]{1,0:T(8,128)(2,1)S(1)}, u32[]{:S(2)}) copy-start(bf16[512,768]{1,0:T(8,128)(2,1)S(1)} %collective-permute-done.10.refs_1_) | copy-start | bytes 2359300
  64.5 7.7 %collective-permute-start.12 = (bf16[512,768]{1,0:T(8,128)(2,1)S(1)}, bf16[512,768]{1,0:T(8,128)(2,1)}, u32[]{:S(2)}, u32[]{:S(2)}) collective-permute-start(bf16[512,768]{1,0:T(8,128)(2,1)S(1)} %collective-permute-done.10.refs_1_), channel_id=1, source_target_pairs={{0,1},{1,0},{2,3},{3,2},{4,5},{5,4},{6,7},{7,6},{8,9},{9,8},{10,11... | collective-permute-start | bytes 2359304 | tf_op jit(solution)/shard_map/ppermute | solution.py:49
  64.5 31.5 %collective-permute-start.13 = (bf16[384,768]{1,0:T(8,128)(2,1)}, bf16[384,768]{1,0:T(8,128)(2,1)S(1)}, u32[]{:S(2)}, u32[]{:S(2)}) collective-permute-start(bf16[384,768]{1,0:T(8,128)(2,1)} %get-tuple-element.93), channel_id=1, source_target_pairs={{0,4},{4,8},{8,12},{12,16},{16,20},{20,24},{24,28},{1,5},{5,9},{9,... | collective-permute-start | bytes 1769480 | tf_op jit(solution)/shard_map/ppermute | solution.py:44
  119.2 4.6 %collective-permute-start.14 = (bf16[1024,768]{1,0:T(8,128)(2,1)}, bf16[1024,768]{1,0:T(8,128)(2,1)S(1)}, u32[]{:S(2)}, u32[]{:S(2)}) collective-permute-start(bf16[1024,768]{1,0:T(8,128)(2,1)} %get-tuple-element.99), channel_id=1, source_target_pairs={{0,1},{1,0},{2,3},{3,2},{4,5},{5,4},{6,7},{7,6},{8,9},{9,8},{10,11... | collective-permute-start | bytes 4718600 | tf_op jit(solution)/shard_map/ppermute | solution.py:49
  123.8 20.6 %copy-start.6 = (bf16[1024,768]{1,0:T(8,128)(2,1)}, bf16[1024,768]{1,0:T(8,128)(2,1)S(1)}, u32[]{:S(2)}) copy-start(bf16[1024,768]{1,0:T(8,128)(2,1)S(1)} %collective-permute-done.14) | copy-start | bytes 4718596
  124.0 26.5 %collective-permute-start.16 = (bf16[512,768]{1,0:T(8,128)(2,1)S(1)}, bf16[512,768]{1,0:T(8,128)(2,1)S(1)}, u32[]{:S(2)}, u32[]{:S(2)}) collective-permute-start(bf16[512,768]{1,0:T(8,128)(2,1)S(1)} %add_convert_fusion.2), channel_id=1, source_target_pairs={{0,2},{1,3},{2,0},{3,1},{4,6},{5,7},{6,4},{7,5},{8,10},{9,11},{10,... | collective-permute-start | bytes 2359304 | tf_op jit(solution)/shard_map/ppermute | solution.py:49
  125.2 25.2 %collective-permute-start.15 = (bf16[384,768]{1,0:T(8,128)(2,1)S(1)}, bf16[384,768]{1,0:T(8,128)(2,1)S(1)}, u32[]{:S(2)}, u32[]{:S(2)}) collective-permute-start(bf16[384,768]{1,0:T(8,128)(2,1)S(1)} %copy-done.30), channel_id=1, source_target_pairs={{4,0},{8,4},{12,8},{16,12},{20,16},{24,20},{28,24},{5,1},{9,5},{13... | collective-permute-start | bytes 1769480 | tf_op jit(solution)/shard_map/ppermute | solution.py:44
  150.5 12.0 %copy-start.13 = (bf16[512,768]{1,0:T(8,128)(2,1)}, bf16[512,768]{1,0:T(8,128)(2,1)S(1)}, u32[]{:S(2)}) copy-start(bf16[512,768]{1,0:T(8,128)(2,1)S(1)} %collective-permute-done.16) | copy-start | bytes 2359300
  162.5 3.7 %collective-permute-start.17 = (bf16[1024,768]{1,0:T(8,128)(2,1)}, bf16[1024,768]{1,0:T(8,128)(2,1)S(1)}, u32[]{:S(2)}, u32[]{:S(2)}) collective-permute-start(bf16[1024,768]{1,0:T(8,128)(2,1)} %get-tuple-element.118), channel_id=1, source_target_pairs={{0,1},{1,0},{2,3},{3,2},{4,5},{5,4},{6,7},{7,6},{8,9},{9,8},{10,11... | collective-permute-start | bytes 4718600 | tf_op jit(solution)/shard_map/ppermute | solution.py:49
  166.2 18.4 %copy-start.2 = (bf16[1024,768]{1,0:T(8,128)(2,1)}, bf16[1024,768]{1,0:T(8,128)(2,1)S(1)}, u32[]{:S(2)}) copy-start(bf16[1024,768]{1,0:T(8,128)(2,1)S(1)} %collective-permute-done.17.came_ref) | copy-start | bytes 4718596
  178.3 7.0 %copy-start.14 = (bf16[512,768]{1,0:T(8,128)(2,1)S(1)}, bf16[512,768]{1,0:T(8,128)(2,1)}, u32[]{:S(2)}) copy-start(bf16[512,768]{1,0:T(8,128)(2,1)} %copy-done.13) | copy-start | bytes 2359300
  184.6 11.2 %collective-permute-start.18 = (bf16[384,384]{1,0:T(8,128)(2,1)}, bf16[384,384]{1,0:T(8,128)(2,1)S(1)}, u32[]{:S(2)}, u32[]{:S(2)}) collective-permute-start(bf16[384,384]{1,0:T(8,128)(2,1)} %get-tuple-element.127), channel_id=1, source_target_pairs={{0,4},{4,0},{8,12},{12,8},{16,20},{20,16},{24,28},{28,24},{1,5},{5... | collective-permute-start | bytes 884744 | tf_op jit(solution)/shard_map/ppermute | solution.py:49
  186.6 30.0 %collective-permute-start.26 = (bf16[512,768]{1,0:T(8,128)(2,1)S(1)}, bf16[512,768]{1,0:T(8,128)(2,1)S(1)}, u32[]{:S(2)}, u32[]{:S(2)}) collective-permute-start(bf16[512,768]{1,0:T(8,128)(2,1)S(1)} %copy-done.12), channel_id=1, source_target_pairs={{0,2},{1,3},{2,0},{3,1},{4,6},{5,7},{6,4},{7,5},{8,10},{9,11},{10,... | collective-permute-start | bytes 2359304 | tf_op jit(solution)/shard_map/ppermute | solution.py:49
  188.1 9.0 %copy-start.20 = (bf16[384,384]{1,0:T(8,128)(2,1)S(1)}, bf16[384,384]{1,0:T(8,128)(2,1)}, u32[]{:S(2)}) copy-start(bf16[384,384]{1,0:T(8,128)(2,1)} %get-tuple-element.130) | copy-start | bytes 884740
  195.7 9.9 %copy-start.19 = (bf16[384,512]{1,0:T(8,128)(2,1)S(1)}, bf16[384,512]{1,0:T(8,128)(2,1)}, u32[]{:S(2)}) copy-start(bf16[384,512]{1,0:T(8,128)(2,1)} %get-tuple-element.125) | copy-start | bytes 1179652
  195.7 9.8 %collective-permute-start.19 = (bf16[384,512]{1,0:T(8,128)(2,1)}, bf16[384,512]{1,0:T(8,128)(2,1)S(1)}, u32[]{:S(2)}, u32[]{:S(2)}) collective-permute-start(bf16[384,512]{1,0:T(8,128)(2,1)} %get-tuple-element.128), channel_id=1, source_target_pairs={{0,4},{4,0},{8,12},{12,8},{16,20},{20,16},{24,28},{28,24},{1,5},{5... | collective-permute-start | bytes 1179656 | tf_op jit(solution)/shard_map/ppermute | solution.py:49
  197.2 9.1 %collective-permute-start.23 = (bf16[96,384]{1,0:T(8,128)(2,1)S(1)}, bf16[96,384]{1,0:T(8,128)(2,1)S(1)}, u32[]{:S(2)}, u32[]{:S(2)}) collective-permute-start(bf16[96,384]{1,0:T(8,128)(2,1)S(1)} %get-tuple-element.193), channel_id=1, source_target_pairs={{0,8},{4,12},{8,0},{12,4},{16,24},{20,28},{24,16},{28,20},{1,9},{5... | collective-permute-start | bytes 221192 | tf_op jit(solution)/shard_map/ppermute | solution.py:49
  198.2 11.6 %collective-permute-start.25 = (bf16[96,384]{1,0:T(8,128)(2,1)S(1)}, bf16[96,384]{1,0:T(8,128)(2,1)S(1)}, u32[]{:S(2)}, u32[]{:S(2)}) collective-permute-start(bf16[96,384]{1,0:T(8,128)(2,1)S(1)} %get-tuple-element.194), channel_id=1, source_target_pairs={{0,24},{4,28},{8,16},{12,20},{16,8},{20,12},{24,0},{28,4},{1,25},{... | collective-permute-start | bytes 221192 | tf_op jit(solution)/shard_map/ppermute | solution.py:49
  200.2 9.5 %collective-permute-start.24 = (bf16[96,384]{1,0:T(8,128)(2,1)S(1)}, bf16[96,384]{1,0:T(8,128)(2,1)S(1)}, u32[]{:S(2)}, u32[]{:S(2)}) collective-permute-start(bf16[96,384]{1,0:T(8,128)(2,1)S(1)} %get-tuple-element.195), channel_id=1, source_target_pairs={{0,16},{4,20},{8,24},{12,28},{16,0},{20,4},{24,8},{28,12},{1,17},{... | collective-permute-start | bytes 221192 | tf_op jit(solution)/shard_map/ppermute | solution.py:49
  205.8 5.7 %collective-permute-start.20 = (bf16[96,512]{1,0:T(8,128)(2,1)S(1)}, bf16[96,512]{1,0:T(8,128)(2,1)S(1)}, u32[]{:S(2)}, u32[]{:S(2)}) collective-permute-start(bf16[96,512]{1,0:T(8,128)(2,1)S(1)} %get-tuple-element.190), channel_id=1, source_target_pairs={{0,8},{4,12},{8,0},{12,4},{16,24},{20,28},{24,16},{28,20},{1,9},{5... | collective-permute-start | bytes 294920 | tf_op jit(solution)/shard_map/ppermute | solution.py:49
  206.3 7.2 %collective-permute-start.22 = (bf16[96,512]{1,0:T(8,128)(2,1)S(1)}, bf16[96,512]{1,0:T(8,128)(2,1)S(1)}, u32[]{:S(2)}, u32[]{:S(2)}) collective-permute-start(bf16[96,512]{1,0:T(8,128)(2,1)S(1)} %get-tuple-element.191), channel_id=1, source_target_pairs={{0,24},{4,28},{8,16},{12,20},{16,8},{20,12},{24,0},{28,4},{1,25},{... | collective-permute-start | bytes 294920 | tf_op jit(solution)/shard_map/ppermute | solution.py:49
  209.8 6.9 %collective-permute-start.21 = (bf16[96,512]{1,0:T(8,128)(2,1)S(1)}, bf16[96,512]{1,0:T(8,128)(2,1)S(1)}, u32[]{:S(2)}, u32[]{:S(2)}) collective-permute-start(bf16[96,512]{1,0:T(8,128)(2,1)S(1)} %get-tuple-element.192), channel_id=1, source_target_pairs={{0,16},{4,20},{8,24},{12,28},{16,0},{20,4},{24,8},{28,12},{1,17},{... | collective-permute-start | bytes 294920 | tf_op jit(solution)/shard_map/ppermute | solution.py:49
  221.2 1.3 collective-permute-start.27
  222.5 5.4 %collective-permute-start.28 = (f32[96,128]{1,0:T(8,128)S(1)}, f32[96,128]{1,0:T(8,128)S(1)}, u32[]{:S(2)}, u32[]{:S(2)}) collective-permute-start(f32[96,128]{1,0:T(8,128)S(1)} %slice_add_fusion.3), channel_id=1, source_target_pairs={{0,2},{1,3},{2,0},{3,1},{4,6},{5,7},{6,4},{7,5},{8,10},{9,11},{10,... | collective-permute-start | bytes 147464 | tf_op jit(solution)/shard_map/ppermute | solution.py:49
  (14 other events, 43.4 us)
Sparse Core Ops, SparseCore 0:
  10.8 58.2 all-gather.1
  95.7 82.5 reduce-scatter.1

commit v6 on v5

--- a/solution.py
+++ b/solution.py
@@ -298,6 +298,12 @@
     return jnp.where((idx >= lo_row) & (idx <= hi_row), 0.0, big_negative)
 
 
+def over_chunks(begin, end, step, carry):
+    pairs = (end - begin) // 2
+    carry = lax.fori_loop(0, pairs, lambda n, c: step([begin + 2 * n, begin + 2 * n + 1], c), carry)
+    return lax.fori_loop(begin + 2 * pairs, end, lambda n, c: step([n], c), carry)
+
+
 def attn_fwd_kernel(heads, halo, first_ref, q_ref, k_ref, v_ref, left_ref, lo_ref, o_ref, lse_ref, keys, values):
     i = pl.program_id(0)
     first = first_ref[i]
@@ -314,21 +320,23 @@
     lo_row = lo_ref[...]
     hi_row = halo + i * BLK + lax.broadcasted_iota(jnp.int32, (1, BLK), 1)
 
-    def step(c, carry):
-        cols = pl.ds(pl.multiple_of(c * BLK, BLK), BLK)
-        mask = key_mask(c, lo_row, hi_row)
-        hs = range(heads)
+    def step(chunks, carry):
+        hs, js = range(heads), range(len(chunks))
         feats = [pl.ds(h * HEAD_DIM, HEAD_DIM) for h in hs]
-        s = [mm(keys[feats[h], cols], q_ref[feats[h], :], 0, 0) + mask for h in hs]
-        tops = [jnp.maximum(carry[h][0], jnp.max(s[h], axis=0, keepdims=True)) for h in hs]
-        p = [jnp.exp(s[h] - tops[h]) for h in hs]
-        pv = [mm(values[feats[h], cols], p[h].astype(bf16), 1, 0) for h in hs]
+        cols = [pl.ds(pl.multiple_of(c * BLK, BLK), BLK) for c in chunks]
+        mask = [key_mask(c, lo_row, hi_row) for c in chunks]
+        s = [[mm(keys[feats[h], cols[j]], q_ref[feats[h], :], 0, 0) + mask[j] for j in js] for h in hs]
+        tops = [carry[h][0] for h in hs]
+        for j in js:
+            tops = [jnp.maximum(tops[h], jnp.max(s[h][j], axis=0, keepdims=True)) for h in hs]
+        p = [[jnp.exp(s[h][j] - tops[h]) for j in js] for h in hs]
+        pv = [[mm(values[feats[h], cols[j]], p[h][j].astype(bf16), 1, 0) for j in js] for h in hs]
         kept = [jnp.exp(carry[h][0] - tops[h]) for h in hs]
         return tuple(
             (
                 tops[h],
-                carry[h][1] * kept[h] + jnp.sum(p[h], axis=0, keepdims=True),
-                carry[h][2] * kept[h] + pv[h],
+                carry[h][1] * kept[h] + sum(jnp.sum(p[h][j], axis=0, keepdims=True) for j in js),
+                carry[h][2] * kept[h] + sum(pv[h]),
             )
             for h in hs
         )
@@ -341,7 +349,7 @@
         )
         for _ in range(heads)
     )
-    done = lax.fori_loop(first, last + 1, step, start)
+    done = over_chunks(first, last + 1, step, start)
     for h in range(heads):
         top, total, acc = done[h]
         o_ref[pl.ds(h * HEAD_DIM, HEAD_DIM), :] = (acc / total).astype(bf16)
@@ -370,22 +378,26 @@
     )(first, q, k, v, left, lo)
 
 
-def attn_bwd_step(heads, c, base, q_ref, k_ref, v_ref, do_ref, lse_ref, lo_row, hi_row, deltas, dq_ref, dk_ref, dv_ref):
-    cols = pl.ds(pl.multiple_of((c - base) * BLK, BLK), BLK)
-    mask = key_mask(c, lo_row, hi_row)
-    hs = range(heads)
+def attn_bwd_step(
+    heads, chunks, base, q_ref, k_ref, v_ref, do_ref, lse_ref, lo_row, hi_row, deltas, dq_ref, dk_ref, dv_ref
+):
+    hs, js = range(heads), range(len(chunks))
     feats = [pl.ds(h * HEAD_DIM, HEAD_DIM) for h in hs]
-    s = [mm(k_ref[feats[h], cols], q_ref[feats[h], :], 0, 0) + mask for h in hs]
-    dp = [mm(v_ref[feats[h], cols], do_ref[feats[h], :], 0, 0) for h in hs]
-    p = [jnp.exp(s[h] - lse_ref[pl.ds(h, 1), :]) for h in hs]
-    ds = [(p[h] * (dp[h] - deltas[h])).astype(bf16) for h in hs]
-    dv = [mm(do_ref[feats[h], :], p[h].astype(bf16), 1, 1) for h in hs]
-    dk = [mm(q_ref[feats[h], :], ds[h], 1, 1) for h in hs]
-    dq = [mm(k_ref[feats[h], cols], ds[h], 1, 0) for h in hs]
+    cols = [pl.ds(pl.multiple_of((c - base) * BLK, BLK), BLK) for c in chunks]
+    mask = [key_mask(c, lo_row, hi_row) for c in chunks]
+    both = [(h, j) for h in hs for j in js]
+    s = [mm(k_ref[feats[h], cols[j]], q_ref[feats[h], :], 0, 0) + mask[j] for h, j in both]
+    dp = [mm(v_ref[feats[h], cols[j]], do_ref[feats[h], :], 0, 0) for h, j in both]
+    p = [jnp.exp(s[n] - lse_ref[pl.ds(h, 1), :]) for n, (h, j) in enumerate(both)]
+    ds = [(p[n] * (dp[n] - deltas[h])).astype(bf16) for n, (h, j) in enumerate(both)]
+    dv = [mm(do_ref[feats[h], :], p[n].astype(bf16), 1, 1) for n, (h, j) in enumerate(both)]
+    dk = [mm(q_ref[feats[h], :], ds[n], 1, 1) for n, (h, j) in enumerate(both)]
+    dq = [mm(k_ref[feats[h], cols[j]], ds[n], 1, 0) for n, (h, j) in enumerate(both)]
+    for n, (h, j) in enumerate(both):
+        dv_ref[feats[h], cols[j]] += dv[n]
+        dk_ref[feats[h], cols[j]] += dk[n]
     for h in hs:
-        dv_ref[feats[h], cols] += dv[h]
-        dk_ref[feats[h], cols] += dk[h]
-        dq_ref[feats[h], :] += dq[h]
+        dq_ref[feats[h], :] += sum(dq[n] for n, (at, j) in enumerate(both) if at == h)
 
 
 def row_deltas(heads, o_ref, do_ref):
@@ -418,7 +430,7 @@
         )
         return carry
 
-    lax.fori_loop(first_ref[i], halo // BLK, step, 0)
+    over_chunks(jnp.minimum(first_ref[i], halo // BLK), halo // BLK, step, 0)
 
     @pl.when(i == pl.num_programs(0) - 1)
     def _():
@@ -455,7 +467,7 @@
         )
         return carry
 
-    lax.fori_loop(jnp.maximum(first_ref[i], base), i + base + 1, step, 0)
+    over_chunks(jnp.maximum(first_ref[i], base), i + base + 1, step, 0)
     dq_ref[...] = dq_ref[...] * HEAD_DIM ** (-0.5)
 
 

time: 236 us -> 235 us (level)
  Pallas kernels: 106 us -> 103 us
    ppermute x2, waiting for transfers between devices: 6.05 us -> 8.9 us  [passed_along(): return lax.ppermute(block, axis, route)]
  transfers between devices with their start and end apart: 31 -> 31, of which waited for: 15 -> 15; matrix products, arithmetic and copies ran while one was open for 8% -> 8% of each run, Pallas kernels for 41% -> 40%
where the time goes in v6:
time: 235 us; the launch traced here: 233 us
  Pallas kernels  103 us (44%)
  waiting for transfers between devices  55.9 us (24%)
  starting transfers between devices  31.8 us (14%)
  local copies, waits for them, and re-layouts  19.2 us (8%)
  between operations  14.5 us (6%)
  other arithmetic  8.78 us (4%)
    pallas_call x1, Pallas kernels, feed_forward(): pl.pallas_call(ff_kernel, grid_spec=pltpu.PrefetchScalarGridSpec(num_scal...  22.5 us
    pallas_call x1, Pallas kernels, backward_own(): pl.pallas_call(functools.partial(own_bwd_kernel, heads, halo), grid_spec=...  16.6 us
    ppermute x20, starting transfers between devices, swapped(): return lax.ppermute(block, axis, route)  15.3 us
    pallas_call x2, Pallas kernels, weight_gradient(): pl.pallas_call(functools.partial(weight_grad_kernel, own_dims), grid_spec...  13.9 us
    ppermute x20, waiting for transfers between devices, swapped(): return lax.ppermute(block, axis, route)  13.6 us
    pallas_call x1, Pallas kernels, attention_forward(): pl.pallas_call(functools.partial(attn_fwd_kernel, heads, halo), grid_spec...  12.5 us
    pallas_call x1, Pallas kernels, input_gradient(): pl.pallas_call(functools.partial(input_grad_kernel, halo), grid_spec=pltp...  11.2 us
    pallas_call x1, Pallas kernels, project(): pl.pallas_call(functools.partial(project_kernel, len(pieces), first), gri...  10.9 us
  transfers between devices with their start and end apart: 31, of which 15 were waited for; matrix products, arithmetic and copies ran while one was open for 8% of the time, Pallas kernels for 40%

profile of v6, /device:TPU:0, one launch (start us, length us, event | category | flops | bytes accessed | tf_op | source)
XLA Modules:
  0.0 233.3 jit_solution(521134366544063482)
XLA Ops:
  7.3 1.8 pad_maximum_fusion
  9.2 3.0 %collective-permute-start.6 = (bf16[512,768]{1,0:T(8,128)(2,1)}, bf16[512,768]{1,0:T(8,128)(2,1)}, u32[]{:S(2)}, u32[]{:S(2)}) collective-permute-start(bf16[512,768]{1,0:T(8,128)(2,1)} %x_ref.1), channel_id=1, source_target_pairs={{0,2},{1,3},{2,0},{3,1},{4,6},{5,7},{6,4},{7,5},{8,10},{9,11},{10,... | collective-permute-start | bytes 2359304 | tf_op jit(solution)/shard_map/ppermute | solution.py:49
  13.1 0.9 copy.56
  14.0 1.1 copy.55
  15.3 1.5 collective-permute-start.1
  17.4 3.8 %collective-permute-done.1.refs_6_ = bf16[96,896]{1,0:T(8,128)(2,1)S(1)} collective-permute-done((bf16[96,896]{1,0:T(8,128)(2,1)S(1)}, bf16[96,896]{1,0:T(8,128)(2,1)S(1)}, u32[]{:S(2)}, u32[]{:S(2)}) %collective-permute-start.1) | collective-permute-done | bytes 172064 | tf_op jit(solution)/shard_map/ppermute | solution.py:77
  21.2 1.3 collective-permute-done.refs_5_
  23.1 1.5 collective-permute-start.3
  25.1 0.9 reshape.74.b_ref
  26.0 4.8 %collective-permute-done.2.refs_7_ = bf16[96,896]{1,0:T(8,128)(2,1)} collective-permute-done((bf16[96,896]{1,0:T(8,128)(2,1)}, bf16[96,896]{1,0:T(8,128)(2,1)}, u32[]{:S(2)}, u32[]{:S(2)}) %collective-permute-start.2) | collective-permute-done | bytes 172064 | tf_op jit(solution)/shard_map/ppermute | solution.py:76
  30.8 2.4 %collective-permute-done.3.refs_8_ = bf16[96,896]{1,0:T(8,128)(2,1)} collective-permute-done((bf16[96,896]{1,0:T(8,128)(2,1)S(1)}, bf16[96,896]{1,0:T(8,128)(2,1)}, u32[]{:S(2)}, u32[]{:S(2)}) %collective-permute-start.3) | collective-permute-done | bytes 172064 | tf_op jit(solution)/shard_map/ppermute | solution.py:77
  33.2 1.4 collective-permute-start.4
  35.2 3.6 %collective-permute-done.4.refs_9_ = bf16[96,896]{1,0:T(8,128)(2,1)S(1)} collective-permute-done((bf16[96,896]{1,0:T(8,128)(2,1)}, bf16[96,896]{1,0:T(8,128)(2,1)S(1)}, u32[]{:S(2)}, u32[]{:S(2)}) %collective-permute-start.4) | collective-permute-done | bytes 172064 | tf_op jit(solution)/shard_map/ppermute | solution.py:76
  38.8 2.5 %collective-permute-done.5.refs_10_ = bf16[96,896]{1,0:T(8,128)(2,1)S(1)} collective-permute-done((bf16[96,896]{1,0:T(8,128)(2,1)}, bf16[96,896]{1,0:T(8,128)(2,1)S(1)}, u32[]{:S(2)}, u32[]{:S(2)}) %collective-permute-start.5) | collective-permute-done | bytes 172064 | tf_op jit(solution)/shard_map/ppermute | solution.py:77
  41.3 1.0 multiply_sine_fusion
  42.3 1.7 collective-permute-start.9
  44.0 1.2 dynamic-slice_bitcast_fusion.start_ref
  45.8 6.9 %collective-permute-done.9.refs_11_ = bf16[96,896]{1,0:T(8,128)(2,1)S(1)} collective-permute-done((bf16[96,896]{1,0:T(8,128)(2,1)S(1)}, bf16[96,896]{1,0:T(8,128)(2,1)S(1)}, u32[]{:S(2)}, u32[]{:S(2)}) %collective-permute-start.9) | collective-permute-done | bytes 172064 | tf_op jit(solution)/shard_map/ppermute | solution.py:83
  53.6 10.9 %project.1 = (bf16[192,2048]{1,0:T(8,128)(2,1)}, bf16[192,2048]{1,0:T(8,128)(2,1)}, bf16[192,2048]{1,0:T(8,128)(2,1)}, bf16[384,768]{1,0:T(8,128)(2,1)}, bf16[20...) custom-call(s32[8]{0:T(128)} %dynamic-slice_bitcast_fusion.start_ref, ...), custom_call_target="tpu_custom_call" | custom-call | flops 113246208 | bytes 737280 | tf_op jit(solution)/shard_map/project/pallas_call | solution.py:263
  64.5 7.1 %collective-permute-start.13 = (bf16[384,768]{1,0:T(8,128)(2,1)}, bf16[384,768]{1,0:T(8,128)(2,1)S(1)}, u32[]{:S(2)}, u32[]{:S(2)}) collective-permute-start(bf16[384,768]{1,0:T(8,128)(2,1)} %get-tuple-element.93), channel_id=1, source_target_pairs={{0,4},{4,8},{8,12},{12,16},{16,20},{20,24},{24,28},{1,5},{5,9},{9,... | collective-permute-start | bytes 1769480 | tf_op jit(solution)/shard_map/ppermute | solution.py:44
  73.2 22.5 %feed_forward.1 = (bf16[2048,768]{1,0:T(8,128)(2,1)}, bf16[2048,768]{1,0:T(8,128)(2,1)}, bf16[2048,768]{1,0:T(8,128)(2,1)}, bf16[768,1536]{1,0:T(8,128)(2,1)}, f32[8,768]{1,0:T(8,128)}) custom-call(bf16[2048,768]{1,0:T(8,128)(2,1)} %get-tuple-element.84.x_ref, f32[2048,128]{1,0:T(8,128)} %get-tuple-element.85.stats_ref, f32[1,768]{1,0:T(1,128)} %reshape.73.b_ref, ...), custom_call_target="tpu_custom_call" | custom-call | flops 905969664 | bytes 1081344 | tf_op jit(solution)/shard_map/feed_forward/pallas_call | solution.py:179
  97.1 12.5 %attention_forward.1 = (bf16[192,2048]{1,0:T(8,128)(2,1)}, f32[8,2048]{1,0:T(8,128)}) custom-call(s32[8]{0:T(128)} %and_select_fusion.first_ref, bf16[192,2048]{1,0:T(8,128)(2,1)} %get-tuple-element.90.q_ref, bf16[192,2048]{1,0:T(8,128)(2,1)} %get-tuple-element.91.k_ref, bf16[192,2048]{1,0:T(8,128)(2,1)} %get-tuple-element.92.v_ref, ...), custom_call_target="tpu_custom_call" | custom-call | flops 402653184 | bytes 196608 | tf_op jit(solution)/shard_map/attention_forward/pallas_call | solution.py:365
  109.6 7.6 %branch_out.1 = (bf16[1024,768]{1,0:T(8,128)(2,1)}, bf16[1024,768]{1,0:T(8,128)(2,1)}, bf16[192,2048]{1,0:T(8,128)(2,1)}) custom-call(s32[4]{0:T(128)} %pad_add_fusion.place_ref, bf16[192,2048]{1,0:T(8,128)(2,1)} %get-tuple-element.94.o_ref.refs_0_, bf16[2048,768]{1,0:T(8,128)(2,1)} %get-tuple-element.95.ff_ref, ...), custom_call_target="tpu_custom_call" | custom-call | flops 75497472 | bytes 589824 | tf_op jit(solution)/shard_map/branch_out/pallas_call | solution.py:574
  117.5 4.4 %attention_backward_left.1 = (f32[192,768]{1,0:T(8,128)}, bf16[384,768]{1,0:T(8,128)(2,1)}) custom-call(s32[8]{0:T(128)} %and_select_fusion.first_ref, bf16[192,2048]{1,0:T(8,128)(2,1)} %get-tuple-element.90.q_ref, bf16[384,768]{1,0:T(8,128)(2,1)} %copy-done.4, s32[1,2048]{1,0:T(1,128)} %bitcast.40, bf16[192,2048]{1,0:T(8,128)(2,1)} %get-tuple-element.94.o_ref.refs_0_, ...), custom_call_target="tpu_custom_call" | custom-call | flops 188743680 | bytes 184320 | tf_op jit(solution)/shard_map/attention_backward_left/pallas_call | solution.py:480
  122.2 1.1 copy-done.30
  123.3 1.5 collective-permute-start.15
  124.9 16.6 %attention_backward_own.1 = (f32[192,2048]{1,0:T(8,128)}, f32[192,2048]{1,0:T(8,128)}, f32[192,2048]{1,0:T(8,128)}) custom-call(s32[8]{0:T(128)} %and_select_fusion.first_ref, bf16[192,2048]{1,0:T(8,128)(2,1)} %get-tuple-element.90.q_ref, bf16[192,2048]{1,0:T(8,128)(2,1)} %get-tuple-element.91.k_ref, bf16[192,2048]{1,0:T(8,128)(2,1)} %get-tuple-element.92.v_ref, ...), custom_call_target="tpu_custom_call" | custom-call | flops 1006632960 | bytes 491520 | tf_op jit(solution)/shard_map/attention_backward_own/pallas_call | solution.py:510
  141.5 8.9 %collective-permute-done.15.back_ref = bf16[384,768]{1,0:T(8,128)(2,1)S(1)} collective-permute-done((bf16[384,768]{1,0:T(8,128)(2,1)S(1)}, bf16[384,768]{1,0:T(8,128)(2,1)S(1)}, u32[]{:S(2)}, u32[]{:S(2)}) %collective-permute-start.15) | collective-permute-done | bytes 589856 | tf_op jit(solution)/shard_map/ppermute | solution.py:44
  151.2 11.2 %input_gradient.1 = (bf16[1024,768]{1,0:T(8,128)(2,1)}, bf16[1024,768]{1,0:T(8,128)(2,1)}, bf16[576,2048]{1,0:T(8,128)(2,1)}, f32[8,768]{1,0:T(8,128)}, f32[576,1]{1,0:T(8,128)}) custom-call(s32[4]{0:T(128)} %pad_add_fusion.place_ref, f32[192,2048]{1,0:T(8,128)} %get-tuple-element.109.dq_ref, f32[192,2048]{1,0:T(8,128)} %get-tuple-element.110.dk_ref, ...), custom_call_target="tpu_custom_call" | custom-call | flops 226492416 | bytes 983040 | tf_op jit(solution)/shard_map/input_gradient/pallas_call | solution.py:644
  164.1 2.1 collective-permute-done.17.came_ref
  166.1 2.8 %add_convert_fusion = bf16[512,768]{1,0:T(8,128)(2,1)} fusion(bf16[1024,768]{1,0:T(8,128)(2,1)S(1)} %collective-permute-done.17.came_ref, bf16[1024,768]{1,0:T(8,128)(2,1)} %get-tuple-element.117.own_ref), kind=kLoop, calls=%fused_computation | loop fusion | flops 1572864 | bytes 2359296 | tf_op jit(solution)/shard_map/convert_element_type | solution.py:94
  168.9 8.1 %reduce-scatter.2.cloned.1.call-done = bf16[96,1536]{1,0:T(8,128)(2,1)} async-done(((bf16[768,1536]{1,0:T(8,128)(2,1)}), bf16[96,1536]{1,0:T(8,128)(2,1)}) %reduce-scatter.2.cloned.1.call-update) | async-done | bytes 294928 | tf_op jit(solution)/shard_map/reduce_scatter | solution.py:863
  177.1 6.3 %weight_gradient.2 = (bf16[384,384]{1,0:T(8,128)(2,1)}, bf16[384,384]{1,0:T(8,128)(2,1)}) custom-call(s32[4]{0:T(128)} %pad_add_fusion.place_ref, s32[8]{0:T(128)} %concatenate.15.chunk_ref, bf16[576,2048]{1,0:T(8,128)(2,1)} %get-tuple-element.121.grad_ref, bf16[2048,768]{1,0:T(8,128)(2,1)} %get-tuple-element.119.normed_ref), custom_call_target="tpu_custom_call" | custom-call | flops 150994944 | bytes 393216 | tf_op jit(solution)/shard_map/weight_gradient/pallas_call | solution.py:710
  184.1 1.4 add_convert_fusion.1
  185.5 1.5 collective-permute-start.26
  186.9 7.6 %weight_gradient.3 = (bf16[384,512]{1,0:T(8,128)(2,1)}, bf16[384,512]{1,0:T(8,128)(2,1)}) custom-call(s32[4]{0:T(128)} %pad_add_fusion.place_ref, s32[8]{0:T(128)} %concatenate.15.chunk_ref, bf16[576,2048]{1,0:T(8,128)(2,1)} %get-tuple-element.121.grad_ref, bf16[2048,768]{1,0:T(8,128)(2,1)} %get-tuple-element.119.normed_ref, ...), custom_call_target="tpu_custom_call" | custom-call | flops 75497472 | bytes 393216 | tf_op jit(solution)/shard_map/weight_gradient/pallas_call | solution.py:710
  194.6 1.4 collective-permute-start.19
  196.1 1.0 collective-permute-start.23
  197.0 2.0 collective-permute-start.25
  199.6 4.8 %collective-permute-done.19 = bf16[384,512]{1,0:T(8,128)(2,1)S(1)} collective-permute-done((bf16[384,512]{1,0:T(8,128)(2,1)}, bf16[384,512]{1,0:T(8,128)(2,1)S(1)}, u32[]{:S(2)}, u32[]{:S(2)}) %collective-permute-start.19) | collective-permute-done | bytes 393248 | tf_op jit(solution)/shard_map/ppermute | solution.py:49
  205.1 1.9 collective-permute-start.22
  207.0 1.2 collective-permute-start.21
  208.2 1.1 collective-permute-done.20
  209.3 2.2 collective-permute-done.22
  211.6 2.9 %collective-permute-done.21 = bf16[96,512]{1,0:T(8,128)(2,1)S(1)} collective-permute-done((bf16[96,512]{1,0:T(8,128)(2,1)S(1)}, bf16[96,512]{1,0:T(8,128)(2,1)S(1)}, u32[]{:S(2)}, u32[]{:S(2)}) %collective-permute-start.21) | collective-permute-done | bytes 98336 | tf_op jit(solution)/shard_map/ppermute | solution.py:49
  214.6 0.9 copy-done.11
  215.5 3.4 %norm_back.1 = bf16[512,768]{1,0:T(8,128)(2,1)} custom-call(bf16[1024,768]{1,0:T(8,128)(2,1)} %get-tuple-element.117.own_ref, bf16[1024,768]{1,0:T(8,128)(2,1)} %copy-done.2, bf16[512,768]{1,0:T(8,128)(2,1)} %copy-done.11, bf16[512,768]{1,0:T(8,128)(2,1)} %x_ref.1, f32[2048,128]{1,0:T(8,128)} %get-tuple-element.85.stats_ref, bf16[512,768]{1,0:T(8,128)(2,1)} %g_ref.1), custom_call_target="tpu_custom_call" | custom-call | flops 491520 | bytes 294912 | tf_op jit(solution)/shard_map/norm_back/pallas_call | solution.py:741
  224.3 0.9 copy.63
  (137 shorter events, 19.8 us)
Async XLA Ops:
  7.2 31.6 %copy-start = (bf16[512,768]{1,0:T(8,128)(2,1)S(1)}, bf16[512,768]{1,0:T(8,128)(2,1)}, u32[]{:S(2)}) copy-start(bf16[512,768]{1,0:T(8,128)(2,1)} %x_ref.1) | copy-start | bytes 2359300
  7.2 17.4 %copy-start.3 = (bf16[512,768]{1,0:T(8,128)(2,1)S(1)}, bf16[512,768]{1,0:T(8,128)(2,1)}, u32[]{:S(2)}) copy-start(bf16[512,768]{1,0:T(8,128)(2,1)} %g_ref.1) | copy-start | bytes 2359300
  7.2 17.9 %copy-start.27 = (bf16[3,192]{1,0:T(4,128)(2,1)S(1)}, bf16[3,192]{1,0:T(4,128)(2,1)}, u32[]{:S(2)}) copy-start(bf16[3,192]{1,0:T(4,128)(2,1)} %param.19) | copy-start | bytes 3460
  7.2 28.0 %copy-start.26 = (s32[2048]{0:T(1024)S(1)}, s32[2048]{0:T(1024)}, u32[]{:S(2)}) copy-start(s32[2048]{0:T(1024)} %param.30) | copy-start | bytes 24580
  7.2 65.1 %all-gather.2.cloned.1.call-start = ((), (), s32[]{:S(2)}) async-start(), calls=%async_computation.1 | async-start | bytes 2654208 | tf_op jit(solution)/shard_map/all_gather | solution.py:837
  9.1 167.9 %reduce-scatter.2.cloned.1.call-start = ((), (), s32[]{:S(2)}) async-start(), calls=%async_computation.2 | async-start | bytes 2654208 | tf_op jit(solution)/shard_map/reduce_scatter | solution.py:863
  9.2 32.1 %collective-permute-start.6 = (bf16[512,768]{1,0:T(8,128)(2,1)}, bf16[512,768]{1,0:T(8,128)(2,1)}, u32[]{:S(2)}, u32[]{:S(2)}) collective-permute-start(bf16[512,768]{1,0:T(8,128)(2,1)} %x_ref.1), channel_id=1, source_target_pairs={{0,2},{1,3},{2,0},{3,1},{4,6},{5,7},{6,4},{7,5},{8,10},{9,11},{10,... | collective-permute-start | bytes 2359304 | tf_op jit(solution)/shard_map/ppermute | solution.py:49
  15.3 37.3 %copy-start.17 = (bf16[96,896]{1,0:T(8,128)(2,1)}, bf16[96,896]{1,0:T(8,128)(2,1)S(1)}, u32[]{:S(2)}) copy-start(bf16[96,896]{1,0:T(8,128)(2,1)S(1)} %fusion.3.refs_4_) | copy-start | bytes 516100
  15.3 5.9 %collective-permute-start.1 = (bf16[96,896]{1,0:T(8,128)(2,1)S(1)}, bf16[96,896]{1,0:T(8,128)(2,1)S(1)}, u32[]{:S(2)}, u32[]{:S(2)}) collective-permute-start(bf16[96,896]{1,0:T(8,128)(2,1)S(1)} %fusion.3.refs_4_), channel_id=1, source_target_pairs={{8,0},{16,8},{24,16},{28,24},{20,28},{12,20},{4,12},{0,4},{9,1},{1... | collective-permute-start | bytes 516104 | tf_op jit(solution)/shard_map/ppermute | solution.py:77
  16.9 5.7 %collective-permute-start = (bf16[96,896]{1,0:T(8,128)(2,1)S(1)}, bf16[96,896]{1,0:T(8,128)(2,1)}, u32[]{:S(2)}, u32[]{:S(2)}) collective-permute-start(bf16[96,896]{1,0:T(8,128)(2,1)S(1)} %fusion.3.refs_4_), channel_id=1, source_target_pairs={{0,8},{8,16},{16,24},{24,28},{28,20},{20,12},{12,4},{4,0},{1,9},{9... | collective-permute-start | bytes 516104 | tf_op jit(solution)/shard_map/ppermute | solution.py:76
  21.2 31.4 %copy-start.21 = (bf16[96,896]{1,0:T(8,128)(2,1)}, bf16[96,896]{1,0:T(8,128)(2,1)S(1)}, u32[]{:S(2)}) copy-start(bf16[96,896]{1,0:T(8,128)(2,1)S(1)} %collective-permute-done.1.refs_6_) | copy-start | bytes 516100
  22.5 8.3 %collective-permute-start.2 = (bf16[96,896]{1,0:T(8,128)(2,1)}, bf16[96,896]{1,0:T(8,128)(2,1)}, u32[]{:S(2)}, u32[]{:S(2)}) collective-permute-start(bf16[96,896]{1,0:T(8,128)(2,1)} %collective-permute-done.refs_5_), channel_id=1, source_target_pairs={{0,8},{8,16},{16,24},{24,28},{28,20},{20,12},{12,4},{4,0},{1,9},{9... | collective-permute-start | bytes 516104 | tf_op jit(solution)/shard_map/ppermute | solution.py:76
  23.1 10.1 %collective-permute-start.3 = (bf16[96,896]{1,0:T(8,128)(2,1)S(1)}, bf16[96,896]{1,0:T(8,128)(2,1)}, u32[]{:S(2)}, u32[]{:S(2)}) collective-permute-start(bf16[96,896]{1,0:T(8,128)(2,1)S(1)} %collective-permute-done.1.refs_6_), channel_id=1, source_target_pairs={{8,0},{16,8},{24,16},{28,24},{20,28},{12,20},{4,12},{0,4},{9,1},{1... | collective-permute-start | bytes 516104 | tf_op jit(solution)/shard_map/ppermute | solution.py:77
  24.6 47.8 %collective-permute-start.11 = (bf16[512,768]{1,0:T(8,128)(2,1)S(1)}, bf16[512,768]{1,0:T(8,128)(2,1)S(1)}, u32[]{:S(2)}, u32[]{:S(2)}) collective-permute-start(bf16[512,768]{1,0:T(8,128)(2,1)S(1)} %copy-done.3), channel_id=1, source_target_pairs={{0,1},{1,0},{2,3},{3,2},{4,5},{5,4},{6,7},{7,6},{8,9},{9,8},{10,11... | collective-permute-start | bytes 2359304 | tf_op jit(solution)/shard_map/ppermute | solution.py:49
  24.6 39.9 %collective-permute-start.10 = (bf16[512,768]{1,0:T(8,128)(2,1)S(1)}, bf16[512,768]{1,0:T(8,128)(2,1)S(1)}, u32[]{:S(2)}, u32[]{:S(2)}) collective-permute-start(bf16[512,768]{1,0:T(8,128)(2,1)S(1)} %copy-done.3), channel_id=1, source_target_pairs={{0,2},{1,3},{2,0},{3,1},{4,6},{5,7},{6,4},{7,5},{8,10},{9,11},{10,... | collective-permute-start | bytes 2359304 | tf_op jit(solution)/shard_map/ppermute | solution.py:49
  33.2 5.6 %collective-permute-start.4 = (bf16[96,896]{1,0:T(8,128)(2,1)}, bf16[96,896]{1,0:T(8,128)(2,1)S(1)}, u32[]{:S(2)}, u32[]{:S(2)}) collective-permute-start(bf16[96,896]{1,0:T(8,128)(2,1)} %collective-permute-done.2.refs_7_), channel_id=1, source_target_pairs={{0,8},{8,16},{16,24},{24,28},{28,20},{20,12},{12,4},{4,0},{1,9},{9... | collective-permute-start | bytes 516104 | tf_op jit(solution)/shard_map/ppermute | solution.py:76
  34.6 6.8 %collective-permute-start.5 = (bf16[96,896]{1,0:T(8,128)(2,1)}, bf16[96,896]{1,0:T(8,128)(2,1)S(1)}, u32[]{:S(2)}, u32[]{:S(2)}) collective-permute-start(bf16[96,896]{1,0:T(8,128)(2,1)} %collective-permute-done.3.refs_8_), channel_id=1, source_target_pairs={{8,0},{16,8},{24,16},{28,24},{20,28},{12,20},{4,12},{0,4},{9,1},{1... | collective-permute-start | bytes 516104 | tf_op jit(solution)/shard_map/ppermute | solution.py:77
  35.2 37.0 %copy-start.25 = (s32[2048]{0:T(1024)}, s32[2048]{0:T(1024)S(1)}, u32[]{:S(2)}) copy-start(s32[2048]{0:T(1024)S(1)} %get-tuple-element.199) | copy-start | bytes 24580
  38.8 13.8 %copy-start.22 = (bf16[96,896]{1,0:T(8,128)(2,1)}, bf16[96,896]{1,0:T(8,128)(2,1)S(1)}, u32[]{:S(2)}) copy-start(bf16[96,896]{1,0:T(8,128)(2,1)S(1)} %collective-permute-done.4.refs_9_) | copy-start | bytes 516100
  38.8 6.9 %collective-permute-start.7 = (bf16[512,768]{1,0:T(8,128)(2,1)S(1)}, bf16[512,768]{1,0:T(8,128)(2,1)S(1)}, u32[]{:S(2)}, u32[]{:S(2)}) collective-permute-start(bf16[512,768]{1,0:T(8,128)(2,1)S(1)} %copy-done), channel_id=1, source_target_pairs={{0,1},{1,0},{2,3},{3,2},{4,5},{5,4},{6,7},{7,6},{8,9},{9,8},{10,11... | collective-permute-start | bytes 2359304 | tf_op jit(solution)/shard_map/ppermute | solution.py:49
  41.3 11.4 %copy-start.23 = (bf16[96,896]{1,0:T(8,128)(2,1)}, bf16[96,896]{1,0:T(8,128)(2,1)S(1)}, u32[]{:S(2)}) copy-start(bf16[96,896]{1,0:T(8,128)(2,1)S(1)} %collective-permute-done.5.refs_10_) | copy-start | bytes 516100
  41.3 11.3 %collective-permute-start.8 = (bf16[512,768]{1,0:T(8,128)(2,1)}, bf16[512,768]{1,0:T(8,128)(2,1)S(1)}, u32[]{:S(2)}, u32[]{:S(2)}) collective-permute-start(bf16[512,768]{1,0:T(8,128)(2,1)} %collective-permute-done.6.refs_1_), channel_id=1, source_target_pairs={{0,1},{1,0},{2,3},{3,2},{4,5},{5,4},{6,7},{7,6},{8,9},{9,8},{10,11... | collective-permute-start | bytes 2359304 | tf_op jit(solution)/shard_map/ppermute | solution.py:49
  42.3 10.3 %collective-permute-start.9 = (bf16[96,896]{1,0:T(8,128)(2,1)S(1)}, bf16[96,896]{1,0:T(8,128)(2,1)S(1)}, u32[]{:S(2)}, u32[]{:S(2)}) collective-permute-start(bf16[96,896]{1,0:T(8,128)(2,1)S(1)} %collective-permute-done.4.refs_9_), channel_id=1, source_target_pairs={{0,8},{8,16},{16,24},{24,28},{28,20},{20,12},{12,4},{4,0},{1,9},{9... | collective-permute-start | bytes 516104 | tf_op jit(solution)/shard_map/ppermute | solution.py:83
  53.6 18.1 %copy-start.28 = (bf16[768]{0:T(1024)(128)(2,1)S(1)}, bf16[768]{0:T(1024)(128)(2,1)}, u32[]{:S(2)}) copy-start(bf16[768]{0:T(1024)(128)(2,1)} %param.23) | copy-start | bytes 4612
  64.4 7.9 %copy-start.10 = (bf16[512,768]{1,0:T(8,128)(2,1)}, bf16[512,768]{1,0:T(8,128)(2,1)S(1)}, u32[]{:S(2)}) copy-start(bf16[512,768]{1,0:T(8,128)(2,1)S(1)} %collective-permute-done.10.refs_1_) | copy-start | bytes 2359300
  64.5 7.9 %collective-permute-start.12 = (bf16[512,768]{1,0:T(8,128)(2,1)S(1)}, bf16[512,768]{1,0:T(8,128)(2,1)}, u32[]{:S(2)}, u32[]{:S(2)}) collective-permute-start(bf16[512,768]{1,0:T(8,128)(2,1)S(1)} %collective-permute-done.10.refs_1_), channel_id=1, source_target_pairs={{0,1},{1,0},{2,3},{3,2},{4,5},{5,4},{6,7},{7,6},{8,9},{9,8},{10,11... | collective-permute-start | bytes 2359304 | tf_op jit(solution)/shard_map/ppermute | solution.py:49
  64.5 31.7 %collective-permute-start.13 = (bf16[384,768]{1,0:T(8,128)(2,1)}, bf16[384,768]{1,0:T(8,128)(2,1)S(1)}, u32[]{:S(2)}, u32[]{:S(2)}) collective-permute-start(bf16[384,768]{1,0:T(8,128)(2,1)} %get-tuple-element.93), channel_id=1, source_target_pairs={{0,4},{4,8},{8,12},{12,16},{16,20},{20,24},{24,28},{1,5},{5,9},{9,... | collective-permute-start | bytes 1769480 | tf_op jit(solution)/shard_map/ppermute | solution.py:44
  117.3 4.6 %collective-permute-start.14 = (bf16[1024,768]{1,0:T(8,128)(2,1)}, bf16[1024,768]{1,0:T(8,128)(2,1)S(1)}, u32[]{:S(2)}, u32[]{:S(2)}) collective-permute-start(bf16[1024,768]{1,0:T(8,128)(2,1)} %get-tuple-element.99), channel_id=1, source_target_pairs={{0,1},{1,0},{2,3},{3,2},{4,5},{5,4},{6,7},{7,6},{8,9},{9,8},{10,11... | collective-permute-start | bytes 4718600 | tf_op jit(solution)/shard_map/ppermute | solution.py:49
  121.9 19.6 %copy-start.6 = (bf16[1024,768]{1,0:T(8,128)(2,1)}, bf16[1024,768]{1,0:T(8,128)(2,1)S(1)}, u32[]{:S(2)}) copy-start(bf16[1024,768]{1,0:T(8,128)(2,1)S(1)} %collective-permute-done.14) | copy-start | bytes 4718596
  122.1 28.3 %collective-permute-start.16 = (bf16[512,768]{1,0:T(8,128)(2,1)S(1)}, bf16[512,768]{1,0:T(8,128)(2,1)S(1)}, u32[]{:S(2)}, u32[]{:S(2)}) collective-permute-start(bf16[512,768]{1,0:T(8,128)(2,1)S(1)} %add_convert_fusion.2), channel_id=1, source_target_pairs={{0,2},{1,3},{2,0},{3,1},{4,6},{5,7},{6,4},{7,5},{8,10},{9,11},{10,... | collective-permute-start | bytes 2359304 | tf_op jit(solution)/shard_map/ppermute | solution.py:49
  123.3 27.1 %collective-permute-start.15 = (bf16[384,768]{1,0:T(8,128)(2,1)S(1)}, bf16[384,768]{1,0:T(8,128)(2,1)S(1)}, u32[]{:S(2)}, u32[]{:S(2)}) collective-permute-start(bf16[384,768]{1,0:T(8,128)(2,1)S(1)} %copy-done.30), channel_id=1, source_target_pairs={{4,0},{8,4},{12,8},{16,12},{20,16},{24,20},{28,24},{5,1},{9,5},{13... | collective-permute-start | bytes 1769480 | tf_op jit(solution)/shard_map/ppermute | solution.py:44
  150.4 12.0 %copy-start.13 = (bf16[512,768]{1,0:T(8,128)(2,1)}, bf16[512,768]{1,0:T(8,128)(2,1)S(1)}, u32[]{:S(2)}) copy-start(bf16[512,768]{1,0:T(8,128)(2,1)S(1)} %collective-permute-done.16) | copy-start | bytes 2359300
  162.5 3.7 %collective-permute-start.17 = (bf16[1024,768]{1,0:T(8,128)(2,1)}, bf16[1024,768]{1,0:T(8,128)(2,1)S(1)}, u32[]{:S(2)}, u32[]{:S(2)}) collective-permute-start(bf16[1024,768]{1,0:T(8,128)(2,1)} %get-tuple-element.118), channel_id=1, source_target_pairs={{0,1},{1,0},{2,3},{3,2},{4,5},{5,4},{6,7},{7,6},{8,9},{9,8},{10,11... | collective-permute-start | bytes 4718600 | tf_op jit(solution)/shard_map/ppermute | solution.py:49
  166.1 17.2 %copy-start.2 = (bf16[1024,768]{1,0:T(8,128)(2,1)}, bf16[1024,768]{1,0:T(8,128)(2,1)S(1)}, u32[]{:S(2)}) copy-start(bf16[1024,768]{1,0:T(8,128)(2,1)S(1)} %collective-permute-done.17.came_ref) | copy-start | bytes 4718596
  177.1 7.0 %copy-start.14 = (bf16[512,768]{1,0:T(8,128)(2,1)S(1)}, bf16[512,768]{1,0:T(8,128)(2,1)}, u32[]{:S(2)}) copy-start(bf16[512,768]{1,0:T(8,128)(2,1)} %copy-done.13) | copy-start | bytes 2359300
  183.4 11.2 %collective-permute-start.18 = (bf16[384,384]{1,0:T(8,128)(2,1)}, bf16[384,384]{1,0:T(8,128)(2,1)S(1)}, u32[]{:S(2)}, u32[]{:S(2)}) collective-permute-start(bf16[384,384]{1,0:T(8,128)(2,1)} %get-tuple-element.127), channel_id=1, source_target_pairs={{0,4},{4,0},{8,12},{12,8},{16,20},{20,16},{24,28},{28,24},{1,5},{5... | collective-permute-start | bytes 884744 | tf_op jit(solution)/shard_map/ppermute | solution.py:49
  185.5 29.1 %collective-permute-start.26 = (bf16[512,768]{1,0:T(8,128)(2,1)S(1)}, bf16[512,768]{1,0:T(8,128)(2,1)S(1)}, u32[]{:S(2)}, u32[]{:S(2)}) collective-permute-start(bf16[512,768]{1,0:T(8,128)(2,1)S(1)} %copy-done.12), channel_id=1, source_target_pairs={{0,2},{1,3},{2,0},{3,1},{4,6},{5,7},{6,4},{7,5},{8,10},{9,11},{10,... | collective-permute-start | bytes 2359304 | tf_op jit(solution)/shard_map/ppermute | solution.py:49
  186.9 9.0 %copy-start.20 = (bf16[384,384]{1,0:T(8,128)(2,1)S(1)}, bf16[384,384]{1,0:T(8,128)(2,1)}, u32[]{:S(2)}) copy-start(bf16[384,384]{1,0:T(8,128)(2,1)} %get-tuple-element.130) | copy-start | bytes 884740
  194.6 9.9 %copy-start.19 = (bf16[384,512]{1,0:T(8,128)(2,1)S(1)}, bf16[384,512]{1,0:T(8,128)(2,1)}, u32[]{:S(2)}) copy-start(bf16[384,512]{1,0:T(8,128)(2,1)} %get-tuple-element.125) | copy-start | bytes 1179652
  194.6 9.8 %collective-permute-start.19 = (bf16[384,512]{1,0:T(8,128)(2,1)}, bf16[384,512]{1,0:T(8,128)(2,1)S(1)}, u32[]{:S(2)}, u32[]{:S(2)}) collective-permute-start(bf16[384,512]{1,0:T(8,128)(2,1)} %get-tuple-element.128), channel_id=1, source_target_pairs={{0,4},{4,0},{8,12},{12,8},{16,20},{20,16},{24,28},{28,24},{1,5},{5... | collective-permute-start | bytes 1179656 | tf_op jit(solution)/shard_map/ppermute | solution.py:49
  196.1 9.0 %collective-permute-start.23 = (bf16[96,384]{1,0:T(8,128)(2,1)S(1)}, bf16[96,384]{1,0:T(8,128)(2,1)S(1)}, u32[]{:S(2)}, u32[]{:S(2)}) collective-permute-start(bf16[96,384]{1,0:T(8,128)(2,1)S(1)} %get-tuple-element.193), channel_id=1, source_target_pairs={{0,8},{4,12},{8,0},{12,4},{16,24},{20,28},{24,16},{28,20},{1,9},{5... | collective-permute-start | bytes 221192 | tf_op jit(solution)/shard_map/ppermute | solution.py:49
  197.0 9.9 %collective-permute-start.25 = (bf16[96,384]{1,0:T(8,128)(2,1)S(1)}, bf16[96,384]{1,0:T(8,128)(2,1)S(1)}, u32[]{:S(2)}, u32[]{:S(2)}) collective-permute-start(bf16[96,384]{1,0:T(8,128)(2,1)S(1)} %get-tuple-element.194), channel_id=1, source_target_pairs={{0,24},{4,28},{8,16},{12,20},{16,8},{20,12},{24,0},{28,4},{1,25},{... | collective-permute-start | bytes 221192 | tf_op jit(solution)/shard_map/ppermute | solution.py:49
  199.0 9.2 %collective-permute-start.24 = (bf16[96,384]{1,0:T(8,128)(2,1)S(1)}, bf16[96,384]{1,0:T(8,128)(2,1)S(1)}, u32[]{:S(2)}, u32[]{:S(2)}) collective-permute-start(bf16[96,384]{1,0:T(8,128)(2,1)S(1)} %get-tuple-element.195), channel_id=1, source_target_pairs={{0,16},{4,20},{8,24},{12,28},{16,0},{20,4},{24,8},{28,12},{1,17},{... | collective-permute-start | bytes 221192 | tf_op jit(solution)/shard_map/ppermute | solution.py:49
  204.6 4.8 %collective-permute-start.20 = (bf16[96,512]{1,0:T(8,128)(2,1)S(1)}, bf16[96,512]{1,0:T(8,128)(2,1)S(1)}, u32[]{:S(2)}, u32[]{:S(2)}) collective-permute-start(bf16[96,512]{1,0:T(8,128)(2,1)S(1)} %get-tuple-element.190), channel_id=1, source_target_pairs={{0,8},{4,12},{8,0},{12,4},{16,24},{20,28},{24,16},{28,20},{1,9},{5... | collective-permute-start | bytes 294920 | tf_op jit(solution)/shard_map/ppermute | solution.py:49
  205.1 6.5 %collective-permute-start.22 = (bf16[96,512]{1,0:T(8,128)(2,1)S(1)}, bf16[96,512]{1,0:T(8,128)(2,1)S(1)}, u32[]{:S(2)}, u32[]{:S(2)}) collective-permute-start(bf16[96,512]{1,0:T(8,128)(2,1)S(1)} %get-tuple-element.191), channel_id=1, source_target_pairs={{0,24},{4,28},{8,16},{12,20},{16,8},{20,12},{24,0},{28,4},{1,25},{... | collective-permute-start | bytes 294920 | tf_op jit(solution)/shard_map/ppermute | solution.py:49
  207.0 7.5 %collective-permute-start.21 = (bf16[96,512]{1,0:T(8,128)(2,1)S(1)}, bf16[96,512]{1,0:T(8,128)(2,1)S(1)}, u32[]{:S(2)}, u32[]{:S(2)}) collective-permute-start(bf16[96,512]{1,0:T(8,128)(2,1)S(1)} %get-tuple-element.192), channel_id=1, source_target_pairs={{0,16},{4,20},{8,24},{12,28},{16,0},{20,4},{24,8},{28,12},{1,17},{... | collective-permute-start | bytes 294920 | tf_op jit(solution)/shard_map/ppermute | solution.py:49
  219.1 1.3 collective-permute-start.27
  220.4 4.8 %collective-permute-start.28 = (f32[96,128]{1,0:T(8,128)S(1)}, f32[96,128]{1,0:T(8,128)S(1)}, u32[]{:S(2)}, u32[]{:S(2)}) collective-permute-start(f32[96,128]{1,0:T(8,128)S(1)} %slice_add_fusion.3), channel_id=1, source_target_pairs={{0,2},{1,3},{2,0},{3,1},{4,6},{5,7},{6,4},{7,5},{8,10},{9,11},{10,... | collective-permute-start | bytes 147464 | tf_op jit(solution)/shard_map/ppermute | solution.py:49
  (14 other events, 43.4 us)
Sparse Core Ops, SparseCore 0:
  10.8 58.2 all-gather.1
  95.8 81.1 reduce-scatter.1
